TPU v7x, 32 devices: a whole 2x2x4 slice. The times are simulated.
32 devices in a mesh: dp: 8 (over y, x, core), mp: 4 (over z).
Axes of the slice: x: 2, y: 2, z: 4, core: 2. Of those that a mesh axis runs over, the one named last changes fastest.
Arguments:
- inputs: bfloat16 [16384, 768], P(('dp', 'mp')), may hold values from -6 to 6
- gain_attn: bfloat16 [768], replicated, may hold values from 0.5 to 1.5
- w_query: bfloat16 [768, 768], P(None, 'mp'), may hold values from -0.109375 to 0.109375
- w_key: bfloat16 [768, 768], P(None, 'mp'), may hold values from -0.109375 to 0.109375
- w_value: bfloat16 [768, 768], P(None, 'mp'), may hold values from -0.21875 to 0.21875
- w_out: bfloat16 [768, 768], P('mp'), may hold values from -1.25 to 1.25
- rel_table: bfloat16 [32, 12], P(None, 'mp'), may hold values from -4 to 4
- gain_ffn: bfloat16 [768], replicated, may hold values from 0.5 to 1.5
- w_in: bfloat16 [768, 3072], P(None, 'mp'), may hold values from -0.21875 to 0.21875
- w_down: bfloat16 [3072, 768], P('mp'), may hold values from -0.109375 to 0.109375
- cotangent: bfloat16 [16384, 768], P(('dp', 'mp')), may hold values from -6 to 6
- bucket: int32 [8], P('dp'), may hold values from 256 to 512, as said below
- lengths: int32 [8, 8], P('dp'), may hold values from 0 to 512, as said below
Outputs:
- outputs: bfloat16 [16384, 768], P(('dp', 'mp'))
- grad_inputs: bfloat16 [16384, 768], P(('dp', 'mp'))
- grad_query: float32 [768, 768], P(None, 'mp')
- grad_key: float32 [768, 768], P(None, 'mp')
- grad_value: float32 [768, 768], P(None, 'mp')
- grad_out: float32 [768, 768], P('mp')
- grad_table: float32 [32, 12], P(None, 'mp')
- grad_gain_attn: float32 [768], replicated
- grad_gain_ffn: float32 [768], replicated
- grad_in: float32 [768, 3072], P(None, 'mp')
- grad_down: float32 [3072, 768], P('mp')
Inputs may be any that keep to these rules, and one draw needn't show every extreme that they name: `bucket`: half of the indices of dp hold 512 and the other half 512 // 2. `lengths`: the sequences of index i of dp fill its 2048 rows in slots of bucket[i] rows; slots beyond 2048 // bucket[i] hold 0; a used slot holds max(bucket[i] // 4, 1) to bucket[i], and one used slot of each index holds exactly bucket[i].
All inputs are finite; a program needn't handle non-finite values.
Results may differ from a plain program's by a relative error of at most 0.014.
The roundings to bfloat16 on the way count: a program that leaves them out, or rounds other values in their place, can miss the bound.
Values may be sent and summed in bfloat16 or wider, within the bound.
No kernel may reach another device: no remote copies, remote signals or barrier semaphores. Data moves between devices by JAX's collectives and lax.ppermute only.
A program may use at most 128 MiB of HBM per device.

v0:
```python
import jax
import jax.numpy as jnp
from jax import lax
from jax.sharding import PartitionSpec as P

BIG = 512


EPS = 1e-06
THRESHOLDS = (12, 16, 23, 32, 46, 64, 91)
MASKED = -1e30


def offset_buckets(block_rows):
    offsets = jnp.arange(2 * block_rows - 1, dtype=jnp.int32) - (block_rows - 1)
    distance = jnp.abs(offsets)
    far_part = 8 + sum(((distance >= threshold).astype(jnp.int32) for threshold in THRESHOLDS))
    nearby = jnp.where(distance < 8, distance, far_part)
    return nearby + jnp.where(offsets > 0, 16, 0).astype(jnp.int32)


def toeplitz_rows(relative, block_rows):
    head_count = relative.shape[0]
    padded = jnp.concatenate([relative, jnp.zeros((head_count, 1), relative.dtype)], axis=1)
    tiled = jnp.tile(padded, (1, block_rows))
    window = tiled[:, block_rows - 1 : block_rows - 1 + block_rows * (2 * block_rows - 1)]
    return window.reshape(head_count, block_rows, 2 * block_rows - 1)[:, :, :block_rows]


def rms_forward(values, gain_vec):
    inv_root = lax.rsqrt(jnp.mean(values * values, axis=1, keepdims=True) + EPS)
    unit_rows = values * inv_root
    return (unit_rows, inv_root, unit_rows * gain_vec)


def rms_backward(grad_normed, unit_rows, inv_root, gain_vec):
    grad_unit = grad_normed * gain_vec
    grad_gain = jnp.sum(grad_normed * unit_rows, axis=0)
    centred = grad_unit - unit_rows * jnp.mean(grad_unit * unit_rows, axis=1, keepdims=True)
    return (inv_root * centred, grad_gain)


def block_scores(query_block, key_block, rel_bias, segment_block, valid_block):
    scores = (
        jnp.einsum("qhd,khd->hqk", query_block, key_block, preferred_element_type=jnp.float32)
        + rel_bias
    )
    allowed = (segment_block[:, None] == segment_block[None, :]) & valid_block[None, :]
    return jnp.where(allowed[None], scores, MASKED)


def contract_rows(left_side, right_side):
    return lax.dot_general(
        left_side, right_side, (((0,), (0,)), ((), ())), preferred_element_type=jnp.float32
    )


def contract_cols(left_side, right_side):
    return lax.dot_general(
        left_side, right_side, (((1,), (1,)), ((), ())), preferred_element_type=jnp.float32
    )


def row_masks(row_ids, bucket_size, length_row, block_rows):
    segment = row_ids // bucket_size
    position = row_ids - segment * bucket_size
    slot_index = jnp.arange(length_row.shape[0], dtype=jnp.int32)
    seq_length = jnp.sum(
        jnp.where(segment[:, None] == slot_index[None, :], length_row[None, :], 0), axis=1
    )
    valid_key = position < seq_length
    return (segment.reshape(-1, block_rows), valid_key.reshape(-1, block_rows))


def attention_forward(
    source_rows, query_w, key_w, value_w, rel_bias, segments, valids, head_count, block_rows
):
    row_count = source_rows.shape[0]
    block_count = row_count // block_rows
    head_width = query_w.shape[1] // head_count

    def project(weight):
        product = jnp.dot(source_rows, weight, preferred_element_type=jnp.float32).astype(
            jnp.bfloat16
        )
        return product.reshape(block_count, block_rows, head_count, head_width)

    queries = project(query_w)
    keys_all = project(key_w)
    values_all = project(value_w)

    def attend(block_items):
        query_block, key_block, value_block, segment_block, valid_block = block_items
        scores = block_scores(query_block, key_block, rel_bias, segment_block, valid_block)
        row_max = jnp.max(scores, axis=2, keepdims=True)
        weights = jnp.exp(scores - row_max)
        row_total = jnp.sum(weights, axis=2, keepdims=True)
        rounded = (weights / row_total).astype(jnp.bfloat16)
        mixed_heads = jnp.einsum(
            "hqk,khd->qhd", rounded, value_block, preferred_element_type=jnp.float32
        )
        return (mixed_heads.astype(jnp.bfloat16), (row_max + jnp.log(row_total))[:, :, 0])

    heads_out, log_totals = lax.map(attend, (queries, keys_all, values_all, segments, valids))
    return (
        queries,
        keys_all,
        values_all,
        heads_out.reshape(row_count, head_count * head_width),
        log_totals,
    )


def attention_backward(
    queries, keys_all, values_all, grad_heads, log_totals, segments, valids, relative, block_rows
):
    rel_bias = toeplitz_rows(relative, block_rows)

    def attend_back(block_items):
        query_block, key_block, value_block, grad_block, total_block, segment_block, valid_block = (
            block_items
        )
        scores = block_scores(query_block, key_block, rel_bias, segment_block, valid_block)
        probability = jnp.exp(scores - total_block[:, :, None])
        rounded = probability.astype(jnp.bfloat16)
        grad_probs = jnp.einsum(
            "qhd,khd->hqk", grad_block, value_block, preferred_element_type=jnp.float32
        )
        grad_values = jnp.einsum(
            "hqk,qhd->khd", rounded, grad_block, preferred_element_type=jnp.float32
        ).astype(jnp.bfloat16)
        inner_sum = jnp.sum(probability * grad_probs, axis=2, keepdims=True)
        grad_scores = (probability * (grad_probs - inner_sum)).astype(jnp.bfloat16)
        grad_queries = jnp.einsum(
            "hqk,khd->qhd", grad_scores, key_block, preferred_element_type=jnp.float32
        ).astype(jnp.bfloat16)
        grad_keys = jnp.einsum(
            "hqk,qhd->khd", grad_scores, query_block, preferred_element_type=jnp.float32
        ).astype(jnp.bfloat16)
        unused_rows, diagonal_back = jax.vjp(
            lambda rel_rows: toeplitz_rows(rel_rows, block_rows), relative
        )
        grad_relative = diagonal_back(grad_scores.astype(jnp.float32))[0]
        return (grad_queries, grad_keys, grad_values, grad_relative)

    grad_q, grad_k, grad_v, grad_rel = lax.map(
        attend_back, (queries, keys_all, values_all, grad_heads, log_totals, segments, valids)
    )
    row_count = grad_q.shape[0] * grad_q.shape[1]
    width = grad_q.shape[2] * grad_q.shape[3]
    return (
        grad_q.reshape(row_count, width),
        grad_k.reshape(row_count, width),
        grad_v.reshape(row_count, width),
        jnp.sum(grad_rel, axis=0),
    )


def body(
    inputs,
    gain_attn,
    w_query,
    w_key,
    w_value,
    w_out,
    rel_table,
    gain_ffn,
    w_in,
    w_down,
    cotangent,
    bucket,
    lengths,
):
    block_rows = BIG
    bucket_size = bucket[0]
    one_hot = (
        offset_buckets(block_rows)[:, None]
        == jnp.arange(rel_table.shape[0], dtype=jnp.int32)[None, :]
    ).astype(jnp.float32)
    x_value = inputs.astype(jnp.float32)
    gain_one = gain_attn.astype(jnp.float32)
    unit_one, root_one, normed_one = rms_forward(x_value, gain_one)
    query_w, key_w, value_w, out_w, table_w = (w_query, w_key, w_value, w_out, rel_table)
    source_rows = lax.all_gather(normed_one.astype(jnp.bfloat16), "mp", axis=0, tiled=True)
    row_ids = jnp.arange(source_rows.shape[0], dtype=jnp.int32)
    head_count = table_w.shape[1]
    segments, valids = row_masks(row_ids, bucket_size, lengths[0], block_rows)
    relative = jnp.dot(one_hot, table_w.astype(jnp.float32), precision=lax.Precision.HIGHEST).T
    rel_bias = toeplitz_rows(relative, block_rows)
    queries, keys_all, values_all, attn_cat, log_totals = attention_forward(
        source_rows, query_w, key_w, value_w, rel_bias, segments, valids, head_count, block_rows
    )
    attn_part = lax.psum_scatter(
        jnp.dot(attn_cat, out_w, preferred_element_type=jnp.float32),
        "mp",
        scatter_dimension=0,
        tiled=True,
    )
    hidden = x_value + attn_part
    gain_two = gain_ffn.astype(jnp.float32)
    unit_two, root_two, normed_two = rms_forward(hidden, gain_two)
    full_two = lax.all_gather(normed_two.astype(jnp.bfloat16), "mp", axis=0, tiled=True)
    pre_act = jnp.dot(full_two, w_in, preferred_element_type=jnp.float32)
    activation = jax.nn.gelu(pre_act, approximate=True).astype(jnp.bfloat16)
    ffn_part = lax.psum_scatter(
        jnp.dot(activation, w_down, preferred_element_type=jnp.float32).astype(jnp.bfloat16),
        "mp",
        scatter_dimension=0,
        tiled=True,
    ).astype(jnp.float32)
    outputs = (hidden + ffn_part).astype(jnp.bfloat16)
    full_grad = lax.all_gather(cotangent, "mp", axis=0, tiled=True)
    grad_down = contract_rows(activation, full_grad)
    grad_activation = contract_cols(full_grad, w_down)
    unused_value, gelu_back = jax.vjp(
        lambda argument: jax.nn.gelu(argument, approximate=True), pre_act
    )
    grad_pre = gelu_back(grad_activation)[0].astype(jnp.bfloat16)
    grad_in = contract_rows(full_two, grad_pre)
    grad_normed_two = lax.psum_scatter(
        contract_cols(grad_pre, w_in), "mp", scatter_dimension=0, tiled=True
    )
    grad_middle, grad_gain_two = rms_backward(grad_normed_two, unit_two, root_two, gain_two)
    grad_hidden = cotangent.astype(jnp.float32) + grad_middle
    hidden_rows = lax.all_gather(grad_hidden.astype(jnp.bfloat16), "mp", axis=0, tiled=True)
    grad_out = contract_rows(attn_cat, hidden_rows)
    grad_heads = contract_cols(hidden_rows, out_w).astype(jnp.bfloat16).reshape(queries.shape)
    grad_q, grad_k, grad_v, grad_rel = attention_backward(
        queries,
        keys_all,
        values_all,
        grad_heads,
        log_totals,
        segments,
        valids,
        relative,
        block_rows,
    )
    grad_query = contract_rows(source_rows, grad_q)
    grad_key = contract_rows(source_rows, grad_k)
    grad_value = contract_rows(source_rows, grad_v)
    grad_table = jnp.dot(one_hot.T, grad_rel.T, precision=lax.Precision.HIGHEST)
    grad_normed_one = lax.psum_scatter(
        contract_cols(grad_q, query_w)
        + contract_cols(grad_k, key_w)
        + contract_cols(grad_v, value_w),
        "mp",
        scatter_dimension=0,
        tiled=True,
    )
    grad_lower, grad_gain_one = rms_backward(grad_normed_one, unit_one, root_one, gain_one)
    grad_inputs = (grad_hidden + grad_lower).astype(jnp.bfloat16)
    grad_gain_one, grad_gain_two = lax.psum((grad_gain_one, grad_gain_two), "mp")
    (
        grad_query,
        grad_key,
        grad_value,
        grad_out,
        grad_table,
        grad_gain_one,
        grad_gain_two,
        grad_in,
        grad_down,
    ) = lax.psum(
        (
            grad_query,
            grad_key,
            grad_value,
            grad_out,
            grad_table,
            grad_gain_one,
            grad_gain_two,
            grad_in,
            grad_down,
        ),
        "dp",
    )
    return (
        outputs,
        grad_inputs,
        grad_query,
        grad_key,
        grad_value,
        grad_out,
        grad_table,
        grad_gain_one,
        grad_gain_two,
        grad_in,
        grad_down,
    )


def solution(mesh):
    placed = (
        P(("dp", "mp"), None),
        P(),
        P(None, "mp"),
        P(None, "mp"),
        P(None, "mp"),
        P("mp", None),
        P(None, "mp"),
        P(),
        P(None, "mp"),
        P("mp", None),
        P(("dp", "mp"), None),
        P("dp"),
        P("dp", None),
    )
    return jax.shard_map(
        body,
        mesh=mesh,
        in_specs=placed,
        out_specs=(
            P(("dp", "mp"), None),
            P(("dp", "mp"), None),
            P(None, "mp"),
            P(None, "mp"),
            P(None, "mp"),
            P("mp", None),
            P(None, "mp"),
            P(),
            P(),
            P(None, "mp"),
            P("mp", None),
        ),
        check_vma=False,
    )
```

profile of v0, /device:TPU:0, one launch (start us, length us, event | category | flops | bytes accessed | tf_op | source)
XLA Modules:
  0.0 1024.1 jit_solution(14102320659425590345)
XLA Ops:
  14.2 3.5 broadcast_bitcast_fusion
  17.7 7.1 copy.77
  24.8 6.4 slice.10
  31.2 13.3 %reshape.270 = f32[3,512,1023]{2,1,0:T(8,128)} reshape(f32[3,523776]{1,0:T(4,128)} %slice.10) | data formatting | bytes 12570624 | tf_op jit(solution)/shard_map/reshape | solution.py:27
  44.5 3.8 slice.11
  48.3 3.9 copy.61
  52.7 26.0 %all-gather.5.cloned.1.call-done = bf16[2048,768]{1,0:T(8,128)(2,1)} async-done(((bf16[512,768]{1,0:T(8,128)(2,1)}), bf16[2048,768]{1,0:T(8,128)(2,1)}) %all-gather.5.cloned.1.call-update) | async-done | bytes 3145744 | tf_op jit(solution)/shard_map/all_gather | solution.py:184
  93.2 21.4 %while.28 = (s32[]{:T(128)}, bf16[4,512,3,64]{1,3,2,0:T(8,128)(2,1)}, f32[4,3,512]{2,1,0:T(4,128)}, bf16[4,512,3,64]{1,3,2,0:T(8,128)(2,1)S(1)}, s32[4,512]{1,0:...) while((s32[]{:T(128)}, ...), condition=%wide.region_5.6_spmd, body=%wide.region_2.5_spmd.sunk | while | flops 208239104 | bytes 13958777 | solution.py:104
  118.1 3.6 fusion.86
  122.6 108.7 %reduce-scatter.5.cloned.1.call-done = f32[512,768]{1,0:T(8,128)} async-done(((f32[2048,768]{1,0:T(8,128)}), f32[512,768]{1,0:T(8,128)}) %reduce-scatter.5.cloned.1.call-update) | async-done | bytes 1572880 | tf_op jit(solution)/shard_map/reduce_scatter | solution.py:193
  234.4 62.5 %all-gather.9.cloned.1.call-done = bf16[2048,768]{1,0:T(8,128)(2,1)} async-done(((bf16[512,768]{1,0:T(8,128)(2,1)}), bf16[2048,768]{1,0:T(8,128)(2,1)}) %all-gather.9.cloned.1.call-update) | async-done | bytes 3145744 | tf_op jit(solution)/shard_map/all_gather | solution.py:212
  297.0 7.4 fusion.87
  304.4 56.7 %all-gather.7.cloned.1.call-done = bf16[2048,768]{1,0:T(8,128)(2,1)} async-done(((bf16[512,768]{1,0:T(8,128)(2,1)}), bf16[2048,768]{1,0:T(8,128)(2,1)}) %all-gather.7.cloned.1.call-update) | async-done | bytes 3145744 | tf_op jit(solution)/shard_map/all_gather | solution.py:202
  361.1 12.2 %fusion.55 = (bf16[2048,768]{1,0:T(8,128)(2,1)S(1)}, f32[2048,768]{1,0:T(8,128)}) fusion(f32[2048,768]{1,0:T(8,128)} %fusion.87, bf16[2048,768]{1,0:T(8,128)(2,1)} %all-gather.7.cloned.1.call-done, bf16[768,768]{1,0:T(8,128)(2,1)S(1)} %copy-done), kind=kOutput, calls=%fused_computation.70 | convolution fusion | flops 2447376384 | bytes 20054016 | tf_op jit(solution)/shard_map/dot_general | solution.py:203
  375.0 4.5 fusion.88
  379.7 109.5 %reduce-scatter.9.cloned.1.call-done = f32[512,768]{1,0:T(8,128)} async-done(((f32[2048,768]{1,0:T(8,128)}), f32[512,768]{1,0:T(8,128)}) %reduce-scatter.9.cloned.1.call-update) | async-done | bytes 1572880 | tf_op jit(solution)/shard_map/reduce_scatter | solution.py:220
  493.3 64.1 %all-gather.11.cloned.1.call-done = bf16[2048,768]{1,0:T(8,128)(2,1)} async-done(((bf16[512,768]{1,0:T(8,128)(2,1)}), bf16[2048,768]{1,0:T(8,128)(2,1)}) %all-gather.11.cloned.1.call-update) | async-done | bytes 3145744 | tf_op jit(solution)/shard_map/all_gather | solution.py:225
  564.1 140.9 %while.29 = (s32[]{:T(128)}, bf16[4,512,3,64]{1,3,2,0:T(8,128)(2,1)}, bf16[4,512,3,64]{1,3,2,0:T(8,128)(2,1)}, bf16[4,512,3,64]{1,3,2,0:T(8,128)(2,1)}, f32[4,3,...) while((s32[]{:T(128)}, ...), condition=%wide.region_14.15_spmd, body=%wide.region_11.14_spmd.sunk | while | flops 514354688 | bytes 84351736 | solution.py:146
  575.3 3.5 pad.7.clone.2
  578.8 7.0 reshape.287
  585.8 5.7 reshape.288
  591.4 4.6 pad_convert_fusion.2
  596.0 3.3 bitcast_reduce_fusion.2
  610.4 3.5 pad.7.clone.2
  613.9 7.0 reshape.287
  620.9 5.7 reshape.288
  626.6 4.6 pad_convert_fusion.2
  631.2 3.3 bitcast_reduce_fusion.2
  645.5 3.5 pad.7.clone.2
  649.0 7.0 reshape.287
  656.1 5.7 reshape.288
  661.7 4.6 pad_convert_fusion.2
  666.3 3.3 bitcast_reduce_fusion.2
  680.7 3.5 pad.7.clone.2
  684.2 7.0 reshape.287
  691.2 5.7 reshape.288
  696.8 4.6 pad_convert_fusion.2
  701.4 3.3 bitcast_reduce_fusion.2
  711.9 3.7 add_add_fusion
  715.7 8.6 convolution_convert_fusion.2
  724.6 7.1 fusion.92
  731.7 7.8 fusion.84
  747.4 77.8 %reduce-scatter.11.cloned.1.call-done = f32[512,768]{1,0:T(8,128)} async-done(((f32[2048,768]{1,0:T(8,128)}), f32[512,768]{1,0:T(8,128)}) %reduce-scatter.11.cloned.1.call-update) | async-done | bytes 1572880 | tf_op jit(solution)/shard_map/reduce_scatter | solution.py:243
  827.2 11.2 %all-reduce.5 = (f32[768]{0:T(1024)S(1)}, f32[768]{0:T(1024)S(1)}) all-reduce(f32[768]{0:T(1024)S(1)} %get-tuple-element.203, f32[768]{0:T(1024)S(1)} %copy-done.38), channel_id=1, replica_groups=mesh['dp'=8,'mp'=4] {'mp'}, use_global_device_ids=true, to_apply=%region_24.25 | all-reduce | flops 1536 | bytes 12288 | tf_op jit(solution)/shard_map/psum | solution.py:253
  838.4 23.2 %all-reduce.3 = (f32[32,3]{0,1:T(4,128)}, f32[768]{0:T(1024)}, f32[768]{0:T(1024)}) all-reduce(f32[32,3]{0,1:T(4,128)S(1)} %fusion.68, f32[768]{0:T(1024)S(1)} %get-tuple-element.258, f32[768]{0:T(1024)S(1)} %get-tuple-element.259), channel_id=1, replica_groups=mesh['dp'=8,'mp'=4] {'dp'}, use_global_device_ids=true, to_apply=%region_22.23 | all-reduce | flops 1632 | bytes 13056 | tf_op jit(solution)/shard_map/psum | solution.py:264
  861.6 26.8 %reduce-scatter.7.cloned.1.call-done = bf16[512,768]{1,0:T(8,128)(2,1)} async-done(((bf16[2048,768]{1,0:T(8,128)(2,1)}), bf16[512,768]{1,0:T(8,128)(2,1)}) %reduce-scatter.7.cloned.1.call-update) | async-done | bytes 786448 | tf_op jit(solution)/shard_map/reduce_scatter | solution.py:205
  888.3 4.1 fusion.65
  892.4 115.2 %all-reduce.8.cloned.1.call-done = (f32[768,192]{0,1:T(8,128)}, f32[768,192]{0,1:T(8,128)}, f32[768,192]{0,1:T(8,128)}, f32[192,768]{1,0:T(8,128)}, f32[768,768]{1,0:T(8,128)}, /*index=5*/f32[768,768]{1,0:T(8,128)}) async-done(((f32[768,192]{0,1:T(8,128)}, f32[768,192]{0,1:T(8,128)}, f32[768,192]{0,1:T(8,128)}, f32[192,768]{1,0:T(8,128)}, f32[768,768]{1,0:T(8,128)}, /*index=5*/f32[768,768]{1,0:T(8,128)}), ...) | async-done | bytes 7077904 | tf_op jit(solution)/shard_map/psum | solution.py:264
  (265 shorter events, 133.0 us)
Async XLA Ops:
  7.2 354.0 %copy-start = (bf16[768,768]{1,0:T(8,128)(2,1)S(1)}, bf16[768,768]{1,0:T(8,128)(2,1)}, u32[]{:S(2)}) copy-start(bf16[768,768]{1,0:T(8,128)(2,1)} %param.25) | copy-start | bytes 3538948
  7.2 5.9 copy-start.42
  7.2 6.7 copy-start.44
  7.2 71.4 %all-gather.5.cloned.1.call-start = ((), (), s32[]{:S(2)}) async-start(), calls=%async_computation.4 | async-start | bytes 3932160 | tf_op jit(solution)/shard_map/all_gather | solution.py:184
  12.3 219.0 %reduce-scatter.5.cloned.1.call-start = ((), (), s32[]{:S(2)}) async-start(), calls=%async_computation.5 | async-start | bytes 7864320 | tf_op jit(solution)/shard_map/reduce_scatter | solution.py:193
  48.3 30.3 %copy-start.27 = (bf16[768,192]{0,1:T(8,128)(2,1)S(1)}, bf16[768,192]{0,1:T(8,128)(2,1)}, u32[]{:S(2)}) copy-start(bf16[768,192]{0,1:T(8,128)(2,1)} %param.20) | copy-start | bytes 884740
  114.6 7.1 copy-start.8
  114.6 7.1 copy-start.10
  114.6 7.1 copy-start.19
  114.6 3.5 copy-start.25
  121.7 109.6 %copy-start.6 = (bf16[512,768]{1,0:T(8,128)(2,1)S(1)}, bf16[512,768]{1,0:T(8,128)(2,1)}, u32[]{:S(2)}) copy-start(bf16[512,768]{1,0:T(8,128)(2,1)} %param.17) | copy-start | bytes 2359300
  121.8 175.2 %all-gather.9.cloned.1.call-start = ((), (), s32[]{:S(2)}) async-start(), calls=%async_computation.8 | async-start | bytes 3932160 | tf_op jit(solution)/shard_map/all_gather | solution.py:212
  122.5 238.6 %all-gather.7.cloned.1.call-start = ((), (), s32[]{:S(2)}) async-start(), calls=%async_computation.6 | async-start | bytes 3932160 | tf_op jit(solution)/shard_map/all_gather | solution.py:202
  233.0 258.8 %copy-start.3 = (f32[512,768]{1,0:T(8,128)}, f32[512,768]{1,0:T(8,128)S(1)}, u32[]{:S(2)}) copy-start(f32[512,768]{1,0:T(8,128)S(1)} %get-tuple-element.261) | copy-start | bytes 4718596
  233.0 258.7 %copy-start.34 = (f32[512]{0:T(512)}, f32[512]{0:T(512)S(1)}, u32[]{:S(2)}) copy-start(f32[512]{0:T(512)S(1)} %add_rsqrt_fusion) | copy-start | bytes 6148
  234.4 254.8 %reduce-scatter.9.cloned.1.call-start = ((), (), s32[]{:S(2)}) async-start(), calls=%async_computation.9 | async-start | bytes 7864320 | tf_op jit(solution)/shard_map/reduce_scatter | solution.py:220
  379.6 112.2 %copy-start.17 = (bf16[512,768]{1,0:T(8,128)(2,1)S(1)}, bf16[512,768]{1,0:T(8,128)(2,1)}, u32[]{:S(2)}) copy-start(bf16[512,768]{1,0:T(8,128)(2,1)} %param.27) | copy-start | bytes 2359300
  379.6 177.8 %all-gather.11.cloned.1.call-start = ((), (), s32[]{:S(2)}) async-start(), calls=%async_computation.10 | async-start | bytes 3932160 | tf_op jit(solution)/shard_map/all_gather | solution.py:225
  491.8 65.6 %copy-start.26 = (bf16[192,768]{1,0:T(8,128)(2,1)S(1)}, bf16[192,768]{1,0:T(8,128)(2,1)}, u32[]{:S(2)}) copy-start(bf16[192,768]{1,0:T(8,128)(2,1)} %param.22) | copy-start | bytes 884740
  493.2 332.0 %reduce-scatter.11.cloned.1.call-start = ((), (), s32[]{:S(2)}) async-start(), calls=%async_computation.11 | async-start | bytes 7864320 | tf_op jit(solution)/shard_map/reduce_scatter | solution.py:243
  560.4 3.6 copy-start.9
  560.5 3.6 copy-start.11
  564.2 4.1 copy-start.15
  596.0 3.3 copy-start.16
  599.3 4.1 copy-start.15
  599.4 2.8 copy-start.2
  631.1 3.3 copy-start.16
  634.5 4.1 copy-start.15
  634.5 2.8 copy-start.2
  666.3 3.3 copy-start.16
  669.6 4.1 copy-start.15
  669.6 2.8 copy-start.2
  701.4 3.3 copy-start.16
  704.9 4.0 copy-start.21
  715.7 172.7 %reduce-scatter.7.cloned.1.call-start = ((), (), s32[]{:S(2)}) async-start(), calls=%async_computation.7 | async-start | bytes 3932160 | tf_op jit(solution)/shard_map/reduce_scatter | solution.py:205
  724.3 283.3 %all-reduce.8.cloned.1.call-start = ((), (), s32[]{:S(2)}) async-start(), calls=%async_computation.12 | async-start | bytes 14155776 | tf_op jit(solution)/shard_map/psum | solution.py:264
  724.6 7.1 copy-start.43
  731.7 7.8 copy-start.14
  731.7 7.8 copy-start.20
  746.4 78.9 %copy-start.7 = (bf16[512,768]{1,0:T(8,128)(2,1)S(1)}, bf16[512,768]{1,0:T(8,128)(2,1)}, u32[]{:S(2)}) copy-start(bf16[512,768]{1,0:T(8,128)(2,1)} %param.17) | copy-start | bytes 2359300
  746.4 78.9 %copy-start.33 = (f32[768]{0:T(1024)S(1)}, f32[768]{0:T(1024)}, u32[]{:S(2)}) copy-start(f32[768]{0:T(1024)} %copy-done.32) | copy-start | bytes 9220
  746.4 78.9 %copy-start.37 = (f32[512]{0:T(512)S(1)}, f32[512]{0:T(512)}, u32[]{:S(2)}) copy-start(f32[512]{0:T(512)} %copy-done.36) | copy-start | bytes 6148
  746.4 80.8 %copy-start.38 = (f32[768]{0:T(1024)S(1)}, f32[768]{0:T(1024)}, u32[]{:S(2)}) copy-start(f32[768]{0:T(1024)} %get-tuple-element.201) | copy-start | bytes 9220
  746.4 142.0 %copy-start.4 = (f32[512,768]{1,0:T(8,128)S(1)}, f32[512,768]{1,0:T(8,128)}, u32[]{:S(2)}) copy-start(f32[512,768]{1,0:T(8,128)} %copy-done.3) | copy-start | bytes 4718596
  746.4 141.9 %copy-start.18 = (bf16[512,768]{1,0:T(8,128)(2,1)S(1)}, bf16[512,768]{1,0:T(8,128)(2,1)}, u32[]{:S(2)}) copy-start(bf16[512,768]{1,0:T(8,128)(2,1)} %param.27) | copy-start | bytes 2359300
  746.4 141.9 %copy-start.35 = (f32[512]{0:T(512)S(1)}, f32[512]{0:T(512)}, u32[]{:S(2)}) copy-start(f32[512]{0:T(512)} %copy-done.34) | copy-start | bytes 6148
  1007.6 5.9 copy-start.24
  1007.6 6.7 copy-start.23
  (16 other events, 24.5 us)
Sparse Core Ops, SparseCore 0:
  12.4 66.1 all-gather.4
  121.9 109.3 reduce-scatter.4
  232.9 64.0 all-gather.8
  299.0 62.1 all-gather.6
  379.7 109.3 reduce-scatter.8
  493.3 64.0 all-gather.10
  715.8 109.3 reduce-scatter.10
  827.5 60.7 reduce-scatter.6
  893.6 114.0 all-reduce.7
where the time goes:
time: 1030 us; the launch traced here: 1020 us
  waiting for transfers between devices  648 us (63%)
  local copies, waits for them, and re-layouts  144 us (14%)
  matrix products  122 us (12%)
  other arithmetic  58.8 us (6%)
  blocking collectives  34.4 us (3%)
  between operations  15.5 us (2%)
    psum x1, waiting for transfers between devices, body(): lax.psum((grad_query, grad_key, grad_value, grad_out, grad_table, grad_ga...  115 us
    reduce_scatter x1, waiting for transfers between devices, body(): lax.psum_scatter(contract_cols(grad_pre, w_in), 'mp', scatter_dimension=0...  109 us
    reduce_scatter x1, waiting for transfers between devices, body(): lax.psum_scatter(jnp.dot(attn_cat, out_w, preferred_element_type=jnp.floa...  109 us
    reduce_scatter x1, waiting for transfers between devices, body(): lax.psum_scatter(contract_cols(grad_q, query_w) + contract_cols(grad_k, k...  77.8 us
    all_gather x1, waiting for transfers between devices, body(): lax.all_gather(grad_hidden.astype(jnp.bfloat16), 'mp', axis=0, tiled=True)  64.1 us
    all_gather x1, waiting for transfers between devices, body(): full_grad = lax.all_gather(cotangent, 'mp', axis=0, tiled=True)  62.5 us
    all_gather x1, waiting for transfers between devices, body(): lax.all_gather(normed_two.astype(jnp.bfloat16), 'mp', axis=0, tiled=True)  56.7 us
    reshape x5, local copies, waits for them, and re-layouts, toeplitz_rows(): window.reshape(head_count, block_rows, 2 * block_rows - 1)  35.9 us
  transfers between devices with their start and end apart: 9, of which 9 were waited for; matrix products, arithmetic and copies ran while one was open for 8% of the time, Pallas kernels for 0%

commit v1 on v0

v1 whole, which is shorter than its diff:
```python
import functools

import jax
import jax.numpy as jnp
import numpy as np
from jax import lax
from jax.experimental import pallas as pl
from jax.experimental.pallas import tpu as pltpu
from jax.sharding import PartitionSpec as P

BIG = 512
HEAD = 64
EPS = 1e-06
THRESHOLDS = (12, 16, 23, 32, 46, 64, 91)
MASKED = -1e30
TILE = 128
SPAN = 1024
BF = jnp.bfloat16
F32 = jnp.float32
MIB = 1024 * 1024


def offset_one_hot(buckets):
    u = np.arange(SPAN)
    offsets = np.where(u < 896, u, u - SPAN) - 3 * TILE
    distance = np.abs(offsets)
    far = 8 + sum((distance >= t).astype(np.int32) for t in THRESHOLDS)
    bucket = np.where(distance < 8, distance, far) + np.where(offsets > 0, 16, 0)
    return (bucket[:, None] == np.arange(buckets)[None, :]).astype(np.float32)


def dot_nn(a, b):
    return lax.dot_general(a, b, (((1,), (0,)), ((), ())), preferred_element_type=F32)


def dot_nt(a, b):
    return lax.dot_general(a, b, (((1,), (1,)), ((), ())), preferred_element_type=F32)


def dot_tn(a, b):
    return lax.dot_general(a, b, (((0,), (0,)), ((), ())), preferred_element_type=F32)


def mask_rows(meta_ref, slots):
    bucket = meta_ref[0]
    half = BIG // 2
    segs, starts = [], []
    for part in range(2):
        first = meta_ref[1] + part * half
        seg = jnp.int32(0)
        for j in range(1, slots):
            seg = seg + jnp.where(first >= j * bucket, 1, 0).astype(jnp.int32)
        segs.append(seg)
        starts.append(first - seg * bucket)
    iota = lax.broadcasted_iota(jnp.int32, (1, half), 1)
    rows = []
    for query_part in range(2):
        cols = []
        for key_part in range(2):
            same = segs[query_part] == segs[key_part]
            limit = jnp.where(same, meta_ref[2 + segs[key_part]] - starts[key_part], 0)
            cols.append(jnp.where(iota < limit, 0.0, MASKED).astype(F32))
        rows.append(jnp.concatenate(cols, axis=1))
    return rows


def bias_band(rel_row):
    wide = jnp.broadcast_to(rel_row, (TILE, SPAN))
    return pltpu.roll(wide, 0, 1, stride=1, stride_axis=0)


def attn_fwd_kernel(slots, heads, meta_ref, n1_ref, a_ref, rel_ref, qkv_ref, o_ref, lse_ref, hp_ref, band):
    step = pl.program_id(0)
    width = heads * HEAD
    qkv_ref[0] = dot_nn(n1_ref[...], a_ref[0]).astype(BF)
    masks = mask_rows(meta_ref, slots)
    for h in range(heads):
        band[...] = bias_band(rel_ref[0, h : h + 1, :].astype(F32))
        q = qkv_ref[0, :, width + h * HEAD : width + (h + 1) * HEAD]
        k = qkv_ref[0, :, 2 * width + h * HEAD : 2 * width + (h + 1) * HEAD]
        v = qkv_ref[0, :, 3 * width + h * HEAD : 3 * width + (h + 1) * HEAD]
        for i in range(BIG // TILE):
            rows = slice(i * TILE, (i + 1) * TILE)
            s = dot_nt(q[rows], k) + band[:, (3 - i) * TILE : (7 - i) * TILE] + masks[i // 2]
            top = jnp.max(s, axis=1, keepdims=True)
            e = jnp.exp(s - top)
            total = jnp.sum(e, axis=1, keepdims=True)
            pb = (e * (1.0 / total)).astype(BF)
            o_ref[0, rows, h * HEAD : (h + 1) * HEAD] = dot_nn(pb, v).astype(BF)
            lse_ref[0, rows, h : h + 1] = top + jnp.log(total)
    part = dot_nt(o_ref[0], a_ref[0, :, :width])

    @pl.when(step == 0)
    def _():
        hp_ref[...] = part

    @pl.when(step > 0)
    def _():
        hp_ref[...] += part


def attn_fwd(meta, n1, a, rel, slots, heads):
    shards, depth, cols = a.shape
    rows = n1.shape[0]
    width = heads * HEAD
    return pl.pallas_call(
        functools.partial(attn_fwd_kernel, slots, heads),
        grid=(shards,),
        in_specs=[
            pl.BlockSpec(memory_space=pltpu.SMEM),
            pl.BlockSpec((rows, depth), lambda s: (0, 0)),
            pl.BlockSpec((1, depth, cols), lambda s: (s, 0, 0)),
            pl.BlockSpec((1,) + rel.shape[1:], lambda s: (s, 0, 0)),
        ],
        out_specs=[
            pl.BlockSpec((1, rows, cols), lambda s: (s, 0, 0)),
            pl.BlockSpec((1, rows, width), lambda s: (s, 0, 0)),
            pl.BlockSpec((1, rows, TILE), lambda s: (s, 0, 0)),
            pl.BlockSpec((rows, depth), lambda s: (0, 0)),
        ],
        out_shape=[
            jax.ShapeDtypeStruct((shards, rows, cols), BF),
            jax.ShapeDtypeStruct((shards, rows, width), BF),
            jax.ShapeDtypeStruct((shards, rows, TILE), F32),
            jax.ShapeDtypeStruct((rows, depth), F32),
        ],
        scratch_shapes=[pltpu.VMEM((TILE, SPAN), F32)],
        compiler_params=pltpu.CompilerParams(vmem_limit_bytes=40 * MIB),
        cost_estimate=pl.CostEstimate(flops=shards * 2 * 10**9, bytes_accessed=shards * 4 * 10**6, transcendentals=0),
        name="attn_fwd",
    )(meta, n1, a, rel)


def ffn_kernel(n2_ref, cot_ref, i_ref, w_ref, out_ref, gn_ref, gi_ref, gw_ref):
    step = pl.program_id(0)
    c0 = 0.7978845608028654
    c1 = 0.044715
    n2 = n2_ref[...]
    cot = cot_ref[...]
    pre = dot_nn(n2, i_ref[0])
    square = pre * pre
    th = jnp.tanh(pre * (c0 + (c0 * c1) * square))
    half = 0.5 * (1.0 + th)
    act = (pre * half).astype(BF)
    slope = half + (0.5 * pre) * (1.0 - th * th) * (c0 + (3.0 * c0 * c1) * square)
    out = dot_nn(act, w_ref[0])
    gp = (dot_nt(cot, w_ref[0]) * slope).astype(BF)
    gn = dot_nt(gp, i_ref[0])

    @pl.when(step == 0)
    def _():
        out_ref[...] = out
        gn_ref[...] = gn

    @pl.when(step > 0)
    def _():
        out_ref[...] += out
        gn_ref[...] += gn

    gi_ref[0] = dot_tn(n2, gp).astype(BF)
    gw_ref[0] = dot_tn(act, cot).astype(BF)


def ffn(n2, cot, i, w):
    shards, depth, units = i.shape
    rows = n2.shape[0]
    full = pl.BlockSpec((rows, depth), lambda s: (0, 0))
    i_spec = pl.BlockSpec((1, depth, units), lambda s: (s, 0, 0))
    w_spec = pl.BlockSpec((1, units, depth), lambda s: (s, 0, 0))
    return pl.pallas_call(
        ffn_kernel,
        grid=(shards,),
        in_specs=[full, full, i_spec, w_spec],
        out_specs=[full, full, i_spec, w_spec],
        out_shape=[
            jax.ShapeDtypeStruct((rows, depth), F32),
            jax.ShapeDtypeStruct((rows, depth), F32),
            jax.ShapeDtypeStruct(i.shape, BF),
            jax.ShapeDtypeStruct(w.shape, BF),
        ],
        compiler_params=pltpu.CompilerParams(vmem_limit_bytes=48 * MIB),
        cost_estimate=pl.CostEstimate(flops=shards * 5 * 10**9, bytes_accessed=shards * 8 * 10**6, transcendentals=0),
        name="ffn",
    )(n2, cot, i, w)


def attn_bwd_kernel(
    slots, heads, meta_ref, n1_ref, gh_ref, a_ref, qkv_ref, o_ref, lse_ref, rel_ref,
    ga_ref, gn_ref, diag_ref, band, acc, gs_all, pb_all, gq_all,
):
    step = pl.program_id(0)
    width = heads * HEAD
    gh = gh_ref[...]
    go_all = dot_nn(gh, a_ref[0, :, :width]).astype(BF)
    masks = mask_rows(meta_ref, slots)
    gq_all[:, :width] = jnp.zeros((gq_all.shape[0], width), BF)
    diag_ref[0] = jnp.zeros(diag_ref.shape[1:], F32)
    for h in range(heads):
        band[...] = bias_band(rel_ref[0, h : h + 1, :].astype(F32))
        acc[...] = jnp.zeros_like(acc)
        q = qkv_ref[0, :, width + h * HEAD : width + (h + 1) * HEAD]
        k = qkv_ref[0, :, 2 * width + h * HEAD : 2 * width + (h + 1) * HEAD]
        v = qkv_ref[0, :, 3 * width + h * HEAD : 3 * width + (h + 1) * HEAD]
        go = go_all[:, h * HEAD : (h + 1) * HEAD]
        for i in range(BIG // TILE):
            rows = slice(i * TILE, (i + 1) * TILE)
            window = slice((3 - i) * TILE, (7 - i) * TILE)
            s = dot_nt(q[rows], k) + band[:, window] + masks[i // 2]
            p = jnp.exp(s - lse_ref[0, rows, h : h + 1])
            dp = dot_nt(go[rows], v)
            inner = jnp.sum(p * dp, axis=1, keepdims=True)
            gs = (p * (dp - inner)).astype(BF)
            gs_all[rows, :] = gs
            pb_all[rows, :] = p.astype(BF)
            acc[:, window] += gs.astype(F32)
        gq_all[:, width + h * HEAD : width + (h + 1) * HEAD] = dot_nn(gs_all[...], k).astype(BF)
        gq_all[:, 2 * width + h * HEAD : 2 * width + (h + 1) * HEAD] = dot_tn(gs_all[...], q).astype(BF)
        gq_all[:, 3 * width + h * HEAD : 3 * width + (h + 1) * HEAD] = dot_tn(pb_all[...], go).astype(BF)
        fold = acc[...]
        n = TILE // 2
        while n >= 8:
            fold = fold[:n] + pltpu.roll(fold[n:], SPAN - n, 1)
            n //= 2
        line = fold[0:1]
        for j in range(1, 8):
            line = line + pltpu.roll(fold[j : j + 1], SPAN - j, 1)
        diag_ref[0, h : h + 1, :] = line
    grads = gq_all[...]
    gn = dot_nt(grads, a_ref[0])

    @pl.when(step == 0)
    def _():
        gn_ref[...] = gn

    @pl.when(step > 0)
    def _():
        gn_ref[...] += gn

    ga_ref[0] = dot_tn(n1_ref[...], grads).astype(BF)
    ga_ref[0, :, :width] = dot_tn(gh, o_ref[0]).astype(BF)


def attn_bwd(meta, n1, gh, a, qkv, o, lse, rel, slots, heads):
    shards, depth, cols = a.shape
    rows = n1.shape[0]
    width = heads * HEAD
    full = pl.BlockSpec((rows, depth), lambda s: (0, 0))
    a_spec = pl.BlockSpec((1, depth, cols), lambda s: (s, 0, 0))
    return pl.pallas_call(
        functools.partial(attn_bwd_kernel, slots, heads),
        grid=(shards,),
        in_specs=[
            pl.BlockSpec(memory_space=pltpu.SMEM),
            full,
            full,
            a_spec,
            pl.BlockSpec((1, rows, cols), lambda s: (s, 0, 0)),
            pl.BlockSpec((1, rows, width), lambda s: (s, 0, 0)),
            pl.BlockSpec((1, rows, TILE), lambda s: (s, 0, 0)),
            pl.BlockSpec((1,) + rel.shape[1:], lambda s: (s, 0, 0)),
        ],
        out_specs=[a_spec, full, pl.BlockSpec((1, 8, SPAN), lambda s: (s, 0, 0))],
        out_shape=[
            jax.ShapeDtypeStruct(a.shape, BF),
            jax.ShapeDtypeStruct((rows, depth), F32),
            jax.ShapeDtypeStruct((shards, 8, SPAN), F32),
        ],
        scratch_shapes=[
            pltpu.VMEM((TILE, SPAN), F32),
            pltpu.VMEM((TILE, SPAN), F32),
            pltpu.VMEM((BIG, BIG), BF),
            pltpu.VMEM((BIG, BIG), BF),
            pltpu.VMEM((rows, cols), BF),
        ],
        compiler_params=pltpu.CompilerParams(vmem_limit_bytes=48 * MIB),
        cost_estimate=pl.CostEstimate(flops=shards * 4 * 10**9, bytes_accessed=shards * 8 * 10**6, transcendentals=0),
        name="attn_bwd",
    )(meta, n1, gh, a, qkv, o, lse, rel)


def place_kernel(starts, count, index_ref, *refs):
    parts, out_ref, sems = refs[:-2], refs[-2], refs[-1]
    rows = parts[0].shape[1]
    copies = []
    j = 0
    for part in parts:
        for e in range(part.shape[0] // count):
            first = pl.multiple_of(index_ref[j] * rows, rows)
            for s in range(count):
                copies.append(
                    pltpu.make_async_copy(
                        part.at[e * count + s],
                        out_ref.at[s, pl.ds(first, rows), :],
                        sems.at[j * count + s],
                    )
                )
            j += 1
    for copy in copies:
        copy.start()
    for copy in copies:
        copy.wait()


def place(index, parts, count):
    blocks = index.shape[0]
    rows, cols = parts[0].shape[1:]
    return pl.pallas_call(
        functools.partial(place_kernel, None, count),
        in_specs=[pl.BlockSpec(memory_space=pltpu.SMEM)] + [pl.BlockSpec(memory_space=pl.ANY)] * len(parts),
        out_specs=pl.BlockSpec(memory_space=pl.ANY),
        out_shape=jax.ShapeDtypeStruct((count, blocks * rows, cols), parts[0].dtype),
        scratch_shapes=[pltpu.SemaphoreType.DMA((blocks * count,))],
        name="place",
    )(index, *parts)


class Ring:
    def __init__(self, n_dp, n_mp, depth):
        self.n_dp, self.n_mp = n_dp, n_mp
        self.all_bits = (n_dp - 1).bit_length()
        self.bits = min(3, self.all_bits)
        self.d = lax.axis_index("dp")
        self.z = lax.axis_index("mp")
        self.blocks = 1 << self.bits
        self.block_rows = depth // self.blocks
        self.low = self.d & (self.blocks - 1)

    def row_block(self, low):
        return ((low & 1) << (self.bits - 1)) | (low >> 1)

    def swap(self, x, bit):
        return lax.ppermute(x, "dp", [(i, i ^ (1 << bit)) for i in range(self.n_dp)])

    def pull(self, x, shift):
        return lax.ppermute(x, "mp", [(i, (i - shift) % self.n_mp) for i in range(self.n_mp)])

    def push(self, x, shift):
        return lax.ppermute(x, "mp", [(i, (i + shift) % self.n_mp) for i in range(self.n_mp)])

    def order(self, flip):
        high = list(range(1, self.bits))
        return (high[::-1] if flip else high) + [0]

    def gather(self, arr, flip):
        count = arr.shape[0]
        order = self.order(flip)
        masks = [0]
        for bit in order[:-1]:
            arr = jnp.concatenate([arr, self.swap(arr, bit)], axis=0)
            masks = masks + [m | (1 << bit) for m in masks]
        parts = [arr, self.swap(arr, order[-1])]
        masks = masks + [m | (1 << order[-1]) for m in masks]
        index = jnp.stack([self.row_block(self.low ^ m) for m in masks]).astype(jnp.int32)
        return place(index, parts, count)

    def own_block(self, mats):
        first = self.row_block(self.low) * self.block_rows
        return lax.dynamic_slice_in_dim(mats, first, self.block_rows, axis=1)

    def scatter(self, mats, flip):
        count, _, cols = mats.shape
        arr = mats.reshape((count,) + (2,) * self.bits + (self.block_rows, cols))
        axes = [0] + list(range(self.bits - 1, 0, -1))
        order = self.order(flip)[::-1]
        for bit in order:
            axis = 1 + axes.index(bit)
            axes.remove(bit)
            mine = (self.low >> bit) & 1
            send = lax.dynamic_index_in_dim(arr, 1 - mine, axis, keepdims=False)
            keep = lax.dynamic_index_in_dim(arr, mine, axis, keepdims=False)
            arr = (keep.astype(F32) + self.swap(send, bit).astype(F32)).astype(BF)
        for bit in range(self.bits, self.all_bits):
            arr = (arr.astype(F32) + self.swap(arr, bit).astype(F32)).astype(BF)
        return arr

    def owners(self, pieces):
        total = pieces[0].astype(F32)
        for s in range(1, self.n_mp):
            total = total + self.push(pieces[s], s).astype(F32)
        return total


def rms_forward(values, gain_vec):
    inv_root = lax.rsqrt(jnp.mean(values * values, axis=1, keepdims=True) + EPS)
    unit_rows = values * inv_root
    return (unit_rows, inv_root, unit_rows * gain_vec)


def rms_backward(grad_normed, unit_rows, inv_root, gain_vec):
    grad_unit = grad_normed * gain_vec
    grad_gain = jnp.sum(grad_normed * unit_rows, axis=0)
    centred = grad_unit - unit_rows * jnp.mean(grad_unit * unit_rows, axis=1, keepdims=True)
    return (inv_root * centred, grad_gain)


def body(
    n_dp, n_mp, inputs, gain_attn, w_query, w_key, w_value, w_out, rel_table, gain_ffn, w_in, w_down,
    cotangent, bucket, lengths,
):
    depth = inputs.shape[1]
    buckets, heads = rel_table.shape
    width = heads * HEAD
    slots = lengths.shape[1]
    ring = Ring(n_dp, n_mp, depth)
    shifts = range(1, n_mp)

    a_own = jnp.concatenate([w_out.T, w_query, w_key, w_value], axis=1)[None]
    i_own = w_in[None]
    w_own = w_down[None]
    one_hot = jnp.asarray(offset_one_hot(buckets), BF)
    rel_own = lax.dot_general(rel_table, one_hot, (((0,), (1,)), ((), ())), preferred_element_type=F32)
    rel_own = jnp.concatenate([rel_own.astype(BF), jnp.zeros((16 - heads, SPAN), BF)], axis=0)[None]

    a_piece = ring.own_block(a_own)
    a_in = jnp.concatenate([ring.pull(a_piece, s) for s in shifts], axis=0)
    rel_rest = jnp.concatenate([ring.pull(rel_own, s) for s in shifts], axis=0)
    f_piece = ring.own_block(jnp.concatenate([i_own, w_own], axis=0))
    f_in = [ring.pull(f_piece, s) for s in shifts]

    a_rest = ring.gather(a_in, False)
    f_full = [ring.gather(f_in[j], j % 2 == 0) for j in range(n_mp - 1)]

    meta = jnp.concatenate([bucket, (ring.z * BIG)[None].astype(jnp.int32), lengths[0]])
    x_value = inputs.astype(F32)
    gain_one = gain_attn.astype(F32)
    unit_one, root_one, normed_one = rms_forward(x_value, gain_one)
    n1 = normed_one.astype(BF)
    qkv0, o0, lse0, hp0 = attn_fwd(meta, n1, a_own, rel_own, slots, heads)
    qkv1, o1, lse1, hp1 = attn_fwd(meta, n1, a_rest, rel_rest, slots, heads)
    hidden = x_value + (hp0 + hp1)
    gain_two = gain_ffn.astype(F32)
    unit_two, root_two, normed_two = rms_forward(hidden, gain_two)
    n2 = normed_two.astype(BF)

    f_mats = [(i_own, w_own)] + [(f[0:1], f[1:2]) for f in f_full]
    outs, gns, f_grads = [], [], []
    for s in range(n_mp):
        out, gn, gi, gw = ffn(n2, cotangent, f_mats[s][0], f_mats[s][1])
        outs.append(out)
        gns.append(gn)
        f_grads.append(ring.scatter(jnp.concatenate([gi, gw], axis=0), s % 2 == 0))
    outputs = (hidden + sum(outs)).astype(BF)
    grad_middle, grad_gain_two = rms_backward(sum(gns), unit_two, root_two, gain_two)
    grad_hidden = cotangent.astype(F32) + grad_middle
    gh = grad_hidden.astype(BF)

    ga0, gn0, diag0 = attn_bwd(meta, n1, gh, a_own, qkv0, o0, lse0, rel_own, slots, heads)
    ga1, gn1, diag1 = attn_bwd(meta, n1, gh, a_rest, qkv1, o1, lse1, rel_rest, slots, heads)
    a_grads = ring.scatter(jnp.concatenate([ga0, ga1], axis=0), False)
    grad_lower, grad_gain_one = rms_backward(gn0 + gn1, unit_one, root_one, gain_one)
    grad_inputs = (grad_hidden + grad_lower).astype(BF)

    f_sum = ring.owners(f_grads).astype(BF)
    f_out = ring.gather(f_sum, True)
    a_sum = ring.owners([a_grads[s] for s in range(n_mp)]).astype(BF)
    a_out = ring.gather(a_sum[None], False)[0].astype(F32)
    grad_in, grad_down = f_out[0].astype(F32), f_out[1].astype(F32)
    grad_out = a_out[:, :width].T
    grad_query, grad_key, grad_value = (a_out[:, j * width : (j + 1) * width] for j in (1, 2, 3))

    diag = jnp.concatenate([diag0, diag1], axis=0)[:, :heads]
    tables = jnp.einsum("shu,ub->sbh", diag, jnp.asarray(offset_one_hot(buckets)), precision=lax.Precision.HIGHEST)
    size = buckets * heads
    small = jnp.concatenate([tables.reshape(-1), grad_gain_one, grad_gain_two])
    for bit in range(ring.all_bits):
        small = small + ring.swap(small, bit)
    gains = small[n_mp * size :]
    mine = [jnp.concatenate([small[s * size : (s + 1) * size], gains]) for s in range(n_mp)]
    total = ring.owners(mine)
    grad_table = total[:size].reshape(buckets, heads)
    grad_gain_one = total[size : size + depth]
    grad_gain_two = total[size + depth :]
    return (
        outputs, grad_inputs, grad_query, grad_key, grad_value, grad_out, grad_table,
        grad_gain_one, grad_gain_two, grad_in, grad_down,
    )


def solution(mesh):
    placed = (
        P(("dp", "mp"), None), P(), P(None, "mp"), P(None, "mp"), P(None, "mp"), P("mp", None),
        P(None, "mp"), P(), P(None, "mp"), P("mp", None), P(("dp", "mp"), None), P("dp"), P("dp", None),
    )
    return jax.shard_map(
        functools.partial(body, mesh.shape["dp"], mesh.shape["mp"]),
        mesh=mesh,
        in_specs=placed,
        out_specs=(
            P(("dp", "mp"), None), P(("dp", "mp"), None), P(None, "mp"), P(None, "mp"), P(None, "mp"),
            P("mp", None), P(None, "mp"), P(), P(), P(None, "mp"), P("mp", None),
        ),
        check_vma=False,
    )
```

time: 1030 us -> 815 us (0.79)
  Pallas kernels: 0 us -> 524 us
  waiting for transfers between devices: 648 us -> 128 us
  matrix products: 122 us -> 1.05 us
  local copies, waits for them, and re-layouts: 144 us -> 51.5 us
  starting transfers between devices: 0.62 us -> 67.7 us
  blocking collectives: 34.4 us -> 0 us
  other arithmetic: 58.8 us -> 32.4 us
  between operations: 15.5 us -> 2.92 us
    pallas_call x0 -> x14, Pallas kernels: none -> 524 us  [the longest x6 440 us: place(): pl.pallas_call(functools.partial(place_kernel, None, count), in_specs=[pl...]
    reduce_scatter x4 -> x0, waiting for transfers between devices: 323 us -> none  [the longest x1 109 us: body(): lax.psum_scatter(contract_cols(grad_pre, w_in), 'mp', scatter_dimension=0...]
    all_gather x4 -> x0, waiting for transfers between devices: 209 us -> none  [the longest x1 64.1 us: body(): lax.all_gather(grad_hidden.astype(jnp.bfloat16), 'mp', axis=0, tiled=True)]
    ppermute x0 -> x54, waiting for transfers between devices: none -> 128 us  [the longest x36 95.4 us: swap(): return lax.ppermute(x, 'dp', [(i, i ^ 1 << bit) for i in range(self.n_dp)])]
    dot_general x48 -> x2, matrix products: 122 us -> 1.05 us  [the longest x1 0.89 us: body(): jnp.einsum('shu,ub->sbh', diag, jnp.asarray(offset_one_hot(buckets)), pre...]
    psum x1 -> x0, waiting for transfers between devices: 115 us -> none  [body(): lax.psum((grad_query, grad_key, grad_value, grad_out, grad_table, grad_ga...]
    ppermute x0 -> x54, starting transfers between devices: none -> 67.7 us  [the longest x36 32.1 us: swap(): return lax.ppermute(x, 'dp', [(i, i ^ 1 << bit) for i in range(self.n_dp)])]
    while x41 -> x0, local copies, waits for them, and re-layouts: 46.6 us -> none
  transfers between devices with their start and end apart: 9 -> 54, of which waited for: 9 -> 23; matrix products, arithmetic and copies ran while one was open for 8% -> 7% of each run, Pallas kernels for 0% -> 41%
where the time goes in v1:
time: 815 us; the launch traced here: 808 us
  Pallas kernels  524 us (64%)
  waiting for transfers between devices  128 us (16%)
  starting transfers between devices  67.7 us (8%)
  local copies, waits for them, and re-layouts  51.5 us (6%)
  other arithmetic  32.4 us (4%)
    pallas_call x6, Pallas kernels, place(): pl.pallas_call(functools.partial(place_kernel, None, count), in_specs=[pl...  440 us
    ppermute x36, waiting for transfers between devices, swap(): return lax.ppermute(x, 'dp', [(i, i ^ 1 << bit) for i in range(self.n_dp)])  95.4 us
    pallas_call x4, Pallas kernels, ffn(): pl.pallas_call(ffn_kernel, grid=(shards,), in_specs=[full, full, i_spec,...  32.5 us
    ppermute x36, starting transfers between devices, swap(): return lax.ppermute(x, 'dp', [(i, i ^ 1 << bit) for i in range(self.n_dp)])  32.1 us
    unnamed x161, local copies, waits for them, and re-layouts  29.6 us
    pallas_call x2, Pallas kernels, attn_bwd(): pl.pallas_call(functools.partial(attn_bwd_kernel, slots, heads), grid=(sh...  27.3 us
    ppermute x9, starting transfers between devices, pull(): lax.ppermute(x, 'mp', [(i, (i - shift) % self.n_mp) for i in range(self.n...  25.9 us
    pallas_call x2, Pallas kernels, attn_fwd(): pl.pallas_call(functools.partial(attn_fwd_kernel, slots, heads), grid=(sh...  24.1 us
  transfers between devices with their start and end apart: 54, of which 23 were waited for; matrix products, arithmetic and copies ran while one was open for 7% of the time, Pallas kernels for 41%

profile of v1, /device:TPU:0, one launch (start us, length us, event | category | flops | bytes accessed | tf_op | source)
XLA Modules:
  0.0 807.9 jit_solution(14648596339780141633)
XLA Ops:
  2.5 4.0 collective-permute-start.13
  11.5 2.9 collective-permute-start
  16.1 9.4 %collective-permute-done.2 = bf16[1,96,768]{2,1,0:T(8,128)(2,1)S(1)} collective-permute-done((bf16[1,96,768]{2,1,0:T(8,128)(2,1)}, bf16[1,96,768]{2,1,0:T(8,128)(2,1)S(1)}, u32[]{:S(2)}, u32[]{:S(2)}) %collective-permute-start.2) | collective-permute-done | bytes 147488 | tf_op jit(solution)/shard_map/ppermute | solution.py:335
  25.6 11.2 %collective-permute-start.17 = (bf16[2,96,768]{2,1,0:T(8,128)(2,1)}, bf16[2,96,768]{2,1,0:T(8,128)(2,1)S(1)}, u32[]{:S(2)}, u32[]{:S(2)}) collective-permute-start(bf16[2,96,768]{2,1,0:T(8,128)(2,1)} %fusion.30), channel_id=1, source_target_pairs={{0,1},{1,2},{2,3},{3,0},{4,5},{5,6},{6,7},{7,4},{8,9},{9,10},{10,1... | collective-permute-start | bytes 884744 | tf_op jit(solution)/shard_map/ppermute | solution.py:335
  36.8 6.3 collective-permute-done.1
  43.1 1.9 collective-permute-start.3
  47.3 1.9 collective-permute-start.10
  50.8 10.0 %collective-permute-done.14 = bf16[2,96,768]{2,1,0:T(8,128)(2,1)S(1)} collective-permute-done((bf16[2,96,768]{2,1,0:T(8,128)(2,1)S(1)}, bf16[2,96,768]{2,1,0:T(8,128)(2,1)S(1)}, u32[]{:S(2)}, u32[]{:S(2)}) %collective-permute-start.14) | collective-permute-done | bytes 294944 | tf_op jit(solution)/shard_map/ppermute | solution.py:332
  67.6 11.2 %collective-permute-done.19 = bf16[4,96,768]{2,1,0:T(8,128)(2,1)S(1)} collective-permute-done((bf16[4,96,768]{2,1,0:T(8,128)(2,1)S(1)}, bf16[4,96,768]{2,1,0:T(8,128)(2,1)S(1)}, u32[]{:S(2)}, u32[]{:S(2)}) %collective-permute-start.19) | collective-permute-done | bytes 589856 | tf_op jit(solution)/shard_map/ppermute | solution.py:332
  79.7 8.4 %collective-permute-done.11 = bf16[4,96,768]{2,1,0:T(8,128)(2,1)S(1)} collective-permute-done((bf16[4,96,768]{2,1,0:T(8,128)(2,1)S(1)}, bf16[4,96,768]{2,1,0:T(8,128)(2,1)S(1)}, u32[]{:S(2)}, u32[]{:S(2)}) %collective-permute-start.11) | collective-permute-done | bytes 589856 | tf_op jit(solution)/shard_map/ppermute | solution.py:332
  94.9 6.2 attn_fwd.2
  106.5 2.3 collective-permute-done.7
  108.9 2.9 collective-permute-start.8
  111.7 3.1 collective-permute-done.8
  114.8 73.4 %place.9 = bf16[2,768,768]{2,1,0:T(8,128)(2,1)} custom-call(s32[8]{0:T(128)} %stack.29.index_ref, bf16[8,96,768]{2,1,0:T(8,128)(2,1)} %constant_dynamic-update-slice_fusion.14.refs_0_, bf16[8,96,768]{2,1,0:T(8,128)(2,1)} %collective-permute-done.20.refs_1_), custom_call_target="tpu_custom_call" | custom-call | tf_op jit(solution)/shard_map/place/pallas_call | solution.py:307
  188.2 73.4 %place.7 = bf16[2,768,768]{2,1,0:T(8,128)(2,1)} custom-call(s32[8]{0:T(128)} %stack.29.index_ref, bf16[8,96,768]{2,1,0:T(8,128)(2,1)} %constant_dynamic-update-slice_fusion.8.refs_0_, bf16[8,96,768]{2,1,0:T(8,128)(2,1)} %collective-permute-done.12.refs_1_), custom_call_target="tpu_custom_call" | custom-call | tf_op jit(solution)/shard_map/place/pallas_call | solution.py:307
  261.6 73.4 %place.8 = bf16[2,768,768]{2,1,0:T(8,128)(2,1)} custom-call(s32[8]{0:T(128)} %stack.28.index_ref, bf16[8,96,768]{2,1,0:T(8,128)(2,1)} %constant_dynamic-update-slice_fusion.11.refs_0_, bf16[8,96,768]{2,1,0:T(8,128)(2,1)} %collective-permute-done.16.refs_1_), custom_call_target="tpu_custom_call" | custom-call | tf_op jit(solution)/shard_map/place/pallas_call | solution.py:307
  335.0 3.4 fusion.42
  342.1 109.2 %place.6.a_ref = bf16[3,768,768]{2,1,0:T(8,128)(2,1)} custom-call(s32[8]{0:T(128)} %stack.28.index_ref, bf16[12,96,768]{2,1,0:T(8,128)(2,1)} %constant_dynamic-update-slice_fusion.refs_0_, bf16[12,96,768]{2,1,0:T(8,128)(2,1)} %collective-permute-done.5.refs_1_), custom_call_target="tpu_custom_call" | custom-call | tf_op jit(solution)/shard_map/place/pallas_call | solution.py:307
  451.3 2.0 copy-done.2
  454.2 18.0 %attn_fwd.3 = (bf16[3,512,768]{2,1,0:T(8,128)(2,1)S(1)}, bf16[3,512,192]{2,1,0:T(8,128)(2,1)S(1)}, f32[3,512,128]{2,1,0:T(8,128)S(1)}, f32[512,768]{1,0:T(8,128)S(1)}) custom-call(s32[10]{0:T(128)S(1)} %pad_add_fusion.meta_ref, bf16[512,768]{1,0:T(8,128)(2,1)S(1)} %fusion.10.n1_ref, bf16[3,768,768]{2,1,0:T(8,128)(2,1)S(1)} %copy-done.2, ...), custom_call_target="tpu_custom_call" | custom-call | flops 6000000000 | bytes 12000000 | tf_op jit(solution)/shard_map/attn_fwd/pallas_call | solution.py:106
  475.6 6.3 ffn.4
  484.0 6.2 ffn.7
  491.4 13.7 %ffn.6 = (f32[512,768]{1,0:T(8,128)}, f32[512,768]{1,0:T(8,128)}, bf16[1,768,768]{2,1,0:T(8,128)(2,1)S(1)}, bf16[1,768,768]{2,1,0:T(8,128)(2,1)S(1)}) custom-call(bf16[512,768]{1,0:T(8,128)(2,1)S(1)} %multiply_convert_fusion.n2_ref, bf16[512,768]{1,0:T(8,128)(2,1)S(1)} %copy-done.3, bf16[1,768,768]{2,1,0:T(8,128)(2,1)S(1)} %copy-done.13, ...), custom_call_target="tpu_custom_call" | custom-call | flops 5000000000 | bytes 8000000 | tf_op jit(solution)/shard_map/ffn/pallas_call | solution.py:170
  505.4 1.9 constant_dynamic-slice_fusion.1
  510.0 6.3 ffn.5
  516.4 4.6 multiply_reduce_fusion
  522.2 20.2 %attn_bwd.3 = (bf16[3,768,768]{2,1,0:T(8,128)(2,1)}, f32[512,768]{1,0:T(8,128)S(1)}, f32[3,8,1024]{2,1,0:T(8,128)S(1)}) custom-call(s32[10]{0:T(128)S(1)} %pad_add_fusion.meta_ref, bf16[512,768]{1,0:T(8,128)(2,1)S(1)} %fusion.10.n1_ref, bf16[512,768]{1,0:T(8,128)(2,1)S(1)} %fusion.39.gh_ref, bf16[3,768,768]{2,1,0:T(8,128)(2,1)} %place.6.a_ref, ...), custom_call_target="tpu_custom_call" | custom-call | flops 12000000000 | bytes 24000000 | tf_op jit(solution)/shard_map/attn_bwd/pallas_call | solution.py:249
  543.6 7.0 attn_bwd.2
  550.6 2.7 fusion.16
  558.0 2.0 pad_maximum_fusion.2
  572.2 10.4 %collective-permute-done.44 = bf16[2,2,96,768]{3,2,0,1:T(8,128)(2,1)S(1)} collective-permute-done((bf16[2,2,96,768]{3,2,0,1:T(8,128)(2,1)S(1)}, bf16[2,2,96,768]{3,2,0,1:T(8,128)(2,1)S(1)}, u32[]{:S(2)}, u32[]{:S(2)}) %collective-permute-start.44) | collective-permute-done | bytes 589856 | tf_op jit(solution)/shard_map/ppermute | solution.py:332
  587.0 7.9 collective-permute-done.37
  600.5 4.7 collective-permute-done.45
  606.7 5.3 collective-permute-done.41
  613.1 17.3 %collective-permute-done.22 = bf16[4,2,96,768]{3,2,0,1:T(8,128)(2,1)S(1)} collective-permute-done((bf16[4,2,96,768]{3,2,0,1:T(8,128)(2,1)S(1)}, bf16[4,2,96,768]{3,2,0,1:T(8,128)(2,1)S(1)}, u32[]{:S(2)}, u32[]{:S(2)}) %collective-permute-start.22) | collective-permute-done | bytes 1179680 | tf_op jit(solution)/shard_map/ppermute | solution.py:332
  631.7 3.6 collective-permute-done.38
  636.2 2.8 collective-permute-done.42
  642.0 7.4 collective-permute-done.31
  655.1 2.9 collective-permute-start.26
  658.0 3.4 collective-permute-done.24
  662.2 4.6 collective-permute-done.25
  668.8 2.4 collective-permute-start.34
  675.6 2.3 fusion.15
  678.8 4.6 collective-permute-done.28
  685.3 73.4 %place.11 = bf16[2,768,768]{2,1,0:T(8,128)(2,1)} custom-call(s32[8]{0:T(128)} %stack.29.index_ref, bf16[8,96,768]{2,1,0:T(8,128)(2,1)} %copy-done.41, bf16[8,96,768]{2,1,0:T(8,128)(2,1)} %collective-permute-done.53.refs_1_), custom_call_target="tpu_custom_call" | custom-call | tf_op jit(solution)/shard_map/place/pallas_call | solution.py:307
  758.7 4.2 fusion.18
  763.7 37.6 %place.10 = bf16[1,768,768]{2,1,0:T(8,128)(2,1)} custom-call(s32[8]{0:T(128)} %stack.28.index_ref, bf16[4,96,768]{2,1,0:T(8,128)(2,1)} %copy-done.43, bf16[4,96,768]{2,1,0:T(8,128)(2,1)} %copy-done.50), custom_call_target="tpu_custom_call" | custom-call | tf_op jit(solution)/shard_map/place/pallas_call | solution.py:307
  (333 shorter events, 105.0 us)
Async XLA Ops:
  2.5 43.9 %collective-permute-start.13 = (bf16[2,96,768]{2,1,0:T(8,128)(2,1)}, bf16[2,96,768]{2,1,0:T(8,128)(2,1)S(1)}, u32[]{:S(2)}, u32[]{:S(2)}) collective-permute-start(bf16[2,96,768]{2,1,0:T(8,128)(2,1)} %fusion.30), channel_id=1, source_target_pairs={{0,2},{1,3},{2,0},{3,1},{4,6},{5,7},{6,4},{7,5},{8,10},{9,11},{10,... | collective-permute-start | bytes 884744 | tf_op jit(solution)/shard_map/ppermute | solution.py:335
  6.5 40.8 %collective-permute-start.9 = (bf16[2,96,768]{2,1,0:T(8,128)(2,1)}, bf16[2,96,768]{2,1,0:T(8,128)(2,1)S(1)}, u32[]{:S(2)}, u32[]{:S(2)}) collective-permute-start(bf16[2,96,768]{2,1,0:T(8,128)(2,1)} %fusion.30), channel_id=1, source_target_pairs={{0,3},{1,0},{2,1},{3,2},{4,7},{5,4},{6,5},{7,6},{8,11},{9,8},{10,9... | collective-permute-start | bytes 884744 | tf_op jit(solution)/shard_map/ppermute | solution.py:335
  9.8 15.7 %collective-permute-start.2 = (bf16[1,96,768]{2,1,0:T(8,128)(2,1)}, bf16[1,96,768]{2,1,0:T(8,128)(2,1)S(1)}, u32[]{:S(2)}, u32[]{:S(2)}) collective-permute-start(bf16[1,96,768]{2,1,0:T(8,128)(2,1)} %dynamic-slice_bitcast_fusion.10), channel_id=1, source_target_pairs={{0,1},{1,2},{2,3},{3,0},{4,5},{5,6},{6,7},{7,4},{8,9},{9,10},{10,1... | collective-permute-start | bytes 442376 | tf_op jit(solution)/shard_map/ppermute | solution.py:335
  10.5 32.6 %collective-permute-start.1 = (bf16[1,96,768]{2,1,0:T(8,128)(2,1)}, bf16[1,96,768]{2,1,0:T(8,128)(2,1)S(1)}, u32[]{:S(2)}, u32[]{:S(2)}) collective-permute-start(bf16[1,96,768]{2,1,0:T(8,128)(2,1)} %dynamic-slice_bitcast_fusion.10), channel_id=1, source_target_pairs={{0,2},{1,3},{2,0},{3,1},{4,6},{5,7},{6,4},{7,5},{8,10},{9,11},{10,... | collective-permute-start | bytes 442376 | tf_op jit(solution)/shard_map/ppermute | solution.py:335
  11.5 31.5 %collective-permute-start = (bf16[1,96,768]{2,1,0:T(8,128)(2,1)}, bf16[1,96,768]{2,1,0:T(8,128)(2,1)S(1)}, u32[]{:S(2)}, u32[]{:S(2)}) collective-permute-start(bf16[1,96,768]{2,1,0:T(8,128)(2,1)} %dynamic-slice_bitcast_fusion.10), channel_id=1, source_target_pairs={{0,3},{1,0},{2,1},{3,2},{4,7},{5,4},{6,5},{7,6},{8,11},{9,8},{10,9... | collective-permute-start | bytes 442376 | tf_op jit(solution)/shard_map/ppermute | solution.py:335
  25.6 23.6 %collective-permute-start.17 = (bf16[2,96,768]{2,1,0:T(8,128)(2,1)}, bf16[2,96,768]{2,1,0:T(8,128)(2,1)S(1)}, u32[]{:S(2)}, u32[]{:S(2)}) collective-permute-start(bf16[2,96,768]{2,1,0:T(8,128)(2,1)} %fusion.30), channel_id=1, source_target_pairs={{0,1},{1,2},{2,3},{3,0},{4,5},{5,6},{6,7},{7,4},{8,9},{9,10},{10,1... | collective-permute-start | bytes 884744 | tf_op jit(solution)/shard_map/ppermute | solution.py:335
  43.1 60.9 %collective-permute-start.6 = (bf16[1,16,1024]{2,1,0:T(8,128)(2,1)S(1)}, bf16[1,16,1024]{2,1,0:T(8,128)(2,1)}, u32[]{:S(2)}, u32[]{:S(2)}) collective-permute-start(bf16[1,16,1024]{2,1,0:T(8,128)(2,1)S(1)} %pad_bitcast_fusion.rel_ref), channel_id=1, source_target_pairs={{0,3},{1,0},{2,1},{3,2},{4,7},{5,4},{6,5},{7,6},{8,11},{9,8},{10,9... | collective-permute-start | bytes 98312 | tf_op jit(solution)/shard_map/ppermute | solution.py:335
  43.1 21.6 %collective-permute-start.3 = (bf16[3,96,768]{2,1,0:T(8,128)(2,1)S(1)}, bf16[3,96,768]{2,1,0:T(8,128)(2,1)S(1)}, u32[]{:S(2)}, u32[]{:S(2)}) collective-permute-start(bf16[3,96,768]{2,1,0:T(8,128)(2,1)S(1)} %pad_maximum_fusion.13), channel_id=1, source_target_pairs={{0,8},{4,12},{8,0},{12,4},{16,24},{20,28},{24,16},{28,20},{1,9},{5... | collective-permute-start | bytes 1327112 | tf_op jit(solution)/shard_map/ppermute | solution.py:332
  46.4 14.5 %collective-permute-start.14 = (bf16[2,96,768]{2,1,0:T(8,128)(2,1)S(1)}, bf16[2,96,768]{2,1,0:T(8,128)(2,1)S(1)}, u32[]{:S(2)}, u32[]{:S(2)}) collective-permute-start(bf16[2,96,768]{2,1,0:T(8,128)(2,1)S(1)} %collective-permute-done.13), channel_id=1, source_target_pairs={{0,8},{4,12},{8,0},{12,4},{16,24},{20,28},{24,16},{28,20},{1,9},{5... | collective-permute-start | bytes 884744 | tf_op jit(solution)/shard_map/ppermute | solution.py:332
  47.3 16.8 %collective-permute-start.10 = (bf16[2,96,768]{2,1,0:T(8,128)(2,1)S(1)}, bf16[2,96,768]{2,1,0:T(8,128)(2,1)S(1)}, u32[]{:S(2)}, u32[]{:S(2)}) collective-permute-start(bf16[2,96,768]{2,1,0:T(8,128)(2,1)S(1)} %collective-permute-done.9), channel_id=1, source_target_pairs={{0,16},{4,20},{8,24},{12,28},{16,0},{20,4},{24,8},{28,12},{1,17},{... | collective-permute-start | bytes 884744 | tf_op jit(solution)/shard_map/ppermute | solution.py:332
  49.2 13.3 %collective-permute-start.18 = (bf16[2,96,768]{2,1,0:T(8,128)(2,1)S(1)}, bf16[2,96,768]{2,1,0:T(8,128)(2,1)S(1)}, u32[]{:S(2)}, u32[]{:S(2)}) collective-permute-start(bf16[2,96,768]{2,1,0:T(8,128)(2,1)S(1)} %collective-permute-done.17), channel_id=1, source_target_pairs={{0,16},{4,20},{8,24},{12,28},{16,0},{20,4},{24,8},{28,12},{1,17},{... | collective-permute-start | bytes 884744 | tf_op jit(solution)/shard_map/ppermute | solution.py:332
  60.9 28.1 %collective-permute-start.15 = (bf16[4,96,768]{2,1,0:T(8,128)(2,1)S(1)}, bf16[4,96,768]{2,1,0:T(8,128)(2,1)S(1)}, u32[]{:S(2)}, u32[]{:S(2)}) collective-permute-start(bf16[4,96,768]{2,1,0:T(8,128)(2,1)S(1)} %pad_maximum_fusion.9), channel_id=1, source_target_pairs={{0,16},{4,20},{8,24},{12,28},{16,0},{20,4},{24,8},{28,12},{1,17},{... | collective-permute-start | bytes 1769480 | tf_op jit(solution)/shard_map/ppermute | solution.py:332
  62.5 16.3 %collective-permute-start.19 = (bf16[4,96,768]{2,1,0:T(8,128)(2,1)S(1)}, bf16[4,96,768]{2,1,0:T(8,128)(2,1)S(1)}, u32[]{:S(2)}, u32[]{:S(2)}) collective-permute-start(bf16[4,96,768]{2,1,0:T(8,128)(2,1)S(1)} %pad_maximum_fusion.10), channel_id=1, source_target_pairs={{0,8},{4,12},{8,0},{12,4},{16,24},{20,28},{24,16},{28,20},{1,9},{5... | collective-permute-start | bytes 1769480 | tf_op jit(solution)/shard_map/ppermute | solution.py:332
  64.1 24.0 %collective-permute-start.11 = (bf16[4,96,768]{2,1,0:T(8,128)(2,1)S(1)}, bf16[4,96,768]{2,1,0:T(8,128)(2,1)S(1)}, u32[]{:S(2)}, u32[]{:S(2)}) collective-permute-start(bf16[4,96,768]{2,1,0:T(8,128)(2,1)S(1)} %pad_maximum_fusion.8), channel_id=1, source_target_pairs={{0,8},{4,12},{8,0},{12,4},{16,24},{20,28},{24,16},{28,20},{1,9},{5... | collective-permute-start | bytes 1769480 | tf_op jit(solution)/shard_map/ppermute | solution.py:332
  64.8 28.6 %collective-permute-start.4 = (bf16[6,96,768]{2,1,0:T(8,128)(2,1)S(1)}, bf16[6,96,768]{2,1,0:T(8,128)(2,1)S(1)}, u32[]{:S(2)}, u32[]{:S(2)}) collective-permute-start(bf16[6,96,768]{2,1,0:T(8,128)(2,1)S(1)} %pad_maximum_fusion.7), channel_id=1, source_target_pairs={{0,16},{4,20},{8,24},{12,28},{16,0},{20,4},{24,8},{28,12},{1,17},{... | collective-permute-start | bytes 2654216 | tf_op jit(solution)/shard_map/ppermute | solution.py:332
  79.7 35.1 %collective-permute-start.20 = (bf16[8,96,768]{2,1,0:T(8,128)(2,1)}, bf16[8,96,768]{2,1,0:T(8,128)(2,1)}, u32[]{:S(2)}, u32[]{:S(2)}) collective-permute-start(bf16[8,96,768]{2,1,0:T(8,128)(2,1)} %constant_dynamic-update-slice_fusion.14.refs_0_), channel_id=1, source_target_pairs={{0,4},{4,0},{8,12},{12,8},{16,20},{20,16},{24,28},{28,24},{1,5},{5... | collective-permute-start | bytes 3538952 | tf_op jit(solution)/shard_map/ppermute | solution.py:332
  89.0 99.2 %collective-permute-start.12 = (bf16[8,96,768]{2,1,0:T(8,128)(2,1)}, bf16[8,96,768]{2,1,0:T(8,128)(2,1)}, u32[]{:S(2)}, u32[]{:S(2)}) collective-permute-start(bf16[8,96,768]{2,1,0:T(8,128)(2,1)} %constant_dynamic-update-slice_fusion.8.refs_0_), channel_id=1, source_target_pairs={{0,4},{4,0},{8,12},{12,8},{16,20},{20,16},{24,28},{28,24},{1,5},{5... | collective-permute-start | bytes 3538952 | tf_op jit(solution)/shard_map/ppermute | solution.py:332
  89.9 171.7 %collective-permute-start.16 = (bf16[8,96,768]{2,1,0:T(8,128)(2,1)}, bf16[8,96,768]{2,1,0:T(8,128)(2,1)}, u32[]{:S(2)}, u32[]{:S(2)}) collective-permute-start(bf16[8,96,768]{2,1,0:T(8,128)(2,1)} %constant_dynamic-update-slice_fusion.11.refs_0_), channel_id=1, source_target_pairs={{0,4},{4,0},{8,12},{12,8},{16,20},{20,16},{24,28},{28,24},{1,5},{5... | collective-permute-start | bytes 3538952 | tf_op jit(solution)/shard_map/ppermute | solution.py:332
  94.5 247.6 %collective-permute-start.5 = (bf16[12,96,768]{2,1,0:T(8,128)(2,1)}, bf16[12,96,768]{2,1,0:T(8,128)(2,1)}, u32[]{:S(2)}, u32[]{:S(2)}) collective-permute-start(bf16[12,96,768]{2,1,0:T(8,128)(2,1)} %constant_dynamic-update-slice_fusion.refs_0_), channel_id=1, source_target_pairs={{0,4},{4,0},{8,12},{12,8},{16,20},{20,16},{24,28},{28,24},{1,5},{5... | collective-permute-start | bytes 5308424 | tf_op jit(solution)/shard_map/ppermute | solution.py:332
  509.5 54.6 %collective-permute-start.43 = (bf16[2,2,2,96,768]{4,3,0,1,2:T(8,128)(2,1)}, bf16[2,2,2,96,768]{4,3,0,1,2:T(8,128)(2,1)}, u32[]{:S(2)}, u32[]{:S(2)}) collective-permute-start(bf16[2,2,2,96,768]{4,3,0,1,2:T(8,128)(2,1)} %bitcast.148), channel_id=1, source_target_pairs={{0,4},{4,0},{8,12},{12,8},{16,20},{20,16},{24,28},{28,24},{1,5},{5... | collective-permute-start | bytes 3538952 | tf_op jit(solution)/shard_map/ppermute | solution.py:332
  509.5 56.9 %collective-permute-start.47 = (bf16[2,2,2,96,768]{4,3,0,2,1:T(8,128)(2,1)}, bf16[2,2,2,96,768]{4,3,0,2,1:T(8,128)(2,1)}, u32[]{:S(2)}, u32[]{:S(2)}) collective-permute-start(bf16[2,2,2,96,768]{4,3,0,2,1:T(8,128)(2,1)} %bitcast.147), channel_id=1, source_target_pairs={{0,4},{4,0},{8,12},{12,8},{16,20},{20,16},{24,28},{28,24},{1,5},{5... | collective-permute-start | bytes 3538952 | tf_op jit(solution)/shard_map/ppermute | solution.py:332
  558.0 82.5 %collective-permute-start.30 = (f32[1920]{0:T(1024)S(1)}, f32[1920]{0:T(1024)S(1)}, u32[]{:S(2)}, u32[]{:S(2)}) collective-permute-start(f32[1920]{0:T(1024)S(1)} %pad_maximum_fusion.17), channel_id=1, source_target_pairs={{0,4},{4,0},{8,12},{12,8},{16,20},{20,16},{24,28},{28,24},{1,5},{5... | collective-permute-start | bytes 23048 | tf_op jit(solution)/shard_map/ppermute | solution.py:332
  561.0 8.2 %collective-permute-start.36 = (bf16[2,2,2,96,768]{4,3,0,1,2:T(8,128)(2,1)S(1)}, bf16[2,2,2,96,768]{4,3,0,1,2:T(8,128)(2,1)S(1)}, u32[]{:S(2)}, u32[]{:S(2)}) collective-permute-start(bf16[2,2,2,96,768]{4,3,0,1,2:T(8,128)(2,1)S(1)} %bitcast.163), channel_id=1, source_target_pairs={{0,4},{4,0},{8,12},{12,8},{16,20},{20,16},{24,28},{28,24},{1,5},{5... | collective-permute-start | bytes 3538952 | tf_op jit(solution)/shard_map/ppermute | solution.py:332
  563.5 7.7 collective-permute-start.39
  564.1 32.1 %collective-permute-start.21 = (bf16[4,2,2,96,768]{4,3,0,2,1:T(8,128)(2,1)S(1)}, bf16[4,2,2,96,768]{4,3,0,2,1:T(8,128)(2,1)S(1)}, u32[]{:S(2)}, u32[]{:S(2)}) collective-permute-start(bf16[4,2,2,96,768]{4,3,0,2,1:T(8,128)(2,1)S(1)} %bitcast.160), channel_id=1, source_target_pairs={{0,4},{4,0},{8,12},{12,8},{16,20},{20,16},{24,28},{28,24},{1,5},{5... | collective-permute-start | bytes 7077896 | tf_op jit(solution)/shard_map/ppermute | solution.py:332
  566.4 16.2 %collective-permute-start.44 = (bf16[2,2,96,768]{3,2,0,1:T(8,128)(2,1)S(1)}, bf16[2,2,96,768]{3,2,0,1:T(8,128)(2,1)S(1)}, u32[]{:S(2)}, u32[]{:S(2)}) collective-permute-start(bf16[2,2,96,768]{3,2,0,1:T(8,128)(2,1)S(1)} %dynamic-slice_bitcast_fusion.2), channel_id=1, source_target_pairs={{0,8},{4,12},{8,0},{12,4},{16,24},{20,28},{24,16},{28,20},{1,9},{5... | collective-permute-start | bytes 1769480 | tf_op jit(solution)/shard_map/ppermute | solution.py:332
  569.2 15.7 %collective-permute-start.48 = (bf16[2,2,96,768]{3,2,0,1:T(8,128)(2,1)S(1)}, bf16[2,2,96,768]{3,2,0,1:T(8,128)(2,1)S(1)}, u32[]{:S(2)}, u32[]{:S(2)}) collective-permute-start(bf16[2,2,96,768]{3,2,0,1:T(8,128)(2,1)S(1)} %dynamic-slice_bitcast_fusion.1), channel_id=1, source_target_pairs={{0,16},{4,20},{8,24},{12,28},{16,0},{20,4},{24,8},{28,12},{1,17},{... | collective-permute-start | bytes 1769480 | tf_op jit(solution)/shard_map/ppermute | solution.py:332
  571.2 23.7 %collective-permute-start.37 = (bf16[2,2,96,768]{3,2,0,1:T(8,128)(2,1)S(1)}, bf16[2,2,96,768]{3,2,0,1:T(8,128)(2,1)S(1)}, u32[]{:S(2)}, u32[]{:S(2)}) collective-permute-start(bf16[2,2,96,768]{3,2,0,1:T(8,128)(2,1)S(1)} %dynamic-slice_bitcast_fusion.4), channel_id=1, source_target_pairs={{0,8},{4,12},{8,0},{12,4},{16,24},{20,28},{24,16},{28,20},{1,9},{5... | collective-permute-start | bytes 1769480 | tf_op jit(solution)/shard_map/ppermute | solution.py:332
  582.6 16.3 %collective-permute-start.40 = (bf16[2,2,96,768]{3,2,0,1:T(8,128)(2,1)S(1)}, bf16[2,2,96,768]{3,2,0,1:T(8,128)(2,1)S(1)}, u32[]{:S(2)}, u32[]{:S(2)}) collective-permute-start(bf16[2,2,96,768]{3,2,0,1:T(8,128)(2,1)S(1)} %dynamic-slice_bitcast_fusion.3), channel_id=1, source_target_pairs={{0,16},{4,20},{8,24},{12,28},{16,0},{20,4},{24,8},{28,12},{1,17},{... | collective-permute-start | bytes 1769480 | tf_op jit(solution)/shard_map/ppermute | solution.py:332
  584.9 20.3 %collective-permute-start.45 = (bf16[2,96,768]{2,1,0:T(8,128)(2,1)S(1)}, bf16[2,96,768]{2,1,0:T(8,128)(2,1)S(1)}, u32[]{:S(2)}, u32[]{:S(2)}) collective-permute-start(bf16[2,96,768]{2,1,0:T(8,128)(2,1)S(1)} %dynamic-slice_bitcast_fusion.7), channel_id=1, source_target_pairs={{0,16},{4,20},{8,24},{12,28},{16,0},{20,4},{24,8},{28,12},{1,17},{... | collective-permute-start | bytes 884744 | tf_op jit(solution)/shard_map/ppermute | solution.py:332
  594.9 11.6 %collective-permute-start.49 = (bf16[2,96,768]{2,1,0:T(8,128)(2,1)S(1)}, bf16[2,96,768]{2,1,0:T(8,128)(2,1)S(1)}, u32[]{:S(2)}, u32[]{:S(2)}) collective-permute-start(bf16[2,96,768]{2,1,0:T(8,128)(2,1)S(1)} %dynamic-slice_bitcast_fusion.6), channel_id=1, source_target_pairs={{0,8},{4,12},{8,0},{12,4},{16,24},{20,28},{24,16},{28,20},{1,9},{5... | collective-permute-start | bytes 884744 | tf_op jit(solution)/shard_map/ppermute | solution.py:332
  597.0 33.5 %collective-permute-start.22 = (bf16[4,2,96,768]{3,2,0,1:T(8,128)(2,1)S(1)}, bf16[4,2,96,768]{3,2,0,1:T(8,128)(2,1)S(1)}, u32[]{:S(2)}, u32[]{:S(2)}) collective-permute-start(bf16[4,2,96,768]{3,2,0,1:T(8,128)(2,1)S(1)} %dynamic-slice_bitcast_fusion), channel_id=1, source_target_pairs={{0,16},{4,20},{8,24},{12,28},{16,0},{20,4},{24,8},{28,12},{1,17},{... | collective-permute-start | bytes 3538952 | tf_op jit(solution)/shard_map/ppermute | solution.py:332
  598.9 36.5 %collective-permute-start.38 = (bf16[2,96,768]{2,1,0:T(8,128)(2,1)S(1)}, bf16[2,96,768]{2,1,0:T(8,128)(2,1)S(1)}, u32[]{:S(2)}, u32[]{:S(2)}) collective-permute-start(bf16[2,96,768]{2,1,0:T(8,128)(2,1)S(1)} %dynamic-slice_bitcast_fusion.9), channel_id=1, source_target_pairs={{0,16},{4,20},{8,24},{12,28},{16,0},{20,4},{24,8},{28,12},{1,17},{... | collective-permute-start | bytes 884744 | tf_op jit(solution)/shard_map/ppermute | solution.py:332
  606.4 29.8 %collective-permute-start.46 = (bf16[2,96,768]{2,1,0:T(8,128)(2,1)S(1)}, bf16[2,96,768]{2,1,0:T(8,128)(2,1)S(1)}, u32[]{:S(2)}, u32[]{:S(2)}) collective-permute-start(bf16[2,96,768]{2,1,0:T(8,128)(2,1)S(1)} %fusion.27), channel_id=1, source_target_pairs={{0,2},{1,3},{2,0},{3,1},{4,6},{5,7},{6,4},{7,5},{8,10},{9,11},{10,... | collective-permute-start | bytes 884744 | tf_op jit(solution)/shard_map/ppermute | solution.py:338
  611.9 24.3 %collective-permute-start.50 = (bf16[2,96,768]{2,1,0:T(8,128)(2,1)S(1)}, bf16[2,96,768]{2,1,0:T(8,128)(2,1)S(1)}, u32[]{:S(2)}, u32[]{:S(2)}) collective-permute-start(bf16[2,96,768]{2,1,0:T(8,128)(2,1)S(1)} %fusion.26), channel_id=1, source_target_pairs={{0,3},{1,0},{2,1},{3,2},{4,7},{5,4},{6,5},{7,6},{8,11},{9,8},{10,9... | collective-permute-start | bytes 884744 | tf_op jit(solution)/shard_map/ppermute | solution.py:338
  630.5 8.5 %collective-permute-start.42 = (bf16[2,96,768]{2,1,0:T(8,128)(2,1)S(1)}, bf16[2,96,768]{2,1,0:T(8,128)(2,1)S(1)}, u32[]{:S(2)}, u32[]{:S(2)}) collective-permute-start(bf16[2,96,768]{2,1,0:T(8,128)(2,1)S(1)} %fusion.28), channel_id=1, source_target_pairs={{0,1},{1,2},{2,3},{3,0},{4,5},{5,6},{6,7},{7,4},{8,9},{9,10},{10,1... | collective-permute-start | bytes 884744 | tf_op jit(solution)/shard_map/ppermute | solution.py:338
  635.3 18.5 %collective-permute-start.23 = (bf16[4,96,768]{2,1,0:T(8,128)(2,1)S(1)}, bf16[4,96,768]{2,1,0:T(8,128)(2,1)S(1)}, u32[]{:S(2)}, u32[]{:S(2)}) collective-permute-start(bf16[4,96,768]{2,1,0:T(8,128)(2,1)S(1)} %dynamic-slice_bitcast_fusion.5), channel_id=1, source_target_pairs={{0,8},{4,12},{8,0},{12,4},{16,24},{20,28},{24,16},{28,20},{1,9},{5... | collective-permute-start | bytes 1769480 | tf_op jit(solution)/shard_map/ppermute | solution.py:332
  639.2 13.9 %collective-permute-start.51 = (bf16[2,96,768]{2,1,0:T(8,128)(2,1)S(1)}, bf16[2,96,768]{2,1,0:T(8,128)(2,1)S(1)}, u32[]{:S(2)}, u32[]{:S(2)}) collective-permute-start(bf16[2,96,768]{2,1,0:T(8,128)(2,1)S(1)} %add_convert_fusion.1), channel_id=1, source_target_pairs={{0,16},{4,20},{8,24},{12,28},{16,0},{20,4},{24,8},{28,12},{1,17},{... | collective-permute-start | bytes 884744 | tf_op jit(solution)/shard_map/ppermute | solution.py:332
  640.5 8.9 %collective-permute-start.31 = (f32[1920]{0:T(1024)S(1)}, f32[1920]{0:T(1024)S(1)}, u32[]{:S(2)}, u32[]{:S(2)}) collective-permute-start(f32[1920]{0:T(1024)S(1)} %fusion.48), channel_id=1, source_target_pairs={{0,8},{4,12},{8,0},{12,4},{16,24},{20,28},{24,16},{28,20},{1,9},{5... | collective-permute-start | bytes 23048 | tf_op jit(solution)/shard_map/ppermute | solution.py:332
  653.1 19.5 %collective-permute-start.52 = (bf16[4,96,768]{2,1,0:T(8,128)(2,1)S(1)}, bf16[4,96,768]{2,1,0:T(8,128)(2,1)S(1)}, u32[]{:S(2)}, u32[]{:S(2)}) collective-permute-start(bf16[4,96,768]{2,1,0:T(8,128)(2,1)S(1)} %pad_maximum_fusion.12), channel_id=1, source_target_pairs={{0,8},{4,12},{8,0},{12,4},{16,24},{20,28},{24,16},{28,20},{1,9},{5... | collective-permute-start | bytes 1769480 | tf_op jit(solution)/shard_map/ppermute | solution.py:332
  654.1 7.4 collective-permute-start.24
  655.1 7.1 collective-permute-start.26
  658.0 8.9 %collective-permute-start.25 = (bf16[96,768]{1,0:T(8,128)(2,1)S(1)}, bf16[96,768]{1,0:T(8,128)(2,1)S(1)}, u32[]{:S(2)}, u32[]{:S(2)}) collective-permute-start(bf16[96,768]{1,0:T(8,128)(2,1)S(1)} %get-tuple-element.126), channel_id=1, source_target_pairs={{0,2},{1,3},{2,0},{3,1},{4,6},{5,7},{6,4},{7,5},{8,10},{9,11},{10,... | collective-permute-start | bytes 442376 | tf_op jit(solution)/shard_map/ppermute | solution.py:338
  668.8 9.1 %collective-permute-start.33 = (f32[1632]{0:T(1024)S(1)}, f32[1632]{0:T(1024)S(1)}, u32[]{:S(2)}, u32[]{:S(2)}) collective-permute-start(f32[1632]{0:T(1024)S(1)} %get-tuple-element.132), channel_id=1, source_target_pairs={{0,1},{1,2},{2,3},{3,0},{4,5},{5,6},{6,7},{7,4},{8,9},{9,10},{10,1... | collective-permute-start | bytes 19592 | tf_op jit(solution)/shard_map/ppermute | solution.py:338
  668.8 9.1 %collective-permute-start.34 = (f32[1632]{0:T(1024)S(1)}, f32[1632]{0:T(1024)S(1)}, u32[]{:S(2)}, u32[]{:S(2)}) collective-permute-start(f32[1632]{0:T(1024)S(1)} %get-tuple-element.133), channel_id=1, source_target_pairs={{0,2},{1,3},{2,0},{3,1},{4,6},{5,7},{6,4},{7,5},{8,10},{9,11},{10,... | collective-permute-start | bytes 19592 | tf_op jit(solution)/shard_map/ppermute | solution.py:338
  672.8 12.5 %collective-permute-start.53 = (bf16[8,96,768]{2,1,0:T(8,128)(2,1)S(1)}, bf16[8,96,768]{2,1,0:T(8,128)(2,1)}, u32[]{:S(2)}, u32[]{:S(2)}) collective-permute-start(bf16[8,96,768]{2,1,0:T(8,128)(2,1)S(1)} %pad_maximum_fusion.6.refs_0_), channel_id=1, source_target_pairs={{0,4},{4,0},{8,12},{12,8},{16,20},{20,16},{24,28},{28,24},{1,5},{5... | collective-permute-start | bytes 3538952 | tf_op jit(solution)/shard_map/ppermute | solution.py:332
  673.8 9.6 %collective-permute-start.28 = (bf16[2,96,768]{2,1,0:T(8,128)(2,1)}, bf16[2,96,768]{2,1,0:T(8,128)(2,1)}, u32[]{:S(2)}, u32[]{:S(2)}) collective-permute-start(bf16[2,96,768]{2,1,0:T(8,128)(2,1)} %pad_maximum_fusion.14), channel_id=1, source_target_pairs={{0,16},{4,20},{8,24},{12,28},{16,0},{20,4},{24,8},{28,12},{1,17},{... | collective-permute-start | bytes 884744 | tf_op jit(solution)/shard_map/ppermute | solution.py:332
  684.5 78.4 %collective-permute-start.29 = (bf16[4,96,768]{2,1,0:T(8,128)(2,1)S(1)}, bf16[4,96,768]{2,1,0:T(8,128)(2,1)S(1)}, u32[]{:S(2)}, u32[]{:S(2)}) collective-permute-start(bf16[4,96,768]{2,1,0:T(8,128)(2,1)S(1)} %pad_maximum_fusion.11.refs_0_), channel_id=1, source_target_pairs={{0,4},{4,0},{8,12},{12,8},{16,20},{20,16},{24,28},{28,24},{1,5},{5... | collective-permute-start | bytes 1769480 | tf_op jit(solution)/shard_map/ppermute | solution.py:332
  (76 other events, 1547.6 us)

commit v2 on v1

v2 whole, which is shorter than its diff:
```python
import functools

import jax
import jax.numpy as jnp
import numpy as np
from jax import lax
from jax.experimental import pallas as pl
from jax.experimental.pallas import tpu as pltpu
from jax.sharding import PartitionSpec as P

BIG = 512
HEAD = 64
EPS = 1e-06
THRESHOLDS = (12, 16, 23, 32, 46, 64, 91)
MASKED = -1e30
TILE = 128
SPAN = 1024
BF = jnp.bfloat16
F32 = jnp.float32
MIB = 1024 * 1024


def offset_one_hot(buckets):
    u = np.arange(SPAN)
    offsets = np.where(u < 896, u, u - SPAN) - 3 * TILE
    distance = np.abs(offsets)
    far = 8 + sum((distance >= t).astype(np.int32) for t in THRESHOLDS)
    bucket = np.where(distance < 8, distance, far) + np.where(offsets > 0, 16, 0)
    return (bucket[:, None] == np.arange(buckets)[None, :]).astype(np.float32)


def dot_nn(a, b):
    return lax.dot_general(a, b, (((1,), (0,)), ((), ())), preferred_element_type=F32)


def dot_nt(a, b):
    return lax.dot_general(a, b, (((1,), (1,)), ((), ())), preferred_element_type=F32)


def dot_tn(a, b):
    return lax.dot_general(a, b, (((0,), (0,)), ((), ())), preferred_element_type=F32)


def mask_rows(meta_ref, slots):
    bucket = meta_ref[0]
    half = BIG // 2
    segs, starts = [], []
    for part in range(2):
        first = meta_ref[1] + part * half
        seg = jnp.int32(0)
        for j in range(1, slots):
            seg = seg + jnp.where(first >= j * bucket, 1, 0).astype(jnp.int32)
        segs.append(seg)
        starts.append(first - seg * bucket)
    iota = lax.broadcasted_iota(jnp.int32, (1, half), 1)
    rows = []
    for query_part in range(2):
        cols = []
        for key_part in range(2):
            same = segs[query_part] == segs[key_part]
            limit = jnp.where(same, meta_ref[2 + segs[key_part]] - starts[key_part], 0)
            cols.append(jnp.where(iota < limit, 0.0, MASKED).astype(F32))
        rows.append(jnp.concatenate(cols, axis=1))
    return rows


def bias_band(rel_row):
    wide = jnp.broadcast_to(rel_row, (TILE, SPAN))
    return pltpu.roll(wide, 0, 1, stride=1, stride_axis=0)


def put_blocks(index_ref, part_refs, mat, which=0):
    if len(part_refs) == 1:
        mat[...] = part_refs[0][which]
        return
    rows = part_refs[0].shape[1]
    for j, part in enumerate(part_refs):
        first = pl.multiple_of(index_ref[j] * rows, rows)
        mat[pl.ds(first, rows), :] = part[which]


def accumulate(step, ref, value):
    @pl.when(step == 0)
    def _():
        ref[...] = value

    @pl.when(step > 0)
    def _():
        ref[...] += value


def attn_fwd_kernel(slots, heads, parts, meta_ref, index_ref, n1_ref, *refs):
    a_parts, (rel_ref, qkv_ref, o_ref, lse_ref, hp_ref, mat, band) = refs[:parts], refs[parts:]
    step = pl.program_id(0)
    width = heads * HEAD
    put_blocks(index_ref, a_parts, mat)
    qkv_ref[0] = dot_nn(n1_ref[...], mat[...]).astype(BF)
    masks = mask_rows(meta_ref, slots)
    for h in range(heads):
        band[...] = bias_band(rel_ref[0, h : h + 1, :].astype(F32))
        q = qkv_ref[0, :, width + h * HEAD : width + (h + 1) * HEAD]
        k = qkv_ref[0, :, 2 * width + h * HEAD : 2 * width + (h + 1) * HEAD]
        v = qkv_ref[0, :, 3 * width + h * HEAD : 3 * width + (h + 1) * HEAD]
        for i in range(BIG // TILE):
            rows = slice(i * TILE, (i + 1) * TILE)
            s = dot_nt(q[rows], k) + band[:, (3 - i) * TILE : (7 - i) * TILE] + masks[i // 2]
            top = jnp.max(s, axis=1, keepdims=True)
            e = jnp.exp(s - top)
            total = jnp.sum(e, axis=1, keepdims=True)
            pb = (e * (1.0 / total)).astype(BF)
            o_ref[0, rows, h * HEAD : (h + 1) * HEAD] = dot_nn(pb, v).astype(BF)
            lse_ref[0, rows, h : h + 1] = top + jnp.log(total)
    accumulate(step, hp_ref, dot_nt(o_ref[0], mat[:, :width]))


def block_specs(parts):
    return [pl.BlockSpec((1,) + part.shape[1:], lambda s: (s, 0, 0)) for part in parts]


SMEM = pl.BlockSpec(memory_space=pltpu.SMEM)


def attn_fwd(meta, index, n1, a_parts, rel, slots, heads):
    shards, _, cols = a_parts[0].shape
    rows, depth = n1.shape
    width = heads * HEAD
    return pl.pallas_call(
        functools.partial(attn_fwd_kernel, slots, heads, len(a_parts)),
        grid=(shards,),
        in_specs=[SMEM, SMEM, pl.BlockSpec((rows, depth), lambda s: (0, 0))]
        + block_specs(a_parts)
        + [pl.BlockSpec((1,) + rel.shape[1:], lambda s: (s, 0, 0))],
        out_specs=[
            pl.BlockSpec((1, rows, cols), lambda s: (s, 0, 0)),
            pl.BlockSpec((1, rows, width), lambda s: (s, 0, 0)),
            pl.BlockSpec((1, rows, TILE), lambda s: (s, 0, 0)),
            pl.BlockSpec((rows, depth), lambda s: (0, 0)),
        ],
        out_shape=[
            jax.ShapeDtypeStruct((shards, rows, cols), BF),
            jax.ShapeDtypeStruct((shards, rows, width), BF),
            jax.ShapeDtypeStruct((shards, rows, TILE), F32),
            jax.ShapeDtypeStruct((rows, depth), F32),
        ],
        scratch_shapes=[pltpu.VMEM((depth, cols), BF), pltpu.VMEM((TILE, SPAN), F32)],
        compiler_params=pltpu.CompilerParams(vmem_limit_bytes=40 * MIB),
        cost_estimate=pl.CostEstimate(flops=shards * 2 * 10**9, bytes_accessed=shards * 4 * 10**6, transcendentals=0),
        name="attn_fwd",
    )(meta, index, n1, *a_parts, rel)


def ffn_kernel(parts, index_ref, side_ref, n2_ref, cot_ref, *refs):
    f_parts, (out_ref, gn_ref, send_ref, keep_ref, i_mat, w_mat, act_ref) = refs[:parts], refs[parts:]
    c0 = 0.7978845608028654
    c1 = 0.044715
    put_blocks(index_ref, f_parts, i_mat, 0)
    put_blocks(index_ref, f_parts, w_mat, 1)
    cot = cot_ref[...]
    pre = dot_nn(n2_ref[...], i_mat[...])
    square = pre * pre
    th = jnp.tanh(pre * (c0 + (c0 * c1) * square))
    half = 0.5 * (1.0 + th)
    act = (pre * half).astype(BF)
    act_ref[...] = act
    slope = half + (0.5 * pre) * (1.0 - th * th) * (c0 + (3.0 * c0 * c1) * square)
    out_ref[...] = dot_nn(act, w_mat[...])
    gp = (dot_nt(cot, w_mat[...]) * slope).astype(BF)
    gn_ref[...] = dot_nt(gp, i_mat[...])
    size = send_ref.shape[1]
    for ref, side in ((send_ref, 1 - side_ref[0]), (keep_ref, side_ref[0])):
        cols = pl.ds(pl.multiple_of(side * size, size), size)
        ref[0] = dot_tn(n2_ref[:, cols], gp).astype(BF)
        ref[1] = dot_tn(act_ref[:, cols], cot).astype(BF)


def ffn(index, side, n2, cot, f_parts):
    rows, depth = n2.shape
    units = f_parts[0].shape[2]
    vmem = pl.BlockSpec(memory_space=pltpu.VMEM)
    half = jax.ShapeDtypeStruct((2, depth // 2, units), BF)
    return pl.pallas_call(
        functools.partial(ffn_kernel, len(f_parts)),
        in_specs=[SMEM, SMEM] + [vmem] * (2 + len(f_parts)),
        out_specs=[vmem] * 4,
        out_shape=[jax.ShapeDtypeStruct((rows, depth), F32), jax.ShapeDtypeStruct((rows, depth), F32), half, half],
        scratch_shapes=[pltpu.VMEM((depth, units), BF), pltpu.VMEM((units, depth), BF), pltpu.VMEM((rows, units), BF)],
        compiler_params=pltpu.CompilerParams(vmem_limit_bytes=48 * MIB),
        cost_estimate=pl.CostEstimate(flops=5 * 10**9, bytes_accessed=8 * 10**6, transcendentals=0),
        name="ffn",
    )(index, side, n2, cot, *f_parts)


def attn_bwd_kernel(slots, heads, parts, meta_ref, index_ref, side_ref, n1_ref, gh_ref, *refs):
    a_parts = refs[:parts]
    qkv_ref, o_ref, lse_ref, rel_ref = refs[parts : parts + 4]
    send_ref, keep_ref, gn_ref, diag_ref, mat, band, acc, gs_all, pb_all, gq_all = refs[parts + 4 :]
    step = pl.program_id(0)
    width = heads * HEAD
    put_blocks(index_ref, a_parts, mat)
    gh = gh_ref[...]
    go_all = dot_nn(gh, mat[:, :width]).astype(BF)
    masks = mask_rows(meta_ref, slots)
    gq_all[:, :width] = jnp.zeros((gq_all.shape[0], width), BF)
    diag_ref[0] = jnp.zeros(diag_ref.shape[1:], F32)
    for h in range(heads):
        band[...] = bias_band(rel_ref[0, h : h + 1, :].astype(F32))
        acc[...] = jnp.zeros_like(acc)
        q = qkv_ref[0, :, width + h * HEAD : width + (h + 1) * HEAD]
        k = qkv_ref[0, :, 2 * width + h * HEAD : 2 * width + (h + 1) * HEAD]
        v = qkv_ref[0, :, 3 * width + h * HEAD : 3 * width + (h + 1) * HEAD]
        go = go_all[:, h * HEAD : (h + 1) * HEAD]
        for i in range(BIG // TILE):
            rows = slice(i * TILE, (i + 1) * TILE)
            window = slice((3 - i) * TILE, (7 - i) * TILE)
            s = dot_nt(q[rows], k) + band[:, window] + masks[i // 2]
            p = jnp.exp(s - lse_ref[0, rows, h : h + 1])
            dp = dot_nt(go[rows], v)
            inner = jnp.sum(p * dp, axis=1, keepdims=True)
            gs = (p * (dp - inner)).astype(BF)
            gs_all[rows, :] = gs
            pb_all[rows, :] = p.astype(BF)
            acc[:, window] += gs.astype(F32)
        gq_all[:, width + h * HEAD : width + (h + 1) * HEAD] = dot_nn(gs_all[...], k).astype(BF)
        gq_all[:, 2 * width + h * HEAD : 2 * width + (h + 1) * HEAD] = dot_tn(gs_all[...], q).astype(BF)
        gq_all[:, 3 * width + h * HEAD : 3 * width + (h + 1) * HEAD] = dot_tn(pb_all[...], go).astype(BF)
        fold = acc[...]
        n = TILE // 2
        while n >= 8:
            fold = fold[:n] + pltpu.roll(fold[n:], SPAN - n, 1)
            n //= 2
        line = fold[0:1]
        for j in range(1, 8):
            line = line + pltpu.roll(fold[j : j + 1], SPAN - j, 1)
        diag_ref[0, h : h + 1, :] = line
    grads = gq_all[...]
    accumulate(step, gn_ref, dot_nt(grads, mat[...]))
    size = send_ref.shape[1]
    for ref, side in ((send_ref, 1 - side_ref[0]), (keep_ref, side_ref[0])):
        cols = pl.ds(pl.multiple_of(side * size, size), size)
        ref[0] = dot_tn(n1_ref[:, cols], grads).astype(BF)
        ref[0, :, :width] = dot_tn(gh_ref[:, cols], o_ref[0]).astype(BF)


def attn_bwd(meta, index, side, n1, gh, a_parts, qkv, o, lse, rel, slots, heads):
    shards, _, cols = a_parts[0].shape
    rows, depth = n1.shape
    full = pl.BlockSpec((rows, depth), lambda s: (0, 0))
    kept = [qkv, o, lse, rel]
    half = pl.BlockSpec((1, depth // 2, cols), lambda s: (s, 0, 0))
    half_shape = jax.ShapeDtypeStruct((shards, depth // 2, cols), BF)
    return pl.pallas_call(
        functools.partial(attn_bwd_kernel, slots, heads, len(a_parts)),
        grid=(shards,),
        in_specs=[SMEM, SMEM, SMEM, full, full] + block_specs(a_parts) + block_specs(kept),
        out_specs=[half, half, full, pl.BlockSpec((1, 8, SPAN), lambda s: (s, 0, 0))],
        out_shape=[
            half_shape,
            half_shape,
            jax.ShapeDtypeStruct((rows, depth), F32),
            jax.ShapeDtypeStruct((shards, 8, SPAN), F32),
        ],
        scratch_shapes=[
            pltpu.VMEM((depth, cols), BF),
            pltpu.VMEM((TILE, SPAN), F32),
            pltpu.VMEM((TILE, SPAN), F32),
            pltpu.VMEM((BIG, BIG), BF),
            pltpu.VMEM((BIG, BIG), BF),
            pltpu.VMEM((rows, cols), BF),
        ],
        compiler_params=pltpu.CompilerParams(vmem_limit_bytes=48 * MIB),
        cost_estimate=pl.CostEstimate(flops=shards * 4 * 10**9, bytes_accessed=shards * 8 * 10**6, transcendentals=0),
        name="attn_bwd",
    )(meta, index, side, n1, gh, *a_parts, qkv, o, lse, rel)


def fold_kernel(axis, side_ref, keep_ref, recv_ref, *out_refs):
    if axis is None:
        out_refs[0][...] = (keep_ref[...].astype(F32) + recv_ref[...].astype(F32)).astype(BF)
        return
    for ref, side in zip(out_refs, (1 - side_ref[0], side_ref[0])):
        at = (slice(None),) * axis + (side,)
        ref[...] = (keep_ref[at].astype(F32) + recv_ref[at].astype(F32)).astype(BF)


def fold(side, keep, recv, axis):
    vmem = pl.BlockSpec(memory_space=pltpu.VMEM)
    shape = keep.shape if axis is None else keep.shape[:axis] + keep.shape[axis + 1 :]
    outs = 1 if axis is None else 2
    return pl.pallas_call(
        functools.partial(fold_kernel, axis),
        in_specs=[SMEM, vmem, vmem],
        out_specs=[vmem] * outs,
        out_shape=[jax.ShapeDtypeStruct(shape, BF)] * outs,
        compiler_params=pltpu.CompilerParams(vmem_limit_bytes=24 * MIB),
        cost_estimate=pl.CostEstimate(flops=10**6, bytes_accessed=4 * 10**6, transcendentals=0),
        name="fold",
    )(side, keep, recv)


def finish_kernel(width, index_ref, *refs):
    parts, (out_ref, q_ref, k_ref, v_ref, mat) = refs[:-5], refs[-5:]
    put_blocks(index_ref, parts, mat)
    out_ref[...] = mat[:, :width].astype(F32).T
    for j, ref in enumerate((q_ref, k_ref, v_ref)):
        ref[...] = mat[:, (j + 1) * width : (j + 2) * width].astype(F32)


def finish(index, parts, width):
    depth = len(parts) * parts[0].shape[1]
    cols = parts[0].shape[2]
    vmem = pl.BlockSpec(memory_space=pltpu.VMEM)
    wide = jax.ShapeDtypeStruct((depth, width), F32)
    return pl.pallas_call(
        functools.partial(finish_kernel, width),
        in_specs=[SMEM] + [vmem] * len(parts),
        out_specs=[vmem] * 4,
        out_shape=[jax.ShapeDtypeStruct((width, depth), F32), wide, wide, wide],
        scratch_shapes=[pltpu.VMEM((depth, cols), BF)],
        compiler_params=pltpu.CompilerParams(vmem_limit_bytes=32 * MIB),
        cost_estimate=pl.CostEstimate(flops=10**6, bytes_accessed=4 * 10**6, transcendentals=0),
        name="finish",
    )(index, *parts)


class Ring:
    def __init__(self, n_dp, n_mp, depth):
        self.n_dp, self.n_mp = n_dp, n_mp
        self.all_bits = (n_dp - 1).bit_length()
        self.bits = min(3, self.all_bits)
        self.d = lax.axis_index("dp")
        self.z = lax.axis_index("mp")
        self.blocks = 1 << self.bits
        self.block_rows = depth // self.blocks
        self.low = self.d & (self.blocks - 1)
        self.sides = [((self.low >> bit) & 1)[None].astype(jnp.int32) for bit in range(self.bits)]
        self.orders = {flip: self.order(flip) for flip in (False, True)}
        self.index = {flip: self.block_index(flip) for flip in (False, True)}

    def row_block(self, low):
        return ((low & 1) << (self.bits - 1)) | (low >> 1)

    def order(self, flip):
        high = list(range(1, self.bits))
        return (high[::-1] if flip else high) + [0]

    def block_index(self, flip):
        masks = [0]
        for bit in self.orders[flip]:
            masks = masks + [m | (1 << bit) for m in masks]
        low = self.low ^ jnp.asarray(masks, jnp.int32)
        return self.row_block(low).astype(jnp.int32)

    def swap(self, x, bit):
        return lax.ppermute(x, "dp", [(i, i ^ (1 << bit)) for i in range(self.n_dp)])

    def pull(self, x, shift):
        return lax.ppermute(x, "mp", [(i, (i - shift) % self.n_mp) for i in range(self.n_mp)])

    def push(self, x, shift):
        return lax.ppermute(x, "mp", [(i, (i + shift) % self.n_mp) for i in range(self.n_mp)])

    def gather(self, arr, flip):
        parts = [arr]
        for bit in self.orders[flip]:
            parts = parts + [self.swap(part, bit) for part in parts]
        return parts

    def own_block(self, mats):
        first = self.row_block(self.low) * self.block_rows
        return lax.dynamic_slice_in_dim(mats, first, self.block_rows, axis=1)

    def scatter(self, send, keep, flip):
        count, _, cols = keep.shape
        shape = (count,) + (2,) * (self.bits - 1) + (self.block_rows, cols)
        axes = list(range(self.bits - 1, 0, -1))
        order = self.orders[flip][-2::-1] + [None]
        bit = 0
        send, keep = send.reshape(shape), keep.reshape(shape)
        for later in order:
            recv = self.swap(send, bit)
            if later is None:
                keep = fold(self.sides[0], keep, recv, None)[0]
            else:
                axis = 1 + axes.index(later)
                axes.remove(later)
                send, keep = fold(self.sides[later], keep, recv, axis)
            bit = later
        for bit in range(self.bits, self.all_bits):
            keep = fold(self.sides[0], keep, self.swap(keep, bit), None)[0]
        return keep

    def owners(self, pieces):
        total = pieces[0].astype(F32)
        for s in range(1, self.n_mp):
            total = total + self.push(pieces[s], s).astype(F32)
        return total

    def gather_all(self, piece):
        groups = [[g + i for i in range(self.blocks)] for g in range(0, self.n_dp, self.blocks)]
        both = lax.all_gather(piece, "dp", axis_index_groups=groups)
        return jnp.concatenate([both[0::2], both[1::2]], axis=0).transpose(1, 0, 2, 3).reshape(
            piece.shape[0], -1, piece.shape[2]
        )


def rms_forward(values, gain_vec):
    inv_root = lax.rsqrt(jnp.mean(values * values, axis=1, keepdims=True) + EPS)
    unit_rows = values * inv_root
    return (unit_rows, inv_root, unit_rows * gain_vec)


def rms_backward(grad_normed, unit_rows, inv_root, gain_vec):
    grad_unit = grad_normed * gain_vec
    grad_gain = jnp.sum(grad_normed * unit_rows, axis=0)
    centred = grad_unit - unit_rows * jnp.mean(grad_unit * unit_rows, axis=1, keepdims=True)
    return (inv_root * centred, grad_gain)


def body(
    n_dp, n_mp, inputs, gain_attn, w_query, w_key, w_value, w_out, rel_table, gain_ffn, w_in, w_down,
    cotangent, bucket, lengths,
):
    depth = inputs.shape[1]
    buckets, heads = rel_table.shape
    width = heads * HEAD
    slots = lengths.shape[1]
    ring = Ring(n_dp, n_mp, depth)
    shifts = range(1, n_mp)

    a_own = jnp.concatenate([w_out.T, w_query, w_key, w_value], axis=1)[None]
    f_own = jnp.stack([w_in, w_down])
    one_hot = jnp.asarray(offset_one_hot(buckets), BF)
    rel_own = lax.dot_general(rel_table, one_hot, (((0,), (1,)), ((), ())), preferred_element_type=F32)
    rel_own = jnp.concatenate([rel_own.astype(BF), jnp.zeros((16 - heads, SPAN), BF)], axis=0)[None]

    a_piece = ring.own_block(a_own)
    a_in = jnp.concatenate([ring.pull(a_piece, s) for s in shifts], axis=0)
    rel_rest = jnp.concatenate([ring.pull(rel_own, s) for s in shifts], axis=0)
    f_piece = ring.own_block(f_own)
    f_in = [ring.pull(f_piece, s) for s in shifts]

    a_rest = ring.gather(a_in, False)
    f_mats = [[f_own]] + [ring.gather(f_in[j], j % 2 == 0) for j in range(n_mp - 1)]

    meta = jnp.concatenate([bucket, (ring.z * BIG)[None].astype(jnp.int32), lengths[0]])
    x_value = inputs.astype(F32)
    gain_one = gain_attn.astype(F32)
    unit_one, root_one, normed_one = rms_forward(x_value, gain_one)
    n1 = normed_one.astype(BF)
    a_index, f_index = ring.index[False], [ring.index[False]] + [ring.index[j % 2 == 0] for j in range(n_mp - 1)]
    qkv0, o0, lse0, hp0 = attn_fwd(meta, a_index, n1, [a_own], rel_own, slots, heads)
    qkv1, o1, lse1, hp1 = attn_fwd(meta, a_index, n1, a_rest, rel_rest, slots, heads)
    hidden = x_value + (hp0 + hp1)
    gain_two = gain_ffn.astype(F32)
    unit_two, root_two, normed_two = rms_forward(hidden, gain_two)
    n2 = normed_two.astype(BF)

    side = ring.sides[0]
    outs, gns, f_grads = [], [], []
    for s in range(n_mp):
        out, gn, send, keep = ffn(f_index[s], side, n2, cotangent, f_mats[s])
        outs.append(out)
        gns.append(gn)
        f_grads.append(ring.scatter(send, keep, s % 2 == 0))
    outputs = (hidden + sum(outs)).astype(BF)
    grad_middle, grad_gain_two = rms_backward(sum(gns), unit_two, root_two, gain_two)
    grad_hidden = cotangent.astype(F32) + grad_middle
    gh = grad_hidden.astype(BF)

    send0, keep0, gn0, diag0 = attn_bwd(meta, a_index, side, n1, gh, [a_own], qkv0, o0, lse0, rel_own, slots, heads)
    send1, keep1, gn1, diag1 = attn_bwd(meta, a_index, side, n1, gh, a_rest, qkv1, o1, lse1, rel_rest, slots, heads)
    a_first = ring.scatter(send0, keep0, True)
    a_later = ring.scatter(send1, keep1, False)
    grad_lower, grad_gain_one = rms_backward(gn0 + gn1, unit_one, root_one, gain_one)
    grad_inputs = (grad_hidden + grad_lower).astype(BF)

    f_out = ring.gather_all(ring.owners(f_grads).astype(BF))
    grad_in, grad_down = f_out[0].astype(F32), f_out[1].astype(F32)
    a_sum = ring.owners([a_first] + [a_later[s : s + 1] for s in range(n_mp - 1)]).astype(BF)
    grad_out, grad_query, grad_key, grad_value = finish(a_index, ring.gather(a_sum, False), width)

    diag = jnp.concatenate([diag0, diag1], axis=0)[:, :heads]
    tables = jnp.einsum("shu,ub->sbh", diag, jnp.asarray(offset_one_hot(buckets)), precision=lax.Precision.HIGHEST)
    size = buckets * heads
    small = jnp.concatenate([tables.reshape(-1), grad_gain_one, grad_gain_two])
    for bit in range(ring.all_bits):
        small = small + ring.swap(small, bit)
    gains = small[n_mp * size :]
    mine = [jnp.concatenate([small[s * size : (s + 1) * size], gains]) for s in range(n_mp)]
    total = ring.owners(mine)
    grad_table = total[:size].reshape(buckets, heads)
    grad_gain_one = total[size : size + depth]
    grad_gain_two = total[size + depth :]
    return (
        outputs, grad_inputs, grad_query, grad_key, grad_value, grad_out, grad_table,
        grad_gain_one, grad_gain_two, grad_in, grad_down,
    )


def solution(mesh):
    placed = (
        P(("dp", "mp"), None), P(), P(None, "mp"), P(None, "mp"), P(None, "mp"), P("mp", None),
        P(None, "mp"), P(), P(None, "mp"), P("mp", None), P(("dp", "mp"), None), P("dp"), P("dp", None),
    )
    return jax.shard_map(
        functools.partial(body, mesh.shape["dp"], mesh.shape["mp"]),
        mesh=mesh,
        in_specs=placed,
        out_specs=(
            P(("dp", "mp"), None), P(("dp", "mp"), None), P(None, "mp"), P(None, "mp"), P(None, "mp"),
            P("mp", None), P(None, "mp"), P(), P(), P(None, "mp"), P("mp", None),
        ),
        check_vma=False,
    )
```

time: 815 us -> 348 us (0.43)
  Pallas kernels: 524 us -> 89.5 us
  local copies, waits for them, and re-layouts: 51.5 us -> 21.1 us
  between operations: 2.92 us -> 16 us
  waiting for transfers between devices: 128 us -> 115 us
  starting transfers between devices: 67.7 us -> 79.8 us
  other arithmetic: 32.4 us -> 23.8 us
    pallas_call x14 -> x27, Pallas kernels: 524 us -> 89.5 us  [the longest x2 27.6 us: attn_bwd(): pl.pallas_call(functools.partial(attn_bwd_kernel, slots, heads, len(a_par...]
    ppermute x36 -> x56, waiting for transfers between devices: 95.4 us -> 72.1 us  [swap(): return lax.ppermute(x, 'dp', [(i, i ^ 1 << bit) for i in range(self.n_dp)])]
    unnamed x161 -> x160, local copies, waits for them, and re-layouts: 29.6 us -> 17.1 us
    ppermute x9, waiting for transfers between devices: 11.5 us -> 23.7 us  [push(): lax.ppermute(x, 'mp', [(i, (i + shift) % self.n_mp) for i in range(self.n...]
    ppermute x9, starting transfers between devices: 25.9 us -> 34 us  [pull(): lax.ppermute(x, 'mp', [(i, (i - shift) % self.n_mp) for i in range(self.n...]
    ppermute x36 -> x56, starting transfers between devices: 32.1 us -> 35.1 us  [swap(): return lax.ppermute(x, 'dp', [(i, i ^ 1 << bit) for i in range(self.n_dp)])]
  transfers between devices with their start and end apart: 54 -> 75, of which waited for: 23 -> 23; matrix products, arithmetic and copies ran while one was open for 7% -> 9% of each run, Pallas kernels for 41% -> 26%
where the time goes in v2:
time: 348 us; the launch traced here: 347 us
  waiting for transfers between devices  115 us (33%)
  Pallas kernels  89.5 us (26%)
  starting transfers between devices  79.8 us (23%)
  other arithmetic  23.8 us (7%)
  local copies, waits for them, and re-layouts  21.1 us (6%)
  between operations  16 us (5%)
    ppermute x56, waiting for transfers between devices, swap(): return lax.ppermute(x, 'dp', [(i, i ^ 1 << bit) for i in range(self.n_dp)])  72.1 us
    ppermute x56, starting transfers between devices, swap(): return lax.ppermute(x, 'dp', [(i, i ^ 1 << bit) for i in range(self.n_dp)])  35.1 us
    ppermute x9, starting transfers between devices, pull(): lax.ppermute(x, 'mp', [(i, (i - shift) % self.n_mp) for i in range(self.n...  34 us
    pallas_call x2, Pallas kernels, attn_bwd(): pl.pallas_call(functools.partial(attn_bwd_kernel, slots, heads, len(a_par...  27.6 us
    pallas_call x4, Pallas kernels, ffn(): pl.pallas_call(functools.partial(ffn_kernel, len(f_parts)), in_specs=[SME...  26.2 us
    pallas_call x2, Pallas kernels, attn_fwd(): pl.pallas_call(functools.partial(attn_fwd_kernel, slots, heads, len(a_par...  24.9 us
    ppermute x9, waiting for transfers between devices, push(): lax.ppermute(x, 'mp', [(i, (i + shift) % self.n_mp) for i in range(self.n...  23.7 us
    ppermute x9, waiting for transfers between devices, pull(): lax.ppermute(x, 'mp', [(i, (i - shift) % self.n_mp) for i in range(self.n...  19.6 us
  transfers between devices with their start and end apart: 75, of which 23 were waited for; matrix products, arithmetic and copies ran while one was open for 9% of the time, Pallas kernels for 26%

profile of v2, /device:TPU:0, one launch (start us, length us, event | category | flops | bytes accessed | tf_op | source)
XLA Modules:
  0.0 347.1 jit_solution(2636219476506443294)
XLA Ops:
  9.0 3.1 collective-permute-start.12
  12.1 2.6 collective-permute-start.11
  19.5 1.6 pad_maximum_fusion.1
  21.4 2.8 collective-permute-start
  25.3 2.6 collective-permute-done
  28.0 8.9 %collective-permute-start.2 = (bf16[1,96,768]{2,1,0:T(8,128)(2,1)S(1)}, bf16[1,96,768]{2,1,0:T(8,128)(2,1)S(1)}, u32[]{:S(2)}, u32[]{:S(2)}) collective-permute-start(bf16[1,96,768]{2,1,0:T(8,128)(2,1)S(1)} %dynamic-slice_bitcast_fusion), channel_id=1, source_target_pairs={{0,1},{1,2},{2,3},{3,0},{4,5},{5,6},{6,7},{7,4},{8,9},{9,10},{10,1... | collective-permute-start | bytes 442376 | tf_op jit(solution)/shard_map/ppermute | solution.py:357
  37.0 2.9 collective-permute-done.2
  41.7 1.6 collective-permute-start.4
  43.3 7.6 %collective-permute-done.3.refs_1_ = bf16[3,96,768]{2,1,0:T(8,128)(2,1)} collective-permute-done((bf16[3,96,768]{2,1,0:T(8,128)(2,1)S(1)}, bf16[3,96,768]{2,1,0:T(8,128)(2,1)}, u32[]{:S(2)}, u32[]{:S(2)}) %collective-permute-start.3) | collective-permute-done | bytes 442400 | tf_op jit(solution)/shard_map/ppermute | solution.py:354
  54.6 2.5 collective-permute-start.29
  57.1 6.2 %attn_fwd.2 = (bf16[1,512,768]{2,1,0:T(8,128)(2,1)S(1)}, bf16[1,512,192]{2,1,0:T(8,128)(2,1)S(1)}, f32[1,512,128]{2,1,0:T(8,128)S(1)}, f32[512,768]{1,0:T(8,128)S(1)}) custom-call(s32[10]{0:T(128)S(1)} %pad_add_fusion.meta_ref, s32[8]{0:T(128)S(1)} %fusion.18.index_ref, bf16[512,768]{1,0:T(8,128)(2,1)S(1)} %fusion.4.n1_ref, ...), custom_call_target="tpu_custom_call" | custom-call | flops 2000000000 | bytes 4000000 | tf_op jit(solution)/shard_map/attn_fwd/pallas_call | solution.py:127
  67.1 3.2 pad_maximum_fusion.refs_0_
  72.7 14.1 %collective-permute-done.21.refs_0_ = bf16[2,96,768]{2,1,0:T(8,128)(2,1)S(1)} collective-permute-done((bf16[2,96,768]{2,1,0:T(8,128)(2,1)}, bf16[2,96,768]{2,1,0:T(8,128)(2,1)S(1)}, u32[]{:S(2)}, u32[]{:S(2)}) %collective-permute-start.21) | collective-permute-done | bytes 294944 | tf_op jit(solution)/shard_map/ppermute | solution.py:357
  86.7 12.4 %collective-permute-start.13 = (bf16[2,96,768]{2,1,0:T(8,128)(2,1)}, bf16[2,96,768]{2,1,0:T(8,128)(2,1)S(1)}, u32[]{:S(2)}, u32[]{:S(2)}) collective-permute-start(bf16[2,96,768]{2,1,0:T(8,128)(2,1)} %fusion.13), channel_id=1, source_target_pairs={{0,3},{1,0},{2,1},{3,2},{4,7},{5,4},{6,5},{7,6},{8,11},{9,8},{10,9... | collective-permute-start | bytes 884744 | tf_op jit(solution)/shard_map/ppermute | solution.py:357
  102.8 18.7 %attn_fwd.3 = (bf16[3,512,768]{2,1,0:T(8,128)(2,1)S(1)}, bf16[3,512,192]{2,1,0:T(8,128)(2,1)S(1)}, f32[3,512,128]{2,1,0:T(8,128)S(1)}, f32[512,768]{1,0:T(8,128)S(1)}) custom-call(s32[10]{0:T(128)S(1)} %pad_add_fusion.meta_ref, s32[8]{0:T(128)S(1)} %fusion.18.index_ref, bf16[512,768]{1,0:T(8,128)(2,1)S(1)} %fusion.4.n1_ref, ...), custom_call_target="tpu_custom_call" | custom-call | flops 6000000000 | bytes 12000000 | tf_op jit(solution)/shard_map/attn_fwd/pallas_call | solution.py:127
  125.2 6.4 %collective-permute-done.22.refs_1_ = bf16[2,96,768]{2,1,0:T(8,128)(2,1)S(1)} collective-permute-done((bf16[2,96,768]{2,1,0:T(8,128)(2,1)S(1)}, bf16[2,96,768]{2,1,0:T(8,128)(2,1)S(1)}, u32[]{:S(2)}, u32[]{:S(2)}) %collective-permute-start.22) | collective-permute-done | bytes 294944 | tf_op jit(solution)/shard_map/ppermute | solution.py:354
  132.2 5.8 %collective-permute-done.32.refs_3_ = bf16[2,96,768]{2,1,0:T(8,128)(2,1)S(1)} collective-permute-done((bf16[2,96,768]{2,1,0:T(8,128)(2,1)S(1)}, bf16[2,96,768]{2,1,0:T(8,128)(2,1)S(1)}, u32[]{:S(2)}, u32[]{:S(2)}) %collective-permute-start.32) | collective-permute-done | bytes 294944 | tf_op jit(solution)/shard_map/ppermute | solution.py:354
  138.2 6.1 %collective-permute-done.15.refs_2_ = bf16[2,96,768]{2,1,0:T(8,128)(2,1)S(1)} collective-permute-done((bf16[2,96,768]{2,1,0:T(8,128)(2,1)S(1)}, bf16[2,96,768]{2,1,0:T(8,128)(2,1)S(1)}, u32[]{:S(2)}, u32[]{:S(2)}) %collective-permute-start.15) | collective-permute-done | bytes 294944 | tf_op jit(solution)/shard_map/ppermute | solution.py:354
  145.2 3.9 %collective-permute-done.16.refs_3_ = bf16[2,96,768]{2,1,0:T(8,128)(2,1)S(1)} collective-permute-done((bf16[2,96,768]{2,1,0:T(8,128)(2,1)S(1)}, bf16[2,96,768]{2,1,0:T(8,128)(2,1)S(1)}, u32[]{:S(2)}, u32[]{:S(2)}) %collective-permute-start.16) | collective-permute-done | bytes 294944 | tf_op jit(solution)/shard_map/ppermute | solution.py:354
  149.6 6.5 %ffn.7 = (f32[512,768]{1,0:T(8,128)}, f32[512,768]{1,0:T(8,128)}, bf16[2,384,768]{2,1,0:T(8,128)(2,1)}, bf16[2,384,768]{2,1,0:T(8,128)(2,1)}) custom-call(s32[8]{0:T(128)S(1)} %fusion.20.index_ref, s32[1]{0:T(128)} %bitcast.7.side_ref, bf16[512,768]{1,0:T(8,128)(2,1)S(1)} %multiply_convert_fusion.n2_ref, bf16[512,768]{1,0:T(8,128)(2,1)S(1)} %copy-done.2, ...), custom_call_target="tpu_custom_call" | custom-call | flops 5000000000 | bytes 8000000 | tf_op jit(solution)/shard_map/ffn/pallas_call | solution.py:181
  157.3 6.5 %ffn.5 = (f32[512,768]{1,0:T(8,128)}, f32[512,768]{1,0:T(8,128)}, bf16[2,384,768]{2,1,0:T(8,128)(2,1)}, bf16[2,384,768]{2,1,0:T(8,128)(2,1)}) custom-call(s32[8]{0:T(128)S(1)} %fusion.20.index_ref, s32[1]{0:T(128)} %bitcast.7.side_ref, bf16[512,768]{1,0:T(8,128)(2,1)S(1)} %multiply_convert_fusion.n2_ref, bf16[512,768]{1,0:T(8,128)(2,1)S(1)} %copy-done.2, ...), custom_call_target="tpu_custom_call" | custom-call | flops 5000000000 | bytes 8000000 | tf_op jit(solution)/shard_map/ffn/pallas_call | solution.py:181
  164.3 6.8 %ffn.6 = (f32[512,768]{1,0:T(8,128)}, f32[512,768]{1,0:T(8,128)}, bf16[2,384,768]{2,1,0:T(8,128)(2,1)}, bf16[2,384,768]{2,1,0:T(8,128)(2,1)}) custom-call(s32[8]{0:T(128)S(1)} %fusion.18.index_ref, s32[1]{0:T(128)} %bitcast.7.side_ref, bf16[512,768]{1,0:T(8,128)(2,1)S(1)} %multiply_convert_fusion.n2_ref, bf16[512,768]{1,0:T(8,128)(2,1)S(1)} %copy-done.2, ...), custom_call_target="tpu_custom_call" | custom-call | flops 5000000000 | bytes 8000000 | tf_op jit(solution)/shard_map/ffn/pallas_call | solution.py:181
  171.1 6.4 %ffn.4 = (f32[512,768]{1,0:T(8,128)S(1)}, f32[512,768]{1,0:T(8,128)}, bf16[2,384,768]{2,1,0:T(8,128)(2,1)}, bf16[2,384,768]{2,1,0:T(8,128)(2,1)S(1)}) custom-call(s32[8]{0:T(128)S(1)} %fusion.18.index_ref, s32[1]{0:T(128)} %bitcast.7.side_ref, bf16[512,768]{1,0:T(8,128)(2,1)S(1)} %multiply_convert_fusion.n2_ref, bf16[512,768]{1,0:T(8,128)(2,1)S(1)} %copy-done.2, ...), custom_call_target="tpu_custom_call" | custom-call | flops 5000000000 | bytes 8000000 | tf_op jit(solution)/shard_map/ffn/pallas_call | solution.py:181
  180.1 4.7 %multiply_reduce_fusion = (f32[768]{0:T(1024)}, f32[512]{0:T(512)S(1)}, f32[512,768]{1,0:T(8,128)S(1)}) fusion(f32[512,768]{1,0:T(8,128)} %copy-done.40, f32[512]{0:T(512)S(1)} %copy-done.61, f32[768]{0:T(1024)S(1)} %convert_element_type.76, f32[512,768]{1,0:T(8,128)} %get-tuple-element.80, f32[512,768]{1,0:T(8,128)} %get-tuple-element.79, ...), kind=kLoop, calls=%fused_computation.19 | loop fusion | flops 3537664 | bytes 9447424 | tf_op jit(solution)/shard_map/reduce_sum | solution.py:414
  189.4 1.6 fold.30
  194.8 20.6 %attn_bwd.3 = (bf16[3,384,768]{2,1,0:T(8,128)(2,1)}, bf16[3,384,768]{2,1,0:T(8,128)(2,1)}, f32[512,768]{1,0:T(8,128)}, f32[3,8,1024]{2,1,0:T(8,128)S(1)}) custom-call(s32[10]{0:T(128)S(1)} %pad_add_fusion.meta_ref, s32[8]{0:T(128)S(1)} %fusion.18.index_ref, s32[1]{0:T(128)} %bitcast.7.side_ref, bf16[512,768]{1,0:T(8,128)(2,1)S(1)} %copy-done.16, ...), custom_call_target="tpu_custom_call" | custom-call | flops 12000000000 | bytes 24000000 | tf_op jit(solution)/shard_map/attn_bwd/pallas_call | solution.py:251
  220.3 5.1 %collective-permute-done.72.recv_ref = bf16[2,96,768]{2,1,0:T(8,128)(2,1)S(1)} collective-permute-done((bf16[2,96,768]{2,1,0:T(8,128)(2,1)S(1)}, bf16[2,96,768]{2,1,0:T(8,128)(2,1)S(1)}, u32[]{:S(2)}, u32[]{:S(2)}) %collective-permute-start.72) | collective-permute-done | bytes 294944 | tf_op jit(solution)/shard_map/ppermute | solution.py:354
  225.7 5.7 %collective-permute-done.64.recv_ref = bf16[2,96,768]{2,1,0:T(8,128)(2,1)S(1)} collective-permute-done((bf16[2,96,768]{2,1,0:T(8,128)(2,1)S(1)}, bf16[2,96,768]{2,1,0:T(8,128)(2,1)S(1)}, u32[]{:S(2)}, u32[]{:S(2)}) %collective-permute-start.64) | collective-permute-done | bytes 294944 | tf_op jit(solution)/shard_map/ppermute | solution.py:354
  233.8 9.6 %collective-permute-done.65 = bf16[2,96,768]{2,1,0:T(8,128)(2,1)S(1)} collective-permute-done((bf16[2,96,768]{2,1,0:T(8,128)(2,1)S(1)}, bf16[2,96,768]{2,1,0:T(8,128)(2,1)S(1)}, u32[]{:S(2)}, u32[]{:S(2)}) %collective-permute-start.65) | collective-permute-done | bytes 294944 | tf_op jit(solution)/shard_map/ppermute | solution.py:360
  243.4 11.1 %collective-permute-done.69 = bf16[2,96,768]{2,1,0:T(8,128)(2,1)S(1)} collective-permute-done((bf16[2,96,768]{2,1,0:T(8,128)(2,1)S(1)}, bf16[2,96,768]{2,1,0:T(8,128)(2,1)S(1)}, u32[]{:S(2)}, u32[]{:S(2)}) %collective-permute-start.69) | collective-permute-done | bytes 294944 | tf_op jit(solution)/shard_map/ppermute | solution.py:360
  255.5 2.9 fold.21
  260.3 7.1 %attn_bwd.2 = (bf16[1,384,768]{2,1,0:T(8,128)(2,1)}, bf16[1,384,768]{2,1,0:T(8,128)(2,1)S(1)}, f32[512,768]{1,0:T(8,128)}, f32[1,8,1024]{2,1,0:T(8,128)S(1)}) custom-call(s32[10]{0:T(128)S(1)} %pad_add_fusion.meta_ref, s32[8]{0:T(128)S(1)} %fusion.18.index_ref, s32[1]{0:T(128)} %bitcast.7.side_ref, bf16[512,768]{1,0:T(8,128)(2,1)S(1)} %copy-done.17, ...), custom_call_target="tpu_custom_call" | custom-call | flops 4000000000 | bytes 8000000 | tf_op jit(solution)/shard_map/attn_bwd/pallas_call | solution.py:251
  268.1 2.9 fusion.10
  273.5 16.0 %collective-permute-done.41.recv_ref = bf16[3,2,96,768]{3,2,1,0:T(8,128)(2,1)S(1)} collective-permute-done((bf16[3,2,96,768]{3,2,1,0:T(8,128)(2,1)}, bf16[3,2,96,768]{3,2,1,0:T(8,128)(2,1)S(1)}, u32[]{:S(2)}, u32[]{:S(2)}) %collective-permute-start.41) | collective-permute-done | bytes 884768 | tf_op jit(solution)/shard_map/ppermute | solution.py:354
  291.9 8.3 %collective-permute-done.54 = f32[1920]{0:T(1024)S(1)} collective-permute-done((f32[1920]{0:T(1024)S(1)}, f32[1920]{0:T(1024)S(1)}, u32[]{:S(2)}, u32[]{:S(2)}) %collective-permute-start.54) | collective-permute-done | bytes 7712 | tf_op jit(solution)/shard_map/ppermute | solution.py:354
  300.2 1.7 collective-permute-start.55
  301.9 2.0 collective-permute-done.55
  304.0 1.8 collective-permute-start.39
  306.0 3.8 %collective-permute-start.45 = (bf16[1,96,768]{2,1,0:T(8,128)(2,1)S(1)}, bf16[1,96,768]{2,1,0:T(8,128)(2,1)S(1)}, u32[]{:S(2)}, u32[]{:S(2)}) collective-permute-start(bf16[1,96,768]{2,1,0:T(8,128)(2,1)S(1)} %get-tuple-element.178), channel_id=1, source_target_pairs={{0,3},{1,0},{2,1},{3,2},{4,7},{5,4},{6,5},{7,6},{8,11},{9,8},{10,9... | collective-permute-start | bytes 442376 | tf_op jit(solution)/shard_map/ppermute | solution.py:360
  310.6 2.4 collective-permute-start.57
  313.8 2.5 collective-permute-start.58
  316.2 1.8 collective-permute-done.44
  318.7 3.5 %fusion.9 = (bf16[512,768]{1,0:T(8,128)(2,1)}, bf16[512,768]{1,0:T(8,128)(2,1)}) fusion(bf16[512,768]{1,0:T(8,128)(2,1)S(1)} %copy-done.45, f32[512]{0:T(512)S(1)} %broadcast_multiply_fusion, f32[768]{0:T(1024)S(1)} %convert_element_type.73, f32[512]{0:T(512)S(1)} %copy-done.66, f32[512,768]{1,0:T(8,128)S(1)} %copy-done.49, f32[512,768]{1,0:T(8,128)S(1)} %copy-done.48, ...), kind=kLoop, calls=%fused_computation.16 | loop fusion | flops 8257536 | bytes 15742976 | tf_op jit(solution)/shard_map/convert_element_type | solution.py:475
  325.6 1.7 collective-permute-done.47.refs_2_
  327.3 1.6 collective-permute-done.48.refs_3_
  330.3 1.6 finish.1
  335.1 1.8 fusion.24
  337.3 2.7 bitcast_convert_fusion
  (338 shorter events, 67.4 us)
Async XLA Ops:
  7.2 327.9 %all-gather.3.cloned.1.call-start = ((), (), s32[]{:S(2)}) async-start(), calls=%async_computation | async-start | bytes 2654208 | tf_op jit(solution)/shard_map/all_gather | solution.py:400
  9.0 45.6 %collective-permute-start.12 = (bf16[1,16,1024]{2,1,0:T(8,128)(2,1)S(1)}, bf16[1,16,1024]{2,1,0:T(8,128)(2,1)}, u32[]{:S(2)}, u32[]{:S(2)}) collective-permute-start(bf16[1,16,1024]{2,1,0:T(8,128)(2,1)S(1)} %pad_bitcast_fusion.refs_1_.refs_4_), channel_id=1, source_target_pairs={{0,1},{1,2},{2,3},{3,0},{4,5},{5,6},{6,7},{7,4},{8,9},{9,10},{10,1... | collective-permute-start | bytes 98312 | tf_op jit(solution)/shard_map/ppermute | solution.py:357
  12.1 53.9 %collective-permute-start.11 = (bf16[1,16,1024]{2,1,0:T(8,128)(2,1)S(1)}, bf16[1,16,1024]{2,1,0:T(8,128)(2,1)}, u32[]{:S(2)}, u32[]{:S(2)}) collective-permute-start(bf16[1,16,1024]{2,1,0:T(8,128)(2,1)S(1)} %pad_bitcast_fusion.refs_1_.refs_4_), channel_id=1, source_target_pairs={{0,2},{1,3},{2,0},{3,1},{4,6},{5,7},{6,4},{7,5},{8,10},{9,11},{10,... | collective-permute-start | bytes 98312 | tf_op jit(solution)/shard_map/ppermute | solution.py:357
  14.7 51.4 %collective-permute-start.10 = (bf16[1,16,1024]{2,1,0:T(8,128)(2,1)S(1)}, bf16[1,16,1024]{2,1,0:T(8,128)(2,1)}, u32[]{:S(2)}, u32[]{:S(2)}) collective-permute-start(bf16[1,16,1024]{2,1,0:T(8,128)(2,1)S(1)} %pad_bitcast_fusion.refs_1_.refs_4_), channel_id=1, source_target_pairs={{0,3},{1,0},{2,1},{3,2},{4,7},{5,4},{6,5},{7,6},{8,11},{9,8},{10,9... | collective-permute-start | bytes 98312 | tf_op jit(solution)/shard_map/ppermute | solution.py:357
  21.1 15.8 %collective-permute-start.1 = (bf16[1,96,768]{2,1,0:T(8,128)(2,1)S(1)}, bf16[1,96,768]{2,1,0:T(8,128)(2,1)S(1)}, u32[]{:S(2)}, u32[]{:S(2)}) collective-permute-start(bf16[1,96,768]{2,1,0:T(8,128)(2,1)S(1)} %dynamic-slice_bitcast_fusion), channel_id=1, source_target_pairs={{0,2},{1,3},{2,0},{3,1},{4,6},{5,7},{6,4},{7,5},{8,10},{9,11},{10,... | collective-permute-start | bytes 442376 | tf_op jit(solution)/shard_map/ppermute | solution.py:357
  28.0 11.9 %collective-permute-start.2 = (bf16[1,96,768]{2,1,0:T(8,128)(2,1)S(1)}, bf16[1,96,768]{2,1,0:T(8,128)(2,1)S(1)}, u32[]{:S(2)}, u32[]{:S(2)}) collective-permute-start(bf16[1,96,768]{2,1,0:T(8,128)(2,1)S(1)} %dynamic-slice_bitcast_fusion), channel_id=1, source_target_pairs={{0,1},{1,2},{2,3},{3,0},{4,5},{5,6},{6,7},{7,4},{8,9},{9,10},{10,1... | collective-permute-start | bytes 442376 | tf_op jit(solution)/shard_map/ppermute | solution.py:357
  41.7 24.8 %collective-permute-start.4 = (bf16[3,96,768]{2,1,0:T(8,128)(2,1)S(1)}, bf16[3,96,768]{2,1,0:T(8,128)(2,1)}, u32[]{:S(2)}, u32[]{:S(2)}) collective-permute-start(bf16[3,96,768]{2,1,0:T(8,128)(2,1)S(1)} %constant_dynamic-update-slice_fusion.refs_0_), channel_id=1, source_target_pairs={{0,16},{4,20},{8,24},{12,28},{16,0},{20,4},{24,8},{28,12},{1,17},{... | collective-permute-start | bytes 1327112 | tf_op jit(solution)/shard_map/ppermute | solution.py:354
  50.8 15.8 %collective-permute-start.5 = (bf16[3,96,768]{2,1,0:T(8,128)(2,1)}, bf16[3,96,768]{2,1,0:T(8,128)(2,1)}, u32[]{:S(2)}, u32[]{:S(2)}) collective-permute-start(bf16[3,96,768]{2,1,0:T(8,128)(2,1)} %collective-permute-done.3.refs_1_), channel_id=1, source_target_pairs={{0,16},{4,20},{8,24},{12,28},{16,0},{20,4},{24,8},{28,12},{1,17},{... | collective-permute-start | bytes 1327112 | tf_op jit(solution)/shard_map/ppermute | solution.py:354
  54.6 15.7 %collective-permute-start.29 = (bf16[2,96,768]{2,1,0:T(8,128)(2,1)}, bf16[2,96,768]{2,1,0:T(8,128)(2,1)S(1)}, u32[]{:S(2)}, u32[]{:S(2)}) collective-permute-start(bf16[2,96,768]{2,1,0:T(8,128)(2,1)} %fusion.13), channel_id=1, source_target_pairs={{0,1},{1,2},{2,3},{3,0},{4,5},{5,6},{6,7},{7,4},{8,9},{9,10},{10,1... | collective-permute-start | bytes 884744 | tf_op jit(solution)/shard_map/ppermute | solution.py:357
  66.0 33.2 %collective-permute-start.6 = (bf16[3,96,768]{2,1,0:T(8,128)(2,1)S(1)}, bf16[3,96,768]{2,1,0:T(8,128)(2,1)S(1)}, u32[]{:S(2)}, u32[]{:S(2)}) collective-permute-start(bf16[3,96,768]{2,1,0:T(8,128)(2,1)S(1)} %constant_dynamic-update-slice_fusion.refs_0_), channel_id=1, source_target_pairs={{0,4},{4,0},{8,12},{12,8},{16,20},{20,16},{24,28},{28,24},{1,5},{5... | collective-permute-start | bytes 1327112 | tf_op jit(solution)/shard_map/ppermute | solution.py:354
  66.0 34.7 %collective-permute-start.7 = (bf16[3,96,768]{2,1,0:T(8,128)(2,1)}, bf16[3,96,768]{2,1,0:T(8,128)(2,1)S(1)}, u32[]{:S(2)}, u32[]{:S(2)}) collective-permute-start(bf16[3,96,768]{2,1,0:T(8,128)(2,1)} %collective-permute-done.3.refs_1_), channel_id=1, source_target_pairs={{0,4},{4,0},{8,12},{12,8},{16,20},{20,16},{24,28},{28,24},{1,5},{5... | collective-permute-start | bytes 1327112 | tf_op jit(solution)/shard_map/ppermute | solution.py:354
  66.5 32.6 %collective-permute-start.8 = (bf16[3,96,768]{2,1,0:T(8,128)(2,1)}, bf16[3,96,768]{2,1,0:T(8,128)(2,1)S(1)}, u32[]{:S(2)}, u32[]{:S(2)}) collective-permute-start(bf16[3,96,768]{2,1,0:T(8,128)(2,1)} %collective-permute-done.4.refs_2_), channel_id=1, source_target_pairs={{0,4},{4,0},{8,12},{12,8},{16,20},{20,16},{24,28},{28,24},{1,5},{5... | collective-permute-start | bytes 1327112 | tf_op jit(solution)/shard_map/ppermute | solution.py:354
  66.6 34.6 %collective-permute-start.9 = (bf16[3,96,768]{2,1,0:T(8,128)(2,1)}, bf16[3,96,768]{2,1,0:T(8,128)(2,1)S(1)}, u32[]{:S(2)}, u32[]{:S(2)}) collective-permute-start(bf16[3,96,768]{2,1,0:T(8,128)(2,1)} %collective-permute-done.5.refs_3_), channel_id=1, source_target_pairs={{0,4},{4,0},{8,12},{12,8},{16,20},{20,16},{24,28},{28,24},{1,5},{5... | collective-permute-start | bytes 1327112 | tf_op jit(solution)/shard_map/ppermute | solution.py:354
  70.3 16.4 %collective-permute-start.21 = (bf16[2,96,768]{2,1,0:T(8,128)(2,1)}, bf16[2,96,768]{2,1,0:T(8,128)(2,1)S(1)}, u32[]{:S(2)}, u32[]{:S(2)}) collective-permute-start(bf16[2,96,768]{2,1,0:T(8,128)(2,1)} %fusion.13), channel_id=1, source_target_pairs={{0,2},{1,3},{2,0},{3,1},{4,6},{5,7},{6,4},{7,5},{8,10},{9,11},{10,... | collective-permute-start | bytes 884744 | tf_op jit(solution)/shard_map/ppermute | solution.py:357
  86.7 34.9 %collective-permute-start.13 = (bf16[2,96,768]{2,1,0:T(8,128)(2,1)}, bf16[2,96,768]{2,1,0:T(8,128)(2,1)S(1)}, u32[]{:S(2)}, u32[]{:S(2)}) collective-permute-start(bf16[2,96,768]{2,1,0:T(8,128)(2,1)} %fusion.13), channel_id=1, source_target_pairs={{0,3},{1,0},{2,1},{3,2},{4,7},{5,4},{6,5},{7,6},{8,11},{9,8},{10,9... | collective-permute-start | bytes 884744 | tf_op jit(solution)/shard_map/ppermute | solution.py:357
  99.2 23.1 %collective-permute-start.33 = (bf16[2,96,768]{2,1,0:T(8,128)(2,1)S(1)}, bf16[2,96,768]{2,1,0:T(8,128)(2,1)S(1)}, u32[]{:S(2)}, u32[]{:S(2)}) collective-permute-start(bf16[2,96,768]{2,1,0:T(8,128)(2,1)S(1)} %collective-permute-done.29.refs_0_), channel_id=1, source_target_pairs={{0,4},{4,0},{8,12},{12,8},{16,20},{20,16},{24,28},{28,24},{1,5},{5... | collective-permute-start | bytes 884744 | tf_op jit(solution)/shard_map/ppermute | solution.py:354
  99.2 25.4 %collective-permute-start.31 = (bf16[2,96,768]{2,1,0:T(8,128)(2,1)S(1)}, bf16[2,96,768]{2,1,0:T(8,128)(2,1)S(1)}, u32[]{:S(2)}, u32[]{:S(2)}) collective-permute-start(bf16[2,96,768]{2,1,0:T(8,128)(2,1)S(1)} %collective-permute-done.29.refs_0_), channel_id=1, source_target_pairs={{0,8},{4,12},{8,0},{12,4},{16,24},{20,28},{24,16},{28,20},{1,9},{5... | collective-permute-start | bytes 884744 | tf_op jit(solution)/shard_map/ppermute | solution.py:354
  100.8 21.9 %collective-permute-start.30 = (bf16[2,96,768]{2,1,0:T(8,128)(2,1)S(1)}, bf16[2,96,768]{2,1,0:T(8,128)(2,1)S(1)}, u32[]{:S(2)}, u32[]{:S(2)}) collective-permute-start(bf16[2,96,768]{2,1,0:T(8,128)(2,1)S(1)} %collective-permute-done.29.refs_0_), channel_id=1, source_target_pairs={{0,16},{4,20},{8,24},{12,28},{16,0},{20,4},{24,8},{28,12},{1,17},{... | collective-permute-start | bytes 884744 | tf_op jit(solution)/shard_map/ppermute | solution.py:354
  101.3 24.0 %collective-permute-start.23 = (bf16[2,96,768]{2,1,0:T(8,128)(2,1)S(1)}, bf16[2,96,768]{2,1,0:T(8,128)(2,1)S(1)}, u32[]{:S(2)}, u32[]{:S(2)}) collective-permute-start(bf16[2,96,768]{2,1,0:T(8,128)(2,1)S(1)} %collective-permute-done.21.refs_0_), channel_id=1, source_target_pairs={{0,16},{4,20},{8,24},{12,28},{16,0},{20,4},{24,8},{28,12},{1,17},{... | collective-permute-start | bytes 884744 | tf_op jit(solution)/shard_map/ppermute | solution.py:354
  122.7 15.2 %collective-permute-start.32 = (bf16[2,96,768]{2,1,0:T(8,128)(2,1)S(1)}, bf16[2,96,768]{2,1,0:T(8,128)(2,1)S(1)}, u32[]{:S(2)}, u32[]{:S(2)}) collective-permute-start(bf16[2,96,768]{2,1,0:T(8,128)(2,1)S(1)} %collective-permute-done.30.refs_1_), channel_id=1, source_target_pairs={{0,8},{4,12},{8,0},{12,4},{16,24},{20,28},{24,16},{28,20},{1,9},{5... | collective-permute-start | bytes 884744 | tf_op jit(solution)/shard_map/ppermute | solution.py:354
  124.6 19.6 %collective-permute-start.15 = (bf16[2,96,768]{2,1,0:T(8,128)(2,1)S(1)}, bf16[2,96,768]{2,1,0:T(8,128)(2,1)S(1)}, u32[]{:S(2)}, u32[]{:S(2)}) collective-permute-start(bf16[2,96,768]{2,1,0:T(8,128)(2,1)S(1)} %collective-permute-done.13.refs_0_), channel_id=1, source_target_pairs={{0,8},{4,12},{8,0},{12,4},{16,24},{20,28},{24,16},{28,20},{1,9},{5... | collective-permute-start | bytes 884744 | tf_op jit(solution)/shard_map/ppermute | solution.py:354
  125.2 19.5 %collective-permute-start.34 = (bf16[2,96,768]{2,1,0:T(8,128)(2,1)S(1)}, bf16[2,96,768]{2,1,0:T(8,128)(2,1)S(1)}, u32[]{:S(2)}, u32[]{:S(2)}) collective-permute-start(bf16[2,96,768]{2,1,0:T(8,128)(2,1)S(1)} %collective-permute-done.30.refs_1_), channel_id=1, source_target_pairs={{0,4},{4,0},{8,12},{12,8},{16,20},{20,16},{24,28},{28,24},{1,5},{5... | collective-permute-start | bytes 884744 | tf_op jit(solution)/shard_map/ppermute | solution.py:354
  131.6 12.6 %collective-permute-start.35 = (bf16[2,96,768]{2,1,0:T(8,128)(2,1)S(1)}, bf16[2,96,768]{2,1,0:T(8,128)(2,1)S(1)}, u32[]{:S(2)}, u32[]{:S(2)}) collective-permute-start(bf16[2,96,768]{2,1,0:T(8,128)(2,1)S(1)} %collective-permute-done.31.refs_2_), channel_id=1, source_target_pairs={{0,4},{4,0},{8,12},{12,8},{16,20},{20,16},{24,28},{28,24},{1,5},{5... | collective-permute-start | bytes 884744 | tf_op jit(solution)/shard_map/ppermute | solution.py:354
  131.6 17.5 %collective-permute-start.16 = (bf16[2,96,768]{2,1,0:T(8,128)(2,1)S(1)}, bf16[2,96,768]{2,1,0:T(8,128)(2,1)S(1)}, u32[]{:S(2)}, u32[]{:S(2)}) collective-permute-start(bf16[2,96,768]{2,1,0:T(8,128)(2,1)S(1)} %collective-permute-done.14.refs_1_), channel_id=1, source_target_pairs={{0,8},{4,12},{8,0},{12,4},{16,24},{20,28},{24,16},{28,20},{1,9},{5... | collective-permute-start | bytes 884744 | tf_op jit(solution)/shard_map/ppermute | solution.py:354
  137.9 11.2 %collective-permute-start.36 = (bf16[2,96,768]{2,1,0:T(8,128)(2,1)S(1)}, bf16[2,96,768]{2,1,0:T(8,128)(2,1)S(1)}, u32[]{:S(2)}, u32[]{:S(2)}) collective-permute-start(bf16[2,96,768]{2,1,0:T(8,128)(2,1)S(1)} %collective-permute-done.32.refs_3_), channel_id=1, source_target_pairs={{0,4},{4,0},{8,12},{12,8},{16,20},{20,16},{24,28},{28,24},{1,5},{5... | collective-permute-start | bytes 884744 | tf_op jit(solution)/shard_map/ppermute | solution.py:354
  144.3 11.9 %collective-permute-start.17 = (bf16[2,96,768]{2,1,0:T(8,128)(2,1)S(1)}, bf16[2,96,768]{2,1,0:T(8,128)(2,1)S(1)}, u32[]{:S(2)}, u32[]{:S(2)}) collective-permute-start(bf16[2,96,768]{2,1,0:T(8,128)(2,1)S(1)} %collective-permute-done.13.refs_0_), channel_id=1, source_target_pairs={{0,4},{4,0},{8,12},{12,8},{16,20},{20,16},{24,28},{28,24},{1,5},{5... | collective-permute-start | bytes 884744 | tf_op jit(solution)/shard_map/ppermute | solution.py:354
  144.3 12.5 %collective-permute-start.18 = (bf16[2,96,768]{2,1,0:T(8,128)(2,1)S(1)}, bf16[2,96,768]{2,1,0:T(8,128)(2,1)S(1)}, u32[]{:S(2)}, u32[]{:S(2)}) collective-permute-start(bf16[2,96,768]{2,1,0:T(8,128)(2,1)S(1)} %collective-permute-done.14.refs_1_), channel_id=1, source_target_pairs={{0,4},{4,0},{8,12},{12,8},{16,20},{20,16},{24,28},{28,24},{1,5},{5... | collective-permute-start | bytes 884744 | tf_op jit(solution)/shard_map/ppermute | solution.py:354
  144.8 11.4 %collective-permute-start.24 = (bf16[2,96,768]{2,1,0:T(8,128)(2,1)S(1)}, bf16[2,96,768]{2,1,0:T(8,128)(2,1)S(1)}, u32[]{:S(2)}, u32[]{:S(2)}) collective-permute-start(bf16[2,96,768]{2,1,0:T(8,128)(2,1)S(1)} %collective-permute-done.22.refs_1_), channel_id=1, source_target_pairs={{0,16},{4,20},{8,24},{12,28},{16,0},{20,4},{24,8},{28,12},{1,17},{... | collective-permute-start | bytes 884744 | tf_op jit(solution)/shard_map/ppermute | solution.py:354
  157.2 28.7 %collective-permute-start.70 = (bf16[2,2,2,96,768]{4,3,2,1,0:T(8,128)(2,1)}, bf16[2,2,2,96,768]{4,3,2,1,0:T(8,128)(2,1)S(1)}, u32[]{:S(2)}, u32[]{:S(2)}) collective-permute-start(bf16[2,2,2,96,768]{4,3,2,1,0:T(8,128)(2,1)} %bitcast.25), channel_id=1, source_target_pairs={{0,4},{4,0},{8,12},{12,8},{16,20},{20,16},{24,28},{28,24},{1,5},{5... | collective-permute-start | bytes 3538952 | tf_op jit(solution)/shard_map/ppermute | solution.py:354
  163.8 23.7 %collective-permute-start.62 = (bf16[2,2,2,96,768]{4,3,2,1,0:T(8,128)(2,1)}, bf16[2,2,2,96,768]{4,3,2,1,0:T(8,128)(2,1)S(1)}, u32[]{:S(2)}, u32[]{:S(2)}) collective-permute-start(bf16[2,2,2,96,768]{4,3,2,1,0:T(8,128)(2,1)} %bitcast.21), channel_id=1, source_target_pairs={{0,4},{4,0},{8,12},{12,8},{16,20},{20,16},{24,28},{28,24},{1,5},{5... | collective-permute-start | bytes 3538952 | tf_op jit(solution)/shard_map/ppermute | solution.py:354
  171.0 18.3 %collective-permute-start.66 = (bf16[2,2,2,96,768]{4,3,2,1,0:T(8,128)(2,1)}, bf16[2,2,2,96,768]{4,3,2,1,0:T(8,128)(2,1)}, u32[]{:S(2)}, u32[]{:S(2)}) collective-permute-start(bf16[2,2,2,96,768]{4,3,2,1,0:T(8,128)(2,1)} %bitcast.23), channel_id=1, source_target_pairs={{0,4},{4,0},{8,12},{12,8},{16,20},{20,16},{24,28},{28,24},{1,5},{5... | collective-permute-start | bytes 3538952 | tf_op jit(solution)/shard_map/ppermute | solution.py:354
  179.7 12.0 %collective-permute-start.59 = (bf16[2,2,2,96,768]{4,3,2,1,0:T(8,128)(2,1)}, bf16[2,2,2,96,768]{4,3,2,1,0:T(8,128)(2,1)}, u32[]{:S(2)}, u32[]{:S(2)}) collective-permute-start(bf16[2,2,2,96,768]{4,3,2,1,0:T(8,128)(2,1)} %bitcast.19), channel_id=1, source_target_pairs={{0,4},{4,0},{8,12},{12,8},{16,20},{20,16},{24,28},{28,24},{1,5},{5... | collective-permute-start | bytes 3538952 | tf_op jit(solution)/shard_map/ppermute | solution.py:354
  186.9 28.5 %collective-permute-start.71 = (bf16[2,2,96,768]{3,2,1,0:T(8,128)(2,1)S(1)}, bf16[2,2,96,768]{3,2,1,0:T(8,128)(2,1)S(1)}, u32[]{:S(2)}, u32[]{:S(2)}) collective-permute-start(bf16[2,2,96,768]{3,2,1,0:T(8,128)(2,1)S(1)} %get-tuple-element.128), channel_id=1, source_target_pairs={{0,16},{4,20},{8,24},{12,28},{16,0},{20,4},{24,8},{28,12},{1,17},{... | collective-permute-start | bytes 1769480 | tf_op jit(solution)/shard_map/ppermute | solution.py:354
  187.9 28.3 %collective-permute-start.63 = (bf16[2,2,96,768]{3,2,1,0:T(8,128)(2,1)S(1)}, bf16[2,2,96,768]{3,2,1,0:T(8,128)(2,1)S(1)}, u32[]{:S(2)}, u32[]{:S(2)}) collective-permute-start(bf16[2,2,96,768]{3,2,1,0:T(8,128)(2,1)S(1)} %get-tuple-element.116), channel_id=1, source_target_pairs={{0,16},{4,20},{8,24},{12,28},{16,0},{20,4},{24,8},{28,12},{1,17},{... | collective-permute-start | bytes 1769480 | tf_op jit(solution)/shard_map/ppermute | solution.py:354
  191.1 26.8 %collective-permute-start.67 = (bf16[2,2,96,768]{3,2,1,0:T(8,128)(2,1)S(1)}, bf16[2,2,96,768]{3,2,1,0:T(8,128)(2,1)S(1)}, u32[]{:S(2)}, u32[]{:S(2)}) collective-permute-start(bf16[2,2,96,768]{3,2,1,0:T(8,128)(2,1)S(1)} %get-tuple-element.122), channel_id=1, source_target_pairs={{0,8},{4,12},{8,0},{12,4},{16,24},{20,28},{24,16},{28,20},{1,9},{5... | collective-permute-start | bytes 1769480 | tf_op jit(solution)/shard_map/ppermute | solution.py:354
  193.2 25.5 %collective-permute-start.60 = (bf16[2,2,96,768]{3,2,1,0:T(8,128)(2,1)S(1)}, bf16[2,2,96,768]{3,2,1,0:T(8,128)(2,1)S(1)}, u32[]{:S(2)}, u32[]{:S(2)}) collective-permute-start(bf16[2,2,96,768]{3,2,1,0:T(8,128)(2,1)S(1)} %get-tuple-element.110), channel_id=1, source_target_pairs={{0,8},{4,12},{8,0},{12,4},{16,24},{20,28},{24,16},{28,20},{1,9},{5... | collective-permute-start | bytes 1769480 | tf_op jit(solution)/shard_map/ppermute | solution.py:354
  215.4 40.1 %collective-permute-start.40 = (bf16[3,2,2,96,768]{4,3,2,1,0:T(8,128)(2,1)}, bf16[3,2,2,96,768]{4,3,2,1,0:T(8,128)(2,1)}, u32[]{:S(2)}, u32[]{:S(2)}) collective-permute-start(bf16[3,2,2,96,768]{4,3,2,1,0:T(8,128)(2,1)} %bitcast.57), channel_id=1, source_target_pairs={{0,4},{4,0},{8,12},{12,8},{16,20},{20,16},{24,28},{28,24},{1,5},{5... | collective-permute-start | bytes 5308424 | tf_op jit(solution)/shard_map/ppermute | solution.py:354
  216.3 15.0 %collective-permute-start.64 = (bf16[2,96,768]{2,1,0:T(8,128)(2,1)S(1)}, bf16[2,96,768]{2,1,0:T(8,128)(2,1)S(1)}, u32[]{:S(2)}, u32[]{:S(2)}) collective-permute-start(bf16[2,96,768]{2,1,0:T(8,128)(2,1)S(1)} %get-tuple-element.118), channel_id=1, source_target_pairs={{0,8},{4,12},{8,0},{12,4},{16,24},{20,28},{24,16},{28,20},{1,9},{5... | collective-permute-start | bytes 884744 | tf_op jit(solution)/shard_map/ppermute | solution.py:354
  218.0 14.5 %collective-permute-start.68 = (bf16[2,96,768]{2,1,0:T(8,128)(2,1)S(1)}, bf16[2,96,768]{2,1,0:T(8,128)(2,1)S(1)}, u32[]{:S(2)}, u32[]{:S(2)}) collective-permute-start(bf16[2,96,768]{2,1,0:T(8,128)(2,1)S(1)} %get-tuple-element.124), channel_id=1, source_target_pairs={{0,16},{4,20},{8,24},{12,28},{16,0},{20,4},{24,8},{28,12},{1,17},{... | collective-permute-start | bytes 884744 | tf_op jit(solution)/shard_map/ppermute | solution.py:354
  218.8 14.4 %collective-permute-start.61 = (bf16[2,96,768]{2,1,0:T(8,128)(2,1)S(1)}, bf16[2,96,768]{2,1,0:T(8,128)(2,1)S(1)}, u32[]{:S(2)}, u32[]{:S(2)}) collective-permute-start(bf16[2,96,768]{2,1,0:T(8,128)(2,1)S(1)} %get-tuple-element.112), channel_id=1, source_target_pairs={{0,16},{4,20},{8,24},{12,28},{16,0},{20,4},{24,8},{28,12},{1,17},{... | collective-permute-start | bytes 884744 | tf_op jit(solution)/shard_map/ppermute | solution.py:354
  231.4 12.0 %collective-permute-start.65 = (bf16[2,96,768]{2,1,0:T(8,128)(2,1)S(1)}, bf16[2,96,768]{2,1,0:T(8,128)(2,1)S(1)}, u32[]{:S(2)}, u32[]{:S(2)}) collective-permute-start(bf16[2,96,768]{2,1,0:T(8,128)(2,1)S(1)} %fold.29), channel_id=1, source_target_pairs={{0,1},{1,2},{2,3},{3,0},{4,5},{5,6},{6,7},{7,4},{8,9},{9,10},{10,1... | collective-permute-start | bytes 884744 | tf_op jit(solution)/shard_map/ppermute | solution.py:360
  232.6 21.9 %collective-permute-start.69 = (bf16[2,96,768]{2,1,0:T(8,128)(2,1)S(1)}, bf16[2,96,768]{2,1,0:T(8,128)(2,1)S(1)}, u32[]{:S(2)}, u32[]{:S(2)}) collective-permute-start(bf16[2,96,768]{2,1,0:T(8,128)(2,1)S(1)} %fold.32), channel_id=1, source_target_pairs={{0,2},{1,3},{2,0},{3,1},{4,6},{5,7},{6,4},{7,5},{8,10},{9,11},{10,... | collective-permute-start | bytes 884744 | tf_op jit(solution)/shard_map/ppermute | solution.py:360
  258.4 31.1 %collective-permute-start.41 = (bf16[3,2,96,768]{3,2,1,0:T(8,128)(2,1)}, bf16[3,2,96,768]{3,2,1,0:T(8,128)(2,1)S(1)}, u32[]{:S(2)}, u32[]{:S(2)}) collective-permute-start(bf16[3,2,96,768]{3,2,1,0:T(8,128)(2,1)} %get-tuple-element.98), channel_id=1, source_target_pairs={{0,16},{4,20},{8,24},{12,28},{16,0},{20,4},{24,8},{28,12},{1,17},{... | collective-permute-start | bytes 2654216 | tf_op jit(solution)/shard_map/ppermute | solution.py:354
  271.0 19.3 %collective-permute-start.53 = (f32[1920]{0:T(1024)S(1)}, f32[1920]{0:T(1024)S(1)}, u32[]{:S(2)}, u32[]{:S(2)}) collective-permute-start(f32[1920]{0:T(1024)S(1)} %pad_maximum_fusion.4), channel_id=1, source_target_pairs={{0,4},{4,0},{8,12},{12,8},{16,20},{20,16},{24,28},{28,24},{1,5},{5... | collective-permute-start | bytes 23048 | tf_op jit(solution)/shard_map/ppermute | solution.py:354
  272.9 31.1 %collective-permute-start.38 = (bf16[1,2,96,768]{3,2,1,0:T(8,128)(2,1)S(1)}, bf16[1,2,96,768]{3,2,1,0:T(8,128)(2,1)S(1)}, u32[]{:S(2)}, u32[]{:S(2)}) collective-permute-start(bf16[1,2,96,768]{3,2,1,0:T(8,128)(2,1)S(1)} %get-tuple-element.92), channel_id=1, source_target_pairs={{0,8},{4,12},{8,0},{12,4},{16,24},{20,28},{24,16},{28,20},{1,9},{5... | collective-permute-start | bytes 884744 | tf_op jit(solution)/shard_map/ppermute | solution.py:354
  289.7 16.1 %collective-permute-start.42 = (bf16[3,96,768]{2,1,0:T(8,128)(2,1)S(1)}, bf16[3,96,768]{2,1,0:T(8,128)(2,1)S(1)}, u32[]{:S(2)}, u32[]{:S(2)}) collective-permute-start(bf16[3,96,768]{2,1,0:T(8,128)(2,1)S(1)} %get-tuple-element.100), channel_id=1, source_target_pairs={{0,8},{4,12},{8,0},{12,4},{16,24},{20,28},{24,16},{28,20},{1,9},{5... | collective-permute-start | bytes 1327112 | tf_op jit(solution)/shard_map/ppermute | solution.py:354
  310.1 14.1 %collective-permute-start.56 = (f32[1632]{0:T(1024)S(1)}, f32[1632]{0:T(1024)S(1)}, u32[]{:S(2)}, u32[]{:S(2)}) collective-permute-start(f32[1632]{0:T(1024)S(1)} %get-tuple-element.185), channel_id=1, source_target_pairs={{0,1},{1,2},{2,3},{3,0},{4,5},{5,6},{6,7},{7,4},{8,9},{9,10},{10,1... | collective-permute-start | bytes 19592 | tf_op jit(solution)/shard_map/ppermute | solution.py:360
  310.6 13.6 %collective-permute-start.57 = (f32[1632]{0:T(1024)S(1)}, f32[1632]{0:T(1024)S(1)}, u32[]{:S(2)}, u32[]{:S(2)}) collective-permute-start(f32[1632]{0:T(1024)S(1)} %get-tuple-element.186), channel_id=1, source_target_pairs={{0,2},{1,3},{2,0},{3,1},{4,6},{5,7},{6,4},{7,5},{8,10},{9,11},{10,... | collective-permute-start | bytes 19592 | tf_op jit(solution)/shard_map/ppermute | solution.py:360
  (101 other events, 1139.4 us)
Sparse Core Ops, SparseCore 0:
  255.6 34.8 all-gather.2

commit v3 on v2

v3 whole, which is shorter than its diff:
```python
import functools

import jax
import jax.numpy as jnp
import numpy as np
from jax import lax
from jax.experimental import pallas as pl
from jax.experimental.pallas import tpu as pltpu
from jax.sharding import PartitionSpec as P

BIG = 512
HEAD = 64
EPS = 1e-06
THRESHOLDS = (12, 16, 23, 32, 46, 64, 91)
MASKED = -1e30
TILE = 128
SPAN = 512
EXTRA = 16
BF = jnp.bfloat16
F32 = jnp.float32
MIB = 1024 * 1024
LIMIT = 60
SMEM = pl.BlockSpec(memory_space=pltpu.SMEM)
VMEM = pl.BlockSpec(memory_space=pltpu.VMEM)
ANY = pl.BlockSpec(memory_space=pl.ANY)


def offset_one_hot(buckets):
    offsets = np.arange(SPAN) - SPAN // 2
    distance = np.abs(offsets)
    far = 8 + sum((distance >= t).astype(np.int32) for t in THRESHOLDS)
    bucket = np.where(distance < 8, distance, far) + np.where(offsets > 0, buckets // 2, 0)
    return (np.arange(TILE)[:, None] == bucket[None, :]).astype(np.float32)


def dot_nn(a, b):
    return lax.dot_general(a, b, (((1,), (0,)), ((), ())), preferred_element_type=F32)


def dot_nt(a, b):
    return lax.dot_general(a, b, (((1,), (1,)), ((), ())), preferred_element_type=F32)


def dot_tn(a, b):
    return lax.dot_general(a, b, (((0,), (0,)), ((), ())), preferred_element_type=F32)


def like(shape, dtype):
    return jax.ShapeDtypeStruct(shape, dtype)


def params(mib):
    return pltpu.CompilerParams(vmem_limit_bytes=mib * MIB)


def cost(micros):
    return pl.CostEstimate(flops=micros * 10**9, bytes_accessed=micros * 10**6, transcendentals=0)


def mask_rows(meta_ref, slots):
    bucket = meta_ref[0]
    half = BIG // 2
    segs, starts = [], []
    for part in range(2):
        first = meta_ref[1] + part * half
        seg = jnp.int32(0)
        for j in range(1, slots):
            seg = seg + jnp.where(first >= j * bucket, 1, 0).astype(jnp.int32)
        segs.append(seg)
        starts.append(first - seg * bucket)
    iota = lax.broadcasted_iota(jnp.int32, (1, half), 1)
    rows = []
    for query_part in range(2):
        cols = []
        for key_part in range(2):
            same = segs[query_part] == segs[key_part]
            limit = jnp.where(same, meta_ref[2 + segs[key_part]] - starts[key_part], 0)
            cols.append(jnp.where(iota < limit, 0.0, MASKED).astype(F32))
        rows.append(jnp.concatenate(cols, axis=1))
    return rows


def bias_band(rel_row):
    return pltpu.roll(jnp.broadcast_to(rel_row, (TILE, SPAN)), 0, 1, stride=1, stride_axis=0)


def masked_bias(i, near, rel_row, mask):
    tiles = []
    for j in range(BIG // TILE):
        keys = mask[:, j * TILE : (j + 1) * TILE]
        if abs(j - i) <= 1:
            tiles.append(near[:, (j - i + 2) * TILE : (j - i + 3) * TILE] + keys)
        else:
            far = rel_row[:, SPAN - 1 :] if j > i else rel_row[:, :1]
            tiles.append(jnp.broadcast_to(far + keys, (TILE, TILE)))
    return jnp.concatenate(tiles, axis=1)


class Mover:
    def __init__(self, sems):
        self.sems, self.used, self.out = sems, 0, []

    def copy(self, source, target):
        one = pltpu.make_async_copy(source, target, self.sems.at[self.used])
        self.used += 1
        one.start()
        return one

    def load(self, source, target):
        return [self.copy(source, target)]

    def blocks(self, index_ref, part_refs, mat, which):
        copies, j, first = [], 0, 0
        for part in part_refs:
            if index_ref is None:
                copies.append(self.copy(part, mat.at[pl.ds(first, part.shape[0])]))
                first += part.shape[0]
                continue
            rows = part.shape[2]
            for e in range(part.shape[0]):
                at = pl.ds(pl.multiple_of(index_ref[j] * rows, rows), rows)
                copies.append(self.copy(part.at[e, which], mat.at[at]))
                j += 1
        return copies

    def store(self, source, target):
        self.out.append(self.copy(source, target))

    def halves(self, side_ref, source, send, keep):
        size = source.shape[0] // 2
        for ref, side in ((send, 1 - side_ref[0]), (keep, side_ref[0])):
            self.store(source.at[pl.ds(pl.multiple_of(side * size, size), size)], ref)

    def finish(self):
        wait(self.out)


def wait(copies):
    for one in copies:
        one.wait()


def put_blocks(index_ref, part_refs, mat, which):
    j = 0
    for part in part_refs:
        rows = part.shape[2]
        for e in range(part.shape[0]):
            mat[pl.ds(pl.multiple_of(index_ref[j] * rows, rows), rows), :] = part[e, which].astype(mat.dtype)
            j += 1


def rms(values):
    root = lax.rsqrt(jnp.mean(values * values, axis=1, keepdims=True) + EPS)
    return values * root, root


def rms_back(grad, unit, root, gain):
    scaled = grad * gain
    centred = scaled - unit * jnp.mean(scaled * unit, axis=1, keepdims=True)
    return root * centred, jnp.sum(grad * unit, axis=0, keepdims=True)


def head_slices(qkv_ref, heads, h):
    width = heads * HEAD
    return [qkv_ref[:, j * width + h * HEAD : j * width + (h + 1) * HEAD] for j in (1, 2, 3)]


def forward_scores(h, band, rel, masks, scores, lse_ref):
    probs = []
    for i in range(BIG // TILE):
        rows = slice(i * TILE, (i + 1) * TILE)
        s = scores[h, rows, :] + masked_bias(i, band[h], rel[h : h + 1], masks[i // 2])
        top = jnp.max(s, axis=1, keepdims=True)
        e = jnp.exp(s - top)
        total = jnp.sum(e, axis=1, keepdims=True)
        probs.append((e * (1.0 / total)).astype(BF))
        lse_ref[rows, h : h + 1] = top + jnp.log(total)
    return jnp.concatenate(probs, axis=0)


def attn_fwd_kernel(slots, heads, parts, start, shards, own, last, meta_ref, *refs):
    refs = list(refs)
    take = lambda n: [refs.pop(0) for _ in range(n)]
    index_ref = None if own else take(1)[0]
    n1_hbm = take(1)[0]
    a_parts = take(parts)
    tab_hbm, hot_hbm, prior_hbm = take(3)
    gain_hbm = take(1)[0] if last else None
    qkv_out, o_out, lse_out, hid_out = take(4)
    n2_out = take(1)[0] if last else None
    n1_ref, mat, tab_ref, hot_ref, prior_ref, gain_ref, qkv_ref, o_ref, lse_ref, hid_ref, n2_ref, band, scores, sems = refs
    move = Mover(sems)
    width = heads * HEAD
    half = BIG // 2
    got_mat = [move.blocks(index_ref, a_parts, mat.at[0], start)]
    got_n1 = move.load(n1_hbm, n1_ref)
    got_tab = move.load(tab_hbm.at[pl.ds(start, shards)], tab_ref) + move.load(hot_hbm, hot_ref)
    masks = mask_rows(meta_ref, slots)
    wait(got_tab)
    wait(got_n1)
    for s in range(shards):
        rel = dot_nn(tab_ref[s], hot_ref[...])
        for h in range(heads):
            band[h] = bias_band(rel[h : h + 1])
        wait(got_mat[s])
        if s == 0:
            got_mat += [move.blocks(index_ref, a_parts, mat.at[t], start + t) for t in range(1, shards)]
            got_prior = move.load(prior_hbm, prior_ref)
            if last:
                got_prior += move.load(gain_hbm, gain_ref)
        qkv_ref[s] = dot_nt(n1_ref[...], mat[s]).astype(BF)
        move.store(qkv_ref.at[s], qkv_out.at[s])
        for h in range(heads):
            q, k, _ = head_slices(qkv_ref.at[s], heads, h)
            scores[h] = dot_nt(q, k)
        for h in range(heads):
            v = head_slices(qkv_ref.at[s], heads, h)[2]
            pb = forward_scores(h, band, rel, masks, scores, lse_ref.at[s])
            o_ref[s, :, h * HEAD : (h + 1) * HEAD] = dot_nn(pb, v).astype(BF)
        move.store(o_ref.at[s], o_out.at[s])
        move.store(lse_ref.at[s], lse_out.at[s])
        if s == 0:
            wait(got_prior)
        for part in range(2):
            rows = pl.ds(part * half, half)
            before = prior_ref[rows, :].astype(F32) if s == 0 else hid_ref[rows, :]
            hidden = before + dot_nn(o_ref[s, rows, :], mat[s, :width, :])
            hid_ref[rows, :] = hidden
            if s == shards - 1:
                move.store(hid_ref.at[rows], hid_out.at[rows])
                if last:
                    n2_ref[rows, :] = (rms(hidden)[0] * gain_ref[...].astype(F32)).astype(BF)
                    move.store(n2_ref.at[rows], n2_out.at[rows])
    move.finish()


HBM = pl.BlockSpec(memory_space=pltpu.HBM)


def attn_fwd(meta, index, n1, a_parts, start, shards, tab, hot, prior, gain, slots, heads):
    own, last = index is None, gain is not None
    rows, depth = n1.shape
    width = heads * HEAD
    cols = 4 * width
    scalars = [meta] if own else [meta, index]
    args = [n1, *a_parts, tab, hot, prior] + ([gain] if last else [])
    out_shape = [
        like((shards, rows, cols), BF),
        like((shards, rows, width), BF),
        like((shards, rows, TILE), F32),
        like((rows, depth), F32),
    ]
    if last:
        out_shape.append(like((rows, depth), BF))
    return pl.pallas_call(
        functools.partial(attn_fwd_kernel, slots, heads, len(a_parts), start, shards, own, last),
        in_specs=[SMEM] * len(scalars) + [ANY] * len(args),
        out_specs=[HBM] * len(out_shape),
        out_shape=out_shape,
        scratch_shapes=[
            pltpu.VMEM((rows, depth), BF),
            pltpu.VMEM((shards, cols, depth), BF),
            pltpu.VMEM((shards,) + tab.shape[1:], BF),
            pltpu.VMEM(hot.shape, BF),
            pltpu.VMEM(prior.shape, prior.dtype),
            pltpu.VMEM((1, depth), BF),
            pltpu.VMEM((shards, rows, cols), BF),
            pltpu.VMEM((shards, rows, width), BF),
            pltpu.VMEM((shards, rows, TILE), F32),
            pltpu.VMEM((rows, depth), F32),
            pltpu.VMEM((rows, depth), BF),
            pltpu.VMEM((heads, TILE, SPAN), F32),
            pltpu.VMEM((heads, BIG, BIG), F32),
            pltpu.SemaphoreType.DMA((12 + 12 * shards,)),
        ],
        compiler_params=params(LIMIT),
        cost_estimate=cost(16 * shards),
        name="attn_fwd",
    )(*scalars, *args)


def attn_bwd_kernel(slots, heads, shards, rest, sources, own, first, befores, meta_ref, side_ref, index_ref, *refs):
    refs = list(refs)
    take = lambda n: [refs.pop(0) for _ in range(n)]
    last = None in shards
    count = len(shards)
    n1_hbm, gh_hbm, hot_hbm = take(3)
    rest_parts = take(rest)
    rest_tab = take(1)[0]
    rest_kept, rest_at = {}, {}
    for places in sources:
        kept = take(3) + [rest_tab]
        for base, which in enumerate(places):
            rest_kept[which], rest_at[which] = kept, base
    own_parts, own_kept = (take(own), take(4)) if last else ([], [])
    prior_hbm = None if first else take(1)[0]
    if last:
        x_hbm, gain_hbm, ghid_hbm, gain2_hbm = take(4)
        tabs_hbm = take(befores)
        send_out, keep_out, gin_out = take(3)
    else:
        send_out, keep_out, gn_out, tabs_out = take(4)
    n1_ref, gh_ref, hot_ref, mat, qkv_ref, o_ref, lse_ref, tab_ref, gn_ref = take(9)
    band, acc, gs_all, pb_all, gq_all, grads_mat, tabs_ref, sems = take(8)
    move = Mover(sems)
    width = heads * HEAD
    half = BIG // 2
    if last:
        x_ref, gain_ref, ghid_ref, gain2_ref, before_ref, small, packed = take(7)

    def load(c):
        which = shards[c]
        parts, kept = (own_parts, own_kept) if which is None else (rest_parts, rest_kept[which])
        at = 0 if which is None else which
        base = 0 if which is None else rest_at[which]
        got_tab = move.load(kept[3].at[at], tab_ref.at[c])
        got_mat = move.blocks(None if which is None else index_ref, parts, mat.at[c], at)
        got_kept = move.load(kept[0].at[base], qkv_ref.at[c]) + move.load(kept[2].at[base], lse_ref.at[c])
        return got_tab, got_mat, got_kept, move.load(kept[1].at[base], o_ref.at[c])

    got_first = move.load(hot_hbm, hot_ref) + move.load(gh_hbm, gh_ref)
    got = [load(0)]
    got_n1 = move.load(n1_hbm, n1_ref)
    masks = mask_rows(meta_ref, slots)
    lane = lax.broadcasted_iota(jnp.int32, (1, SPAN), 1)
    wait(got_first)
    gh = gh_ref[...]
    for c in range(count):
        got_tab, got_mat, got_kept, got_late = got[c]
        acc[...] = jnp.zeros(acc.shape, F32)
        gq_all[c, :, :width] = jnp.zeros((gq_all.shape[1], width), BF)
        wait(got_tab)
        rel = dot_nn(tab_ref[c], hot_ref[...])
        for h in range(heads):
            band[h] = bias_band(rel[h : h + 1])
        wait(got_mat)
        go_all = dot_nt(gh, mat[c, :width, :]).astype(BF)
        wait(got_kept)
        if c == 0:
            got += [load(t) for t in range(1, count)]
            got_prior = [] if first else move.load(prior_hbm, gn_ref)
            if last:
                got_prior += move.load(x_hbm, x_ref) + move.load(gain_hbm, gain_ref)
                got_prior += move.load(ghid_hbm, ghid_ref) + move.load(gain2_hbm, gain2_ref)
                done = 0
                for ref in tabs_hbm:
                    got_prior += move.load(ref, before_ref.at[pl.ds(done, ref.shape[0])])
                    done += ref.shape[0]
        far = []
        for h in range(heads):
            q, k, v = head_slices(qkv_ref.at[c], heads, h)
            go = go_all[:, h * HEAD : (h + 1) * HEAD]
            low = jnp.zeros((1, TILE), F32)
            high = jnp.zeros((1, TILE), F32)
            for i in range(BIG // TILE):
                rows = slice(i * TILE, (i + 1) * TILE)
                s = dot_nt(q[rows], k) + masked_bias(i, band[h], rel[h : h + 1], masks[i // 2])
                p = jnp.exp(s - lse_ref[c, rows, h : h + 1])
                dp = dot_nt(go[rows], v)
                inner = jnp.sum(p * dp, axis=1, keepdims=True)
                gs = (p * (dp - inner)).astype(BF)
                gs_all[h, rows, :] = gs
                pb_all[h, rows, :] = p.astype(BF)
                wide = gs.astype(F32)
                for j in range(BIG // TILE):
                    tile = wide[:, j * TILE : (j + 1) * TILE]
                    if abs(j - i) <= 1:
                        acc[h, :, (j - i + 2) * TILE : (j - i + 3) * TILE] += tile
                    elif j > i:
                        high = high + jnp.sum(tile, axis=0, keepdims=True)
                    else:
                        low = low + jnp.sum(tile, axis=0, keepdims=True)
            at = lambda j: slice(j * width + h * HEAD, j * width + (h + 1) * HEAD)
            gq_all[c, :, at(1)] = dot_nn(gs_all[h], k).astype(BF)
            gq_all[c, :, at(2)] = dot_tn(gs_all[h], q).astype(BF)
            gq_all[c, :, at(3)] = dot_tn(pb_all[h], go).astype(BF)
            far.append((low, high))
        wait(got_late)
        if c == 0:
            wait(got_n1)
        grads_mat[c] = dot_tn(gq_all[c], n1_ref[...]).astype(BF)
        grads_mat[c, :width, :] = dot_tn(o_ref[c], gh).astype(BF)
        size = pl.ds(0, grads_mat.shape[1] // 2)
        move.halves(side_ref, grads_mat.at[c], send_out.at[c, size], keep_out.at[c, size])
        near = acc[...]
        n = TILE // 2
        while n >= 8:
            near = near[:, :n] + pltpu.roll(near[:, n:], SPAN - n, 2)
            n //= 2
        line = near[:, 0:1]
        for j in range(1, 8):
            line = line + pltpu.roll(near[:, j : j + 1], SPAN - j, 2)
        lines = []
        for h, (low, high) in enumerate(far):
            ends = jnp.where(lane == 0, jnp.sum(low, axis=1, keepdims=True), 0.0)
            ends = ends + jnp.where(lane == SPAN - 1, jnp.sum(high, axis=1, keepdims=True), 0.0)
            lines.append(line[h] + ends)
        lines = jnp.concatenate(lines + [jnp.zeros((8 - heads, SPAN), F32)], axis=0)
        tabs_ref[c] = lax.dot_general(
            lines, hot_ref[...].astype(F32), (((1,), (1,)), ((), ())),
            precision=lax.Precision.HIGHEST, preferred_element_type=F32,
        )
        if c == 0:
            wait(got_prior)
        for part in range(2):
            rows = pl.ds(part * half, half)
            gn = dot_nn(gq_all[c, rows, :], mat[c])
            if not (first and c == 0):
                gn = gn + gn_ref[rows, :]
            gn_ref[rows, :] = gn
            if c == count - 1 and not last:
                move.store(gn_ref.at[rows], gn_out.at[rows])
    if not last:
        move.store(tabs_ref, tabs_out)
        move.finish()
        return
    unit, root = rms(x_ref[...].astype(F32))
    back, gain_grad = rms_back(gn_ref[...], unit, root, gain_ref[...].astype(F32))
    small[...] = jnp.zeros_like(small)
    total = before_ref.shape[0] + count
    tables = [tabs_ref[count - 1]] + [before_ref[j] for j in range(total - count)]
    tables += [tabs_ref[c] for c in range(count - 1)]
    for row, value in enumerate(tables):
        for h in range(heads):
            small[row : row + 1, h * TILE : (h + 1) * TILE] = value[h : h + 1]
    small[total : total + 1, :] = gain_grad
    small[total + 1 : total + 2, :] = gain2_ref[0:1, :]
    packed[...] = split_small(small[...])
    tail = pl.ds(grads_mat.shape[1] // 2, EXTRA)
    for c in range(count):
        move.store(packed, send_out.at[c, tail])
        move.store(packed, keep_out.at[c, tail])
    gh_ref[...] = (ghid_ref[...] + back).astype(BF)
    move.store(gh_ref, gin_out)
    move.finish()


def split_small(value):
    high = value.astype(BF)
    low = (value - high.astype(F32)).astype(BF)
    return jnp.concatenate([high.astype(F32), low.astype(F32)], axis=0).astype(BF)


def join_small(packed):
    wide = packed.astype(F32)
    return wide[: EXTRA // 2] + wide[EXTRA // 2 :]


def attn_bwd(meta, index, side, n1, gh, hot, shards, rest, own, prior, final, slots, heads):
    last, first = None in shards, prior is None
    count = len(shards)
    rows, depth = n1.shape
    width = heads * HEAD
    cols = 4 * width
    parts, tab, sources = rest
    sources = [(places, kept) for places, kept in sources if set(places) & set(shards)]
    args = [n1, gh, hot, *parts, tab] + [k for _, kept in sources for k in kept]
    args += [*own[0], *own[1]] if last else []
    args += ([] if first else [prior]) + (list(final) if last else [])
    befores = len(final) - 4 if last else 0
    half = like((count, cols // 2 + (EXTRA if last else 0), depth), BF)
    if last:
        out_shape = [half, half, like((rows, depth), BF)]
    else:
        out_shape = [half, half, like((rows, depth), F32), like((count, 8, TILE), F32)]
    scratch = [
        pltpu.VMEM((rows, depth), BF),
        pltpu.VMEM((rows, depth), BF),
        pltpu.VMEM(hot.shape, BF),
        pltpu.VMEM((count, cols, depth), BF),
        pltpu.VMEM((count, rows, cols), BF),
        pltpu.VMEM((count, rows, width), BF),
        pltpu.VMEM((count, rows, TILE), F32),
        pltpu.VMEM((count,) + tab.shape[1:], BF),
        pltpu.VMEM((rows, depth), F32),
        pltpu.VMEM((heads, TILE, SPAN), F32),
        pltpu.VMEM((heads, TILE, SPAN), F32),
        pltpu.VMEM((heads, BIG, BIG), BF),
        pltpu.VMEM((heads, BIG, BIG), BF),
        pltpu.VMEM((count, rows, cols), BF),
        pltpu.VMEM((count, cols, depth), BF),
        pltpu.VMEM((count, 8, TILE), F32),
        pltpu.SemaphoreType.DMA((16 + 18 * count,)),
    ]
    if last:
        scratch += [
            pltpu.VMEM((rows, depth), BF),
            pltpu.VMEM((1, depth), BF),
            pltpu.VMEM((rows, depth), F32),
            pltpu.VMEM((8, depth), F32),
            pltpu.VMEM((sum(f.shape[0] for f in final[4:]), 8, TILE), F32),
            pltpu.VMEM((8, depth), F32),
            pltpu.VMEM((EXTRA, depth), BF),
        ]
    return pl.pallas_call(
        functools.partial(
            attn_bwd_kernel, slots, heads, tuple(shards), len(parts), tuple(p for p, _ in sources),
            len(own[0]) if last else 0, first, befores,
        ),
        in_specs=[SMEM] * 3 + [ANY] * len(args),
        out_specs=[HBM] * len(out_shape),
        out_shape=out_shape,
        scratch_shapes=scratch,
        compiler_params=params(LIMIT),
        cost_estimate=cost(32 * count),
        name="attn_bwd",
    )(meta, side, index, *args)


def ffn_kernel(parts, first, last, side_ref, *refs):
    refs = list(refs)
    take = lambda n: [refs.pop(0) for _ in range(n)]
    count = len(parts)
    index_refs = take(sum(1 for n in parts if n))
    n2_hbm, cot_hbm = take(2)
    f_parts = [take(n or 2) for n in parts]
    out_in, gn_in = (None, None) if first else take(2)
    if last:
        hid_in, gain_in = take(2)
        out_out, send_out, keep_out, ghid_out, gh_out, gg_out = take(6)
    else:
        out_out, gn_out, send_out, keep_out = take(4)
    n2_ref, cot_ref, i_mat, w_mat, act_ref, gp_ref, gi_mat, gw_mat, out_ref, gn_ref, sems = take(11)
    move = Mover(sems)
    hid_ref, gain_ref, y_ref, gg_ref = take(4) if last else [None] * 4

    def load(c):
        if not parts[c]:
            return move.load(f_parts[c][0], i_mat.at[c]), move.load(f_parts[c][1], w_mat.at[c])
        index_ref = index_refs[sum(1 for n in parts[:c] if n)]
        return tuple(move.blocks(index_ref, f_parts[c], mat.at[c], j) for j, mat in enumerate((i_mat, w_mat)))

    got_n2 = move.load(n2_hbm, n2_ref)
    got = [load(0)]
    got_cot = move.load(cot_hbm, cot_ref)
    c0 = 0.7978845608028654
    c1 = 0.044715
    size = n2_ref.shape[0] // 2
    gain_grad = None
    for c in range(count):
        wait(got[c][0])
        if c == 0:
            wait(got_n2)
            got += [load(t) for t in range(1, count)]
            got_sums = [] if first else move.load(out_in, out_ref) + move.load(gn_in, gn_ref)
            if last:
                got_sums += move.load(hid_in, hid_ref) + move.load(gain_in, gain_ref)
        pre = dot_nn(n2_ref[...], i_mat[c])
        square = pre * pre
        th = jnp.tanh(pre * (c0 + (c0 * c1) * square))
        half = 0.5 * (1.0 + th)
        act_ref[c] = (pre * half).astype(BF)
        slope = half + (0.5 * pre) * (1.0 - th * th) * (c0 + (3.0 * c0 * c1) * square)
        wait(got[c][1])
        if c == 0:
            wait(got_cot)
        cot = cot_ref[...]
        gp_ref[c] = (dot_nt(cot, w_mat[c]) * slope).astype(BF)
        gw_mat[c] = dot_tn(act_ref[c], cot).astype(BF)
        move.halves(side_ref, gw_mat.at[c], send_out.at[2 * c + 1], keep_out.at[2 * c + 1])
        gi_mat[c] = dot_tn(n2_ref[...], gp_ref[c]).astype(BF)
        move.halves(side_ref, gi_mat.at[c], send_out.at[2 * c], keep_out.at[2 * c])
        if c == 0:
            wait(got_sums)
        ending = c == count - 1
        for part in range(2):
            rows = pl.ds(part * size, size)
            gn = dot_nt(gp_ref[c, rows, :], i_mat[c])
            out = dot_nn(act_ref[c, rows, :], w_mat[c])
            if not (first and c == 0):
                out = out + out_ref[rows, :]
                gn = gn + gn_ref[rows, :]
            if not (last and ending):
                gn_ref[rows, :] = gn
                out_ref[rows, :] = out
                if ending:
                    move.store(gn_ref.at[rows], gn_out.at[rows])
                    move.store(out_ref.at[rows], out_out.at[rows])
                continue
            hidden = hid_ref[rows, :]
            y_ref[rows, :] = (hidden + out).astype(BF)
            move.store(y_ref.at[rows], out_out.at[rows])
            unit, root = rms(hidden)
            back, gain_part = rms_back(gn, unit, root, gain_ref[...].astype(F32))
            gain_grad = gain_part if gain_grad is None else gain_grad + gain_part
            grad_hidden = cot_ref[rows, :].astype(F32) + back
            gn_ref[rows, :] = grad_hidden
            move.store(gn_ref.at[rows], ghid_out.at[rows])
            n2_ref[rows, :] = grad_hidden.astype(BF)
            move.store(n2_ref.at[rows], gh_out.at[rows])
    if last:
        gg_ref[...] = jnp.broadcast_to(gain_grad, gg_ref.shape)
        move.store(gg_ref, gg_out)
    move.finish()


def ffn(side, n2, cot, shards, sums, final):
    first, last = sums is None, final is not None
    rows, depth = n2.shape
    count = len(shards)
    units = shards[-1][1][0].shape[-1]
    half = like((2 * count, depth // 2, units), BF)
    total = like((rows, depth), F32)
    scalars = [side] + [index for index, _ in shards if index is not None]
    args = [n2, cot] + [p for _, ps in shards for p in ps]
    args += ([] if first else list(sums)) + ([] if not last else list(final))
    if last:
        out_shape = [like((rows, depth), BF), half, half, total, like((rows, depth), BF), like((8, depth), F32)]
    else:
        out_shape = [total, total, half, half]
    scratch = [
        pltpu.VMEM((rows, depth), BF),
        pltpu.VMEM((rows, depth), BF),
        pltpu.VMEM((count, depth, units), BF),
        pltpu.VMEM((count, units, depth), BF),
        pltpu.VMEM((count, rows, units), BF),
        pltpu.VMEM((count, rows, units), BF),
        pltpu.VMEM((count, depth, units), BF),
        pltpu.VMEM((count, units, depth), BF),
        pltpu.VMEM((rows, depth), F32),
        pltpu.VMEM((rows, depth), F32),
        pltpu.SemaphoreType.DMA((20 + 20 * count,)),
    ]
    if last:
        scratch += [
            pltpu.VMEM((rows, depth), F32),
            pltpu.VMEM((1, depth), BF),
            pltpu.VMEM((rows, depth), BF),
            pltpu.VMEM((8, depth), F32),
        ]
    return pl.pallas_call(
        functools.partial(ffn_kernel, tuple(0 if i is None else len(p) for i, p in shards), first, last),
        in_specs=[SMEM] * len(scalars) + [ANY] * len(args),
        out_specs=[HBM] * len(out_shape),
        out_shape=out_shape,
        scratch_shapes=scratch,
        compiler_params=params(LIMIT),
        cost_estimate=cost(32 * count),
        name="ffn",
    )(*scalars, *args)


def prep_kernel(rows, count, index_ref, *refs):
    mats, (tab_ref, in_ref, down_ref, a_ref, f_ref, sems) = refs[:count], refs[count:]
    block = index_ref[0]
    first = pl.ds(pl.multiple_of(block * rows, rows), rows)
    copies = [
        pltpu.make_async_copy(in_ref.at[first], f_ref.at[0], sems.at[0]),
        pltpu.make_async_copy(down_ref.at[first], f_ref.at[1], sems.at[1]),
    ]
    per = mats[0].shape[0] // rows

    def piece(j, mat):
        at = pl.ds(pl.multiple_of((block - j * per) * rows, rows), rows)
        return pltpu.make_async_copy(mat.at[at], a_ref.at[pl.ds(0, rows)], sems.at[2])

    for j, mat in enumerate(mats):
        @pl.when(block // per == j)
        def _():
            piece(j, mat).start()

    for copy in copies:
        copy.start()
    a_ref[rows:, :] = jnp.zeros((EXTRA, a_ref.shape[1]), BF)
    a_ref[rows:, :TILE] = tab_ref[...]
    for j, mat in enumerate(mats):
        @pl.when(block // per == j)
        def _():
            piece(j, mat).wait()

    for copy in copies:
        copy.wait()


def prep(index, mats, tab, w_in, w_down, rows):
    depth = w_in.shape[0]
    return pl.pallas_call(
        functools.partial(prep_kernel, rows, len(mats)),
        in_specs=[SMEM] + [ANY] * len(mats) + [VMEM, ANY, ANY],
        out_specs=[VMEM, VMEM],
        out_shape=[like((rows + EXTRA, depth), BF), like((2, rows, depth), BF)],
        scratch_shapes=[pltpu.SemaphoreType.DMA((3,))],
        compiler_params=params(60),
        cost_estimate=cost(1),
        name="prep",
    )(index, *mats, tab, w_in, w_down)


def join_kernel(count, *refs):
    parts, (a_ref, tab_ref) = refs[:count], refs[count:]
    rows = a_ref.shape[1]
    for j, part in enumerate(parts):
        a_ref[j] = part[:rows, :]
        tab_ref[j] = part[rows:, :TILE]


def join(parts):
    rows, depth = parts[0].shape
    return pl.pallas_call(
        functools.partial(join_kernel, len(parts)),
        in_specs=[VMEM] * len(parts),
        out_specs=[VMEM, VMEM],
        out_shape=[like((len(parts), rows - EXTRA, depth), BF), like((len(parts), EXTRA, TILE), BF)],
        compiler_params=params(16),
        cost_estimate=cost(1),
        name="join",
    )(*parts)


def row_runs(left, bit, rows):
    inner = rows
    for b in left[left.index(bit) + 1 :]:
        inner *= 2
    outer = 1
    for b in left[: left.index(bit)]:
        outer *= 2
    return [(o * 2 * inner, inner, o * inner) for o in range(outer)]


def fold_kernel(runs, extra, joined, sides_ref, *refs):
    if joined:
        keep_ref, recv_ref = refs[:2]
        n = keep_ref.shape[0] // 2
        ins = [(keep_ref.at[pl.ds(g * n, n)], recv_ref.at[pl.ds(g * n, n)]) for g in range(2)]
        outs = refs[2:]
    else:
        ins, outs = [refs[0:2], refs[2:4]], refs[4:]
    packed = None
    if extra:
        keep, recv = ins[1]
        tail = pl.ds(keep.shape[1] - extra, extra)
        packed = split_small(join_small(keep[0, tail, :]) + join_small(recv[0, tail, :]))
    for g, (keep, recv) in enumerate(ins):
        def total(rows):
            return (keep[:, rows, :].astype(F32) + recv[:, rows, :].astype(F32)).astype(BF)

        if runs is None:
            rows, n = outs[0].shape[1], outs[0].shape[0] // 2
            outs[0][g * n : (g + 1) * n] = total(pl.ds(0, rows))
            continue
        bit, group_runs = runs[g]
        mine = sides_ref[bit]
        for ref, side in ((outs[2 * g], 1 - mine), (outs[2 * g + 1], mine)):
            for source, length, target in group_runs:
                ref[:, target : target + length, :] = total(pl.ds(pl.multiple_of(source + side * length, length), length))
            if extra and g == 1:
                done = sum(length for _, length, _ in group_runs)
                for m in range(ref.shape[0]):
                    ref[m, done:, :] = packed
    if extra and runs is None:
        outs[1][...] = packed


def fold(sides, groups, runs, extra):
    joined = len(groups) == 1
    arrays = [a for group in groups for a in group]
    if joined:
        count = arrays[0].shape[0] // 2
        bodies = [arrays[0].shape[1] - extra] * 2
    else:
        count = arrays[0].shape[0]
        bodies = [arrays[0].shape[1], arrays[2].shape[1] - extra]
    cols = arrays[0].shape[2]
    if runs is None:
        out_shape = [like((2 * count, bodies[0], cols), BF)] + ([like((extra, cols), BF)] if extra else [])
    else:
        tails = (0, extra)
        out_shape = [like((count, bodies[g] // 2 + tails[g], cols), BF) for g in (0, 0, 1, 1)]
    return pl.pallas_call(
        functools.partial(fold_kernel, runs, extra, joined),
        in_specs=[SMEM] + [VMEM] * len(arrays),
        out_specs=[VMEM] * len(out_shape),
        out_shape=out_shape,
        compiler_params=params(24),
        cost_estimate=cost(1),
        name="fold",
    )(sides, *arrays)


def add_kernel(a_ref, b_ref, out_ref):
    out_ref[...] = (a_ref[...].astype(F32) + b_ref[...].astype(F32)).astype(BF)


def add(a, b):
    return pl.pallas_call(
        add_kernel, in_specs=[VMEM, VMEM], out_specs=VMEM, out_shape=like(a.shape, BF),
        compiler_params=params(16), cost_estimate=cost(1), name="add",
    )(a, b)


def add_small_kernel(a_ref, b_ref, out_ref):
    out_ref[...] = split_small(join_small(a_ref[...]) + join_small(b_ref[...]))


def add_small(a, b):
    return pl.pallas_call(
        add_small_kernel, in_specs=[VMEM, VMEM], out_specs=VMEM, out_shape=like(a.shape, BF),
        compiler_params=params(16), cost_estimate=cost(1), name="add_small",
    )(a, b)


def total_kernel(count, *refs):
    parts, out_ref = refs[:count], refs[count]
    total = parts[0][...].astype(F32)
    for part in parts[1:]:
        total = total + part[...].astype(F32)
    out_ref[...] = total.astype(BF)


def total_of(parts):
    return pl.pallas_call(
        functools.partial(total_kernel, len(parts)),
        in_specs=[VMEM] * len(parts),
        out_specs=VMEM,
        out_shape=like(parts[0].shape, BF),
        compiler_params=params(16),
        cost_estimate=cost(1),
        name="total",
    )(*parts)


def small_kernel(count, *refs):
    parts, (tab_ref, gains_ref) = refs[:count], refs[count:]
    table, gains = None, None
    for j, part in enumerate(parts):
        wide = join_small(part[...])
        table = wide[j : j + 1] if table is None else table + wide[j : j + 1]
        gains = wide if gains is None else gains + wide
    tab_ref[...] = jnp.broadcast_to(table, tab_ref.shape)
    gains_ref[...] = gains


def small_of(parts):
    depth = parts[0].shape[1]
    shape = like((EXTRA // 2, depth), F32)
    return pl.pallas_call(
        functools.partial(small_kernel, len(parts)),
        in_specs=[VMEM] * len(parts),
        out_specs=[VMEM, VMEM],
        out_shape=[shape, shape],
        compiler_params=params(16),
        cost_estimate=cost(1),
        name="small",
    )(*parts)


def cat_kernel(count, *refs):
    for j in range(count):
        refs[count][j] = refs[j][...]


def cat(parts):
    return pl.pallas_call(
        functools.partial(cat_kernel, len(parts)),
        in_specs=[VMEM] * len(parts),
        out_specs=VMEM,
        out_shape=like((len(parts),) + parts[0].shape, BF),
        compiler_params=params(16),
        cost_estimate=cost(1),
        name="cat",
    )(*parts)


def finish_kernel(count, split, index_ref, *refs):
    parts, out_refs, mat = refs[:count], refs[count:-1], refs[-1]
    for j in range(parts[0].shape[1]):
        if split:
            put_blocks(index_ref, parts, mat, j)
            rows = mat.shape[0] // len(out_refs)
            for i, ref in enumerate(out_refs):
                ref[...] = mat[i * rows : (i + 1) * rows, :].astype(F32)
        else:
            put_blocks(index_ref, parts, out_refs[j], j)


def finish(index, parts, outs, rows):
    depth = parts[0].shape[-1]
    split = parts[0].shape[1] != outs
    return pl.pallas_call(
        functools.partial(finish_kernel, len(parts), split),
        in_specs=[SMEM] + [VMEM] * len(parts),
        out_specs=[VMEM] * outs,
        out_shape=[like((rows, depth), F32)] * outs,
        scratch_shapes=[pltpu.VMEM((depth, depth), BF)],
        compiler_params=params(24),
        cost_estimate=cost(2),
        name="finish",
    )(index, *parts)


def bar(*values):
    return list(lax.optimization_barrier(values))


def after(x, *deps):
    return lax.optimization_barrier((x,) + deps)[0]


class Ring:
    def __init__(self, n_dp, n_mp, depth):
        self.n_dp, self.n_mp = n_dp, n_mp
        self.all_bits = (n_dp - 1).bit_length()
        self.bits = min(3, self.all_bits)
        self.z = lax.axis_index("mp")
        self.blocks = 1 << self.bits
        self.rows = depth // self.blocks
        self.low = lax.axis_index("dp") & (self.blocks - 1)
        self.sides = [((self.low >> bit) & 1)[None].astype(jnp.int32) for bit in range(self.bits)]
        self.all_sides = jnp.concatenate(self.sides)
        self.mine = self.row_block(self.low)[None].astype(jnp.int32)
        self.orders = {flip: self.order(flip) for flip in (False, True)}
        self.index = {flip: self.block_index(flip) for flip in (False, True)}

    def row_block(self, low):
        return ((low & 1) << (self.bits - 1)) | (low >> 1)

    def order(self, flip):
        high = list(range(1, self.bits))
        return (high[::-1] if flip else high) + [0]

    def block_index(self, flip):
        masks = [0]
        for bit in self.orders[flip]:
            masks = masks + [m | (1 << bit) for m in masks]
        low = self.low ^ jnp.asarray(masks, jnp.int32)
        return self.row_block(low).astype(jnp.int32)

    def swap(self, x, mask):
        return lax.ppermute(x, "dp", [(i, i ^ mask) for i in range(self.n_dp)])

    def pull(self, x, shift):
        return lax.ppermute(x, "mp", [(i, (i - shift) % self.n_mp) for i in range(self.n_mp)])

    def push(self, x, shift):
        return lax.ppermute(x, "mp", [(i, (i + shift) % self.n_mp) for i in range(self.n_mp)])

    def gather_all(self, piece):
        groups = [[g + i for i in range(self.blocks)] for g in range(0, self.n_dp, self.blocks)]
        return lax.all_gather(piece, "dp", axis_index_groups=groups)

    def group_index(self):
        return jnp.asarray([self.row_block(low) for low in range(self.blocks)], jnp.int32)


class Reduce:
    def __init__(self, ring, send, keep, extra=0):
        self.ring, self.extra = ring, extra
        order = list(range(1, ring.bits))
        self.orders = [order, order[::-1]]
        self.left = [order[::-1], order[::-1]]
        self.groups = [[keep, ring.swap(send, 1)]]
        self.done = False

    def received(self):
        return [group[1] for group in self.groups]

    def set_received(self, values):
        for group, value in zip(self.groups, values):
            group[1] = value

    def step(self):
        ring = self.ring
        if not self.orders[0]:
            out = fold(ring.all_sides, self.groups, None, self.extra)
            self.out, self.small = out[0], out[1] if self.extra else None
            for bit in range(ring.bits, ring.all_bits):
                self.out = add(self.out, ring.swap(self.out, 1 << bit))
                if self.extra:
                    self.small = add_small(self.small, ring.swap(self.small, 1 << bit))
            self.done = True
            return [self.out]
        runs, bits = [], []
        for g in range(2):
            bit = self.orders[g].pop(0)
            runs.append((bit, row_runs(self.left[g], bit, ring.rows)))
            self.left[g] = [b for b in self.left[g] if b != bit]
            bits.append(bit)
        outs = fold(ring.all_sides, self.groups, runs, self.extra)
        self.groups = [[outs[2 * g + 1], ring.swap(outs[2 * g], 1 << bits[g])] for g in range(2)]
        return [outs[1], outs[3]]


def body(
    n_dp, n_mp, inputs, gain_attn, w_query, w_key, w_value, w_out, rel_table, gain_ffn, w_in, w_down,
    cotangent, bucket, lengths,
):
    rows, depth = inputs.shape
    buckets, heads = rel_table.shape
    width = heads * HEAD
    slots = lengths.shape[1]
    ring = Ring(n_dp, n_mp, depth)
    side = ring.sides[0]
    shifts = list(range(1, n_mp))
    meta = jnp.concatenate([bucket, (ring.z * BIG)[None].astype(jnp.int32), lengths[0]])
    hot = jnp.asarray(offset_one_hot(buckets), BF)
    gain_one, gain_two = gain_attn[None], gain_ffn[None]

    a_own = [w_out, w_query.T, w_key.T, w_value.T]
    tab_own = jnp.pad(rel_table.T, ((0, EXTRA - heads), (0, TILE - buckets)))
    a_piece, f_piece = prep(ring.mine, a_own, tab_own, w_in, w_down, ring.rows)
    tab_own = tab_own[None]
    v = {}

    def close(*keys):
        v.update(zip(keys, bar(*[v[key] for key in keys])))

    def swap(new, old, mask):
        v[new] = ring.swap(v[old], mask)

    shift_order = [s for s in shifts if s != n_mp // 2] + [n_mp // 2]
    f1, f3, f2 = shift_order
    v["piece"] = f_piece
    for s in shifts:
        v["z", s] = ring.pull(a_piece, s)
    x_value = inputs.astype(F32)
    n1 = (rms(x_value)[0] * gain_attn.astype(F32)).astype(BF)
    *kept_own, v["hidden"] = attn_fwd(meta, None, n1, a_own, 0, 1, tab_own, hot, inputs, None, slots, heads)
    close(*[("z", s) for s in shifts], "hidden")
    v["a"], tab_rest = join([v["z", s] for s in shifts])
    close("a", "piece")
    swap("ax", "a", 2)
    swap("ay", "a", 4)
    v["f", f1] = ring.pull(v["piece"], f1)
    v["f", f3] = ring.pull(v["piece"], f3)
    close("ax", "ay", "a", ("f", f1), "piece")
    swap("ayx", "ax", 4)
    v["a3"] = cat([v["a"], v["ax"], v["ay"]])
    swap("a3c", "a3", 1)
    swap(("fx", f1), ("f", f1), 2)
    v["f", f2] = ring.pull(v["piece"], f2)
    close("ayx", "a3c", ("fx", f1), ("f", f3))
    v["a1"] = v["ayx"][None]
    swap("a1c", "a1", 1)
    v["cat", f1] = cat([v["f", f1], v["fx", f1]])
    swap(("far", f1), ("cat", f1), 4)
    swap(("fy", f3), ("f", f3), 4)
    close("a1c", "hidden")
    a_parts = [v["a3"], v["a1"], v["a3c"], v["a1c"]]
    a_index = ring.index[False]
    cut = n_mp - 2
    *kept_one, v["hidden"] = attn_fwd(
        meta, a_index, n1, a_parts, 0, cut, tab_rest, hot, v["hidden"], None, slots, heads
    )
    close("hidden", ("f", f2))
    swap(("fx", f2), ("f", f2), 2)
    *kept_two, v["hidden"], v["n2"] = attn_fwd(
        meta, a_index, n1, a_parts, cut, 1, tab_rest, hot, v["hidden"], gain_two, slots, heads
    )
    close("hidden", "n2", ("far", f1), ("fy", f3), ("fx", f2))

    def cores(s):
        swap(("catc", s), ("cat", s), 1)
        swap(("farc", s), ("far", s), 1)

    def parts_of(s):
        return ring.index[s == f3], [v["cat", s], v["far", s], v["catc", s], v["farc", s]]

    cores(f1)
    v["cat", f3] = cat([v["f", f3], v["fy", f3]])
    swap(("far", f3), ("cat", f3), 2)
    v["cat", f2] = cat([v["f", f2], v["fx", f2]])
    swap(("far", f2), ("cat", f2), 4)
    close("n2", ("catc", f1), ("farc", f1))
    v["out"], v["gn"], v["send"], v["keep"] = ffn(
        side, v["n2"], cotangent, [(None, [w_in, w_down]), parts_of(f1)], None, None
    )
    close("out", "gn", "n2", "send", "keep", ("far", f3), ("far", f2))
    red = {}

    def reduce(name, extra=0):
        red[name] = Reduce(ring, v["send"], v["keep"], extra)

    def close_with(names, *keys):
        groups = [group for name in names for group in red[name].groups]
        values = bar(*[group[1] for group in groups], *[v[key] for key in keys])
        for group, value in zip(groups, values):
            group[1] = value
        v.update(zip(keys, values[len(groups) :]))

    def folded(names, *keys):
        outs = [out for name in names for out in red[name].step()]
        v.update(zip(keys, bar(*[v[key] for key in keys], *outs)))

    cores(f3)
    cores(f2)
    reduce("a")
    close_with(["a"], "n2", "out", "gn", ("catc", f3), ("farc", f3), ("catc", f2), ("farc", f2))
    folded(["a"], "n2", "out", "gn")
    outputs, v["send"], v["keep"], grad_hidden, v["gh"], gg = ffn(
        side, v["n2"], cotangent, [parts_of(f3), parts_of(f2)], (v["out"], v["gn"]), (v["hidden"], gain_two)
    )
    close_with(["a"], "send", "keep", "gh")
    folded(["a"], "gh")
    reduce("b")

    places = [(tuple(range(cut)), kept_one), ((cut,), kept_two)]
    rest = (a_parts, tab_rest, places)
    own = (a_own, [*kept_own, tab_own])
    v["send"], v["keep"], v["gn"], tabs = attn_bwd(
        meta, a_index, side, n1, v["gh"], hot, list(range(cut)), rest, None, None, None, slots, heads
    )
    close_with(["a", "b"], "send", "keep", "gh", "gn")
    reduce("c")
    folded(["b", "a"], "gh", "gn")
    v["f1"] = ring.push(red["a"].out[2:], f1)
    close_with(["c"], "gh", "gn")
    folded(["c"], "gh", "gn")
    final = (inputs, gain_one, grad_hidden, gg, tabs)
    v["send"], v["keep"], v["gin"] = attn_bwd(
        meta, a_index, side, n1, v["gh"], hot, [cut, None], rest, own, v["gn"], final, slots, heads
    )
    close_with(["b", "c"], "send", "keep", "gin", "f1")
    grad_inputs = v["gin"]
    reduce("d", EXTRA)
    folded(["b", "c"], "gin")
    close_with(["d"], "gin")
    folded(["d"], "gin")
    close_with(["b", "c"], "gin")
    folded(["b", "c"], "gin")
    v["f3"] = ring.push(red["b"].out[:2], f3)
    v["f2"] = ring.push(red["b"].out[2:], f2)
    v["a1"], v["a2"] = ring.push(red["c"].out[:1], 1), ring.push(red["c"].out[1:], 2)
    close_with(["d"], "gin")
    folded(["d"], "gin")
    close("f3", "f2", "gin")

    def spread(name, piece):
        v[name, 0] = piece
        for mask in (2, 4, 6):
            v[name, mask] = ring.swap(piece, mask)

    def gathered(name):
        v[name] = cat([v[name, mask] for mask in (0, 2, 4, 6)])
        v[name, 1] = ring.swap(v[name], 1)

    spread("f", total_of([red["a"].out[:2], v["f1"], v["f3"], v["f2"]]))
    close_with(["d"], "gin")
    folded(["d"], "gin")
    v["a3"] = ring.push(red["d"].out[:1], 3)
    small = red["d"].small
    smalls = [ring.push(small, s) for s in shifts]
    close("a1", "a2", "a3", ("f", 2), ("f", 4), ("f", 6))
    spread("a", total_of([red["d"].out[1:], v["a1"], v["a2"], v["a3"]]))
    gathered("f")
    close(("f", 1), ("a", 2), ("a", 4), ("a", 6))
    gathered("a")
    v["f_done"] = finish(a_index, [v["f"], v["f", 1]], 2, depth)
    grad_in, grad_down = v["f_done"]
    grads = finish(a_index, [v["a"], v["a", 1]], 4, width)
    grad_out, grad_query, grad_key, grad_value = grads[0], grads[1].T, grads[2].T, grads[3].T

    table, gains = small_of([small] + smalls)
    grad_table = table[0, : heads * TILE].reshape(heads, TILE)[:, :buckets].T
    return (
        outputs, grad_inputs, grad_query, grad_key, grad_value, grad_out, grad_table,
        gains[n_mp], gains[n_mp + 1], grad_in, grad_down,
    )


def solution(mesh):
    placed = (
        P(("dp", "mp"), None), P(), P(None, "mp"), P(None, "mp"), P(None, "mp"), P("mp", None),
        P(None, "mp"), P(), P(None, "mp"), P("mp", None), P(("dp", "mp"), None), P("dp"), P("dp", None),
    )
    return jax.shard_map(
        functools.partial(body, mesh.shape["dp"], mesh.shape["mp"]),
        mesh=mesh,
        in_specs=placed,
        out_specs=(
            P(("dp", "mp"), None), P(("dp", "mp"), None), P(None, "mp"), P(None, "mp"), P(None, "mp"),
            P("mp", None), P(None, "mp"), P(), P(), P(None, "mp"), P("mp", None),
        ),
        check_vma=False,
    )
```

time: 348 us -> 262 us (0.75); the launches traced: 347 us -> 257 us
  waiting for transfers between devices: 115 us -> 75.4 us
  starting transfers between devices: 79.8 us -> 54.8 us
  other arithmetic: 23.8 us -> 2.66 us
  Pallas kernels: 89.5 us -> 107 us
  between operations: 16 us -> 2.34 us
  local copies, waits for them, and re-layouts: 21.1 us -> 15.2 us
    ppermute x56 -> x45, waiting for transfers between devices: 72.1 us -> 30.3 us  [swap(): return lax.ppermute(x, 'dp', [(i, i ^ mask) for i in range(self.n_dp)])]
    ppermute x9 -> x6, starting transfers between devices: 34 us -> 9.74 us  [pull(): lax.ppermute(x, 'mp', [(i, (i - shift) % self.n_mp) for i in range(self.n...]
    pallas_call x25 -> x29, Pallas kernels: 64.6 us -> 81.9 us  [the longest x2 32.9 us: attn_bwd(): pl.pallas_call(functools.partial(attn_bwd_kernel, slots, heads, tuple(sha...]
    reduce_sum x4 -> x1, other arithmetic: 8.15 us -> 0.23 us  [rms(): root = lax.rsqrt(jnp.mean(values * values, axis=1, keepdims=True) + EPS)]
    convert_element_type x9 -> x2, other arithmetic: 8.07 us -> 1.16 us  [body(): n1 = (rms(x_value)[0] * gain_attn.astype(F32)).astype(BF)]
    unnamed x160 -> x70, local copies, waits for them, and re-layouts: 17.1 us -> 10.5 us
    another operation x2 -> x0, other arithmetic: 3.99 us -> none  [body(): f_own = jnp.stack([w_in, w_down])]
    ppermute x9 -> x6, waiting for transfers between devices: 19.6 us -> 22.6 us  [pull(): lax.ppermute(x, 'mp', [(i, (i - shift) % self.n_mp) for i in range(self.n...]
  transfers between devices with their start and end apart: 75 -> 60, of which waited for: 23 -> 25; matrix products, arithmetic and copies ran while one was open for 9% -> 2% of each run, Pallas kernels for 26% -> 38%
where the time goes in v3:
time: 262 us; the launch traced here: 257 us
  Pallas kernels  107 us (41%)
  waiting for transfers between devices  75.4 us (29%)
  starting transfers between devices  54.8 us (21%)
  local copies, waits for them, and re-layouts  15.2 us (6%)
  other arithmetic  2.66 us (1%)
    ppermute x45, starting transfers between devices, swap(): return lax.ppermute(x, 'dp', [(i, i ^ mask) for i in range(self.n_dp)])  33.6 us
    pallas_call x2, Pallas kernels, attn_bwd(): pl.pallas_call(functools.partial(attn_bwd_kernel, slots, heads, tuple(sha...  32.9 us
    ppermute x45, waiting for transfers between devices, swap(): return lax.ppermute(x, 'dp', [(i, i ^ mask) for i in range(self.n_dp)])  30.3 us
    pallas_call x2, Pallas kernels, ffn(): pl.pallas_call(functools.partial(ffn_kernel, tuple((0 if i is None else l...  27.9 us
    pallas_call x3, Pallas kernels, attn_fwd(): pl.pallas_call(functools.partial(attn_fwd_kernel, slots, heads, len(a_par...  25 us
    ppermute x6, waiting for transfers between devices, pull(): lax.ppermute(x, 'mp', [(i, (i - shift) % self.n_mp) for i in range(self.n...  22.6 us
    ppermute x9, waiting for transfers between devices, push(): lax.ppermute(x, 'mp', [(i, (i + shift) % self.n_mp) for i in range(self.n...  22.5 us
    pallas_call x12, Pallas kernels, fold(): pl.pallas_call(functools.partial(fold_kernel, runs, extra, joined), in_sp...  12.7 us
  transfers between devices with their start and end apart: 60, of which 25 were waited for; matrix products, arithmetic and copies ran while one was open for 2% of the time, Pallas kernels for 38%

profile of v3, /device:TPU:0, one launch (start us, length us, event | category | flops | bytes accessed | tf_op | source)
XLA Modules:
  0.0 257.3 jit_solution(14492141365068689511)
XLA Ops:
  0.6 1.3 pad_bitcast_fusion
  1.9 2.6 %prep.1 = (bf16[112,768]{1,0:T(8,128)(2,1)}, bf16[2,96,768]{2,1,0:T(8,128)(2,1)}) custom-call(s32[1]{0:T(128)} %bitcast.3.index_ref, bf16[192,768]{1,0:T(8,128)(2,1)} %refs_11_.1, bf16[192,768]{1,0:T(8,128)(2,1)} %bitcast.27, bf16[192,768]{1,0:T(8,128)(2,1)} %bitcast.30, bf16[192,768]{1,0:T(8,128)(2,1)} %bitcast.33, ...), custom_call_target="tpu_custom_call" | custom-call | flops 1000000000 | bytes 1000000 | tf_op jit(solution)/shard_map/prep/pallas_call | solution.py:677
  4.6 5.1 %collective-permute-start = (bf16[112,768]{1,0:T(8,128)(2,1)}, bf16[112,768]{1,0:T(8,128)(2,1)S(1)}, u32[]{:S(2)}, u32[]{:S(2)}) collective-permute-start(bf16[112,768]{1,0:T(8,128)(2,1)} %get-tuple-element.180), channel_id=1, source_target_pairs={{0,3},{1,0},{2,1},{3,2},{4,7},{5,4},{6,5},{7,6},{8,11},{9,8},{10,9... | collective-permute-start | bytes 516104 | tf_op jit(solution)/shard_map/ppermute | solution.py:932
  13.4 7.0 %attn_fwd.3 = (bf16[1,512,768]{2,1,0:T(8,128)(2,1)}, bf16[1,512,192]{2,1,0:T(8,128)(2,1)}, f32[1,512,128]{2,1,0:T(8,128)}, f32[512,768]{1,0:T(8,128)}) custom-call(s32[10]{0:T(128)} %pad_add_fusion.meta_ref, bf16[512,768]{1,0:T(8,128)(2,1)} %fusion.2.refs_0_.refs_1_, bf16[192,768]{1,0:T(8,128)(2,1)} %refs_11_.1, bf16[192,768]{1,0:T(8,128)(2,1)} %bitcast.28, ...), custom_call_target="tpu_custom_call" | custom-call | flops 16000000000 | bytes 16000000 | tf_op jit(solution)/shard_map/attn_fwd/pallas_call | solution.py:255
  20.4 4.1 %collective-permute-done.1.refs_1_ = bf16[112,768]{1,0:T(8,128)(2,1)S(1)} collective-permute-done((bf16[112,768]{1,0:T(8,128)(2,1)}, bf16[112,768]{1,0:T(8,128)(2,1)S(1)}, u32[]{:S(2)}, u32[]{:S(2)}) %collective-permute-start.1) | collective-permute-done | bytes 172064 | tf_op jit(solution)/shard_map/ppermute | solution.py:932
  25.1 1.5 collective-permute-start.3
  26.6 1.5 collective-permute-start.4
  29.0 7.4 %collective-permute-done.5.refs_0_ = bf16[2,96,768]{2,1,0:T(8,128)(2,1)S(1)} collective-permute-done((bf16[2,96,768]{2,1,0:T(8,128)(2,1)}, bf16[2,96,768]{2,1,0:T(8,128)(2,1)S(1)}, u32[]{:S(2)}, u32[]{:S(2)}) %collective-permute-start.5) | collective-permute-done | bytes 294944 | tf_op jit(solution)/shard_map/ppermute | solution.py:932
  36.9 1.2 collective-permute-done.4.refs_2_
  38.3 1.6 collective-permute-start.6
  41.1 10.0 %collective-permute-done.9.refs_0_ = bf16[2,96,768]{2,1,0:T(8,128)(2,1)S(1)} collective-permute-done((bf16[2,96,768]{2,1,0:T(8,128)(2,1)}, bf16[2,96,768]{2,1,0:T(8,128)(2,1)S(1)}, u32[]{:S(2)}, u32[]{:S(2)}) %collective-permute-start.9) | collective-permute-done | bytes 294944 | tf_op jit(solution)/shard_map/ppermute | solution.py:932
  52.6 2.0 collective-permute-start.11
  54.7 1.6 collective-permute-start.12
  57.5 10.5 %attn_fwd.4 = (bf16[2,512,768]{2,1,0:T(8,128)(2,1)}, bf16[2,512,192]{2,1,0:T(8,128)(2,1)}, f32[2,512,128]{2,1,0:T(8,128)}, f32[512,768]{1,0:T(8,128)}) custom-call(s32[10]{0:T(128)} %pad_add_fusion.meta_ref, s32[8]{0:T(128)} %get-tuple-element.362.refs_0_.refs_1_.index_ref, bf16[512,768]{1,0:T(8,128)(2,1)} %fusion.2.refs_0_.refs_1_, ...), custom_call_target="tpu_custom_call" | custom-call | flops 32000000000 | bytes 32000000 | tf_op jit(solution)/shard_map/attn_fwd/pallas_call | solution.py:255
  69.8 7.4 %attn_fwd.5 = (bf16[1,512,768]{2,1,0:T(8,128)(2,1)}, bf16[1,512,192]{2,1,0:T(8,128)(2,1)}, f32[1,512,128]{2,1,0:T(8,128)}, f32[512,768]{1,0:T(8,128)}, bf16[512,768]{1,0:T(8,128)(2,1)}) custom-call(s32[10]{0:T(128)} %pad_add_fusion.meta_ref, s32[8]{0:T(128)} %get-tuple-element.362.refs_0_.refs_1_.index_ref, bf16[512,768]{1,0:T(8,128)(2,1)} %fusion.2.refs_0_.refs_1_, ...), custom_call_target="tpu_custom_call" | custom-call | flops 16000000000 | bytes 16000000 | tf_op jit(solution)/shard_map/attn_fwd/pallas_call | solution.py:255
  78.2 1.3 collective-permute-start.18
  80.5 13.9 %ffn.2 = (f32[512,768]{1,0:T(8,128)}, f32[512,768]{1,0:T(8,128)}, bf16[4,384,768]{2,1,0:T(8,128)(2,1)}, bf16[4,384,768]{2,1,0:T(8,128)(2,1)}) custom-call(s32[1]{0:T(128)} %bitcast.side_ref, s32[8]{0:T(128)} %get-tuple-element.362.refs_0_.refs_1_.index_ref, bf16[512,768]{1,0:T(8,128)(2,1)} %get-tuple-element.231.refs_1_.refs_2_, bf16[512,768]{1,0:T(8,128)(2,1)} %refs_3_.3, ...), custom_call_target="tpu_custom_call" | custom-call | flops 64000000000 | bytes 64000000 | tf_op jit(solution)/shard_map/ffn/pallas_call | solution.py:631
  97.1 4.8 %collective-permute-done.22.refs_10_ = bf16[2,2,96,768]{3,2,1,0:T(8,128)(2,1)} collective-permute-done((bf16[2,2,96,768]{3,2,1,0:T(8,128)(2,1)S(1)}, bf16[2,2,96,768]{3,2,1,0:T(8,128)(2,1)}, u32[]{:S(2)}, u32[]{:S(2)}) %collective-permute-start.22) | collective-permute-done | bytes 589856 | tf_op jit(solution)/shard_map/ppermute | solution.py:929
  101.9 1.7 collective-permute-done.20.refs_6_
  104.0 1.7 copy-done.1
  105.7 2.0 fold.12
  109.2 14.0 %ffn.3 = (bf16[512,768]{1,0:T(8,128)(2,1)}, bf16[4,384,768]{2,1,0:T(8,128)(2,1)}, bf16[4,384,768]{2,1,0:T(8,128)(2,1)}, f32[512,768]{1,0:T(8,128)}, bf16[512,768]{1,0:T(8,128)(2,1)}, /*index=5*/f32[8,768]{1,0:T(8,128)}) custom-call(s32[1]{0:T(128)} %bitcast.side_ref, s32[8]{0:T(128)} %get-tuple-element.361.refs_0_, ...), custom_call_target="tpu_custom_call" | custom-call | flops 64000000000 | bytes 64000000 | tf_op jit(solution)/shard_map/ffn/pallas_call | solution.py:631
  123.6 1.6 fold.13
  127.4 1.4 collective-permute-start.27
  128.8 15.9 %attn_bwd.2 = (bf16[2,384,768]{2,1,0:T(8,128)(2,1)}, bf16[2,384,768]{2,1,0:T(8,128)(2,1)}, f32[512,768]{1,0:T(8,128)}, f32[2,8,128]{2,1,0:T(8,128)}) custom-call(s32[10]{0:T(128)} %pad_add_fusion.meta_ref, s32[1]{0:T(128)} %bitcast.side_ref, s32[8]{0:T(128)} %get-tuple-element.362.refs_0_.refs_1_.index_ref, bf16[512,768]{1,0:T(8,128)(2,1)} %fusion.2.refs_0_.refs_1_, ...), custom_call_target="tpu_custom_call" | custom-call | flops 64000000000 | bytes 64000000 | tf_op jit(solution)/shard_map/attn_bwd/pallas_call | solution.py:495
  147.1 2.0 fold.14
  150.6 1.2 collective-permute-start.30
  151.7 1.5 fold.16
  154.7 1.4 collective-permute-start.32
  156.9 17.0 %attn_bwd.3 = (bf16[2,400,768]{2,1,0:T(8,128)(2,1)}, bf16[2,400,768]{2,1,0:T(8,128)(2,1)}, bf16[512,768]{1,0:T(8,128)(2,1)}) custom-call(s32[10]{0:T(128)} %pad_add_fusion.meta_ref, s32[1]{0:T(128)} %bitcast.side_ref, s32[8]{0:T(128)} %get-tuple-element.362.refs_0_.refs_1_.index_ref, bf16[512,768]{1,0:T(8,128)(2,1)} %fusion.2.refs_0_.refs_1_, ...), custom_call_target="tpu_custom_call" | custom-call | flops 64000000000 | bytes 64000000 | tf_op jit(solution)/shard_map/attn_bwd/pallas_call | solution.py:495
  177.0 1.3 collective-permute-start.40
  180.6 1.4 collective-permute-start.43
  182.0 7.7 %collective-permute-done.42.refs_1_ = bf16[1,96,768]{2,1,0:T(8,128)(2,1)S(1)} collective-permute-done((bf16[1,96,768]{2,1,0:T(8,128)(2,1)S(1)}, bf16[1,96,768]{2,1,0:T(8,128)(2,1)S(1)}, u32[]{:S(2)}, u32[]{:S(2)}) %collective-permute-start.42) | collective-permute-done | bytes 147488 | tf_op jit(solution)/shard_map/ppermute | solution.py:929
  194.3 3.9 %collective-permute-start.47 = (bf16[2,96,768]{2,1,0:T(8,128)(2,1)S(1)}, bf16[2,96,768]{2,1,0:T(8,128)(2,1)S(1)}, u32[]{:S(2)}, u32[]{:S(2)}) collective-permute-start(bf16[2,96,768]{2,1,0:T(8,128)(2,1)S(1)} %get-tuple-element.352), channel_id=1, source_target_pairs={{0,3},{1,0},{2,1},{3,2},{4,7},{5,4},{6,5},{7,6},{8,11},{9,8},{10,9... | collective-permute-start | bytes 884744 | tf_op jit(solution)/shard_map/ppermute | solution.py:935
  198.8 2.8 %collective-permute-done.36.refs_1_ = bf16[1,192,768]{2,1,0:T(8,128)(2,1)S(1)} collective-permute-done((bf16[1,192,768]{2,1,0:T(8,128)(2,1)S(1)}, bf16[1,192,768]{2,1,0:T(8,128)(2,1)S(1)}, u32[]{:S(2)}, u32[]{:S(2)}) %collective-permute-start.36) | collective-permute-done | bytes 294944 | tf_op jit(solution)/shard_map/ppermute | solution.py:929
  205.6 3.1 %collective-permute-start.45 = (bf16[1,96,768]{2,1,0:T(8,128)(2,1)S(1)}, bf16[1,96,768]{2,1,0:T(8,128)(2,1)S(1)}, u32[]{:S(2)}, u32[]{:S(2)}) collective-permute-start(bf16[1,96,768]{2,1,0:T(8,128)(2,1)S(1)} %get-tuple-element.357), channel_id=1, source_target_pairs={{0,2},{1,3},{2,0},{3,1},{4,6},{5,7},{6,4},{7,5},{8,10},{9,11},{10,... | collective-permute-start | bytes 442376 | tf_op jit(solution)/shard_map/ppermute | solution.py:935
  208.7 14.3 %collective-permute-done.48.refs_3_ = bf16[2,96,768]{2,1,0:T(8,128)(2,1)S(1)} collective-permute-done((bf16[2,96,768]{2,1,0:T(8,128)(2,1)S(1)}, bf16[2,96,768]{2,1,0:T(8,128)(2,1)S(1)}, u32[]{:S(2)}, u32[]{:S(2)}) %collective-permute-start.48) | collective-permute-done | bytes 294944 | tf_op jit(solution)/shard_map/ppermute | solution.py:935
  224.3 1.2 collective-permute-start.50
  225.5 1.2 collective-permute-start.51
  228.1 3.2 %collective-permute-done.49.refs_1_ = bf16[2,96,768]{2,1,0:T(8,128)(2,1)S(1)} collective-permute-done((bf16[2,96,768]{2,1,0:T(8,128)(2,1)S(1)}, bf16[2,96,768]{2,1,0:T(8,128)(2,1)S(1)}, u32[]{:S(2)}, u32[]{:S(2)}) %collective-permute-start.49) | collective-permute-done | bytes 294944 | tf_op jit(solution)/shard_map/ppermute | solution.py:929
  231.3 4.6 %collective-permute-done.50.refs_2_ = bf16[2,96,768]{2,1,0:T(8,128)(2,1)S(1)} collective-permute-done((bf16[2,96,768]{2,1,0:T(8,128)(2,1)S(1)}, bf16[2,96,768]{2,1,0:T(8,128)(2,1)S(1)}, u32[]{:S(2)}, u32[]{:S(2)}) %collective-permute-start.50) | collective-permute-done | bytes 294944 | tf_op jit(solution)/shard_map/ppermute | solution.py:929
  238.2 1.6 collective-permute-start.55
  239.8 2.0 collective-permute-done.57.refs_1_
  242.8 3.7 %collective-permute-done.58.refs_2_ = bf16[16,768]{1,0:T(8,128)(2,1)S(1)} collective-permute-done((bf16[16,768]{1,0:T(8,128)(2,1)S(1)}, bf16[16,768]{1,0:T(8,128)(2,1)S(1)}, u32[]{:S(2)}, u32[]{:S(2)}) %collective-permute-start.58) | collective-permute-done | bytes 24608 | tf_op jit(solution)/shard_map/ppermute | solution.py:935
  246.5 2.1 collective-permute-start.59
  248.6 1.7 collective-permute-done.59.refs_3_
  251.7 3.0 %finish.3 = (f32[768,768]{1,0:T(8,128)}, f32[768,768]{1,0:T(8,128)}) custom-call(s32[8]{0:T(128)S(1)} %copy-done.2, bf16[4,2,96,768]{3,2,1,0:T(8,128)(2,1)S(1)} %cat.10.refs_0_, bf16[4,2,96,768]{3,2,1,0:T(8,128)(2,1)S(1)} %collective-permute-done.52.refs_1_), custom_call_target="tpu_custom_call" | custom-call | flops 2000000000 | bytes 2000000 | tf_op jit(solution)/shard_map/finish/pallas_call | solution.py:879
  254.8 2.1 finish.2
  (191 shorter events, 47.9 us)
Async XLA Ops:
  4.6 15.8 %collective-permute-start = (bf16[112,768]{1,0:T(8,128)(2,1)}, bf16[112,768]{1,0:T(8,128)(2,1)S(1)}, u32[]{:S(2)}, u32[]{:S(2)}) collective-permute-start(bf16[112,768]{1,0:T(8,128)(2,1)} %get-tuple-element.180), channel_id=1, source_target_pairs={{0,3},{1,0},{2,1},{3,2},{4,7},{5,4},{6,5},{7,6},{8,11},{9,8},{10,9... | collective-permute-start | bytes 516104 | tf_op jit(solution)/shard_map/ppermute | solution.py:932
  9.7 14.8 %collective-permute-start.1 = (bf16[112,768]{1,0:T(8,128)(2,1)}, bf16[112,768]{1,0:T(8,128)(2,1)S(1)}, u32[]{:S(2)}, u32[]{:S(2)}) collective-permute-start(bf16[112,768]{1,0:T(8,128)(2,1)} %get-tuple-element.180), channel_id=1, source_target_pairs={{0,2},{1,3},{2,0},{3,1},{4,6},{5,7},{6,4},{7,5},{8,10},{9,11},{10,... | collective-permute-start | bytes 516104 | tf_op jit(solution)/shard_map/ppermute | solution.py:932
  9.7 14.8 %collective-permute-start.2 = (bf16[112,768]{1,0:T(8,128)(2,1)}, bf16[112,768]{1,0:T(8,128)(2,1)S(1)}, u32[]{:S(2)}, u32[]{:S(2)}) collective-permute-start(bf16[112,768]{1,0:T(8,128)(2,1)} %get-tuple-element.180), channel_id=1, source_target_pairs={{0,1},{1,2},{2,3},{3,0},{4,5},{5,6},{6,7},{7,4},{8,9},{9,10},{10,1... | collective-permute-start | bytes 516104 | tf_op jit(solution)/shard_map/ppermute | solution.py:932
  25.1 11.8 %collective-permute-start.3 = (bf16[3,96,768]{2,1,0:T(8,128)(2,1)S(1)}, bf16[3,96,768]{2,1,0:T(8,128)(2,1)S(1)}, u32[]{:S(2)}, u32[]{:S(2)}) collective-permute-start(bf16[3,96,768]{2,1,0:T(8,128)(2,1)S(1)} %get-tuple-element.189.refs_0_), channel_id=1, source_target_pairs={{0,8},{4,12},{8,0},{12,4},{16,24},{20,28},{24,16},{28,20},{1,9},{5... | collective-permute-start | bytes 1327112 | tf_op jit(solution)/shard_map/ppermute | solution.py:929
  26.6 11.5 %collective-permute-start.4 = (bf16[3,96,768]{2,1,0:T(8,128)(2,1)S(1)}, bf16[3,96,768]{2,1,0:T(8,128)(2,1)S(1)}, u32[]{:S(2)}, u32[]{:S(2)}) collective-permute-start(bf16[3,96,768]{2,1,0:T(8,128)(2,1)S(1)} %get-tuple-element.189.refs_0_), channel_id=1, source_target_pairs={{0,16},{4,20},{8,24},{12,28},{16,0},{20,4},{24,8},{28,12},{1,17},{... | collective-permute-start | bytes 1327112 | tf_op jit(solution)/shard_map/ppermute | solution.py:929
  28.1 8.3 %collective-permute-start.5 = (bf16[2,96,768]{2,1,0:T(8,128)(2,1)}, bf16[2,96,768]{2,1,0:T(8,128)(2,1)S(1)}, u32[]{:S(2)}, u32[]{:S(2)}) collective-permute-start(bf16[2,96,768]{2,1,0:T(8,128)(2,1)} %get-tuple-element.200), channel_id=1, source_target_pairs={{0,3},{1,0},{2,1},{3,2},{4,7},{5,4},{6,5},{7,6},{8,11},{9,8},{10,9... | collective-permute-start | bytes 884744 | tf_op jit(solution)/shard_map/ppermute | solution.py:932
  38.2 13.0 %collective-permute-start.7 = (bf16[3,3,96,768]{3,2,1,0:T(8,128)(2,1)S(1)}, bf16[3,3,96,768]{3,2,1,0:T(8,128)(2,1)S(1)}, u32[]{:S(2)}, u32[]{:S(2)}) collective-permute-start(bf16[3,3,96,768]{3,2,1,0:T(8,128)(2,1)S(1)} %cat.6.refs_2_.refs_3_), channel_id=1, source_target_pairs={{0,4},{4,0},{8,12},{12,8},{16,20},{20,16},{24,28},{28,24},{1,5},{5... | collective-permute-start | bytes 3981320 | tf_op jit(solution)/shard_map/ppermute | solution.py:929
  38.3 12.9 %collective-permute-start.6 = (bf16[3,96,768]{2,1,0:T(8,128)(2,1)S(1)}, bf16[3,96,768]{2,1,0:T(8,128)(2,1)S(1)}, u32[]{:S(2)}, u32[]{:S(2)}) collective-permute-start(bf16[3,96,768]{2,1,0:T(8,128)(2,1)S(1)} %collective-permute-done.3.refs_1_), channel_id=1, source_target_pairs={{0,16},{4,20},{8,24},{12,28},{16,0},{20,4},{24,8},{28,12},{1,17},{... | collective-permute-start | bytes 1327112 | tf_op jit(solution)/shard_map/ppermute | solution.py:929
  39.9 11.3 %collective-permute-start.9 = (bf16[2,96,768]{2,1,0:T(8,128)(2,1)}, bf16[2,96,768]{2,1,0:T(8,128)(2,1)S(1)}, u32[]{:S(2)}, u32[]{:S(2)}) collective-permute-start(bf16[2,96,768]{2,1,0:T(8,128)(2,1)} %get-tuple-element.200), channel_id=1, source_target_pairs={{0,1},{1,2},{2,3},{3,0},{4,5},{5,6},{6,7},{7,4},{8,9},{9,10},{10,1... | collective-permute-start | bytes 884744 | tf_op jit(solution)/shard_map/ppermute | solution.py:932
  40.6 10.6 %collective-permute-start.8 = (bf16[2,96,768]{2,1,0:T(8,128)(2,1)S(1)}, bf16[2,96,768]{2,1,0:T(8,128)(2,1)S(1)}, u32[]{:S(2)}, u32[]{:S(2)}) collective-permute-start(bf16[2,96,768]{2,1,0:T(8,128)(2,1)S(1)} %collective-permute-done.5.refs_0_), channel_id=1, source_target_pairs={{0,8},{4,12},{8,0},{12,4},{16,24},{20,28},{24,16},{28,20},{1,9},{5... | collective-permute-start | bytes 884744 | tf_op jit(solution)/shard_map/ppermute | solution.py:929
  52.6 16.7 %collective-permute-start.11 = (bf16[2,96,768]{2,1,0:T(8,128)(2,1)}, bf16[2,96,768]{2,1,0:T(8,128)(2,1)S(1)}, u32[]{:S(2)}, u32[]{:S(2)}) collective-permute-start(bf16[2,96,768]{2,1,0:T(8,128)(2,1)} %get-tuple-element.200), channel_id=1, source_target_pairs={{0,2},{1,3},{2,0},{3,1},{4,6},{5,7},{6,4},{7,5},{8,10},{9,11},{10,... | collective-permute-start | bytes 884744 | tf_op jit(solution)/shard_map/ppermute | solution.py:932
  54.7 22.6 %collective-permute-start.12 = (bf16[2,2,96,768]{3,2,1,0:T(8,128)(2,1)S(1)}, bf16[2,2,96,768]{3,2,1,0:T(8,128)(2,1)}, u32[]{:S(2)}, u32[]{:S(2)}) collective-permute-start(bf16[2,2,96,768]{3,2,1,0:T(8,128)(2,1)S(1)} %cat.7.refs_5_), channel_id=1, source_target_pairs={{0,16},{4,20},{8,24},{12,28},{16,0},{20,4},{24,8},{28,12},{1,17},{... | collective-permute-start | bytes 1769480 | tf_op jit(solution)/shard_map/ppermute | solution.py:929
  56.3 24.0 %collective-permute-start.15 = (bf16[2,2,96,768]{3,2,1,0:T(8,128)(2,1)S(1)}, bf16[2,2,96,768]{3,2,1,0:T(8,128)(2,1)}, u32[]{:S(2)}, u32[]{:S(2)}) collective-permute-start(bf16[2,2,96,768]{3,2,1,0:T(8,128)(2,1)S(1)} %cat.7.refs_5_), channel_id=1, source_target_pairs={{0,4},{4,0},{8,12},{12,8},{16,20},{20,16},{24,28},{28,24},{1,5},{5... | collective-permute-start | bytes 1769480 | tf_op jit(solution)/shard_map/ppermute | solution.py:929
  56.3 21.0 %collective-permute-start.13 = (bf16[2,96,768]{2,1,0:T(8,128)(2,1)S(1)}, bf16[2,96,768]{2,1,0:T(8,128)(2,1)S(1)}, u32[]{:S(2)}, u32[]{:S(2)}) collective-permute-start(bf16[2,96,768]{2,1,0:T(8,128)(2,1)S(1)} %collective-permute-done.9.refs_0_), channel_id=1, source_target_pairs={{0,16},{4,20},{8,24},{12,28},{16,0},{20,4},{24,8},{28,12},{1,17},{... | collective-permute-start | bytes 884744 | tf_op jit(solution)/shard_map/ppermute | solution.py:929
  69.3 8.9 %collective-permute-start.14 = (bf16[2,96,768]{2,1,0:T(8,128)(2,1)S(1)}, bf16[2,96,768]{2,1,0:T(8,128)(2,1)S(1)}, u32[]{:S(2)}, u32[]{:S(2)}) collective-permute-start(bf16[2,96,768]{2,1,0:T(8,128)(2,1)S(1)} %collective-permute-done.11.refs_0_), channel_id=1, source_target_pairs={{0,8},{4,12},{8,0},{12,4},{16,24},{20,28},{24,16},{28,20},{1,9},{5... | collective-permute-start | bytes 884744 | tf_op jit(solution)/shard_map/ppermute | solution.py:929
  78.2 16.2 %collective-permute-start.18 = (bf16[2,2,96,768]{3,2,1,0:T(8,128)(2,1)S(1)}, bf16[2,2,96,768]{3,2,1,0:T(8,128)(2,1)}, u32[]{:S(2)}, u32[]{:S(2)}) collective-permute-start(bf16[2,2,96,768]{3,2,1,0:T(8,128)(2,1)S(1)} %cat.9.refs_8_), channel_id=1, source_target_pairs={{0,16},{4,20},{8,24},{12,28},{16,0},{20,4},{24,8},{28,12},{1,17},{... | collective-permute-start | bytes 1769480 | tf_op jit(solution)/shard_map/ppermute | solution.py:929
  79.6 15.5 %collective-permute-start.17 = (bf16[2,2,96,768]{3,2,1,0:T(8,128)(2,1)S(1)}, bf16[2,2,96,768]{3,2,1,0:T(8,128)(2,1)S(1)}, u32[]{:S(2)}, u32[]{:S(2)}) collective-permute-start(bf16[2,2,96,768]{3,2,1,0:T(8,128)(2,1)S(1)} %cat.8.refs_4_), channel_id=1, source_target_pairs={{0,8},{4,12},{8,0},{12,4},{16,24},{20,28},{24,16},{28,20},{1,9},{5... | collective-permute-start | bytes 1769480 | tf_op jit(solution)/shard_map/ppermute | solution.py:929
  95.9 8.1 %collective-permute-start.19 = (bf16[4,384,768]{2,1,0:T(8,128)(2,1)}, bf16[4,384,768]{2,1,0:T(8,128)(2,1)S(1)}, u32[]{:S(2)}, u32[]{:S(2)}) collective-permute-start(bf16[4,384,768]{2,1,0:T(8,128)(2,1)} %get-tuple-element.218), channel_id=1, source_target_pairs={{0,4},{4,0},{8,12},{12,8},{16,20},{20,16},{24,28},{28,24},{1,5},{5... | collective-permute-start | bytes 7077896 | tf_op jit(solution)/shard_map/ppermute | solution.py:929
  107.7 15.6 %collective-permute-start.24 = (bf16[2,192,768]{2,1,0:T(8,128)(2,1)}, bf16[2,192,768]{2,1,0:T(8,128)(2,1)S(1)}, u32[]{:S(2)}, u32[]{:S(2)}) collective-permute-start(bf16[2,192,768]{2,1,0:T(8,128)(2,1)} %get-tuple-element.240), channel_id=1, source_target_pairs={{0,8},{4,12},{8,0},{12,4},{16,24},{20,28},{24,16},{28,20},{1,9},{5... | collective-permute-start | bytes 1769480 | tf_op jit(solution)/shard_map/ppermute | solution.py:929
  108.3 15.3 %collective-permute-start.25 = (bf16[2,192,768]{2,1,0:T(8,128)(2,1)}, bf16[2,192,768]{2,1,0:T(8,128)(2,1)S(1)}, u32[]{:S(2)}, u32[]{:S(2)}) collective-permute-start(bf16[2,192,768]{2,1,0:T(8,128)(2,1)} %get-tuple-element.241), channel_id=1, source_target_pairs={{0,16},{4,20},{8,24},{12,28},{16,0},{20,4},{24,8},{28,12},{1,17},{... | collective-permute-start | bytes 1769480 | tf_op jit(solution)/shard_map/ppermute | solution.py:929
  126.6 18.2 %collective-permute-start.28 = (bf16[4,384,768]{2,1,0:T(8,128)(2,1)}, bf16[4,384,768]{2,1,0:T(8,128)(2,1)S(1)}, u32[]{:S(2)}, u32[]{:S(2)}) collective-permute-start(bf16[4,384,768]{2,1,0:T(8,128)(2,1)} %get-tuple-element.250), channel_id=1, source_target_pairs={{0,4},{4,0},{8,12},{12,8},{16,20},{20,16},{24,28},{28,24},{1,5},{5... | collective-permute-start | bytes 7077896 | tf_op jit(solution)/shard_map/ppermute | solution.py:929
  126.6 18.1 %collective-permute-start.26 = (bf16[2,96,768]{2,1,0:T(8,128)(2,1)}, bf16[2,96,768]{2,1,0:T(8,128)(2,1)S(1)}, u32[]{:S(2)}, u32[]{:S(2)}) collective-permute-start(bf16[2,96,768]{2,1,0:T(8,128)(2,1)} %get-tuple-element.248), channel_id=1, source_target_pairs={{0,16},{4,20},{8,24},{12,28},{16,0},{20,4},{24,8},{28,12},{1,17},{... | collective-permute-start | bytes 884744 | tf_op jit(solution)/shard_map/ppermute | solution.py:929
  127.4 17.3 %collective-permute-start.27 = (bf16[2,96,768]{2,1,0:T(8,128)(2,1)}, bf16[2,96,768]{2,1,0:T(8,128)(2,1)S(1)}, u32[]{:S(2)}, u32[]{:S(2)}) collective-permute-start(bf16[2,96,768]{2,1,0:T(8,128)(2,1)} %get-tuple-element.249), channel_id=1, source_target_pairs={{0,8},{4,12},{8,0},{12,4},{16,24},{20,28},{24,16},{28,20},{1,9},{5... | collective-permute-start | bytes 884744 | tf_op jit(solution)/shard_map/ppermute | solution.py:929
  149.9 24.0 %collective-permute-start.34 = (bf16[2,96,768]{2,1,0:T(8,128)(2,1)}, bf16[2,96,768]{2,1,0:T(8,128)(2,1)S(1)}, u32[]{:S(2)}, u32[]{:S(2)}) collective-permute-start(bf16[2,96,768]{2,1,0:T(8,128)(2,1)} %get-tuple-element.354), channel_id=1, source_target_pairs={{0,1},{1,2},{2,3},{3,0},{4,5},{5,6},{6,7},{7,4},{8,9},{9,10},{10,1... | collective-permute-start | bytes 884744 | tf_op jit(solution)/shard_map/ppermute | solution.py:935
  149.9 24.8 %collective-permute-start.29 = (bf16[2,192,768]{2,1,0:T(8,128)(2,1)}, bf16[2,192,768]{2,1,0:T(8,128)(2,1)S(1)}, u32[]{:S(2)}, u32[]{:S(2)}) collective-permute-start(bf16[2,192,768]{2,1,0:T(8,128)(2,1)} %get-tuple-element.262), channel_id=1, source_target_pairs={{0,8},{4,12},{8,0},{12,4},{16,24},{20,28},{24,16},{28,20},{1,9},{5... | collective-permute-start | bytes 1769480 | tf_op jit(solution)/shard_map/ppermute | solution.py:929
  150.6 24.1 %collective-permute-start.30 = (bf16[2,192,768]{2,1,0:T(8,128)(2,1)}, bf16[2,192,768]{2,1,0:T(8,128)(2,1)S(1)}, u32[]{:S(2)}, u32[]{:S(2)}) collective-permute-start(bf16[2,192,768]{2,1,0:T(8,128)(2,1)} %get-tuple-element.263), channel_id=1, source_target_pairs={{0,16},{4,20},{8,24},{12,28},{16,0},{20,4},{24,8},{28,12},{1,17},{... | collective-permute-start | bytes 1769480 | tf_op jit(solution)/shard_map/ppermute | solution.py:929
  154.7 20.0 %collective-permute-start.32 = (bf16[1,192,768]{2,1,0:T(8,128)(2,1)}, bf16[1,192,768]{2,1,0:T(8,128)(2,1)S(1)}, u32[]{:S(2)}, u32[]{:S(2)}) collective-permute-start(bf16[1,192,768]{2,1,0:T(8,128)(2,1)} %get-tuple-element.275), channel_id=1, source_target_pairs={{0,8},{4,12},{8,0},{12,4},{16,24},{20,28},{24,16},{28,20},{1,9},{5... | collective-permute-start | bytes 884744 | tf_op jit(solution)/shard_map/ppermute | solution.py:929
  156.1 19.3 %collective-permute-start.33 = (bf16[1,192,768]{2,1,0:T(8,128)(2,1)S(1)}, bf16[1,192,768]{2,1,0:T(8,128)(2,1)S(1)}, u32[]{:S(2)}, u32[]{:S(2)}) collective-permute-start(bf16[1,192,768]{2,1,0:T(8,128)(2,1)S(1)} %get-tuple-element.276), channel_id=1, source_target_pairs={{0,16},{4,20},{8,24},{12,28},{16,0},{20,4},{24,8},{28,12},{1,17},{... | collective-permute-start | bytes 884744 | tf_op jit(solution)/shard_map/ppermute | solution.py:929
  176.1 15.2 %collective-permute-start.35 = (bf16[2,400,768]{2,1,0:T(8,128)(2,1)}, bf16[2,400,768]{2,1,0:T(8,128)(2,1)S(1)}, u32[]{:S(2)}, u32[]{:S(2)}) collective-permute-start(bf16[2,400,768]{2,1,0:T(8,128)(2,1)} %get-tuple-element.297), channel_id=1, source_target_pairs={{0,4},{4,0},{8,12},{12,8},{16,20},{20,16},{24,28},{28,24},{1,5},{5... | collective-permute-start | bytes 3686408 | tf_op jit(solution)/shard_map/ppermute | solution.py:929
  177.0 13.6 %collective-permute-start.40 = (bf16[2,96,768]{2,1,0:T(8,128)(2,1)S(1)}, bf16[2,96,768]{2,1,0:T(8,128)(2,1)S(1)}, u32[]{:S(2)}, u32[]{:S(2)}) collective-permute-start(bf16[2,96,768]{2,1,0:T(8,128)(2,1)S(1)} %get-tuple-element.316), channel_id=1, source_target_pairs={{0,16},{4,20},{8,24},{12,28},{16,0},{20,4},{24,8},{28,12},{1,17},{... | collective-permute-start | bytes 884744 | tf_op jit(solution)/shard_map/ppermute | solution.py:929
  178.3 12.3 %collective-permute-start.41 = (bf16[2,96,768]{2,1,0:T(8,128)(2,1)S(1)}, bf16[2,96,768]{2,1,0:T(8,128)(2,1)S(1)}, u32[]{:S(2)}, u32[]{:S(2)}) collective-permute-start(bf16[2,96,768]{2,1,0:T(8,128)(2,1)S(1)} %get-tuple-element.317), channel_id=1, source_target_pairs={{0,8},{4,12},{8,0},{12,4},{16,24},{20,28},{24,16},{28,20},{1,9},{5... | collective-permute-start | bytes 884744 | tf_op jit(solution)/shard_map/ppermute | solution.py:929
  179.7 10.0 %collective-permute-start.42 = (bf16[1,96,768]{2,1,0:T(8,128)(2,1)S(1)}, bf16[1,96,768]{2,1,0:T(8,128)(2,1)S(1)}, u32[]{:S(2)}, u32[]{:S(2)}) collective-permute-start(bf16[1,96,768]{2,1,0:T(8,128)(2,1)S(1)} %get-tuple-element.318), channel_id=1, source_target_pairs={{0,16},{4,20},{8,24},{12,28},{16,0},{20,4},{24,8},{28,12},{1,17},{... | collective-permute-start | bytes 442376 | tf_op jit(solution)/shard_map/ppermute | solution.py:929
  180.6 10.0 %collective-permute-start.43 = (bf16[1,96,768]{2,1,0:T(8,128)(2,1)S(1)}, bf16[1,96,768]{2,1,0:T(8,128)(2,1)S(1)}, u32[]{:S(2)}, u32[]{:S(2)}) collective-permute-start(bf16[1,96,768]{2,1,0:T(8,128)(2,1)S(1)} %get-tuple-element.319), channel_id=1, source_target_pairs={{0,8},{4,12},{8,0},{12,4},{16,24},{20,28},{24,16},{28,20},{1,9},{5... | collective-permute-start | bytes 442376 | tf_op jit(solution)/shard_map/ppermute | solution.py:929
  192.8 8.9 %collective-permute-start.37 = (bf16[1,208,768]{2,1,0:T(8,128)(2,1)S(1)}, bf16[1,208,768]{2,1,0:T(8,128)(2,1)S(1)}, u32[]{:S(2)}, u32[]{:S(2)}) collective-permute-start(bf16[1,208,768]{2,1,0:T(8,128)(2,1)S(1)} %get-tuple-element.300), channel_id=1, source_target_pairs={{0,16},{4,20},{8,24},{12,28},{16,0},{20,4},{24,8},{28,12},{1,17},{... | collective-permute-start | bytes 958472 | tf_op jit(solution)/shard_map/ppermute | solution.py:929
  194.3 11.3 %collective-permute-start.47 = (bf16[2,96,768]{2,1,0:T(8,128)(2,1)S(1)}, bf16[2,96,768]{2,1,0:T(8,128)(2,1)S(1)}, u32[]{:S(2)}, u32[]{:S(2)}) collective-permute-start(bf16[2,96,768]{2,1,0:T(8,128)(2,1)S(1)} %get-tuple-element.352), channel_id=1, source_target_pairs={{0,3},{1,0},{2,1},{3,2},{4,7},{5,4},{6,5},{7,6},{8,11},{9,8},{10,9... | collective-permute-start | bytes 884744 | tf_op jit(solution)/shard_map/ppermute | solution.py:935
  198.2 24.8 %collective-permute-start.48 = (bf16[2,96,768]{2,1,0:T(8,128)(2,1)S(1)}, bf16[2,96,768]{2,1,0:T(8,128)(2,1)S(1)}, u32[]{:S(2)}, u32[]{:S(2)}) collective-permute-start(bf16[2,96,768]{2,1,0:T(8,128)(2,1)S(1)} %get-tuple-element.351), channel_id=1, source_target_pairs={{0,2},{1,3},{2,0},{3,1},{4,6},{5,7},{6,4},{7,5},{8,10},{9,11},{10,... | collective-permute-start | bytes 884744 | tf_op jit(solution)/shard_map/ppermute | solution.py:935
  202.4 23.1 %collective-permute-start.39 = (bf16[1,112,768]{2,1,0:T(8,128)(2,1)S(1)}, bf16[1,112,768]{2,1,0:T(8,128)(2,1)S(1)}, u32[]{:S(2)}, u32[]{:S(2)}) collective-permute-start(bf16[1,112,768]{2,1,0:T(8,128)(2,1)S(1)} %get-tuple-element.306), channel_id=1, source_target_pairs={{0,8},{4,12},{8,0},{12,4},{16,24},{20,28},{24,16},{28,20},{1,9},{5... | collective-permute-start | bytes 516104 | tf_op jit(solution)/shard_map/ppermute | solution.py:929
  203.1 21.2 %collective-permute-start.38 = (bf16[1,96,768]{2,1,0:T(8,128)(2,1)S(1)}, bf16[1,96,768]{2,1,0:T(8,128)(2,1)S(1)}, u32[]{:S(2)}, u32[]{:S(2)}) collective-permute-start(bf16[1,96,768]{2,1,0:T(8,128)(2,1)S(1)} %get-tuple-element.305), channel_id=1, source_target_pairs={{0,16},{4,20},{8,24},{12,28},{16,0},{20,4},{24,8},{28,12},{1,17},{... | collective-permute-start | bytes 442376 | tf_op jit(solution)/shard_map/ppermute | solution.py:929
  204.3 23.1 %collective-permute-start.44 = (bf16[1,96,768]{2,1,0:T(8,128)(2,1)S(1)}, bf16[1,96,768]{2,1,0:T(8,128)(2,1)S(1)}, u32[]{:S(2)}, u32[]{:S(2)}) collective-permute-start(bf16[1,96,768]{2,1,0:T(8,128)(2,1)S(1)} %get-tuple-element.358), channel_id=1, source_target_pairs={{0,1},{1,2},{2,3},{3,0},{4,5},{5,6},{6,7},{7,4},{8,9},{9,10},{10,1... | collective-permute-start | bytes 442376 | tf_op jit(solution)/shard_map/ppermute | solution.py:935
  205.6 22.5 %collective-permute-start.45 = (bf16[1,96,768]{2,1,0:T(8,128)(2,1)S(1)}, bf16[1,96,768]{2,1,0:T(8,128)(2,1)S(1)}, u32[]{:S(2)}, u32[]{:S(2)}) collective-permute-start(bf16[1,96,768]{2,1,0:T(8,128)(2,1)S(1)} %get-tuple-element.357), channel_id=1, source_target_pairs={{0,2},{1,3},{2,0},{3,1},{4,6},{5,7},{6,4},{7,5},{8,10},{9,11},{10,... | collective-permute-start | bytes 442376 | tf_op jit(solution)/shard_map/ppermute | solution.py:935
  223.2 8.2 %collective-permute-start.49 = (bf16[2,96,768]{2,1,0:T(8,128)(2,1)S(1)}, bf16[2,96,768]{2,1,0:T(8,128)(2,1)S(1)}, u32[]{:S(2)}, u32[]{:S(2)}) collective-permute-start(bf16[2,96,768]{2,1,0:T(8,128)(2,1)S(1)} %total.2.refs_0_), channel_id=1, source_target_pairs={{0,8},{4,12},{8,0},{12,4},{16,24},{20,28},{24,16},{28,20},{1,9},{5... | collective-permute-start | bytes 884744 | tf_op jit(solution)/shard_map/ppermute | solution.py:929
  224.3 11.6 %collective-permute-start.50 = (bf16[2,96,768]{2,1,0:T(8,128)(2,1)S(1)}, bf16[2,96,768]{2,1,0:T(8,128)(2,1)S(1)}, u32[]{:S(2)}, u32[]{:S(2)}) collective-permute-start(bf16[2,96,768]{2,1,0:T(8,128)(2,1)S(1)} %total.2.refs_0_), channel_id=1, source_target_pairs={{0,16},{4,20},{8,24},{12,28},{16,0},{20,4},{24,8},{28,12},{1,17},{... | collective-permute-start | bytes 884744 | tf_op jit(solution)/shard_map/ppermute | solution.py:929
  225.5 10.4 %collective-permute-start.51 = (bf16[2,96,768]{2,1,0:T(8,128)(2,1)S(1)}, bf16[2,96,768]{2,1,0:T(8,128)(2,1)S(1)}, u32[]{:S(2)}, u32[]{:S(2)}) collective-permute-start(bf16[2,96,768]{2,1,0:T(8,128)(2,1)S(1)} %total.2.refs_0_), channel_id=1, source_target_pairs={{0,24},{4,28},{8,16},{12,20},{16,8},{20,12},{24,0},{28,4},{1,25},{... | collective-permute-start | bytes 884744 | tf_op jit(solution)/shard_map/ppermute | solution.py:929
  227.4 8.5 %collective-permute-start.46 = (bf16[1,96,768]{2,1,0:T(8,128)(2,1)S(1)}, bf16[1,96,768]{2,1,0:T(8,128)(2,1)S(1)}, u32[]{:S(2)}, u32[]{:S(2)}) collective-permute-start(bf16[1,96,768]{2,1,0:T(8,128)(2,1)S(1)} %get-tuple-element.355), channel_id=1, source_target_pairs={{0,3},{1,0},{2,1},{3,2},{4,7},{5,4},{6,5},{7,6},{8,11},{9,8},{10,9... | collective-permute-start | bytes 442376 | tf_op jit(solution)/shard_map/ppermute | solution.py:935
  236.0 14.4 %collective-permute-start.52 = (bf16[4,2,96,768]{3,2,1,0:T(8,128)(2,1)S(1)}, bf16[4,2,96,768]{3,2,1,0:T(8,128)(2,1)S(1)}, u32[]{:S(2)}, u32[]{:S(2)}) collective-permute-start(bf16[4,2,96,768]{3,2,1,0:T(8,128)(2,1)S(1)} %cat.10.refs_0_), channel_id=1, source_target_pairs={{0,4},{4,0},{8,12},{12,8},{16,20},{20,16},{24,28},{28,24},{1,5},{5... | collective-permute-start | bytes 3538952 | tf_op jit(solution)/shard_map/ppermute | solution.py:929
  236.2 14.1 %collective-permute-start.53 = (bf16[1,96,768]{2,1,0:T(8,128)(2,1)S(1)}, bf16[1,96,768]{2,1,0:T(8,128)(2,1)S(1)}, u32[]{:S(2)}, u32[]{:S(2)}) collective-permute-start(bf16[1,96,768]{2,1,0:T(8,128)(2,1)S(1)} %total.3.refs_0_), channel_id=1, source_target_pairs={{0,8},{4,12},{8,0},{12,4},{16,24},{20,28},{24,16},{28,20},{1,9},{5... | collective-permute-start | bytes 442376 | tf_op jit(solution)/shard_map/ppermute | solution.py:929
  237.4 13.0 %collective-permute-start.54 = (bf16[1,96,768]{2,1,0:T(8,128)(2,1)S(1)}, bf16[1,96,768]{2,1,0:T(8,128)(2,1)S(1)}, u32[]{:S(2)}, u32[]{:S(2)}) collective-permute-start(bf16[1,96,768]{2,1,0:T(8,128)(2,1)S(1)} %total.3.refs_0_), channel_id=1, source_target_pairs={{0,16},{4,20},{8,24},{12,28},{16,0},{20,4},{24,8},{28,12},{1,17},{... | collective-permute-start | bytes 442376 | tf_op jit(solution)/shard_map/ppermute | solution.py:929
  238.2 12.2 %collective-permute-start.55 = (bf16[1,96,768]{2,1,0:T(8,128)(2,1)S(1)}, bf16[1,96,768]{2,1,0:T(8,128)(2,1)S(1)}, u32[]{:S(2)}, u32[]{:S(2)}) collective-permute-start(bf16[1,96,768]{2,1,0:T(8,128)(2,1)S(1)} %total.3.refs_0_), channel_id=1, source_target_pairs={{0,24},{4,28},{8,16},{12,20},{16,8},{20,12},{24,0},{28,4},{1,25},{... | collective-permute-start | bytes 442376 | tf_op jit(solution)/shard_map/ppermute | solution.py:929
  (47 other events, 346.9 us)

commit v4 on v3

--- a/solution.py
+++ b/solution.py
@@ -57,12 +57,12 @@
     return pl.CostEstimate(flops=micros * 10**9, bytes_accessed=micros * 10**6, transcendentals=0)
 
 
-def mask_rows(meta_ref, slots):
-    bucket = meta_ref[0]
+def mask_rows(ids_ref, slots):
+    bucket = ids_ref[1]
     half = BIG // 2
     segs, starts = [], []
     for part in range(2):
-        first = meta_ref[1] + part * half
+        first = ids_ref[2] + part * half
         seg = jnp.int32(0)
         for j in range(1, slots):
             seg = seg + jnp.where(first >= j * bucket, 1, 0).astype(jnp.int32)
@@ -74,7 +74,7 @@
         cols = []
         for key_part in range(2):
             same = segs[query_part] == segs[key_part]
-            limit = jnp.where(same, meta_ref[2 + segs[key_part]] - starts[key_part], 0)
+            limit = jnp.where(same, ids_ref[3 + segs[key_part]] - starts[key_part], 0)
             cols.append(jnp.where(iota < limit, 0.0, MASKED).astype(F32))
         rows.append(jnp.concatenate(cols, axis=1))
     return rows
@@ -96,6 +96,18 @@
     return jnp.concatenate(tiles, axis=1)
 
 
+def row_block(low, bits):
+    return ((low & 1) << (bits - 1)) | (low >> 1)
+
+
+def side_of(ids_ref, bit):
+    return (ids_ref[0] >> bit) & 1
+
+
+def block_rows(ids_ref, mask, bits, rows):
+    return pl.ds(pl.multiple_of(row_block(ids_ref[0] ^ mask, bits) * rows, rows), rows)
+
+
 class Mover:
     def __init__(self, sems):
         self.sems, self.used, self.out = sems, 0, []
@@ -109,26 +121,25 @@
     def load(self, source, target):
         return [self.copy(source, target)]
 
-    def blocks(self, index_ref, part_refs, mat, which):
+    def blocks(self, ids_ref, masks, part_refs, mat, which):
         copies, j, first = [], 0, 0
         for part in part_refs:
-            if index_ref is None:
+            if masks is None:
                 copies.append(self.copy(part, mat.at[pl.ds(first, part.shape[0])]))
                 first += part.shape[0]
                 continue
-            rows = part.shape[2]
+            bits = (len(masks) - 1).bit_length()
             for e in range(part.shape[0]):
-                at = pl.ds(pl.multiple_of(index_ref[j] * rows, rows), rows)
-                copies.append(self.copy(part.at[e, which], mat.at[at]))
+                copies.append(self.copy(part.at[e, which], mat.at[block_rows(ids_ref, masks[j], bits, part.shape[2])]))
                 j += 1
         return copies
 
     def store(self, source, target):
         self.out.append(self.copy(source, target))
 
-    def halves(self, side_ref, source, send, keep):
+    def halves(self, ids_ref, source, send, keep):
         size = source.shape[0] // 2
-        for ref, side in ((send, 1 - side_ref[0]), (keep, side_ref[0])):
+        for ref, side in ((send, 1 - side_of(ids_ref, 0)), (keep, side_of(ids_ref, 0))):
             self.store(source.at[pl.ds(pl.multiple_of(side * size, size), size)], ref)
 
     def finish(self):
@@ -140,12 +151,11 @@
         one.wait()
 
 
-def put_blocks(index_ref, part_refs, mat, which):
-    j = 0
+def put_blocks(ids_ref, masks, part_refs, mat, which):
+    j, bits = 0, (len(masks) - 1).bit_length()
     for part in part_refs:
-        rows = part.shape[2]
         for e in range(part.shape[0]):
-            mat[pl.ds(pl.multiple_of(index_ref[j] * rows, rows), rows), :] = part[e, which].astype(mat.dtype)
+            mat[block_rows(ids_ref, masks[j], bits, part.shape[2]), :] = part[e, which].astype(mat.dtype)
             j += 1
 
 
@@ -178,10 +188,9 @@
     return jnp.concatenate(probs, axis=0)
 
 
-def attn_fwd_kernel(slots, heads, parts, start, shards, own, last, meta_ref, *refs):
+def attn_fwd_kernel(slots, heads, parts, masks, start, shards, last, ids_ref, *refs):
     refs = list(refs)
     take = lambda n: [refs.pop(0) for _ in range(n)]
-    index_ref = None if own else take(1)[0]
     n1_hbm = take(1)[0]
     a_parts = take(parts)
     tab_hbm, hot_hbm, prior_hbm = take(3)
@@ -192,10 +201,10 @@
     move = Mover(sems)
     width = heads * HEAD
     half = BIG // 2
-    got_mat = [move.blocks(index_ref, a_parts, mat.at[0], start)]
+    got_mat = [move.blocks(ids_ref, masks, a_parts, mat.at[0], start)]
     got_n1 = move.load(n1_hbm, n1_ref)
     got_tab = move.load(tab_hbm.at[pl.ds(start, shards)], tab_ref) + move.load(hot_hbm, hot_ref)
-    masks = mask_rows(meta_ref, slots)
+    allowed = mask_rows(ids_ref, slots)
     wait(got_tab)
     wait(got_n1)
     for s in range(shards):
@@ -204,7 +213,7 @@
             band[h] = bias_band(rel[h : h + 1])
         wait(got_mat[s])
         if s == 0:
-            got_mat += [move.blocks(index_ref, a_parts, mat.at[t], start + t) for t in range(1, shards)]
+            got_mat += [move.blocks(ids_ref, masks, a_parts, mat.at[t], start + t) for t in range(1, shards)]
             got_prior = move.load(prior_hbm, prior_ref)
             if last:
                 got_prior += move.load(gain_hbm, gain_ref)
@@ -215,7 +224,7 @@
             scores[h] = dot_nt(q, k)
         for h in range(heads):
             v = head_slices(qkv_ref.at[s], heads, h)[2]
-            pb = forward_scores(h, band, rel, masks, scores, lse_ref.at[s])
+            pb = forward_scores(h, band, rel, allowed, scores, lse_ref.at[s])
             o_ref[s, :, h * HEAD : (h + 1) * HEAD] = dot_nn(pb, v).astype(BF)
         move.store(o_ref.at[s], o_out.at[s])
         move.store(lse_ref.at[s], lse_out.at[s])
@@ -237,12 +246,11 @@
 HBM = pl.BlockSpec(memory_space=pltpu.HBM)
 
 
-def attn_fwd(meta, index, n1, a_parts, start, shards, tab, hot, prior, gain, slots, heads):
-    own, last = index is None, gain is not None
+def attn_fwd(ids, masks, n1, a_parts, start, shards, tab, hot, prior, gain, slots, heads):
+    last = gain is not None
     rows, depth = n1.shape
     width = heads * HEAD
     cols = 4 * width
-    scalars = [meta] if own else [meta, index]
     args = [n1, *a_parts, tab, hot, prior] + ([gain] if last else [])
     out_shape = [
         like((shards, rows, cols), BF),
@@ -253,8 +261,8 @@
     if last:
         out_shape.append(like((rows, depth), BF))
     return pl.pallas_call(
-        functools.partial(attn_fwd_kernel, slots, heads, len(a_parts), start, shards, own, last),
-        in_specs=[SMEM] * len(scalars) + [ANY] * len(args),
+        functools.partial(attn_fwd_kernel, slots, heads, len(a_parts), masks, start, shards, last),
+        in_specs=[SMEM] + [ANY] * len(args),
         out_specs=[HBM] * len(out_shape),
         out_shape=out_shape,
         scratch_shapes=[
@@ -276,10 +284,10 @@
         compiler_params=params(LIMIT),
         cost_estimate=cost(16 * shards),
         name="attn_fwd",
-    )(*scalars, *args)
-
-
-def attn_bwd_kernel(slots, heads, shards, rest, sources, own, first, befores, meta_ref, side_ref, index_ref, *refs):
+    )(ids, *args)
+
+
+def attn_bwd_kernel(slots, heads, masks, shards, rest, sources, own, first, befores, ids_ref, *refs):
     refs = list(refs)
     take = lambda n: [refs.pop(0) for _ in range(n)]
     last = None in shards
@@ -314,14 +322,14 @@
         at = 0 if which is None else which
         base = 0 if which is None else rest_at[which]
         got_tab = move.load(kept[3].at[at], tab_ref.at[c])
-        got_mat = move.blocks(None if which is None else index_ref, parts, mat.at[c], at)
+        got_mat = move.blocks(ids_ref, None if which is None else masks, parts, mat.at[c], at)
         got_kept = move.load(kept[0].at[base], qkv_ref.at[c]) + move.load(kept[2].at[base], lse_ref.at[c])
         return got_tab, got_mat, got_kept, move.load(kept[1].at[base], o_ref.at[c])
 
     got_first = move.load(hot_hbm, hot_ref) + move.load(gh_hbm, gh_ref)
     got = [load(0)]
     got_n1 = move.load(n1_hbm, n1_ref)
-    masks = mask_rows(meta_ref, slots)
+    allowed = mask_rows(ids_ref, slots)
     lane = lax.broadcasted_iota(jnp.int32, (1, SPAN), 1)
     wait(got_first)
     gh = gh_ref[...]
@@ -354,7 +362,7 @@
             high = jnp.zeros((1, TILE), F32)
             for i in range(BIG // TILE):
                 rows = slice(i * TILE, (i + 1) * TILE)
-                s = dot_nt(q[rows], k) + masked_bias(i, band[h], rel[h : h + 1], masks[i // 2])
+                s = dot_nt(q[rows], k) + masked_bias(i, band[h], rel[h : h + 1], allowed[i // 2])
                 p = jnp.exp(s - lse_ref[c, rows, h : h + 1])
                 dp = dot_nt(go[rows], v)
                 inner = jnp.sum(p * dp, axis=1, keepdims=True)
@@ -381,7 +389,7 @@
         grads_mat[c] = dot_tn(gq_all[c], n1_ref[...]).astype(BF)
         grads_mat[c, :width, :] = dot_tn(o_ref[c], gh).astype(BF)
         size = pl.ds(0, grads_mat.shape[1] // 2)
-        move.halves(side_ref, grads_mat.at[c], send_out.at[c, size], keep_out.at[c, size])
+        move.halves(ids_ref, grads_mat.at[c], send_out.at[c, size], keep_out.at[c, size])
         near = acc[...]
         n = TILE // 2
         while n >= 8:
@@ -446,7 +454,7 @@
     return wide[: EXTRA // 2] + wide[EXTRA // 2 :]
 
 
-def attn_bwd(meta, index, side, n1, gh, hot, shards, rest, own, prior, final, slots, heads):
+def attn_bwd(ids, masks, n1, gh, hot, shards, rest, own, prior, final, slots, heads):
     last, first = None in shards, prior is None
     count = len(shards)
     rows, depth = n1.shape
@@ -494,24 +502,23 @@
         ]
     return pl.pallas_call(
         functools.partial(
-            attn_bwd_kernel, slots, heads, tuple(shards), len(parts), tuple(p for p, _ in sources),
+            attn_bwd_kernel, slots, heads, masks, tuple(shards), len(parts), tuple(p for p, _ in sources),
             len(own[0]) if last else 0, first, befores,
         ),
-        in_specs=[SMEM] * 3 + [ANY] * len(args),
+        in_specs=[SMEM] + [ANY] * len(args),
         out_specs=[HBM] * len(out_shape),
         out_shape=out_shape,
         scratch_shapes=scratch,
         compiler_params=params(LIMIT),
         cost_estimate=cost(32 * count),
         name="attn_bwd",
-    )(meta, side, index, *args)
-
-
-def ffn_kernel(parts, first, last, side_ref, *refs):
+    )(ids, *args)
+
+
+def ffn_kernel(parts, masks, first, last, ids_ref, *refs):
     refs = list(refs)
     take = lambda n: [refs.pop(0) for _ in range(n)]
     count = len(parts)
-    index_refs = take(sum(1 for n in parts if n))
     n2_hbm, cot_hbm = take(2)
     f_parts = [take(n or 2) for n in parts]
     out_in, gn_in = (None, None) if first else take(2)
@@ -527,8 +534,7 @@
     def load(c):
         if not parts[c]:
             return move.load(f_parts[c][0], i_mat.at[c]), move.load(f_parts[c][1], w_mat.at[c])
-        index_ref = index_refs[sum(1 for n in parts[:c] if n)]
-        return tuple(move.blocks(index_ref, f_parts[c], mat.at[c], j) for j, mat in enumerate((i_mat, w_mat)))
+        return tuple(move.blocks(ids_ref, masks[c], f_parts[c], mat.at[c], j) for j, mat in enumerate((i_mat, w_mat)))
 
     got_n2 = move.load(n2_hbm, n2_ref)
     got = [load(0)]
@@ -557,9 +563,9 @@
         cot = cot_ref[...]
         gp_ref[c] = (dot_nt(cot, w_mat[c]) * slope).astype(BF)
         gw_mat[c] = dot_tn(act_ref[c], cot).astype(BF)
-        move.halves(side_ref, gw_mat.at[c], send_out.at[2 * c + 1], keep_out.at[2 * c + 1])
+        move.halves(ids_ref, gw_mat.at[c], send_out.at[2 * c + 1], keep_out.at[2 * c + 1])
         gi_mat[c] = dot_tn(n2_ref[...], gp_ref[c]).astype(BF)
-        move.halves(side_ref, gi_mat.at[c], send_out.at[2 * c], keep_out.at[2 * c])
+        move.halves(ids_ref, gi_mat.at[c], send_out.at[2 * c], keep_out.at[2 * c])
         if c == 0:
             wait(got_sums)
         ending = c == count - 1
@@ -594,14 +600,13 @@
     move.finish()
 
 
-def ffn(side, n2, cot, shards, sums, final):
+def ffn(ids, n2, cot, shards, sums, final):
     first, last = sums is None, final is not None
     rows, depth = n2.shape
     count = len(shards)
     units = shards[-1][1][0].shape[-1]
     half = like((2 * count, depth // 2, units), BF)
     total = like((rows, depth), F32)
-    scalars = [side] + [index for index, _ in shards if index is not None]
     args = [n2, cot] + [p for _, ps in shards for p in ps]
     args += ([] if first else list(sums)) + ([] if not last else list(final))
     if last:
@@ -629,20 +634,22 @@
             pltpu.VMEM((8, depth), F32),
         ]
     return pl.pallas_call(
-        functools.partial(ffn_kernel, tuple(0 if i is None else len(p) for i, p in shards), first, last),
-        in_specs=[SMEM] * len(scalars) + [ANY] * len(args),
+        functools.partial(
+            ffn_kernel, tuple(0 if m is None else len(p) for m, p in shards), [m for m, _ in shards], first, last
+        ),
+        in_specs=[SMEM] + [ANY] * len(args),
         out_specs=[HBM] * len(out_shape),
         out_shape=out_shape,
         scratch_shapes=scratch,
         compiler_params=params(LIMIT),
         cost_estimate=cost(32 * count),
         name="ffn",
-    )(*scalars, *args)
-
-
-def prep_kernel(rows, count, index_ref, *refs):
-    mats, (tab_ref, in_ref, down_ref, a_ref, f_ref, sems) = refs[:count], refs[count:]
-    block = index_ref[0]
+    )(ids, *args)
+
+
+def prep_kernel(rows, bits, count, ids_ref, *refs):
+    mats, (tab_ref, in_ref, down_ref, a_ref, f_ref, wide_ref, sems) = refs[:count], refs[count:]
+    block = row_block(ids_ref[0], bits)
     first = pl.ds(pl.multiple_of(block * rows, rows), rows)
     copies = [
         pltpu.make_async_copy(in_ref.at[first], f_ref.at[0], sems.at[0]),
@@ -661,8 +668,13 @@
 
     for copy in copies:
         copy.start()
+    tab = tab_ref[...].astype(F32)
+    heads, buckets = tab.shape
+    tab = jnp.concatenate([tab, jnp.zeros((heads, TILE - buckets), F32)], axis=1)
+    tab = jnp.concatenate([tab, jnp.zeros((EXTRA - heads, TILE), F32)], axis=0).astype(BF)
+    wide_ref[0] = tab
     a_ref[rows:, :] = jnp.zeros((EXTRA, a_ref.shape[1]), BF)
-    a_ref[rows:, :TILE] = tab_ref[...]
+    a_ref[rows:, :TILE] = tab
     for j, mat in enumerate(mats):
         @pl.when(block // per == j)
         def _():
@@ -672,18 +684,18 @@
         copy.wait()
 
 
-def prep(index, mats, tab, w_in, w_down, rows):
+def prep(ids, mats, tab, w_in, w_down, rows, bits):
     depth = w_in.shape[0]
     return pl.pallas_call(
-        functools.partial(prep_kernel, rows, len(mats)),
+        functools.partial(prep_kernel, rows, bits, len(mats)),
         in_specs=[SMEM] + [ANY] * len(mats) + [VMEM, ANY, ANY],
-        out_specs=[VMEM, VMEM],
-        out_shape=[like((rows + EXTRA, depth), BF), like((2, rows, depth), BF)],
+        out_specs=[VMEM, VMEM, VMEM],
+        out_shape=[like((rows + EXTRA, depth), BF), like((2, rows, depth), BF), like((1, EXTRA, TILE), BF)],
         scratch_shapes=[pltpu.SemaphoreType.DMA((3,))],
         compiler_params=params(60),
-        cost_estimate=cost(1),
+        cost_estimate=cost(0),
         name="prep",
-    )(index, *mats, tab, w_in, w_down)
+    )(ids, *mats, tab, w_in, w_down)
 
 
 def join_kernel(count, *refs):
@@ -702,7 +714,7 @@
         out_specs=[VMEM, VMEM],
         out_shape=[like((len(parts), rows - EXTRA, depth), BF), like((len(parts), EXTRA, TILE), BF)],
         compiler_params=params(16),
-        cost_estimate=cost(1),
+        cost_estimate=cost(0),
         name="join",
     )(*parts)
 
@@ -717,7 +729,7 @@
     return [(o * 2 * inner, inner, o * inner) for o in range(outer)]
 
 
-def fold_kernel(runs, extra, joined, sides_ref, *refs):
+def fold_kernel(runs, extra, joined, ids_ref, *refs):
     if joined:
         keep_ref, recv_ref = refs[:2]
         n = keep_ref.shape[0] // 2
@@ -739,7 +751,7 @@
             outs[0][g * n : (g + 1) * n] = total(pl.ds(0, rows))
             continue
         bit, group_runs = runs[g]
-        mine = sides_ref[bit]
+        mine = side_of(ids_ref, bit)
         for ref, side in ((outs[2 * g], 1 - mine), (outs[2 * g + 1], mine)):
             for source, length, target in group_runs:
                 ref[:, target : target + length, :] = total(pl.ds(pl.multiple_of(source + side * length, length), length))
@@ -751,7 +763,7 @@
         outs[1][...] = packed
 
 
-def fold(sides, groups, runs, extra):
+def fold(ids, groups, runs, extra):
     joined = len(groups) == 1
     arrays = [a for group in groups for a in group]
     if joined:
@@ -772,9 +784,9 @@
         out_specs=[VMEM] * len(out_shape),
         out_shape=out_shape,
         compiler_params=params(24),
-        cost_estimate=cost(1),
+        cost_estimate=cost(0),
         name="fold",
-    )(sides, *arrays)
+    )(ids, *arrays)
 
 
 def add_kernel(a_ref, b_ref, out_ref):
@@ -784,7 +796,7 @@
 def add(a, b):
     return pl.pallas_call(
         add_kernel, in_specs=[VMEM, VMEM], out_specs=VMEM, out_shape=like(a.shape, BF),
-        compiler_params=params(16), cost_estimate=cost(1), name="add",
+        compiler_params=params(16), cost_estimate=cost(0), name="add",
     )(a, b)
 
 
@@ -795,7 +807,7 @@
 def add_small(a, b):
     return pl.pallas_call(
         add_small_kernel, in_specs=[VMEM, VMEM], out_specs=VMEM, out_shape=like(a.shape, BF),
-        compiler_params=params(16), cost_estimate=cost(1), name="add_small",
+        compiler_params=params(16), cost_estimate=cost(0), name="add_small",
     )(a, b)
 
 
@@ -814,33 +826,58 @@
         out_specs=VMEM,
         out_shape=like(parts[0].shape, BF),
         compiler_params=params(16),
-        cost_estimate=cost(1),
+        cost_estimate=cost(0),
         name="total",
     )(*parts)
 
 
-def small_kernel(count, *refs):
-    parts, (tab_ref, gains_ref) = refs[:count], refs[count:]
-    table, gains = None, None
+def pack_kernel(places, count, *refs):
+    parts, small_ref, outs = refs[:count], refs[count], refs[count + 1 :]
+    for (j, m), ref in zip(places, outs):
+        rows = parts[j].shape[1]
+        ref[:rows, :] = parts[j][m]
+        ref[rows:, :] = small_ref[...]
+
+
+def pack(places, parts, small):
+    rows, cols = parts[0].shape[1:]
+    return pl.pallas_call(
+        functools.partial(pack_kernel, places, len(parts)),
+        in_specs=[VMEM] * (len(parts) + 1),
+        out_specs=[VMEM] * len(places),
+        out_shape=[like((rows + EXTRA, cols), BF)] * len(places),
+        compiler_params=params(16),
+        cost_estimate=cost(0),
+        name="pack",
+    )(*parts, small)
+
+
+def unpack_kernel(count, *refs):
+    parts, (out_ref, tab_ref, gains_ref) = refs[:count], refs[count:]
+    rows = out_ref.shape[1]
+    total, table, gains = None, None, None
     for j, part in enumerate(parts):
-        wide = join_small(part[...])
+        piece = part[:rows, :].astype(F32)
+        wide = join_small(part[rows:, :])
+        total = piece if total is None else total + piece
         table = wide[j : j + 1] if table is None else table + wide[j : j + 1]
         gains = wide if gains is None else gains + wide
+    out_ref[0] = total.astype(BF)
     tab_ref[...] = jnp.broadcast_to(table, tab_ref.shape)
     gains_ref[...] = gains
 
 
-def small_of(parts):
-    depth = parts[0].shape[1]
-    shape = like((EXTRA // 2, depth), F32)
-    return pl.pallas_call(
-        functools.partial(small_kernel, len(parts)),
+def unpack(parts):
+    rows, cols = parts[0].shape
+    shape = like((EXTRA // 2, cols), F32)
+    return pl.pallas_call(
+        functools.partial(unpack_kernel, len(parts)),
         in_specs=[VMEM] * len(parts),
-        out_specs=[VMEM, VMEM],
-        out_shape=[shape, shape],
+        out_specs=[VMEM] * 3,
+        out_shape=[like((1, rows - EXTRA, cols), BF), shape, shape],
         compiler_params=params(16),
-        cost_estimate=cost(1),
-        name="small",
+        cost_estimate=cost(0),
+        name="unpack",
     )(*parts)
 
 
@@ -856,36 +893,36 @@
         out_specs=VMEM,
         out_shape=like((len(parts),) + parts[0].shape, BF),
         compiler_params=params(16),
-        cost_estimate=cost(1),
+        cost_estimate=cost(0),
         name="cat",
     )(*parts)
 
 
-def finish_kernel(count, split, index_ref, *refs):
+def finish_kernel(count, split, masks, ids_ref, *refs):
     parts, out_refs, mat = refs[:count], refs[count:-1], refs[-1]
     for j in range(parts[0].shape[1]):
         if split:
-            put_blocks(index_ref, parts, mat, j)
+            put_blocks(ids_ref, masks, parts, mat, j)
             rows = mat.shape[0] // len(out_refs)
             for i, ref in enumerate(out_refs):
                 ref[...] = mat[i * rows : (i + 1) * rows, :].astype(F32)
         else:
-            put_blocks(index_ref, parts, out_refs[j], j)
-
-
-def finish(index, parts, outs, rows):
+            put_blocks(ids_ref, masks, parts, out_refs[j], j)
+
+
+def finish(ids, masks, parts, outs, rows):
     depth = parts[0].shape[-1]
     split = parts[0].shape[1] != outs
     return pl.pallas_call(
-        functools.partial(finish_kernel, len(parts), split),
+        functools.partial(finish_kernel, len(parts), split, masks),
         in_specs=[SMEM] + [VMEM] * len(parts),
         out_specs=[VMEM] * outs,
         out_shape=[like((rows, depth), F32)] * outs,
         scratch_shapes=[pltpu.VMEM((depth, depth), BF)],
         compiler_params=params(24),
-        cost_estimate=cost(2),
+        cost_estimate=cost(0),
         name="finish",
-    )(index, *parts)
+    )(ids, *parts)
 
 
 def bar(*values):
@@ -897,33 +934,19 @@
 
 
 class Ring:
-    def __init__(self, n_dp, n_mp, depth):
+    def __init__(self, n_dp, n_mp, depth, ids):
         self.n_dp, self.n_mp = n_dp, n_mp
         self.all_bits = (n_dp - 1).bit_length()
         self.bits = min(3, self.all_bits)
-        self.z = lax.axis_index("mp")
-        self.blocks = 1 << self.bits
-        self.rows = depth // self.blocks
-        self.low = lax.axis_index("dp") & (self.blocks - 1)
-        self.sides = [((self.low >> bit) & 1)[None].astype(jnp.int32) for bit in range(self.bits)]
-        self.all_sides = jnp.concatenate(self.sides)
-        self.mine = self.row_block(self.low)[None].astype(jnp.int32)
-        self.orders = {flip: self.order(flip) for flip in (False, True)}
-        self.index = {flip: self.block_index(flip) for flip in (False, True)}
-
-    def row_block(self, low):
-        return ((low & 1) << (self.bits - 1)) | (low >> 1)
-
-    def order(self, flip):
-        high = list(range(1, self.bits))
-        return (high[::-1] if flip else high) + [0]
-
-    def block_index(self, flip):
-        masks = [0]
-        for bit in self.orders[flip]:
+        self.rows = depth // (1 << self.bits)
+        self.ids = ids
+        self.masks = {flip: self.block_masks(flip) for flip in (False, True)}
+
+    def block_masks(self, flip):
+        masks, high = [0], list(range(1, self.bits))
+        for bit in (high[::-1] if flip else high) + [0]:
             masks = masks + [m | (1 << bit) for m in masks]
-        low = self.low ^ jnp.asarray(masks, jnp.int32)
-        return self.row_block(low).astype(jnp.int32)
+        return masks
 
     def swap(self, x, mask):
         return lax.ppermute(x, "dp", [(i, i ^ mask) for i in range(self.n_dp)])
@@ -933,13 +956,6 @@
 
     def push(self, x, shift):
         return lax.ppermute(x, "mp", [(i, (i + shift) % self.n_mp) for i in range(self.n_mp)])
-
-    def gather_all(self, piece):
-        groups = [[g + i for i in range(self.blocks)] for g in range(0, self.n_dp, self.blocks)]
-        return lax.all_gather(piece, "dp", axis_index_groups=groups)
-
-    def group_index(self):
-        return jnp.asarray([self.row_block(low) for low in range(self.blocks)], jnp.int32)
 
 
 class Reduce:
@@ -961,7 +977,7 @@
     def step(self):
         ring = self.ring
         if not self.orders[0]:
-            out = fold(ring.all_sides, self.groups, None, self.extra)
+            out = fold(ring.ids, self.groups, None, self.extra)
             self.out, self.small = out[0], out[1] if self.extra else None
             for bit in range(ring.bits, ring.all_bits):
                 self.out = add(self.out, ring.swap(self.out, 1 << bit))
@@ -975,7 +991,7 @@
             runs.append((bit, row_runs(self.left[g], bit, ring.rows)))
             self.left[g] = [b for b in self.left[g] if b != bit]
             bits.append(bit)
-        outs = fold(ring.all_sides, self.groups, runs, self.extra)
+        outs = fold(ring.ids, self.groups, runs, self.extra)
         self.groups = [[outs[2 * g + 1], ring.swap(outs[2 * g], 1 << bits[g])] for g in range(2)]
         return [outs[1], outs[3]]
 
@@ -988,17 +1004,16 @@
     buckets, heads = rel_table.shape
     width = heads * HEAD
     slots = lengths.shape[1]
-    ring = Ring(n_dp, n_mp, depth)
-    side = ring.sides[0]
+    low = lax.axis_index("dp") & ((1 << min(3, (n_dp - 1).bit_length())) - 1)
+    first_row = lax.axis_index("mp") * BIG
+    ids = jnp.concatenate([low[None].astype(jnp.int32), bucket, first_row[None].astype(jnp.int32), lengths[0]])
+    ring = Ring(n_dp, n_mp, depth, ids)
     shifts = list(range(1, n_mp))
-    meta = jnp.concatenate([bucket, (ring.z * BIG)[None].astype(jnp.int32), lengths[0]])
     hot = jnp.asarray(offset_one_hot(buckets), BF)
     gain_one, gain_two = gain_attn[None], gain_ffn[None]
 
     a_own = [w_out, w_query.T, w_key.T, w_value.T]
-    tab_own = jnp.pad(rel_table.T, ((0, EXTRA - heads), (0, TILE - buckets)))
-    a_piece, f_piece = prep(ring.mine, a_own, tab_own, w_in, w_down, ring.rows)
-    tab_own = tab_own[None]
+    a_piece, f_piece, tab_own = prep(ids, a_own, rel_table.T, w_in, w_down, ring.rows, ring.bits)
     v = {}
 
     def close(*keys):
@@ -1007,64 +1022,62 @@
     def swap(new, old, mask):
         v[new] = ring.swap(v[old], mask)
 
-    shift_order = [s for s in shifts if s != n_mp // 2] + [n_mp // 2]
-    f1, f3, f2 = shift_order
+    f3 = n_mp // 2
+    f1, f2 = [s for s in shifts if s != f3]
+    masks = ring.masks[False]
     v["piece"] = f_piece
     for s in shifts:
         v["z", s] = ring.pull(a_piece, s)
     x_value = inputs.astype(F32)
     n1 = (rms(x_value)[0] * gain_attn.astype(F32)).astype(BF)
-    *kept_own, v["hidden"] = attn_fwd(meta, None, n1, a_own, 0, 1, tab_own, hot, inputs, None, slots, heads)
+    *kept_own, v["hidden"] = attn_fwd(ids, None, n1, a_own, 0, 1, tab_own, hot, inputs, None, slots, heads)
     close(*[("z", s) for s in shifts], "hidden")
     v["a"], tab_rest = join([v["z", s] for s in shifts])
     close("a", "piece")
     swap("ax", "a", 2)
     swap("ay", "a", 4)
     v["f", f1] = ring.pull(v["piece"], f1)
-    v["f", f3] = ring.pull(v["piece"], f3)
     close("ax", "ay", "a", ("f", f1), "piece")
     swap("ayx", "ax", 4)
     v["a3"] = cat([v["a"], v["ax"], v["ay"]])
     swap("a3c", "a3", 1)
     swap(("fx", f1), ("f", f1), 2)
     v["f", f2] = ring.pull(v["piece"], f2)
-    close("ayx", "a3c", ("fx", f1), ("f", f3))
+    close("ayx", "a3c", ("fx", f1), ("f", f2), "piece")
     v["a1"] = v["ayx"][None]
     swap("a1c", "a1", 1)
+    close("a1c", "hidden")
     v["cat", f1] = cat([v["f", f1], v["fx", f1]])
     swap(("far", f1), ("cat", f1), 4)
-    swap(("fy", f3), ("f", f3), 4)
-    close("a1c", "hidden")
+    swap(("fx", f2), ("f", f2), 2)
+    v["f", f3] = ring.pull(v["piece"], f3)
     a_parts = [v["a3"], v["a1"], v["a3c"], v["a1c"]]
-    a_index = ring.index[False]
     cut = n_mp - 2
     *kept_one, v["hidden"] = attn_fwd(
-        meta, a_index, n1, a_parts, 0, cut, tab_rest, hot, v["hidden"], None, slots, heads
+        ids, masks, n1, a_parts, 0, cut, tab_rest, hot, v["hidden"], None, slots, heads
     )
-    close("hidden", ("f", f2))
-    swap(("fx", f2), ("f", f2), 2)
-    *kept_two, v["hidden"], v["n2"] = attn_fwd(
-        meta, a_index, n1, a_parts, cut, 1, tab_rest, hot, v["hidden"], gain_two, slots, heads
-    )
-    close("hidden", "n2", ("far", f1), ("fy", f3), ("fx", f2))
-
-    def cores(s):
-        swap(("catc", s), ("cat", s), 1)
-        swap(("farc", s), ("far", s), 1)
-
-    def parts_of(s):
-        return ring.index[s == f3], [v["cat", s], v["far", s], v["catc", s], v["farc", s]]
-
-    cores(f1)
-    v["cat", f3] = cat([v["f", f3], v["fy", f3]])
-    swap(("far", f3), ("cat", f3), 2)
+    close("hidden", ("fx", f2), ("f", f3), ("far", f1))
     v["cat", f2] = cat([v["f", f2], v["fx", f2]])
     swap(("far", f2), ("cat", f2), 4)
-    close("n2", ("catc", f1), ("farc", f1))
+    swap(("fx", f3), ("f", f3), 2)
+    swap(("catc", f1), ("cat", f1), 1)
+    swap(("farc", f1), ("far", f1), 1)
+    *kept_two, v["hidden"], v["n2"] = attn_fwd(
+        ids, masks, n1, a_parts, cut, 1, tab_rest, hot, v["hidden"], gain_two, slots, heads
+    )
+    close("hidden", "n2", ("fx", f3), ("catc", f1), ("farc", f1))
+    v["cat", f3] = cat([v["f", f3], v["fx", f3]])
+    swap(("far", f3), ("cat", f3), 4)
+    swap(("catc", f2), ("cat", f2), 1)
+    swap(("catc", f3), ("cat", f3), 1)
+
+    def parts_of(s):
+        return masks, [v["cat", s], v["far", s], v["catc", s], v["farc", s]]
+
     v["out"], v["gn"], v["send"], v["keep"] = ffn(
-        side, v["n2"], cotangent, [(None, [w_in, w_down]), parts_of(f1)], None, None
+        ids, v["n2"], cotangent, [(None, [w_in, w_down]), parts_of(f1)], None, None
     )
-    close("out", "gn", "n2", "send", "keep", ("far", f3), ("far", f2))
+    close("out", "gn", "n2", "send", "keep", ("far", f3), ("far", f2), ("catc", f3), ("catc", f2))
     red = {}
 
     def reduce(name, extra=0):
@@ -1081,23 +1094,25 @@
         outs = [out for name in names for out in red[name].step()]
         v.update(zip(keys, bar(*[v[key] for key in keys], *outs)))
 
-    cores(f3)
-    cores(f2)
+    swap(("farc", f2), ("far", f2), 1)
+    swap(("farc", f3), ("far", f3), 1)
     reduce("a")
-    close_with(["a"], "n2", "out", "gn", ("catc", f3), ("farc", f3), ("catc", f2), ("farc", f2))
+    close_with(["a"], "n2", "out", "gn", ("farc", f3), ("farc", f2))
     folded(["a"], "n2", "out", "gn")
     outputs, v["send"], v["keep"], grad_hidden, v["gh"], gg = ffn(
-        side, v["n2"], cotangent, [parts_of(f3), parts_of(f2)], (v["out"], v["gn"]), (v["hidden"], gain_two)
+        ids, v["n2"], cotangent, [parts_of(f2), parts_of(f3)], (v["out"], v["gn"]), (v["hidden"], gain_two)
     )
     close_with(["a"], "send", "keep", "gh")
+    reduce("b")
     folded(["a"], "gh")
-    reduce("b")
+    close_with(["b"], "gh")
+    folded(["b"], "gh")
 
     places = [(tuple(range(cut)), kept_one), ((cut,), kept_two)]
     rest = (a_parts, tab_rest, places)
     own = (a_own, [*kept_own, tab_own])
     v["send"], v["keep"], v["gn"], tabs = attn_bwd(
-        meta, a_index, side, n1, v["gh"], hot, list(range(cut)), rest, None, None, None, slots, heads
+        ids, masks, n1, v["gh"], hot, list(range(cut)), rest, None, None, None, slots, heads
     )
     close_with(["a", "b"], "send", "keep", "gh", "gn")
     reduce("c")
@@ -1107,22 +1122,25 @@
     folded(["c"], "gh", "gn")
     final = (inputs, gain_one, grad_hidden, gg, tabs)
     v["send"], v["keep"], v["gin"] = attn_bwd(
-        meta, a_index, side, n1, v["gh"], hot, [cut, None], rest, own, v["gn"], final, slots, heads
+        ids, masks, n1, v["gh"], hot, [cut, None], rest, own, v["gn"], final, slots, heads
     )
     close_with(["b", "c"], "send", "keep", "gin", "f1")
-    grad_inputs = v["gin"]
     reduce("d", EXTRA)
     folded(["b", "c"], "gin")
+    v["f2"] = ring.push(red["b"].out[:2], f2)
+    v["f3"] = ring.push(red["b"].out[2:], f3)
     close_with(["d"], "gin")
     folded(["d"], "gin")
-    close_with(["b", "c"], "gin")
-    folded(["b", "c"], "gin")
-    v["f3"] = ring.push(red["b"].out[:2], f3)
-    v["f2"] = ring.push(red["b"].out[2:], f2)
-    v["a1"], v["a2"] = ring.push(red["c"].out[:1], 1), ring.push(red["c"].out[1:], 2)
+    close_with(["c"], "gin")
+    folded(["c"], "gin")
     close_with(["d"], "gin")
     folded(["d"], "gin")
-    close("f3", "f2", "gin")
+    close_with(["d"], "gin")
+    folded(["d"], "gin")
+    packed = pack(((1, 1), (0, 0), (0, 1), (1, 0)), [red["c"].out, red["d"].out], red["d"].small)
+    for s in shifts:
+        v["a", s] = ring.push(packed[s], s)
+    close("f2", "f3", "gin")
 
     def spread(name, piece):
         v[name, 0] = piece
@@ -1133,23 +1151,20 @@
         v[name] = cat([v[name, mask] for mask in (0, 2, 4, 6)])
         v[name, 1] = ring.swap(v[name], 1)
 
-    spread("f", total_of([red["a"].out[:2], v["f1"], v["f3"], v["f2"]]))
-    close_with(["d"], "gin")
-    folded(["d"], "gin")
-    v["a3"] = ring.push(red["d"].out[:1], 3)
-    small = red["d"].small
-    smalls = [ring.push(small, s) for s in shifts]
-    close("a1", "a2", "a3", ("f", 2), ("f", 4), ("f", 6))
-    spread("a", total_of([red["d"].out[1:], v["a1"], v["a2"], v["a3"]]))
+    spread("f", total_of([red["a"].out[:2], v["f1"], v["f2"], v["f3"]]))
+    close(*[("a", s) for s in shifts], "gin")
+    a_total, table, gains = unpack([packed[0]] + [v["a", s] for s in shifts])
+    spread("a", a_total)
+    close(("f", 2), ("f", 4), ("f", 6), "gin")
     gathered("f")
-    close(("f", 1), ("a", 2), ("a", 4), ("a", 6))
+    close(("f", 1), "gin")
+    v["in"], v["down"] = finish(ids, masks, [v["f"], v["f", 1]], 2, depth)
+    close("in", "down", ("a", 2), ("a", 4), ("a", 6), "gin")
     gathered("a")
-    v["f_done"] = finish(a_index, [v["f"], v["f", 1]], 2, depth)
-    grad_in, grad_down = v["f_done"]
-    grads = finish(a_index, [v["a"], v["a", 1]], 4, width)
+    grad_in, grad_down, grad_inputs = v["in"], v["down"], v["gin"]
+    grads = finish(ids, masks, [v["a"], v["a", 1]], 4, width)
     grad_out, grad_query, grad_key, grad_value = grads[0], grads[1].T, grads[2].T, grads[3].T
 
-    table, gains = small_of([small] + smalls)
     grad_table = table[0, : heads * TILE].reshape(heads, TILE)[:, :buckets].T
     return (
         outputs, grad_inputs, grad_query, grad_key, grad_value, grad_out, grad_table,

time: 262 us -> 242 us (0.924)
  waiting for transfers between devices: 75.4 us -> 65.5 us
  local copies, waits for them, and re-layouts: 15.2 us -> 8.89 us
  starting transfers between devices: 54.8 us -> 51.7 us
    ppermute x9 -> x6, waiting for transfers between devices: 22.5 us -> 15.4 us  [push(): lax.ppermute(x, 'mp', [(i, (i + shift) % self.n_mp) for i in range(self.n...]
    ppermute x6, waiting for transfers between devices: 22.6 us -> 17 us  [pull(): lax.ppermute(x, 'mp', [(i, (i - shift) % self.n_mp) for i in range(self.n...]
    ppermute x9 -> x6, starting transfers between devices: 11.5 us -> 6.42 us  [push(): lax.ppermute(x, 'mp', [(i, (i + shift) % self.n_mp) for i in range(self.n...]
    unnamed x70 -> x56, local copies, waits for them, and re-layouts: 10.5 us -> 6.44 us
    ppermute x45, waiting for transfers between devices: 30.3 us -> 33 us  [swap(): return lax.ppermute(x, 'dp', [(i, i ^ mask) for i in range(self.n_dp)])]
    pallas_call x8 -> x9, Pallas kernels: 68.6 us -> 68.9 us  [the longest x2 33 us: attn_bwd(): pl.pallas_call(functools.partial(attn_bwd_kernel, slots, heads, masks, tu...]
  transfers between devices with their start and end apart: 60 -> 57, of which waited for: 25 -> 21; matrix products, arithmetic and copies ran while one was open for 2% -> 2% of each run, Pallas kernels for 38% -> 42%
where the time goes in v4:
time: 242 us; the launch traced here: 238 us
  Pallas kernels  107 us (44%)
  waiting for transfers between devices  65.5 us (27%)
  starting transfers between devices  51.7 us (21%)
  local copies, waits for them, and re-layouts  8.89 us (4%)
  other arithmetic  2.64 us (1%)
    ppermute x45, starting transfers between devices, swap(): return lax.ppermute(x, 'dp', [(i, i ^ mask) for i in range(self.n_dp)])  35.5 us
    ppermute x45, waiting for transfers between devices, swap(): return lax.ppermute(x, 'dp', [(i, i ^ mask) for i in range(self.n_dp)])  33 us
    pallas_call x2, Pallas kernels, attn_bwd(): pl.pallas_call(functools.partial(attn_bwd_kernel, slots, heads, masks, tu...  33 us
    pallas_call x2, Pallas kernels, ffn(): pl.pallas_call(functools.partial(ffn_kernel, tuple((0 if m is None else l...  27.9 us
    pallas_call x3, Pallas kernels, attn_fwd(): pl.pallas_call(functools.partial(attn_fwd_kernel, slots, heads, len(a_par...  25.1 us
    ppermute x6, waiting for transfers between devices, pull(): lax.ppermute(x, 'mp', [(i, (i - shift) % self.n_mp) for i in range(self.n...  17 us
    ppermute x6, waiting for transfers between devices, push(): lax.ppermute(x, 'mp', [(i, (i + shift) % self.n_mp) for i in range(self.n...  15.4 us
    pallas_call x12, Pallas kernels, fold(): pl.pallas_call(functools.partial(fold_kernel, runs, extra, joined), in_sp...  12.4 us
  transfers between devices with their start and end apart: 57, of which 21 were waited for; matrix products, arithmetic and copies ran while one was open for 2% of the time, Pallas kernels for 42%

profile of v4, /device:TPU:0, one launch (start us, length us, event | category | flops | bytes accessed | tf_op | source)
XLA Modules:
  0.0 237.9 jit_solution(8326539245134210978)
XLA Ops:
  2.6 2.7 %prep.1 = (bf16[112,768]{1,0:T(8,128)(2,1)}, bf16[2,96,768]{2,1,0:T(8,128)(2,1)}, bf16[1,16,128]{2,1,0:T(8,128)(2,1)}) custom-call(s32[11]{0:T(128)} %pad_add_fusion.ids_ref, bf16[192,768]{1,0:T(8,128)(2,1)} %refs_11_.1, bf16[192,768]{1,0:T(8,128)(2,1)} %bitcast.14, bf16[192,768]{1,0:T(8,128)(2,1)} %bitcast.17, bf16[192,768]{1,0:T(8,128)(2,1)} %bitcast.20, ...), custom_call_target="tpu_custom_call" | custom-call | tf_op jit(solution)/shard_map/prep/pallas_call | solution.py:689
  5.2 5.1 %collective-permute-start = (bf16[112,768]{1,0:T(8,128)(2,1)}, bf16[112,768]{1,0:T(8,128)(2,1)S(1)}, u32[]{:S(2)}, u32[]{:S(2)}) collective-permute-start(bf16[112,768]{1,0:T(8,128)(2,1)} %get-tuple-element.205), channel_id=1, source_target_pairs={{0,3},{1,0},{2,1},{3,2},{4,7},{5,4},{6,5},{7,6},{8,11},{9,8},{10,9... | collective-permute-start | bytes 516104 | tf_op jit(solution)/shard_map/ppermute | solution.py:955
  12.7 7.1 %attn_fwd.3 = (bf16[1,512,768]{2,1,0:T(8,128)(2,1)}, bf16[1,512,192]{2,1,0:T(8,128)(2,1)}, f32[1,512,128]{2,1,0:T(8,128)}, f32[512,768]{1,0:T(8,128)}) custom-call(s32[11]{0:T(128)} %pad_add_fusion.ids_ref, bf16[512,768]{1,0:T(8,128)(2,1)} %fusion.2.refs_0_, bf16[192,768]{1,0:T(8,128)(2,1)} %refs_11_.1, bf16[192,768]{1,0:T(8,128)(2,1)} %bitcast.15, ...), custom_call_target="tpu_custom_call" | custom-call | flops 16000000000 | bytes 16000000 | tf_op jit(solution)/shard_map/attn_fwd/pallas_call | solution.py:263
  19.9 5.2 %collective-permute-done.1.refs_1_ = bf16[112,768]{1,0:T(8,128)(2,1)S(1)} collective-permute-done((bf16[112,768]{1,0:T(8,128)(2,1)}, bf16[112,768]{1,0:T(8,128)(2,1)S(1)}, u32[]{:S(2)}, u32[]{:S(2)}) %collective-permute-start.1) | collective-permute-done | bytes 172064 | tf_op jit(solution)/shard_map/ppermute | solution.py:955
  25.8 1.5 collective-permute-start.3
  27.2 1.5 collective-permute-start.4
  29.7 7.2 %collective-permute-done.5.refs_0_ = bf16[2,96,768]{2,1,0:T(8,128)(2,1)S(1)} collective-permute-done((bf16[2,96,768]{2,1,0:T(8,128)(2,1)S(1)}, bf16[2,96,768]{2,1,0:T(8,128)(2,1)S(1)}, u32[]{:S(2)}, u32[]{:S(2)}) %collective-permute-start.5) | collective-permute-done | bytes 294944 | tf_op jit(solution)/shard_map/ppermute | solution.py:955
  38.9 1.6 collective-permute-start.6
  41.8 7.8 %collective-permute-done.8.refs_1_ = bf16[2,96,768]{2,1,0:T(8,128)(2,1)S(1)} collective-permute-done((bf16[2,96,768]{2,1,0:T(8,128)(2,1)S(1)}, bf16[2,96,768]{2,1,0:T(8,128)(2,1)S(1)}, u32[]{:S(2)}, u32[]{:S(2)}) %collective-permute-start.8) | collective-permute-done | bytes 294944 | tf_op jit(solution)/shard_map/ppermute | solution.py:952
  49.6 2.2 collective-permute-done.9.refs_0_
  53.6 1.3 collective-permute-start.13
  55.9 2.1 collective-permute-start.12
  58.7 10.5 %attn_fwd.4 = (bf16[2,512,768]{2,1,0:T(8,128)(2,1)}, bf16[2,512,192]{2,1,0:T(8,128)(2,1)}, f32[2,512,128]{2,1,0:T(8,128)}, f32[512,768]{1,0:T(8,128)}) custom-call(s32[11]{0:T(128)} %pad_add_fusion.ids_ref, bf16[512,768]{1,0:T(8,128)(2,1)} %fusion.2.refs_0_, bf16[3,3,96,768]{3,2,1,0:T(8,128)(2,1)} %copy-done.2, bf16[1,3,96,768]{3,2,1,0:T(8,128)(2,1)} %bitcast.30, ...), custom_call_target="tpu_custom_call" | custom-call | flops 32000000000 | bytes 32000000 | tf_op jit(solution)/shard_map/attn_fwd/pallas_call | solution.py:263
  69.3 2.4 %collective-permute-done.12.refs_0_ = bf16[2,96,768]{2,1,0:T(8,128)(2,1)S(1)} collective-permute-done((bf16[2,96,768]{2,1,0:T(8,128)(2,1)S(1)}, bf16[2,96,768]{2,1,0:T(8,128)(2,1)S(1)}, u32[]{:S(2)}, u32[]{:S(2)}) %collective-permute-start.12) | collective-permute-done | bytes 294944 | tf_op jit(solution)/shard_map/ppermute | solution.py:955
  72.8 1.5 collective-permute-start.14
  74.3 7.4 %attn_fwd.5 = (bf16[1,512,768]{2,1,0:T(8,128)(2,1)}, bf16[1,512,192]{2,1,0:T(8,128)(2,1)}, f32[1,512,128]{2,1,0:T(8,128)}, f32[512,768]{1,0:T(8,128)}, bf16[512,768]{1,0:T(8,128)(2,1)}) custom-call(s32[11]{0:T(128)} %pad_add_fusion.ids_ref, bf16[512,768]{1,0:T(8,128)(2,1)} %fusion.2.refs_0_, bf16[3,3,96,768]{3,2,1,0:T(8,128)(2,1)} %copy-done.2, ...), custom_call_target="tpu_custom_call" | custom-call | flops 16000000000 | bytes 16000000 | tf_op jit(solution)/shard_map/attn_fwd/pallas_call | solution.py:263
  82.7 1.6 collective-permute-start.17
  84.2 13.9 %ffn.2 = (f32[512,768]{1,0:T(8,128)}, f32[512,768]{1,0:T(8,128)}, bf16[4,384,768]{2,1,0:T(8,128)(2,1)}, bf16[4,384,768]{2,1,0:T(8,128)(2,1)}) custom-call(s32[11]{0:T(128)} %pad_add_fusion.ids_ref, bf16[512,768]{1,0:T(8,128)(2,1)} %get-tuple-element.257.refs_0_, bf16[512,768]{1,0:T(8,128)(2,1)} %refs_1_.5, bf16[768,768]{1,0:T(8,128)(2,1)} %refs_2_.3, ...), custom_call_target="tpu_custom_call" | custom-call | flops 64000000000 | bytes 64000000 | tf_op jit(solution)/shard_map/ffn/pallas_call | solution.py:636
  98.3 1.5 collective-permute-done.17.refs_7_
  100.4 4.4 %collective-permute-done.22.refs_9_ = bf16[2,2,96,768]{3,2,1,0:T(8,128)(2,1)S(1)} collective-permute-done((bf16[2,2,96,768]{3,2,1,0:T(8,128)(2,1)S(1)}, bf16[2,2,96,768]{3,2,1,0:T(8,128)(2,1)S(1)}, u32[]{:S(2)}, u32[]{:S(2)}) %collective-permute-start.22) | collective-permute-done | bytes 589856 | tf_op jit(solution)/shard_map/ppermute | solution.py:952
  106.5 1.7 copy-done.1
  108.1 1.8 fold.12
  110.0 1.5 collective-permute-start.24
  112.0 14.0 %ffn.3 = (bf16[512,768]{1,0:T(8,128)(2,1)}, bf16[4,384,768]{2,1,0:T(8,128)(2,1)}, bf16[4,384,768]{2,1,0:T(8,128)(2,1)}, f32[512,768]{1,0:T(8,128)}, bf16[512,768]{1,0:T(8,128)(2,1)}, /*index=5*/f32[8,768]{1,0:T(8,128)}) custom-call(s32[11]{0:T(128)} %pad_add_fusion.ids_ref, bf16[512,768]{1,0:T(8,128)(2,1)} %get-tuple-element.257.refs_0_, ...), custom_call_target="tpu_custom_call" | custom-call | flops 64000000000 | bytes 64000000 | tf_op jit(solution)/shard_map/ffn/pallas_call | solution.py:636
  126.8 1.3 fold.13
  129.5 2.0 collective-permute-done.28.refs_1_
  131.5 2.0 fold.14
  134.9 15.9 %attn_bwd.2 = (bf16[2,384,768]{2,1,0:T(8,128)(2,1)}, bf16[2,384,768]{2,1,0:T(8,128)(2,1)}, f32[512,768]{1,0:T(8,128)}, f32[2,8,128]{2,1,0:T(8,128)}) custom-call(s32[11]{0:T(128)} %pad_add_fusion.ids_ref, bf16[512,768]{1,0:T(8,128)(2,1)} %fusion.2.refs_0_, bf16[512,768]{1,0:T(8,128)(2,1)} %get-tuple-element.315.refs_1_, ...), custom_call_target="tpu_custom_call" | custom-call | flops 64000000000 | bytes 64000000 | tf_op jit(solution)/shard_map/attn_bwd/pallas_call | solution.py:503
  152.1 1.6 fold.16
  154.4 1.3 collective-permute-start.31
  155.6 1.5 collective-permute-start.32
  159.5 17.2 %attn_bwd.3 = (bf16[2,400,768]{2,1,0:T(8,128)(2,1)}, bf16[2,400,768]{2,1,0:T(8,128)(2,1)}, bf16[512,768]{1,0:T(8,128)(2,1)}) custom-call(s32[11]{0:T(128)} %pad_add_fusion.ids_ref, bf16[512,768]{1,0:T(8,128)(2,1)} %fusion.2.refs_0_, bf16[512,768]{1,0:T(8,128)(2,1)} %get-tuple-element.315.refs_1_, bf16[128,512]{1,0:T(8,128)(2,1)} %constant.22.clone.refs_6_.refs_2_, ...), custom_call_target="tpu_custom_call" | custom-call | flops 64000000000 | bytes 64000000 | tf_op jit(solution)/shard_map/attn_bwd/pallas_call | solution.py:503
  178.2 1.3 collective-permute-start.42
  179.5 1.5 collective-permute-start.43
  183.6 3.8 %collective-permute-start.37 = (bf16[2,96,768]{2,1,0:T(8,128)(2,1)S(1)}, bf16[2,96,768]{2,1,0:T(8,128)(2,1)S(1)}, u32[]{:S(2)}, u32[]{:S(2)}) collective-permute-start(bf16[2,96,768]{2,1,0:T(8,128)(2,1)S(1)} %get-tuple-element.402), channel_id=1, source_target_pairs={{0,3},{1,0},{2,1},{3,2},{4,7},{5,4},{6,5},{7,6},{8,11},{9,8},{10,9... | collective-permute-start | bytes 884744 | tf_op jit(solution)/shard_map/ppermute | solution.py:958
  188.1 3.7 %collective-permute-done.40.refs_1_ = bf16[1,192,768]{2,1,0:T(8,128)(2,1)S(1)} collective-permute-done((bf16[1,192,768]{2,1,0:T(8,128)(2,1)S(1)}, bf16[1,192,768]{2,1,0:T(8,128)(2,1)S(1)}, u32[]{:S(2)}, u32[]{:S(2)}) %collective-permute-start.40) | collective-permute-done | bytes 294944 | tf_op jit(solution)/shard_map/ppermute | solution.py:952
  192.5 1.6 collective-permute-start.45
  194.8 4.3 %collective-permute-done.44.refs_1_ = bf16[1,96,768]{2,1,0:T(8,128)(2,1)S(1)} collective-permute-done((bf16[1,96,768]{2,1,0:T(8,128)(2,1)S(1)}, bf16[1,96,768]{2,1,0:T(8,128)(2,1)S(1)}, u32[]{:S(2)}, u32[]{:S(2)}) %collective-permute-start.44) | collective-permute-done | bytes 147488 | tf_op jit(solution)/shard_map/ppermute | solution.py:952
  200.0 8.1 %collective-permute-done.38.refs_3_ = bf16[2,96,768]{2,1,0:T(8,128)(2,1)S(1)} collective-permute-done((bf16[2,96,768]{2,1,0:T(8,128)(2,1)S(1)}, bf16[2,96,768]{2,1,0:T(8,128)(2,1)S(1)}, u32[]{:S(2)}, u32[]{:S(2)}) %collective-permute-start.38) | collective-permute-done | bytes 294944 | tf_op jit(solution)/shard_map/ppermute | solution.py:958
  210.4 1.4 collective-permute-start.48
  211.8 2.4 %collective-permute-start.51 = (bf16[112,768]{1,0:T(8,128)(2,1)S(1)}, bf16[112,768]{1,0:T(8,128)(2,1)S(1)}, u32[]{:S(2)}, u32[]{:S(2)}) collective-permute-start(bf16[112,768]{1,0:T(8,128)(2,1)S(1)} %get-tuple-element.371), channel_id=1, source_target_pairs={{0,3},{1,0},{2,1},{3,2},{4,7},{5,4},{6,5},{7,6},{8,11},{9,8},{10,9... | collective-permute-start | bytes 516104 | tf_op jit(solution)/shard_map/ppermute | solution.py:958
  214.2 7.3 %collective-permute-done.50.refs_2_ = bf16[112,768]{1,0:T(8,128)(2,1)S(1)} collective-permute-done((bf16[112,768]{1,0:T(8,128)(2,1)S(1)}, bf16[112,768]{1,0:T(8,128)(2,1)S(1)}, u32[]{:S(2)}, u32[]{:S(2)}) %collective-permute-start.50) | collective-permute-done | bytes 172064 | tf_op jit(solution)/shard_map/ppermute | solution.py:958
  222.6 1.5 collective-permute-start.53
  224.8 1.4 collective-permute-start.55
  226.2 3.0 %finish.2 = (f32[768,768]{1,0:T(8,128)}, f32[768,768]{1,0:T(8,128)}) custom-call(s32[11]{0:T(128)S(1)} %copy-done.11, bf16[4,2,96,768]{3,2,1,0:T(8,128)(2,1)S(1)} %cat.10.refs_0_, bf16[4,2,96,768]{3,2,1,0:T(8,128)(2,1)S(1)} %collective-permute-done.52.refs_1_), custom_call_target="tpu_custom_call" | custom-call | tf_op jit(solution)/shard_map/finish/pallas_call | solution.py:916
  229.3 2.1 collective-permute-done.54.refs_2_
  231.4 1.8 collective-permute-done.55.refs_3_
  235.4 2.1 finish.3
  (166 shorter events, 37.9 us)
Async XLA Ops:
  5.2 14.7 %collective-permute-start = (bf16[112,768]{1,0:T(8,128)(2,1)}, bf16[112,768]{1,0:T(8,128)(2,1)S(1)}, u32[]{:S(2)}, u32[]{:S(2)}) collective-permute-start(bf16[112,768]{1,0:T(8,128)(2,1)} %get-tuple-element.205), channel_id=1, source_target_pairs={{0,3},{1,0},{2,1},{3,2},{4,7},{5,4},{6,5},{7,6},{8,11},{9,8},{10,9... | collective-permute-start | bytes 516104 | tf_op jit(solution)/shard_map/ppermute | solution.py:955
  10.3 14.8 %collective-permute-start.1 = (bf16[112,768]{1,0:T(8,128)(2,1)}, bf16[112,768]{1,0:T(8,128)(2,1)S(1)}, u32[]{:S(2)}, u32[]{:S(2)}) collective-permute-start(bf16[112,768]{1,0:T(8,128)(2,1)} %get-tuple-element.205), channel_id=1, source_target_pairs={{0,2},{1,3},{2,0},{3,1},{4,6},{5,7},{6,4},{7,5},{8,10},{9,11},{10,... | collective-permute-start | bytes 516104 | tf_op jit(solution)/shard_map/ppermute | solution.py:955
  10.3 14.8 %collective-permute-start.2 = (bf16[112,768]{1,0:T(8,128)(2,1)}, bf16[112,768]{1,0:T(8,128)(2,1)S(1)}, u32[]{:S(2)}, u32[]{:S(2)}) collective-permute-start(bf16[112,768]{1,0:T(8,128)(2,1)} %get-tuple-element.205), channel_id=1, source_target_pairs={{0,1},{1,2},{2,3},{3,0},{4,5},{5,6},{6,7},{7,4},{8,9},{9,10},{10,1... | collective-permute-start | bytes 516104 | tf_op jit(solution)/shard_map/ppermute | solution.py:955
  25.8 11.8 %collective-permute-start.3 = (bf16[3,96,768]{2,1,0:T(8,128)(2,1)S(1)}, bf16[3,96,768]{2,1,0:T(8,128)(2,1)S(1)}, u32[]{:S(2)}, u32[]{:S(2)}) collective-permute-start(bf16[3,96,768]{2,1,0:T(8,128)(2,1)S(1)} %get-tuple-element.215.refs_0_), channel_id=1, source_target_pairs={{0,8},{4,12},{8,0},{12,4},{16,24},{20,28},{24,16},{28,20},{1,9},{5... | collective-permute-start | bytes 1327112 | tf_op jit(solution)/shard_map/ppermute | solution.py:952
  27.2 11.5 %collective-permute-start.4 = (bf16[3,96,768]{2,1,0:T(8,128)(2,1)S(1)}, bf16[3,96,768]{2,1,0:T(8,128)(2,1)S(1)}, u32[]{:S(2)}, u32[]{:S(2)}) collective-permute-start(bf16[3,96,768]{2,1,0:T(8,128)(2,1)S(1)} %get-tuple-element.215.refs_0_), channel_id=1, source_target_pairs={{0,16},{4,20},{8,24},{12,28},{16,0},{20,4},{24,8},{28,12},{1,17},{... | collective-permute-start | bytes 1327112 | tf_op jit(solution)/shard_map/ppermute | solution.py:952
  28.8 8.1 %collective-permute-start.5 = (bf16[2,96,768]{2,1,0:T(8,128)(2,1)S(1)}, bf16[2,96,768]{2,1,0:T(8,128)(2,1)S(1)}, u32[]{:S(2)}, u32[]{:S(2)}) collective-permute-start(bf16[2,96,768]{2,1,0:T(8,128)(2,1)S(1)} %copy-done.27), channel_id=1, source_target_pairs={{0,3},{1,0},{2,1},{3,2},{4,7},{5,4},{6,5},{7,6},{8,11},{9,8},{10,9... | collective-permute-start | bytes 884744 | tf_op jit(solution)/shard_map/ppermute | solution.py:955
  38.8 13.0 %collective-permute-start.7 = (bf16[3,3,96,768]{3,2,1,0:T(8,128)(2,1)S(1)}, bf16[3,3,96,768]{3,2,1,0:T(8,128)(2,1)S(1)}, u32[]{:S(2)}, u32[]{:S(2)}) collective-permute-start(bf16[3,3,96,768]{3,2,1,0:T(8,128)(2,1)S(1)} %cat.6.refs_1_.refs_3_), channel_id=1, source_target_pairs={{0,4},{4,0},{8,12},{12,8},{16,20},{20,16},{24,28},{28,24},{1,5},{5... | collective-permute-start | bytes 3981320 | tf_op jit(solution)/shard_map/ppermute | solution.py:952
  38.9 12.9 %collective-permute-start.6 = (bf16[3,96,768]{2,1,0:T(8,128)(2,1)S(1)}, bf16[3,96,768]{2,1,0:T(8,128)(2,1)S(1)}, u32[]{:S(2)}, u32[]{:S(2)}) collective-permute-start(bf16[3,96,768]{2,1,0:T(8,128)(2,1)S(1)} %collective-permute-done.3.refs_1_), channel_id=1, source_target_pairs={{0,16},{4,20},{8,24},{12,28},{16,0},{20,4},{24,8},{28,12},{1,17},{... | collective-permute-start | bytes 1327112 | tf_op jit(solution)/shard_map/ppermute | solution.py:952
  40.5 9.1 %collective-permute-start.8 = (bf16[2,96,768]{2,1,0:T(8,128)(2,1)S(1)}, bf16[2,96,768]{2,1,0:T(8,128)(2,1)S(1)}, u32[]{:S(2)}, u32[]{:S(2)}) collective-permute-start(bf16[2,96,768]{2,1,0:T(8,128)(2,1)S(1)} %collective-permute-done.5.refs_0_), channel_id=1, source_target_pairs={{0,8},{4,12},{8,0},{12,4},{16,24},{20,28},{24,16},{28,20},{1,9},{5... | collective-permute-start | bytes 884744 | tf_op jit(solution)/shard_map/ppermute | solution.py:952
  41.0 10.8 %collective-permute-start.9 = (bf16[2,96,768]{2,1,0:T(8,128)(2,1)S(1)}, bf16[2,96,768]{2,1,0:T(8,128)(2,1)S(1)}, u32[]{:S(2)}, u32[]{:S(2)}) collective-permute-start(bf16[2,96,768]{2,1,0:T(8,128)(2,1)S(1)} %copy-done.27), channel_id=1, source_target_pairs={{0,1},{1,2},{2,3},{3,0},{4,5},{5,6},{6,7},{7,4},{8,9},{9,10},{10,1... | collective-permute-start | bytes 884744 | tf_op jit(solution)/shard_map/ppermute | solution.py:955
  53.6 18.1 %collective-permute-start.13 = (bf16[2,2,96,768]{3,2,1,0:T(8,128)(2,1)S(1)}, bf16[2,2,96,768]{3,2,1,0:T(8,128)(2,1)}, u32[]{:S(2)}, u32[]{:S(2)}) collective-permute-start(bf16[2,2,96,768]{3,2,1,0:T(8,128)(2,1)S(1)} %cat.7.refs_4_), channel_id=1, source_target_pairs={{0,16},{4,20},{8,24},{12,28},{16,0},{20,4},{24,8},{28,12},{1,17},{... | collective-permute-start | bytes 1769480 | tf_op jit(solution)/shard_map/ppermute | solution.py:952
  54.8 26.9 %collective-permute-start.15 = (bf16[2,2,96,768]{3,2,1,0:T(8,128)(2,1)S(1)}, bf16[2,2,96,768]{3,2,1,0:T(8,128)(2,1)}, u32[]{:S(2)}, u32[]{:S(2)}) collective-permute-start(bf16[2,2,96,768]{3,2,1,0:T(8,128)(2,1)S(1)} %cat.7.refs_4_), channel_id=1, source_target_pairs={{0,4},{4,0},{8,12},{12,8},{16,20},{20,16},{24,28},{28,24},{1,5},{5... | collective-permute-start | bytes 1769480 | tf_op jit(solution)/shard_map/ppermute | solution.py:952
  55.1 14.2 %collective-permute-start.11 = (bf16[2,96,768]{2,1,0:T(8,128)(2,1)S(1)}, bf16[2,96,768]{2,1,0:T(8,128)(2,1)S(1)}, u32[]{:S(2)}, u32[]{:S(2)}) collective-permute-start(bf16[2,96,768]{2,1,0:T(8,128)(2,1)S(1)} %collective-permute-done.9.refs_0_), channel_id=1, source_target_pairs={{0,8},{4,12},{8,0},{12,4},{16,24},{20,28},{24,16},{28,20},{1,9},{5... | collective-permute-start | bytes 884744 | tf_op jit(solution)/shard_map/ppermute | solution.py:952
  55.9 15.8 %collective-permute-start.12 = (bf16[2,96,768]{2,1,0:T(8,128)(2,1)S(1)}, bf16[2,96,768]{2,1,0:T(8,128)(2,1)S(1)}, u32[]{:S(2)}, u32[]{:S(2)}) collective-permute-start(bf16[2,96,768]{2,1,0:T(8,128)(2,1)S(1)} %copy-done.27), channel_id=1, source_target_pairs={{0,2},{1,3},{2,0},{3,1},{4,6},{5,7},{6,4},{7,5},{8,10},{9,11},{10,... | collective-permute-start | bytes 884744 | tf_op jit(solution)/shard_map/ppermute | solution.py:955
  71.7 26.5 %collective-permute-start.18 = (bf16[2,2,96,768]{3,2,1,0:T(8,128)(2,1)S(1)}, bf16[2,2,96,768]{3,2,1,0:T(8,128)(2,1)S(1)}, u32[]{:S(2)}, u32[]{:S(2)}) collective-permute-start(bf16[2,2,96,768]{3,2,1,0:T(8,128)(2,1)S(1)} %cat.9.refs_2_), channel_id=1, source_target_pairs={{0,16},{4,20},{8,24},{12,28},{16,0},{20,4},{24,8},{28,12},{1,17},{... | collective-permute-start | bytes 1769480 | tf_op jit(solution)/shard_map/ppermute | solution.py:952
  72.3 25.9 %collective-permute-start.20 = (bf16[2,2,96,768]{3,2,1,0:T(8,128)(2,1)S(1)}, bf16[2,2,96,768]{3,2,1,0:T(8,128)(2,1)S(1)}, u32[]{:S(2)}, u32[]{:S(2)}) collective-permute-start(bf16[2,2,96,768]{3,2,1,0:T(8,128)(2,1)S(1)} %cat.9.refs_2_), channel_id=1, source_target_pairs={{0,4},{4,0},{8,12},{12,8},{16,20},{20,16},{24,28},{28,24},{1,5},{5... | collective-permute-start | bytes 1769480 | tf_op jit(solution)/shard_map/ppermute | solution.py:952
  72.3 9.5 %collective-permute-start.16 = (bf16[2,2,96,768]{3,2,1,0:T(8,128)(2,1)}, bf16[2,2,96,768]{3,2,1,0:T(8,128)(2,1)S(1)}, u32[]{:S(2)}, u32[]{:S(2)}) collective-permute-start(bf16[2,2,96,768]{3,2,1,0:T(8,128)(2,1)} %collective-permute-done.13.refs_5_), channel_id=1, source_target_pairs={{0,4},{4,0},{8,12},{12,8},{16,20},{20,16},{24,28},{28,24},{1,5},{5... | collective-permute-start | bytes 1769480 | tf_op jit(solution)/shard_map/ppermute | solution.py:952
  72.8 8.9 %collective-permute-start.14 = (bf16[2,96,768]{2,1,0:T(8,128)(2,1)S(1)}, bf16[2,96,768]{2,1,0:T(8,128)(2,1)S(1)}, u32[]{:S(2)}, u32[]{:S(2)}) collective-permute-start(bf16[2,96,768]{2,1,0:T(8,128)(2,1)S(1)} %collective-permute-done.12.refs_0_), channel_id=1, source_target_pairs={{0,8},{4,12},{8,0},{12,4},{16,24},{20,28},{24,16},{28,20},{1,9},{5... | collective-permute-start | bytes 884744 | tf_op jit(solution)/shard_map/ppermute | solution.py:952
  82.7 17.0 %collective-permute-start.17 = (bf16[2,2,96,768]{3,2,1,0:T(8,128)(2,1)S(1)}, bf16[2,2,96,768]{3,2,1,0:T(8,128)(2,1)S(1)}, u32[]{:S(2)}, u32[]{:S(2)}) collective-permute-start(bf16[2,2,96,768]{3,2,1,0:T(8,128)(2,1)S(1)} %cat.8.refs_6_), channel_id=1, source_target_pairs={{0,16},{4,20},{8,24},{12,28},{16,0},{20,4},{24,8},{28,12},{1,17},{... | collective-permute-start | bytes 1769480 | tf_op jit(solution)/shard_map/ppermute | solution.py:952
  84.2 15.5 %collective-permute-start.19 = (bf16[2,2,96,768]{3,2,1,0:T(8,128)(2,1)S(1)}, bf16[2,2,96,768]{3,2,1,0:T(8,128)(2,1)S(1)}, u32[]{:S(2)}, u32[]{:S(2)}) collective-permute-start(bf16[2,2,96,768]{3,2,1,0:T(8,128)(2,1)S(1)} %cat.8.refs_6_), channel_id=1, source_target_pairs={{0,4},{4,0},{8,12},{12,8},{16,20},{20,16},{24,28},{28,24},{1,5},{5... | collective-permute-start | bytes 1769480 | tf_op jit(solution)/shard_map/ppermute | solution.py:952
  99.7 6.7 %collective-permute-start.21 = (bf16[4,384,768]{2,1,0:T(8,128)(2,1)}, bf16[4,384,768]{2,1,0:T(8,128)(2,1)S(1)}, u32[]{:S(2)}, u32[]{:S(2)}) collective-permute-start(bf16[4,384,768]{2,1,0:T(8,128)(2,1)} %get-tuple-element.244), channel_id=1, source_target_pairs={{0,4},{4,0},{8,12},{12,8},{16,20},{20,16},{24,28},{28,24},{1,5},{5... | collective-permute-start | bytes 7077896 | tf_op jit(solution)/shard_map/ppermute | solution.py:952
  110.0 16.0 %collective-permute-start.24 = (bf16[2,192,768]{2,1,0:T(8,128)(2,1)}, bf16[2,192,768]{2,1,0:T(8,128)(2,1)S(1)}, u32[]{:S(2)}, u32[]{:S(2)}) collective-permute-start(bf16[2,192,768]{2,1,0:T(8,128)(2,1)} %get-tuple-element.266), channel_id=1, source_target_pairs={{0,8},{4,12},{8,0},{12,4},{16,24},{20,28},{24,16},{28,20},{1,9},{5... | collective-permute-start | bytes 1769480 | tf_op jit(solution)/shard_map/ppermute | solution.py:952
  111.5 15.3 %collective-permute-start.25 = (bf16[2,192,768]{2,1,0:T(8,128)(2,1)S(1)}, bf16[2,192,768]{2,1,0:T(8,128)(2,1)S(1)}, u32[]{:S(2)}, u32[]{:S(2)}) collective-permute-start(bf16[2,192,768]{2,1,0:T(8,128)(2,1)S(1)} %get-tuple-element.267), channel_id=1, source_target_pairs={{0,16},{4,20},{8,24},{12,28},{16,0},{20,4},{24,8},{28,12},{1,17},{... | collective-permute-start | bytes 1769480 | tf_op jit(solution)/shard_map/ppermute | solution.py:952
  128.1 22.7 %collective-permute-start.26 = (bf16[2,96,768]{2,1,0:T(8,128)(2,1)}, bf16[2,96,768]{2,1,0:T(8,128)(2,1)S(1)}, u32[]{:S(2)}, u32[]{:S(2)}) collective-permute-start(bf16[2,96,768]{2,1,0:T(8,128)(2,1)} %get-tuple-element.274), channel_id=1, source_target_pairs={{0,16},{4,20},{8,24},{12,28},{16,0},{20,4},{24,8},{28,12},{1,17},{... | collective-permute-start | bytes 884744 | tf_op jit(solution)/shard_map/ppermute | solution.py:952
  129.0 21.8 %collective-permute-start.27 = (bf16[2,96,768]{2,1,0:T(8,128)(2,1)S(1)}, bf16[2,96,768]{2,1,0:T(8,128)(2,1)S(1)}, u32[]{:S(2)}, u32[]{:S(2)}) collective-permute-start(bf16[2,96,768]{2,1,0:T(8,128)(2,1)S(1)} %get-tuple-element.275), channel_id=1, source_target_pairs={{0,8},{4,12},{8,0},{12,4},{16,24},{20,28},{24,16},{28,20},{1,9},{5... | collective-permute-start | bytes 884744 | tf_op jit(solution)/shard_map/ppermute | solution.py:952
  133.6 17.3 %collective-permute-start.29 = (bf16[2,192,768]{2,1,0:T(8,128)(2,1)}, bf16[2,192,768]{2,1,0:T(8,128)(2,1)S(1)}, u32[]{:S(2)}, u32[]{:S(2)}) collective-permute-start(bf16[2,192,768]{2,1,0:T(8,128)(2,1)} %get-tuple-element.282), channel_id=1, source_target_pairs={{0,8},{4,12},{8,0},{12,4},{16,24},{20,28},{24,16},{28,20},{1,9},{5... | collective-permute-start | bytes 1769480 | tf_op jit(solution)/shard_map/ppermute | solution.py:952
  134.1 16.7 %collective-permute-start.30 = (bf16[2,192,768]{2,1,0:T(8,128)(2,1)}, bf16[2,192,768]{2,1,0:T(8,128)(2,1)S(1)}, u32[]{:S(2)}, u32[]{:S(2)}) collective-permute-start(bf16[2,192,768]{2,1,0:T(8,128)(2,1)} %get-tuple-element.283), channel_id=1, source_target_pairs={{0,16},{4,20},{8,24},{12,28},{16,0},{20,4},{24,8},{28,12},{1,17},{... | collective-permute-start | bytes 1769480 | tf_op jit(solution)/shard_map/ppermute | solution.py:952
  154.4 22.3 %collective-permute-start.31 = (bf16[2,96,768]{2,1,0:T(8,128)(2,1)}, bf16[2,96,768]{2,1,0:T(8,128)(2,1)S(1)}, u32[]{:S(2)}, u32[]{:S(2)}) collective-permute-start(bf16[2,96,768]{2,1,0:T(8,128)(2,1)} %get-tuple-element.298), channel_id=1, source_target_pairs={{0,16},{4,20},{8,24},{12,28},{16,0},{20,4},{24,8},{28,12},{1,17},{... | collective-permute-start | bytes 884744 | tf_op jit(solution)/shard_map/ppermute | solution.py:952
  155.6 21.1 %collective-permute-start.32 = (bf16[2,96,768]{2,1,0:T(8,128)(2,1)}, bf16[2,96,768]{2,1,0:T(8,128)(2,1)S(1)}, u32[]{:S(2)}, u32[]{:S(2)}) collective-permute-start(bf16[2,96,768]{2,1,0:T(8,128)(2,1)} %get-tuple-element.299), channel_id=1, source_target_pairs={{0,8},{4,12},{8,0},{12,4},{16,24},{20,28},{24,16},{28,20},{1,9},{5... | collective-permute-start | bytes 884744 | tf_op jit(solution)/shard_map/ppermute | solution.py:952
  157.2 19.5 %collective-permute-start.36 = (bf16[2,96,768]{2,1,0:T(8,128)(2,1)S(1)}, bf16[2,96,768]{2,1,0:T(8,128)(2,1)S(1)}, u32[]{:S(2)}, u32[]{:S(2)}) collective-permute-start(bf16[2,96,768]{2,1,0:T(8,128)(2,1)S(1)} %get-tuple-element.403), channel_id=1, source_target_pairs={{0,1},{1,2},{2,3},{3,0},{4,5},{5,6},{6,7},{7,4},{8,9},{9,10},{10,1... | collective-permute-start | bytes 884744 | tf_op jit(solution)/shard_map/ppermute | solution.py:958
  158.1 18.6 %collective-permute-start.34 = (bf16[1,192,768]{2,1,0:T(8,128)(2,1)S(1)}, bf16[1,192,768]{2,1,0:T(8,128)(2,1)S(1)}, u32[]{:S(2)}, u32[]{:S(2)}) collective-permute-start(bf16[1,192,768]{2,1,0:T(8,128)(2,1)S(1)} %get-tuple-element.309), channel_id=1, source_target_pairs={{0,8},{4,12},{8,0},{12,4},{16,24},{20,28},{24,16},{28,20},{1,9},{5... | collective-permute-start | bytes 884744 | tf_op jit(solution)/shard_map/ppermute | solution.py:952
  158.7 18.0 %collective-permute-start.35 = (bf16[1,192,768]{2,1,0:T(8,128)(2,1)S(1)}, bf16[1,192,768]{2,1,0:T(8,128)(2,1)S(1)}, u32[]{:S(2)}, u32[]{:S(2)}) collective-permute-start(bf16[1,192,768]{2,1,0:T(8,128)(2,1)S(1)} %get-tuple-element.310), channel_id=1, source_target_pairs={{0,16},{4,20},{8,24},{12,28},{16,0},{20,4},{24,8},{28,12},{1,17},{... | collective-permute-start | bytes 884744 | tf_op jit(solution)/shard_map/ppermute | solution.py:952
  178.2 9.2 %collective-permute-start.42 = (bf16[1,96,768]{2,1,0:T(8,128)(2,1)S(1)}, bf16[1,96,768]{2,1,0:T(8,128)(2,1)S(1)}, u32[]{:S(2)}, u32[]{:S(2)}) collective-permute-start(bf16[1,96,768]{2,1,0:T(8,128)(2,1)S(1)} %get-tuple-element.344), channel_id=1, source_target_pairs={{0,16},{4,20},{8,24},{12,28},{16,0},{20,4},{24,8},{28,12},{1,17},{... | collective-permute-start | bytes 442376 | tf_op jit(solution)/shard_map/ppermute | solution.py:952
  179.5 8.0 %collective-permute-start.43 = (bf16[1,96,768]{2,1,0:T(8,128)(2,1)S(1)}, bf16[1,96,768]{2,1,0:T(8,128)(2,1)S(1)}, u32[]{:S(2)}, u32[]{:S(2)}) collective-permute-start(bf16[1,96,768]{2,1,0:T(8,128)(2,1)S(1)} %get-tuple-element.345), channel_id=1, source_target_pairs={{0,8},{4,12},{8,0},{12,4},{16,24},{20,28},{24,16},{28,20},{1,9},{5... | collective-permute-start | bytes 442376 | tf_op jit(solution)/shard_map/ppermute | solution.py:952
  181.8 9.9 %collective-permute-start.41 = (bf16[1,208,768]{2,1,0:T(8,128)(2,1)S(1)}, bf16[1,208,768]{2,1,0:T(8,128)(2,1)S(1)}, u32[]{:S(2)}, u32[]{:S(2)}) collective-permute-start(bf16[1,208,768]{2,1,0:T(8,128)(2,1)S(1)} %get-tuple-element.343), channel_id=1, source_target_pairs={{0,16},{4,20},{8,24},{12,28},{16,0},{20,4},{24,8},{28,12},{1,17},{... | collective-permute-start | bytes 958472 | tf_op jit(solution)/shard_map/ppermute | solution.py:952
  182.7 9.1 %collective-permute-start.40 = (bf16[1,192,768]{2,1,0:T(8,128)(2,1)S(1)}, bf16[1,192,768]{2,1,0:T(8,128)(2,1)S(1)}, u32[]{:S(2)}, u32[]{:S(2)}) collective-permute-start(bf16[1,192,768]{2,1,0:T(8,128)(2,1)S(1)} %get-tuple-element.342), channel_id=1, source_target_pairs={{0,8},{4,12},{8,0},{12,4},{16,24},{20,28},{24,16},{28,20},{1,9},{5... | collective-permute-start | bytes 884744 | tf_op jit(solution)/shard_map/ppermute | solution.py:952
  183.6 16.4 %collective-permute-start.37 = (bf16[2,96,768]{2,1,0:T(8,128)(2,1)S(1)}, bf16[2,96,768]{2,1,0:T(8,128)(2,1)S(1)}, u32[]{:S(2)}, u32[]{:S(2)}) collective-permute-start(bf16[2,96,768]{2,1,0:T(8,128)(2,1)S(1)} %get-tuple-element.402), channel_id=1, source_target_pairs={{0,3},{1,0},{2,1},{3,2},{4,7},{5,4},{6,5},{7,6},{8,11},{9,8},{10,9... | collective-permute-start | bytes 884744 | tf_op jit(solution)/shard_map/ppermute | solution.py:958
  187.4 20.7 %collective-permute-start.38 = (bf16[2,96,768]{2,1,0:T(8,128)(2,1)S(1)}, bf16[2,96,768]{2,1,0:T(8,128)(2,1)S(1)}, u32[]{:S(2)}, u32[]{:S(2)}) collective-permute-start(bf16[2,96,768]{2,1,0:T(8,128)(2,1)S(1)} %get-tuple-element.401), channel_id=1, source_target_pairs={{0,2},{1,3},{2,0},{3,1},{4,6},{5,7},{6,4},{7,5},{8,10},{9,11},{10,... | collective-permute-start | bytes 884744 | tf_op jit(solution)/shard_map/ppermute | solution.py:958
  192.5 6.7 %collective-permute-start.45 = (bf16[1,112,768]{2,1,0:T(8,128)(2,1)S(1)}, bf16[1,112,768]{2,1,0:T(8,128)(2,1)S(1)}, u32[]{:S(2)}, u32[]{:S(2)}) collective-permute-start(bf16[1,112,768]{2,1,0:T(8,128)(2,1)S(1)} %get-tuple-element.356), channel_id=1, source_target_pairs={{0,8},{4,12},{8,0},{12,4},{16,24},{20,28},{24,16},{28,20},{1,9},{5... | collective-permute-start | bytes 516104 | tf_op jit(solution)/shard_map/ppermute | solution.py:952
  199.9 12.0 %collective-permute-start.49 = (bf16[112,768]{1,0:T(8,128)(2,1)S(1)}, bf16[112,768]{1,0:T(8,128)(2,1)S(1)}, u32[]{:S(2)}, u32[]{:S(2)}) collective-permute-start(bf16[112,768]{1,0:T(8,128)(2,1)S(1)} %get-tuple-element.369), channel_id=1, source_target_pairs={{0,1},{1,2},{2,3},{3,0},{4,5},{5,6},{6,7},{7,4},{8,9},{9,10},{10,1... | collective-permute-start | bytes 516104 | tf_op jit(solution)/shard_map/ppermute | solution.py:958
  208.2 13.3 %collective-permute-start.46 = (bf16[2,96,768]{2,1,0:T(8,128)(2,1)S(1)}, bf16[2,96,768]{2,1,0:T(8,128)(2,1)S(1)}, u32[]{:S(2)}, u32[]{:S(2)}) collective-permute-start(bf16[2,96,768]{2,1,0:T(8,128)(2,1)S(1)} %total.1.refs_0_), channel_id=1, source_target_pairs={{0,8},{4,12},{8,0},{12,4},{16,24},{20,28},{24,16},{28,20},{1,9},{5... | collective-permute-start | bytes 884744 | tf_op jit(solution)/shard_map/ppermute | solution.py:952
  209.2 13.2 %collective-permute-start.47 = (bf16[2,96,768]{2,1,0:T(8,128)(2,1)S(1)}, bf16[2,96,768]{2,1,0:T(8,128)(2,1)S(1)}, u32[]{:S(2)}, u32[]{:S(2)}) collective-permute-start(bf16[2,96,768]{2,1,0:T(8,128)(2,1)S(1)} %total.1.refs_0_), channel_id=1, source_target_pairs={{0,16},{4,20},{8,24},{12,28},{16,0},{20,4},{24,8},{28,12},{1,17},{... | collective-permute-start | bytes 884744 | tf_op jit(solution)/shard_map/ppermute | solution.py:952
  210.4 12.0 %collective-permute-start.48 = (bf16[2,96,768]{2,1,0:T(8,128)(2,1)S(1)}, bf16[2,96,768]{2,1,0:T(8,128)(2,1)S(1)}, u32[]{:S(2)}, u32[]{:S(2)}) collective-permute-start(bf16[2,96,768]{2,1,0:T(8,128)(2,1)S(1)} %total.1.refs_0_), channel_id=1, source_target_pairs={{0,24},{4,28},{8,16},{12,20},{16,8},{20,12},{24,0},{28,4},{1,25},{... | collective-permute-start | bytes 884744 | tf_op jit(solution)/shard_map/ppermute | solution.py:952
  211.8 9.7 %collective-permute-start.50 = (bf16[112,768]{1,0:T(8,128)(2,1)S(1)}, bf16[112,768]{1,0:T(8,128)(2,1)S(1)}, u32[]{:S(2)}, u32[]{:S(2)}) collective-permute-start(bf16[112,768]{1,0:T(8,128)(2,1)S(1)} %get-tuple-element.370), channel_id=1, source_target_pairs={{0,2},{1,3},{2,0},{3,1},{4,6},{5,7},{6,4},{7,5},{8,10},{9,11},{10,... | collective-permute-start | bytes 516104 | tf_op jit(solution)/shard_map/ppermute | solution.py:958
  211.8 9.7 %collective-permute-start.51 = (bf16[112,768]{1,0:T(8,128)(2,1)S(1)}, bf16[112,768]{1,0:T(8,128)(2,1)S(1)}, u32[]{:S(2)}, u32[]{:S(2)}) collective-permute-start(bf16[112,768]{1,0:T(8,128)(2,1)S(1)} %get-tuple-element.371), channel_id=1, source_target_pairs={{0,3},{1,0},{2,1},{3,2},{4,7},{5,4},{6,5},{7,6},{8,11},{9,8},{10,9... | collective-permute-start | bytes 516104 | tf_op jit(solution)/shard_map/ppermute | solution.py:958
  222.6 6.7 %collective-permute-start.53 = (bf16[1,96,768]{2,1,0:T(8,128)(2,1)S(1)}, bf16[1,96,768]{2,1,0:T(8,128)(2,1)S(1)}, u32[]{:S(2)}, u32[]{:S(2)}) collective-permute-start(bf16[1,96,768]{2,1,0:T(8,128)(2,1)S(1)} %get-tuple-element.385.refs_0_), channel_id=1, source_target_pairs={{0,8},{4,12},{8,0},{12,4},{16,24},{20,28},{24,16},{28,20},{1,9},{5... | collective-permute-start | bytes 442376 | tf_op jit(solution)/shard_map/ppermute | solution.py:952
  224.1 7.3 %collective-permute-start.54 = (bf16[1,96,768]{2,1,0:T(8,128)(2,1)S(1)}, bf16[1,96,768]{2,1,0:T(8,128)(2,1)S(1)}, u32[]{:S(2)}, u32[]{:S(2)}) collective-permute-start(bf16[1,96,768]{2,1,0:T(8,128)(2,1)S(1)} %get-tuple-element.385.refs_0_), channel_id=1, source_target_pairs={{0,16},{4,20},{8,24},{12,28},{16,0},{20,4},{24,8},{28,12},{1,17},{... | collective-permute-start | bytes 442376 | tf_op jit(solution)/shard_map/ppermute | solution.py:952
  224.8 8.5 %collective-permute-start.55 = (bf16[1,96,768]{2,1,0:T(8,128)(2,1)S(1)}, bf16[1,96,768]{2,1,0:T(8,128)(2,1)S(1)}, u32[]{:S(2)}, u32[]{:S(2)}) collective-permute-start(bf16[1,96,768]{2,1,0:T(8,128)(2,1)S(1)} %get-tuple-element.385.refs_0_), channel_id=1, source_target_pairs={{0,24},{4,28},{8,16},{12,20},{16,8},{20,12},{24,0},{28,4},{1,25},{... | collective-permute-start | bytes 442376 | tf_op jit(solution)/shard_map/ppermute | solution.py:952
  (37 other events, 299.8 us)

commit v5 on v4

--- a/solution.py
+++ b/solution.py
@@ -19,7 +19,7 @@
 BF = jnp.bfloat16
 F32 = jnp.float32
 MIB = 1024 * 1024
-LIMIT = 60
+LIMIT = 56
 SMEM = pl.BlockSpec(memory_space=pltpu.SMEM)
 VMEM = pl.BlockSpec(memory_space=pltpu.VMEM)
 ANY = pl.BlockSpec(memory_space=pl.ANY)
@@ -647,9 +647,9 @@
     )(ids, *args)
 
 
-def prep_kernel(rows, bits, count, ids_ref, *refs):
+def prep_kernel(rows, bits, count, *refs):
     mats, (tab_ref, in_ref, down_ref, a_ref, f_ref, wide_ref, sems) = refs[:count], refs[count:]
-    block = row_block(ids_ref[0], bits)
+    block = row_block(lax.axis_index("dp") & ((1 << bits) - 1), bits)
     first = pl.ds(pl.multiple_of(block * rows, rows), rows)
     copies = [
         pltpu.make_async_copy(in_ref.at[first], f_ref.at[0], sems.at[0]),
@@ -684,18 +684,18 @@
         copy.wait()
 
 
-def prep(ids, mats, tab, w_in, w_down, rows, bits):
+def prep(mats, tab, w_in, w_down, rows, bits):
     depth = w_in.shape[0]
     return pl.pallas_call(
         functools.partial(prep_kernel, rows, bits, len(mats)),
-        in_specs=[SMEM] + [ANY] * len(mats) + [VMEM, ANY, ANY],
+        in_specs=[ANY] * len(mats) + [VMEM, ANY, ANY],
         out_specs=[VMEM, VMEM, VMEM],
         out_shape=[like((rows + EXTRA, depth), BF), like((2, rows, depth), BF), like((1, EXTRA, TILE), BF)],
         scratch_shapes=[pltpu.SemaphoreType.DMA((3,))],
         compiler_params=params(60),
         cost_estimate=cost(0),
         name="prep",
-    )(ids, *mats, tab, w_in, w_down)
+    )(*mats, tab, w_in, w_down)
 
 
 def join_kernel(count, *refs):
@@ -729,7 +729,7 @@
     return [(o * 2 * inner, inner, o * inner) for o in range(outer)]
 
 
-def fold_kernel(runs, extra, joined, ids_ref, *refs):
+def fold_kernel(runs, extra, joined, split, ids_ref, *refs):
     if joined:
         keep_ref, recv_ref = refs[:2]
         n = keep_ref.shape[0] // 2
@@ -747,8 +747,10 @@
             return (keep[:, rows, :].astype(F32) + recv[:, rows, :].astype(F32)).astype(BF)
 
         if runs is None:
-            rows, n = outs[0].shape[1], outs[0].shape[0] // 2
-            outs[0][g * n : (g + 1) * n] = total(pl.ds(0, rows))
+            value, done = total(pl.ds(0, outs[0].shape[1])), 0
+            for ref in outs[: split[0]] if g == 0 else outs[split[0] : split[0] + split[1]]:
+                ref[...] = value[done : done + ref.shape[0]]
+                done += ref.shape[0]
             continue
         bit, group_runs = runs[g]
         mine = side_of(ids_ref, bit)
@@ -760,10 +762,10 @@
                 for m in range(ref.shape[0]):
                     ref[m, done:, :] = packed
     if extra and runs is None:
-        outs[1][...] = packed
-
-
-def fold(ids, groups, runs, extra):
+        outs[-1][...] = packed
+
+
+def fold(ids, groups, runs, extra, split=(1, 1)):
     joined = len(groups) == 1
     arrays = [a for group in groups for a in group]
     if joined:
@@ -774,12 +776,13 @@
         bodies = [arrays[0].shape[1], arrays[2].shape[1] - extra]
     cols = arrays[0].shape[2]
     if runs is None:
-        out_shape = [like((2 * count, bodies[0], cols), BF)] + ([like((extra, cols), BF)] if extra else [])
+        out_shape = [like((count // n, bodies[0], cols), BF) for n in split for _ in range(n)]
+        out_shape += [like((extra, cols), BF)] if extra else []
     else:
         tails = (0, extra)
         out_shape = [like((count, bodies[g] // 2 + tails[g], cols), BF) for g in (0, 0, 1, 1)]
     return pl.pallas_call(
-        functools.partial(fold_kernel, runs, extra, joined),
+        functools.partial(fold_kernel, runs, extra, joined, split),
         in_specs=[SMEM] + [VMEM] * len(arrays),
         out_specs=[VMEM] * len(out_shape),
         out_shape=out_shape,
@@ -811,23 +814,17 @@
     )(a, b)
 
 
-def total_kernel(count, *refs):
-    parts, out_ref = refs[:count], refs[count]
-    total = parts[0][...].astype(F32)
-    for part in parts[1:]:
-        total = total + part[...].astype(F32)
-    out_ref[...] = total.astype(BF)
+def total_kernel(*refs):
+    total = refs[0][...].astype(F32)
+    for ref in refs[1:-1]:
+        total = total + ref[...].astype(F32)
+    refs[-1][...] = total.astype(BF)
 
 
 def total_of(parts):
     return pl.pallas_call(
-        functools.partial(total_kernel, len(parts)),
-        in_specs=[VMEM] * len(parts),
-        out_specs=VMEM,
-        out_shape=like(parts[0].shape, BF),
-        compiler_params=params(16),
-        cost_estimate=cost(0),
-        name="total",
+        total_kernel, in_specs=[VMEM] * len(parts), out_specs=VMEM, out_shape=like(parts[0].shape, BF),
+        compiler_params=params(16), cost_estimate=cost(0), name="total",
     )(*parts)
 
 
@@ -959,8 +956,8 @@
 
 
 class Reduce:
-    def __init__(self, ring, send, keep, extra=0):
-        self.ring, self.extra = ring, extra
+    def __init__(self, ring, send, keep, extra=0, split=(1, 1)):
+        self.ring, self.extra, self.split = ring, extra, split
         order = list(range(1, ring.bits))
         self.orders = [order, order[::-1]]
         self.left = [order[::-1], order[::-1]]
@@ -977,14 +974,14 @@
     def step(self):
         ring = self.ring
         if not self.orders[0]:
-            out = fold(ring.ids, self.groups, None, self.extra)
-            self.out, self.small = out[0], out[1] if self.extra else None
+            out = fold(ring.ids, self.groups, None, self.extra, self.split)
+            self.out, self.small = list(out[: sum(self.split)]), out[-1] if self.extra else None
             for bit in range(ring.bits, ring.all_bits):
-                self.out = add(self.out, ring.swap(self.out, 1 << bit))
+                self.out = [add(out, ring.swap(out, 1 << bit)) for out in self.out]
                 if self.extra:
                     self.small = add_small(self.small, ring.swap(self.small, 1 << bit))
             self.done = True
-            return [self.out]
+            return list(self.out)
         runs, bits = [], []
         for g in range(2):
             bit = self.orders[g].pop(0)
@@ -1013,7 +1010,7 @@
     gain_one, gain_two = gain_attn[None], gain_ffn[None]
 
     a_own = [w_out, w_query.T, w_key.T, w_value.T]
-    a_piece, f_piece, tab_own = prep(ids, a_own, rel_table.T, w_in, w_down, ring.rows, ring.bits)
+    a_piece, f_piece, tab_own = prep(a_own, rel_table.T, w_in, w_down, ring.rows, ring.bits)
     v = {}
 
     def close(*keys):
@@ -1031,7 +1028,9 @@
     x_value = inputs.astype(F32)
     n1 = (rms(x_value)[0] * gain_attn.astype(F32)).astype(BF)
     *kept_own, v["hidden"] = attn_fwd(ids, None, n1, a_own, 0, 1, tab_own, hot, inputs, None, slots, heads)
-    close(*[("z", s) for s in shifts], "hidden")
+    v["gain1"], v["gain2"] = gain_one, gain_two
+    close(*[("z", s) for s in shifts], "hidden", "gain1", "gain2")
+    gain_one, gain_two = v["gain1"], v["gain2"]
     v["a"], tab_rest = join([v["z", s] for s in shifts])
     close("a", "piece")
     swap("ax", "a", 2)
@@ -1080,8 +1079,8 @@
     close("out", "gn", "n2", "send", "keep", ("far", f3), ("far", f2), ("catc", f3), ("catc", f2))
     red = {}
 
-    def reduce(name, extra=0):
-        red[name] = Reduce(ring, v["send"], v["keep"], extra)
+    def reduce(name, extra=0, split=(1, 1)):
+        red[name] = Reduce(ring, v["send"], v["keep"], extra, split)
 
     def close_with(names, *keys):
         groups = [group for name in names for group in red[name].groups]
@@ -1117,7 +1116,7 @@
     close_with(["a", "b"], "send", "keep", "gh", "gn")
     reduce("c")
     folded(["b", "a"], "gh", "gn")
-    v["f1"] = ring.push(red["a"].out[2:], f1)
+    v["f1"] = ring.push(red["a"].out[1], f1)
     close_with(["c"], "gh", "gn")
     folded(["c"], "gh", "gn")
     final = (inputs, gain_one, grad_hidden, gg, tabs)
@@ -1127,20 +1126,8 @@
     close_with(["b", "c"], "send", "keep", "gin", "f1")
     reduce("d", EXTRA)
     folded(["b", "c"], "gin")
-    v["f2"] = ring.push(red["b"].out[:2], f2)
-    v["f3"] = ring.push(red["b"].out[2:], f3)
-    close_with(["d"], "gin")
-    folded(["d"], "gin")
-    close_with(["c"], "gin")
-    folded(["c"], "gin")
-    close_with(["d"], "gin")
-    folded(["d"], "gin")
-    close_with(["d"], "gin")
-    folded(["d"], "gin")
-    packed = pack(((1, 1), (0, 0), (0, 1), (1, 0)), [red["c"].out, red["d"].out], red["d"].small)
-    for s in shifts:
-        v["a", s] = ring.push(packed[s], s)
-    close("f2", "f3", "gin")
+    v["f2"] = ring.push(red["b"].out[0], f2)
+    v["f3"] = ring.push(red["b"].out[1], f3)
 
     def spread(name, piece):
         v[name, 0] = piece
@@ -1151,7 +1138,16 @@
         v[name] = cat([v[name, mask] for mask in (0, 2, 4, 6)])
         v[name, 1] = ring.swap(v[name], 1)
 
-    spread("f", total_of([red["a"].out[:2], v["f1"], v["f2"], v["f3"]]))
+    close_with(["d", "c"], "gin", "f2")
+    folded(["d", "c"], "gin")
+    close_with(["d"], "gin")
+    folded(["d"], "gin")
+    close_with(["d"], "gin", "f3")
+    folded(["d"], "gin")
+    packed = pack(((3, 0), (0, 0), (1, 0), (2, 0)), [*red["c"].out, *red["d"].out], red["d"].small)
+    for s in shifts:
+        v["a", s] = ring.push(packed[s], s)
+    spread("f", total_of([red["a"].out[0], v["f1"], v["f2"], v["f3"]]))
     close(*[("a", s) for s in shifts], "gin")
     a_total, table, gains = unpack([packed[0]] + [v["a", s] for s in shifts])
     spread("a", a_total)
@@ -1159,16 +1155,17 @@
     gathered("f")
     close(("f", 1), "gin")
     v["in"], v["down"] = finish(ids, masks, [v["f"], v["f", 1]], 2, depth)
-    close("in", "down", ("a", 2), ("a", 4), ("a", 6), "gin")
+    v["table"] = table[0, : heads * TILE].reshape(heads, TILE)[:, :buckets].T
+    v["gain_attn"], v["gain_ffn"] = gains[n_mp], gains[n_mp + 1]
+    close("in", "down", "table", "gain_attn", "gain_ffn", ("a", 2), ("a", 4), ("a", 6), "gin")
     gathered("a")
     grad_in, grad_down, grad_inputs = v["in"], v["down"], v["gin"]
     grads = finish(ids, masks, [v["a"], v["a", 1]], 4, width)
     grad_out, grad_query, grad_key, grad_value = grads[0], grads[1].T, grads[2].T, grads[3].T
 
-    grad_table = table[0, : heads * TILE].reshape(heads, TILE)[:, :buckets].T
     return (
-        outputs, grad_inputs, grad_query, grad_key, grad_value, grad_out, grad_table,
-        gains[n_mp], gains[n_mp + 1], grad_in, grad_down,
+        outputs, grad_inputs, grad_query, grad_key, grad_value, grad_out, v["table"],
+        v["gain_attn"], v["gain_ffn"], grad_in, grad_down,
     )
 
 

time: 242 us -> 235 us (0.971)
  waiting for transfers between devices: 65.5 us -> 52.3 us
  starting transfers between devices: 51.7 us -> 64.3 us
  local copies, waits for them, and re-layouts: 8.89 us -> 5.51 us
  Pallas kernels: 107 us -> 104 us
    ppermute x6, starting transfers between devices: 9.78 us -> 17.2 us  [pull(): lax.ppermute(x, 'mp', [(i, (i - shift) % self.n_mp) for i in range(self.n...]
    ppermute x6, waiting for transfers between devices: 17 us -> 10.7 us  [pull(): lax.ppermute(x, 'mp', [(i, (i - shift) % self.n_mp) for i in range(self.n...]
    ppermute x45, waiting for transfers between devices: 33 us -> 28.4 us  [swap(): return lax.ppermute(x, 'dp', [(i, i ^ mask) for i in range(self.n_dp)])]
    ppermute x6, starting transfers between devices: 6.42 us -> 10.7 us  [push(): lax.ppermute(x, 'mp', [(i, (i + shift) % self.n_mp) for i in range(self.n...]
    unnamed x56 -> x60, local copies, waits for them, and re-layouts: 6.44 us -> 3.13 us
    pallas_call x13, Pallas kernels: 12.5 us -> 9.56 us  [the longest x12 9.41 us: fold(): pl.pallas_call(functools.partial(fold_kernel, runs, extra, joined, split)...]
  transfers between devices with their start and end apart: 57 -> 57, of which waited for: 21 -> 19; matrix products, arithmetic and copies ran while one was open for 2% -> 2% of each run, Pallas kernels for 42% -> 42%
where the time goes in v5:
time: 235 us; the launch traced here: 230 us
  Pallas kernels  104 us (44%)
  starting transfers between devices  64.3 us (27%)
  waiting for transfers between devices  52.3 us (22%)
  local copies, waits for them, and re-layouts  5.51 us (2%)
  between operations  2.46 us (1%)
    ppermute x45, starting transfers between devices, swap(): return lax.ppermute(x, 'dp', [(i, i ^ mask) for i in range(self.n_dp)])  36.4 us
    pallas_call x2, Pallas kernels, attn_bwd(): pl.pallas_call(functools.partial(attn_bwd_kernel, slots, heads, masks, tu...  33 us
    ppermute x45, waiting for transfers between devices, swap(): return lax.ppermute(x, 'dp', [(i, i ^ mask) for i in range(self.n_dp)])  28.4 us
    pallas_call x2, Pallas kernels, ffn(): pl.pallas_call(functools.partial(ffn_kernel, tuple((0 if m is None else l...  27.9 us
    pallas_call x3, Pallas kernels, attn_fwd(): pl.pallas_call(functools.partial(attn_fwd_kernel, slots, heads, len(a_par...  25.1 us
    ppermute x6, starting transfers between devices, pull(): lax.ppermute(x, 'mp', [(i, (i - shift) % self.n_mp) for i in range(self.n...  17.2 us
    ppermute x6, waiting for transfers between devices, push(): lax.ppermute(x, 'mp', [(i, (i + shift) % self.n_mp) for i in range(self.n...  13.2 us
    ppermute x6, waiting for transfers between devices, pull(): lax.ppermute(x, 'mp', [(i, (i - shift) % self.n_mp) for i in range(self.n...  10.7 us
  transfers between devices with their start and end apart: 57, of which 19 were waited for; matrix products, arithmetic and copies ran while one was open for 2% of the time, Pallas kernels for 42%

profile of v5, /device:TPU:0, one launch (start us, length us, event | category | flops | bytes accessed | tf_op | source)
XLA Modules:
  0.0 230.3 jit_solution(2788150504206304858)
XLA Ops:
  0.7 2.6 %prep.1 = (bf16[112,768]{1,0:T(8,128)(2,1)}, bf16[2,96,768]{2,1,0:T(8,128)(2,1)}, bf16[1,16,128]{2,1,0:T(8,128)(2,1)}) custom-call(bf16[192,768]{1,0:T(8,128)(2,1)} %refs_11_.1, bf16[192,768]{1,0:T(8,128)(2,1)} %bitcast.14, bf16[192,768]{1,0:T(8,128)(2,1)} %bitcast.17, bf16[192,768]{1,0:T(8,128)(2,1)} %bitcast.20, bf16[3,32]{1,0:T(4,128)(2,1)} %bitcast.24, ...), custom_call_target="tpu_custom_call" | custom-call | tf_op jit(solution)/shard_map/prep/pallas_call | solution.py:689
  3.3 3.1 %collective-permute-start.2 = (bf16[112,768]{1,0:T(8,128)(2,1)}, bf16[112,768]{1,0:T(8,128)(2,1)S(1)}, u32[]{:S(2)}, u32[]{:S(2)}) collective-permute-start(bf16[112,768]{1,0:T(8,128)(2,1)} %get-tuple-element.214), channel_id=1, source_target_pairs={{0,1},{1,2},{2,3},{3,0},{4,5},{5,6},{6,7},{7,4},{8,9},{9,10},{10,1... | collective-permute-start | bytes 516104 | tf_op jit(solution)/shard_map/ppermute | solution.py:952
  6.4 2.6 %collective-permute-start.1 = (bf16[112,768]{1,0:T(8,128)(2,1)}, bf16[112,768]{1,0:T(8,128)(2,1)S(1)}, u32[]{:S(2)}, u32[]{:S(2)}) collective-permute-start(bf16[112,768]{1,0:T(8,128)(2,1)} %get-tuple-element.214), channel_id=1, source_target_pairs={{0,2},{1,3},{2,0},{3,1},{4,6},{5,7},{6,4},{7,5},{8,10},{9,11},{10,... | collective-permute-start | bytes 516104 | tf_op jit(solution)/shard_map/ppermute | solution.py:952
  9.0 1.3 collective-permute-start
  13.0 7.1 %attn_fwd.3 = (bf16[1,512,768]{2,1,0:T(8,128)(2,1)}, bf16[1,512,192]{2,1,0:T(8,128)(2,1)}, f32[1,512,128]{2,1,0:T(8,128)}, f32[512,768]{1,0:T(8,128)}) custom-call(s32[11]{0:T(128)} %pad_add_fusion.ids_ref, bf16[512,768]{1,0:T(8,128)(2,1)} %fusion.2.refs_0_, bf16[192,768]{1,0:T(8,128)(2,1)} %refs_11_.1, bf16[192,768]{1,0:T(8,128)(2,1)} %bitcast.15, ...), custom_call_target="tpu_custom_call" | custom-call | flops 16000000000 | bytes 16000000 | tf_op jit(solution)/shard_map/attn_fwd/pallas_call | solution.py:263
  22.0 1.5 collective-permute-start.4
  23.5 1.5 collective-permute-start.3
  25.0 4.3 %collective-permute-start.5 = (bf16[2,96,768]{2,1,0:T(8,128)(2,1)S(1)}, bf16[2,96,768]{2,1,0:T(8,128)(2,1)S(1)}, u32[]{:S(2)}, u32[]{:S(2)}) collective-permute-start(bf16[2,96,768]{2,1,0:T(8,128)(2,1)S(1)} %copy-done.29), channel_id=1, source_target_pairs={{0,3},{1,0},{2,1},{3,2},{4,7},{5,4},{6,5},{7,6},{8,11},{9,8},{10,9... | collective-permute-start | bytes 884744 | tf_op jit(solution)/shard_map/ppermute | solution.py:952
  29.3 5.6 %collective-permute-done.5.refs_0_ = bf16[2,96,768]{2,1,0:T(8,128)(2,1)S(1)} collective-permute-done((bf16[2,96,768]{2,1,0:T(8,128)(2,1)S(1)}, bf16[2,96,768]{2,1,0:T(8,128)(2,1)S(1)}, u32[]{:S(2)}, u32[]{:S(2)}) %collective-permute-start.5) | collective-permute-done | bytes 294944 | tf_op jit(solution)/shard_map/ppermute | solution.py:952
  36.6 4.4 %collective-permute-start.9 = (bf16[2,96,768]{2,1,0:T(8,128)(2,1)S(1)}, bf16[2,96,768]{2,1,0:T(8,128)(2,1)S(1)}, u32[]{:S(2)}, u32[]{:S(2)}) collective-permute-start(bf16[2,96,768]{2,1,0:T(8,128)(2,1)S(1)} %copy-done.29), channel_id=1, source_target_pairs={{0,1},{1,2},{2,3},{3,0},{4,5},{5,6},{6,7},{7,4},{8,9},{9,10},{10,1... | collective-permute-start | bytes 884744 | tf_op jit(solution)/shard_map/ppermute | solution.py:952
  41.0 3.7 %collective-permute-done.8.refs_1_ = bf16[2,96,768]{2,1,0:T(8,128)(2,1)S(1)} collective-permute-done((bf16[2,96,768]{2,1,0:T(8,128)(2,1)S(1)}, bf16[2,96,768]{2,1,0:T(8,128)(2,1)S(1)}, u32[]{:S(2)}, u32[]{:S(2)}) %collective-permute-start.8) | collective-permute-done | bytes 294944 | tf_op jit(solution)/shard_map/ppermute | solution.py:949
  44.7 3.4 %collective-permute-done.9.refs_0_ = bf16[2,96,768]{2,1,0:T(8,128)(2,1)S(1)} collective-permute-done((bf16[2,96,768]{2,1,0:T(8,128)(2,1)S(1)}, bf16[2,96,768]{2,1,0:T(8,128)(2,1)S(1)}, u32[]{:S(2)}, u32[]{:S(2)}) %collective-permute-start.9) | collective-permute-done | bytes 294944 | tf_op jit(solution)/shard_map/ppermute | solution.py:952
  48.8 1.5 collective-permute-start.13
  50.3 1.4 collective-permute-start.12
  51.8 1.4 collective-permute-start.11
  53.9 10.5 %attn_fwd.4 = (bf16[2,512,768]{2,1,0:T(8,128)(2,1)}, bf16[2,512,192]{2,1,0:T(8,128)(2,1)}, f32[2,512,128]{2,1,0:T(8,128)}, f32[512,768]{1,0:T(8,128)}) custom-call(s32[11]{0:T(128)} %pad_add_fusion.ids_ref, bf16[512,768]{1,0:T(8,128)(2,1)} %fusion.2.refs_0_, bf16[3,3,96,768]{3,2,1,0:T(8,128)(2,1)} %copy-done.2, bf16[1,3,96,768]{3,2,1,0:T(8,128)(2,1)} %bitcast.30, ...), custom_call_target="tpu_custom_call" | custom-call | flops 32000000000 | bytes 32000000 | tf_op jit(solution)/shard_map/attn_fwd/pallas_call | solution.py:263
  64.4 1.8 collective-permute-done.12.refs_0_
  68.1 7.4 %attn_fwd.5 = (bf16[1,512,768]{2,1,0:T(8,128)(2,1)}, bf16[1,512,192]{2,1,0:T(8,128)(2,1)}, f32[1,512,128]{2,1,0:T(8,128)}, f32[512,768]{1,0:T(8,128)}, bf16[512,768]{1,0:T(8,128)(2,1)}) custom-call(s32[11]{0:T(128)} %pad_add_fusion.ids_ref, bf16[512,768]{1,0:T(8,128)(2,1)} %fusion.2.refs_0_, bf16[3,3,96,768]{3,2,1,0:T(8,128)(2,1)} %copy-done.2, ...), custom_call_target="tpu_custom_call" | custom-call | flops 16000000000 | bytes 16000000 | tf_op jit(solution)/shard_map/attn_fwd/pallas_call | solution.py:263
  76.3 1.5 collective-permute-start.17
  77.8 13.9 %ffn.2 = (f32[512,768]{1,0:T(8,128)}, f32[512,768]{1,0:T(8,128)}, bf16[4,384,768]{2,1,0:T(8,128)(2,1)}, bf16[4,384,768]{2,1,0:T(8,128)(2,1)}) custom-call(s32[11]{0:T(128)} %pad_add_fusion.ids_ref, bf16[512,768]{1,0:T(8,128)(2,1)} %get-tuple-element.267.refs_0_, bf16[512,768]{1,0:T(8,128)(2,1)} %refs_1_.5, bf16[768,768]{1,0:T(8,128)(2,1)} %refs_2_.3, ...), custom_call_target="tpu_custom_call" | custom-call | flops 64000000000 | bytes 64000000 | tf_op jit(solution)/shard_map/ffn/pallas_call | solution.py:636
  91.8 3.0 %collective-permute-done.17.refs_7_ = bf16[2,2,96,768]{3,2,1,0:T(8,128)(2,1)S(1)} collective-permute-done((bf16[2,2,96,768]{3,2,1,0:T(8,128)(2,1)S(1)}, bf16[2,2,96,768]{3,2,1,0:T(8,128)(2,1)S(1)}, u32[]{:S(2)}, u32[]{:S(2)}) %collective-permute-start.17) | collective-permute-done | bytes 589856 | tf_op jit(solution)/shard_map/ppermute | solution.py:949
  95.3 4.5 %collective-permute-done.22.refs_9_ = bf16[2,2,96,768]{3,2,1,0:T(8,128)(2,1)S(1)} collective-permute-done((bf16[2,2,96,768]{3,2,1,0:T(8,128)(2,1)S(1)}, bf16[2,2,96,768]{3,2,1,0:T(8,128)(2,1)S(1)}, u32[]{:S(2)}, u32[]{:S(2)}) %collective-permute-start.22) | collective-permute-done | bytes 589856 | tf_op jit(solution)/shard_map/ppermute | solution.py:949
  101.2 1.7 copy-done.1
  105.8 14.0 %ffn.3 = (bf16[512,768]{1,0:T(8,128)(2,1)}, bf16[4,384,768]{2,1,0:T(8,128)(2,1)}, bf16[4,384,768]{2,1,0:T(8,128)(2,1)}, f32[512,768]{1,0:T(8,128)}, bf16[512,768]{1,0:T(8,128)(2,1)}, /*index=5*/f32[8,768]{1,0:T(8,128)}) custom-call(s32[11]{0:T(128)} %pad_add_fusion.ids_ref, bf16[512,768]{1,0:T(8,128)(2,1)} %get-tuple-element.267.refs_0_, ...), custom_call_target="tpu_custom_call" | custom-call | flops 64000000000 | bytes 64000000 | tf_op jit(solution)/shard_map/ffn/pallas_call | solution.py:636
  121.8 1.4 collective-permute-start.27
  123.2 1.5 collective-permute-done.28.refs_1_
  125.7 1.4 collective-permute-start.29
  128.1 15.9 %attn_bwd.2 = (bf16[2,384,768]{2,1,0:T(8,128)(2,1)}, bf16[2,384,768]{2,1,0:T(8,128)(2,1)}, f32[512,768]{1,0:T(8,128)}, f32[2,8,128]{2,1,0:T(8,128)}) custom-call(s32[11]{0:T(128)} %pad_add_fusion.ids_ref, bf16[512,768]{1,0:T(8,128)(2,1)} %fusion.2.refs_0_, bf16[512,768]{1,0:T(8,128)(2,1)} %get-tuple-element.327.refs_1_, ...), custom_call_target="tpu_custom_call" | custom-call | flops 64000000000 | bytes 64000000 | tf_op jit(solution)/shard_map/attn_bwd/pallas_call | solution.py:503
  144.9 1.4 collective-permute-start.36
  148.1 1.3 collective-permute-start.32
  152.1 17.2 %attn_bwd.3 = (bf16[2,400,768]{2,1,0:T(8,128)(2,1)}, bf16[2,400,768]{2,1,0:T(8,128)(2,1)}, bf16[512,768]{1,0:T(8,128)(2,1)}) custom-call(s32[11]{0:T(128)} %pad_add_fusion.ids_ref, bf16[512,768]{1,0:T(8,128)(2,1)} %fusion.2.refs_0_, bf16[512,768]{1,0:T(8,128)(2,1)} %get-tuple-element.327.refs_1_, bf16[128,512]{1,0:T(8,128)(2,1)} %constant.22.clone.refs_6_.refs_2_, ...), custom_call_target="tpu_custom_call" | custom-call | flops 64000000000 | bytes 64000000 | tf_op jit(solution)/shard_map/attn_bwd/pallas_call | solution.py:503
  170.1 2.6 %collective-permute-start.40 = (bf16[2,96,768]{2,1,0:T(8,128)(2,1)S(1)}, bf16[2,96,768]{2,1,0:T(8,128)(2,1)S(1)}, u32[]{:S(2)}, u32[]{:S(2)}) collective-permute-start(bf16[2,96,768]{2,1,0:T(8,128)(2,1)S(1)} %get-tuple-element.351), channel_id=1, source_target_pairs={{0,3},{1,0},{2,1},{3,2},{4,7},{5,4},{6,5},{7,6},{8,11},{9,8},{10,9... | collective-permute-start | bytes 884744 | tf_op jit(solution)/shard_map/ppermute | solution.py:955
  175.1 4.2 %collective-permute-done.38.refs_1_ = bf16[1,96,768]{2,1,0:T(8,128)(2,1)S(1)} collective-permute-done((bf16[1,96,768]{2,1,0:T(8,128)(2,1)S(1)}, bf16[1,96,768]{2,1,0:T(8,128)(2,1)S(1)}, u32[]{:S(2)}, u32[]{:S(2)}) %collective-permute-start.38) | collective-permute-done | bytes 147488 | tf_op jit(solution)/shard_map/ppermute | solution.py:949
  182.8 2.1 collective-permute-start.45
  185.5 4.3 %collective-permute-done.41.refs_1_ = bf16[1,192,768]{2,1,0:T(8,128)(2,1)S(1)} collective-permute-done((bf16[1,192,768]{2,1,0:T(8,128)(2,1)S(1)}, bf16[1,192,768]{2,1,0:T(8,128)(2,1)S(1)}, u32[]{:S(2)}, u32[]{:S(2)}) %collective-permute-start.41) | collective-permute-done | bytes 294944 | tf_op jit(solution)/shard_map/ppermute | solution.py:949
  190.5 1.3 collective-permute-start.44
  192.8 5.1 %collective-permute-done.45.refs_3_ = bf16[2,96,768]{2,1,0:T(8,128)(2,1)S(1)} collective-permute-done((bf16[2,96,768]{2,1,0:T(8,128)(2,1)S(1)}, bf16[2,96,768]{2,1,0:T(8,128)(2,1)S(1)}, u32[]{:S(2)}, u32[]{:S(2)}) %collective-permute-start.45) | collective-permute-done | bytes 294944 | tf_op jit(solution)/shard_map/ppermute | solution.py:955
  199.2 1.3 collective-permute-start.48
  201.4 1.3 collective-permute-start.46
  202.7 3.4 %collective-permute-start.50 = (bf16[112,768]{1,0:T(8,128)(2,1)S(1)}, bf16[112,768]{1,0:T(8,128)(2,1)S(1)}, u32[]{:S(2)}, u32[]{:S(2)}) collective-permute-start(bf16[112,768]{1,0:T(8,128)(2,1)S(1)} %get-tuple-element.384), channel_id=1, source_target_pairs={{0,2},{1,3},{2,0},{3,1},{4,6},{5,7},{6,4},{7,5},{8,10},{9,11},{10,... | collective-permute-start | bytes 516104 | tf_op jit(solution)/shard_map/ppermute | solution.py:955
  208.1 5.8 %collective-permute-done.50.refs_2_ = bf16[112,768]{1,0:T(8,128)(2,1)S(1)} collective-permute-done((bf16[112,768]{1,0:T(8,128)(2,1)S(1)}, bf16[112,768]{1,0:T(8,128)(2,1)S(1)}, u32[]{:S(2)}, u32[]{:S(2)}) %collective-permute-start.50) | collective-permute-done | bytes 172064 | tf_op jit(solution)/shard_map/ppermute | solution.py:955
  213.9 1.2 collective-permute-done.51.refs_3_
  215.4 1.3 collective-permute-start.55
  217.7 1.3 collective-permute-start.53
  220.1 3.0 %finish.2 = (f32[768,768]{1,0:T(8,128)}, f32[768,768]{1,0:T(8,128)}) custom-call(s32[11]{0:T(128)S(1)} %copy-done.11, bf16[4,2,96,768]{3,2,1,0:T(8,128)(2,1)S(1)} %cat.10.refs_0_, bf16[4,2,96,768]{3,2,1,0:T(8,128)(2,1)S(1)} %collective-permute-done.52.refs_1_), custom_call_target="tpu_custom_call" | custom-call | tf_op jit(solution)/shard_map/finish/pallas_call | solution.py:913
  223.2 2.6 %collective-permute-done.54.refs_2_ = bf16[1,96,768]{2,1,0:T(8,128)(2,1)S(1)} collective-permute-done((bf16[1,96,768]{2,1,0:T(8,128)(2,1)S(1)}, bf16[1,96,768]{2,1,0:T(8,128)(2,1)S(1)}, u32[]{:S(2)}, u32[]{:S(2)}) %collective-permute-start.54) | collective-permute-done | bytes 147488 | tf_op jit(solution)/shard_map/ppermute | solution.py:949
  225.9 2.0 collective-permute-done.56.refs_1_
  227.8 2.1 finish.3
  (168 shorter events, 39.5 us)
Async XLA Ops:
  3.3 18.0 %collective-permute-start.2 = (bf16[112,768]{1,0:T(8,128)(2,1)}, bf16[112,768]{1,0:T(8,128)(2,1)S(1)}, u32[]{:S(2)}, u32[]{:S(2)}) collective-permute-start(bf16[112,768]{1,0:T(8,128)(2,1)} %get-tuple-element.214), channel_id=1, source_target_pairs={{0,1},{1,2},{2,3},{3,0},{4,5},{5,6},{6,7},{7,4},{8,9},{9,10},{10,1... | collective-permute-start | bytes 516104 | tf_op jit(solution)/shard_map/ppermute | solution.py:952
  6.4 15.0 %collective-permute-start.1 = (bf16[112,768]{1,0:T(8,128)(2,1)}, bf16[112,768]{1,0:T(8,128)(2,1)S(1)}, u32[]{:S(2)}, u32[]{:S(2)}) collective-permute-start(bf16[112,768]{1,0:T(8,128)(2,1)} %get-tuple-element.214), channel_id=1, source_target_pairs={{0,2},{1,3},{2,0},{3,1},{4,6},{5,7},{6,4},{7,5},{8,10},{9,11},{10,... | collective-permute-start | bytes 516104 | tf_op jit(solution)/shard_map/ppermute | solution.py:952
  9.0 12.4 %collective-permute-start = (bf16[112,768]{1,0:T(8,128)(2,1)}, bf16[112,768]{1,0:T(8,128)(2,1)S(1)}, u32[]{:S(2)}, u32[]{:S(2)}) collective-permute-start(bf16[112,768]{1,0:T(8,128)(2,1)} %get-tuple-element.214), channel_id=1, source_target_pairs={{0,3},{1,0},{2,1},{3,2},{4,7},{5,4},{6,5},{7,6},{8,11},{9,8},{10,9... | collective-permute-start | bytes 516104 | tf_op jit(solution)/shard_map/ppermute | solution.py:952
  22.0 12.9 %collective-permute-start.4 = (bf16[3,96,768]{2,1,0:T(8,128)(2,1)S(1)}, bf16[3,96,768]{2,1,0:T(8,128)(2,1)S(1)}, u32[]{:S(2)}, u32[]{:S(2)}) collective-permute-start(bf16[3,96,768]{2,1,0:T(8,128)(2,1)S(1)} %get-tuple-element.224.refs_0_), channel_id=1, source_target_pairs={{0,16},{4,20},{8,24},{12,28},{16,0},{20,4},{24,8},{28,12},{1,17},{... | collective-permute-start | bytes 1327112 | tf_op jit(solution)/shard_map/ppermute | solution.py:949
  23.5 11.4 %collective-permute-start.3 = (bf16[3,96,768]{2,1,0:T(8,128)(2,1)S(1)}, bf16[3,96,768]{2,1,0:T(8,128)(2,1)S(1)}, u32[]{:S(2)}, u32[]{:S(2)}) collective-permute-start(bf16[3,96,768]{2,1,0:T(8,128)(2,1)S(1)} %get-tuple-element.224.refs_0_), channel_id=1, source_target_pairs={{0,8},{4,12},{8,0},{12,4},{16,24},{20,28},{24,16},{28,20},{1,9},{5... | collective-permute-start | bytes 1327112 | tf_op jit(solution)/shard_map/ppermute | solution.py:949
  25.0 9.9 %collective-permute-start.5 = (bf16[2,96,768]{2,1,0:T(8,128)(2,1)S(1)}, bf16[2,96,768]{2,1,0:T(8,128)(2,1)S(1)}, u32[]{:S(2)}, u32[]{:S(2)}) collective-permute-start(bf16[2,96,768]{2,1,0:T(8,128)(2,1)S(1)} %copy-done.29), channel_id=1, source_target_pairs={{0,3},{1,0},{2,1},{3,2},{4,7},{5,4},{6,5},{7,6},{8,11},{9,8},{10,9... | collective-permute-start | bytes 884744 | tf_op jit(solution)/shard_map/ppermute | solution.py:952
  35.0 13.1 %collective-permute-start.7 = (bf16[3,3,96,768]{3,2,1,0:T(8,128)(2,1)S(1)}, bf16[3,3,96,768]{3,2,1,0:T(8,128)(2,1)S(1)}, u32[]{:S(2)}, u32[]{:S(2)}) collective-permute-start(bf16[3,3,96,768]{3,2,1,0:T(8,128)(2,1)S(1)} %cat.6.refs_1_.refs_3_), channel_id=1, source_target_pairs={{0,4},{4,0},{8,12},{12,8},{16,20},{20,16},{24,28},{28,24},{1,5},{5... | collective-permute-start | bytes 3981320 | tf_op jit(solution)/shard_map/ppermute | solution.py:949
  35.1 13.0 %collective-permute-start.6 = (bf16[3,96,768]{2,1,0:T(8,128)(2,1)S(1)}, bf16[3,96,768]{2,1,0:T(8,128)(2,1)S(1)}, u32[]{:S(2)}, u32[]{:S(2)}) collective-permute-start(bf16[3,96,768]{2,1,0:T(8,128)(2,1)S(1)} %collective-permute-done.3.refs_1_), channel_id=1, source_target_pairs={{0,16},{4,20},{8,24},{12,28},{16,0},{20,4},{24,8},{28,12},{1,17},{... | collective-permute-start | bytes 1327112 | tf_op jit(solution)/shard_map/ppermute | solution.py:949
  35.6 9.1 %collective-permute-start.8 = (bf16[2,96,768]{2,1,0:T(8,128)(2,1)S(1)}, bf16[2,96,768]{2,1,0:T(8,128)(2,1)S(1)}, u32[]{:S(2)}, u32[]{:S(2)}) collective-permute-start(bf16[2,96,768]{2,1,0:T(8,128)(2,1)S(1)} %collective-permute-done.5.refs_0_), channel_id=1, source_target_pairs={{0,8},{4,12},{8,0},{12,4},{16,24},{20,28},{24,16},{28,20},{1,9},{5... | collective-permute-start | bytes 884744 | tf_op jit(solution)/shard_map/ppermute | solution.py:949
  36.6 11.5 %collective-permute-start.9 = (bf16[2,96,768]{2,1,0:T(8,128)(2,1)S(1)}, bf16[2,96,768]{2,1,0:T(8,128)(2,1)S(1)}, u32[]{:S(2)}, u32[]{:S(2)}) collective-permute-start(bf16[2,96,768]{2,1,0:T(8,128)(2,1)S(1)} %copy-done.29), channel_id=1, source_target_pairs={{0,1},{1,2},{2,3},{3,0},{4,5},{5,6},{6,7},{7,4},{8,9},{9,10},{10,1... | collective-permute-start | bytes 884744 | tf_op jit(solution)/shard_map/ppermute | solution.py:952
  48.2 27.3 %collective-permute-start.15 = (bf16[2,2,96,768]{3,2,1,0:T(8,128)(2,1)S(1)}, bf16[2,2,96,768]{3,2,1,0:T(8,128)(2,1)S(1)}, u32[]{:S(2)}, u32[]{:S(2)}) collective-permute-start(bf16[2,2,96,768]{3,2,1,0:T(8,128)(2,1)S(1)} %cat.7.refs_4_), channel_id=1, source_target_pairs={{0,4},{4,0},{8,12},{12,8},{16,20},{20,16},{24,28},{28,24},{1,5},{5... | collective-permute-start | bytes 1769480 | tf_op jit(solution)/shard_map/ppermute | solution.py:949
  48.8 17.5 %collective-permute-start.13 = (bf16[2,2,96,768]{3,2,1,0:T(8,128)(2,1)S(1)}, bf16[2,2,96,768]{3,2,1,0:T(8,128)(2,1)S(1)}, u32[]{:S(2)}, u32[]{:S(2)}) collective-permute-start(bf16[2,2,96,768]{3,2,1,0:T(8,128)(2,1)S(1)} %cat.7.refs_4_), channel_id=1, source_target_pairs={{0,16},{4,20},{8,24},{12,28},{16,0},{20,4},{24,8},{28,12},{1,17},{... | collective-permute-start | bytes 1769480 | tf_op jit(solution)/shard_map/ppermute | solution.py:949
  50.3 15.9 %collective-permute-start.12 = (bf16[2,96,768]{2,1,0:T(8,128)(2,1)S(1)}, bf16[2,96,768]{2,1,0:T(8,128)(2,1)S(1)}, u32[]{:S(2)}, u32[]{:S(2)}) collective-permute-start(bf16[2,96,768]{2,1,0:T(8,128)(2,1)S(1)} %copy-done.29), channel_id=1, source_target_pairs={{0,2},{1,3},{2,0},{3,1},{4,6},{5,7},{6,4},{7,5},{8,10},{9,11},{10,... | collective-permute-start | bytes 884744 | tf_op jit(solution)/shard_map/ppermute | solution.py:952
  51.8 14.5 %collective-permute-start.11 = (bf16[2,96,768]{2,1,0:T(8,128)(2,1)S(1)}, bf16[2,96,768]{2,1,0:T(8,128)(2,1)S(1)}, u32[]{:S(2)}, u32[]{:S(2)}) collective-permute-start(bf16[2,96,768]{2,1,0:T(8,128)(2,1)S(1)} %collective-permute-done.9.refs_0_), channel_id=1, source_target_pairs={{0,8},{4,12},{8,0},{12,4},{16,24},{20,28},{24,16},{28,20},{1,9},{5... | collective-permute-start | bytes 884744 | tf_op jit(solution)/shard_map/ppermute | solution.py:949
  66.3 25.4 %collective-permute-start.20 = (bf16[2,2,96,768]{3,2,1,0:T(8,128)(2,1)S(1)}, bf16[2,2,96,768]{3,2,1,0:T(8,128)(2,1)S(1)}, u32[]{:S(2)}, u32[]{:S(2)}) collective-permute-start(bf16[2,2,96,768]{3,2,1,0:T(8,128)(2,1)S(1)} %cat.9.refs_2_), channel_id=1, source_target_pairs={{0,4},{4,0},{8,12},{12,8},{16,20},{20,16},{24,28},{28,24},{1,5},{5... | collective-permute-start | bytes 1769480 | tf_op jit(solution)/shard_map/ppermute | solution.py:949
  66.4 25.3 %collective-permute-start.18 = (bf16[2,2,96,768]{3,2,1,0:T(8,128)(2,1)S(1)}, bf16[2,2,96,768]{3,2,1,0:T(8,128)(2,1)S(1)}, u32[]{:S(2)}, u32[]{:S(2)}) collective-permute-start(bf16[2,2,96,768]{3,2,1,0:T(8,128)(2,1)S(1)} %cat.9.refs_2_), channel_id=1, source_target_pairs={{0,16},{4,20},{8,24},{12,28},{16,0},{20,4},{24,8},{28,12},{1,17},{... | collective-permute-start | bytes 1769480 | tf_op jit(solution)/shard_map/ppermute | solution.py:949
  67.0 9.1 %collective-permute-start.14 = (bf16[2,96,768]{2,1,0:T(8,128)(2,1)S(1)}, bf16[2,96,768]{2,1,0:T(8,128)(2,1)S(1)}, u32[]{:S(2)}, u32[]{:S(2)}) collective-permute-start(bf16[2,96,768]{2,1,0:T(8,128)(2,1)S(1)} %collective-permute-done.12.refs_0_), channel_id=1, source_target_pairs={{0,8},{4,12},{8,0},{12,4},{16,24},{20,28},{24,16},{28,20},{1,9},{5... | collective-permute-start | bytes 884744 | tf_op jit(solution)/shard_map/ppermute | solution.py:949
  68.1 7.9 %collective-permute-start.16 = (bf16[2,2,96,768]{3,2,1,0:T(8,128)(2,1)S(1)}, bf16[2,2,96,768]{3,2,1,0:T(8,128)(2,1)S(1)}, u32[]{:S(2)}, u32[]{:S(2)}) collective-permute-start(bf16[2,2,96,768]{3,2,1,0:T(8,128)(2,1)S(1)} %collective-permute-done.13.refs_5_), channel_id=1, source_target_pairs={{0,4},{4,0},{8,12},{12,8},{16,20},{20,16},{24,28},{28,24},{1,5},{5... | collective-permute-start | bytes 1769480 | tf_op jit(solution)/shard_map/ppermute | solution.py:949
  76.1 15.6 %collective-permute-start.19 = (bf16[2,2,96,768]{3,2,1,0:T(8,128)(2,1)S(1)}, bf16[2,2,96,768]{3,2,1,0:T(8,128)(2,1)S(1)}, u32[]{:S(2)}, u32[]{:S(2)}) collective-permute-start(bf16[2,2,96,768]{3,2,1,0:T(8,128)(2,1)S(1)} %cat.8.refs_6_), channel_id=1, source_target_pairs={{0,4},{4,0},{8,12},{12,8},{16,20},{20,16},{24,28},{28,24},{1,5},{5... | collective-permute-start | bytes 1769480 | tf_op jit(solution)/shard_map/ppermute | solution.py:949
  76.3 18.5 %collective-permute-start.17 = (bf16[2,2,96,768]{3,2,1,0:T(8,128)(2,1)S(1)}, bf16[2,2,96,768]{3,2,1,0:T(8,128)(2,1)S(1)}, u32[]{:S(2)}, u32[]{:S(2)}) collective-permute-start(bf16[2,2,96,768]{3,2,1,0:T(8,128)(2,1)S(1)} %cat.8.refs_6_), channel_id=1, source_target_pairs={{0,16},{4,20},{8,24},{12,28},{16,0},{20,4},{24,8},{28,12},{1,17},{... | collective-permute-start | bytes 1769480 | tf_op jit(solution)/shard_map/ppermute | solution.py:949
  94.8 6.4 %collective-permute-start.21 = (bf16[4,384,768]{2,1,0:T(8,128)(2,1)}, bf16[4,384,768]{2,1,0:T(8,128)(2,1)S(1)}, u32[]{:S(2)}, u32[]{:S(2)}) collective-permute-start(bf16[4,384,768]{2,1,0:T(8,128)(2,1)} %get-tuple-element.254), channel_id=1, source_target_pairs={{0,4},{4,0},{8,12},{12,8},{16,20},{20,16},{24,28},{28,24},{1,5},{5... | collective-permute-start | bytes 7077896 | tf_op jit(solution)/shard_map/ppermute | solution.py:949
  104.0 15.8 %collective-permute-start.24 = (bf16[2,192,768]{2,1,0:T(8,128)(2,1)S(1)}, bf16[2,192,768]{2,1,0:T(8,128)(2,1)S(1)}, u32[]{:S(2)}, u32[]{:S(2)}) collective-permute-start(bf16[2,192,768]{2,1,0:T(8,128)(2,1)S(1)} %get-tuple-element.276), channel_id=1, source_target_pairs={{0,8},{4,12},{8,0},{12,4},{16,24},{20,28},{24,16},{28,20},{1,9},{5... | collective-permute-start | bytes 1769480 | tf_op jit(solution)/shard_map/ppermute | solution.py:949
  104.6 15.2 %collective-permute-start.25 = (bf16[2,192,768]{2,1,0:T(8,128)(2,1)S(1)}, bf16[2,192,768]{2,1,0:T(8,128)(2,1)S(1)}, u32[]{:S(2)}, u32[]{:S(2)}) collective-permute-start(bf16[2,192,768]{2,1,0:T(8,128)(2,1)S(1)} %get-tuple-element.277), channel_id=1, source_target_pairs={{0,16},{4,20},{8,24},{12,28},{16,0},{20,4},{24,8},{28,12},{1,17},{... | collective-permute-start | bytes 1769480 | tf_op jit(solution)/shard_map/ppermute | solution.py:949
  120.7 23.3 %collective-permute-start.26 = (bf16[2,96,768]{2,1,0:T(8,128)(2,1)S(1)}, bf16[2,96,768]{2,1,0:T(8,128)(2,1)S(1)}, u32[]{:S(2)}, u32[]{:S(2)}) collective-permute-start(bf16[2,96,768]{2,1,0:T(8,128)(2,1)S(1)} %get-tuple-element.284), channel_id=1, source_target_pairs={{0,16},{4,20},{8,24},{12,28},{16,0},{20,4},{24,8},{28,12},{1,17},{... | collective-permute-start | bytes 884744 | tf_op jit(solution)/shard_map/ppermute | solution.py:949
  121.8 22.3 %collective-permute-start.27 = (bf16[2,96,768]{2,1,0:T(8,128)(2,1)S(1)}, bf16[2,96,768]{2,1,0:T(8,128)(2,1)S(1)}, u32[]{:S(2)}, u32[]{:S(2)}) collective-permute-start(bf16[2,96,768]{2,1,0:T(8,128)(2,1)S(1)} %get-tuple-element.285), channel_id=1, source_target_pairs={{0,8},{4,12},{8,0},{12,4},{16,24},{20,28},{24,16},{28,20},{1,9},{5... | collective-permute-start | bytes 884744 | tf_op jit(solution)/shard_map/ppermute | solution.py:949
  125.7 18.4 %collective-permute-start.29 = (bf16[2,192,768]{2,1,0:T(8,128)(2,1)S(1)}, bf16[2,192,768]{2,1,0:T(8,128)(2,1)S(1)}, u32[]{:S(2)}, u32[]{:S(2)}) collective-permute-start(bf16[2,192,768]{2,1,0:T(8,128)(2,1)S(1)} %get-tuple-element.292), channel_id=1, source_target_pairs={{0,8},{4,12},{8,0},{12,4},{16,24},{20,28},{24,16},{28,20},{1,9},{5... | collective-permute-start | bytes 1769480 | tf_op jit(solution)/shard_map/ppermute | solution.py:949
  127.1 17.0 %collective-permute-start.30 = (bf16[2,192,768]{2,1,0:T(8,128)(2,1)S(1)}, bf16[2,192,768]{2,1,0:T(8,128)(2,1)S(1)}, u32[]{:S(2)}, u32[]{:S(2)}) collective-permute-start(bf16[2,192,768]{2,1,0:T(8,128)(2,1)S(1)} %get-tuple-element.293), channel_id=1, source_target_pairs={{0,16},{4,20},{8,24},{12,28},{16,0},{20,4},{24,8},{28,12},{1,17},{... | collective-permute-start | bytes 1769480 | tf_op jit(solution)/shard_map/ppermute | solution.py:949
  144.9 24.4 %collective-permute-start.36 = (bf16[2,96,768]{2,1,0:T(8,128)(2,1)S(1)}, bf16[2,96,768]{2,1,0:T(8,128)(2,1)S(1)}, u32[]{:S(2)}, u32[]{:S(2)}) collective-permute-start(bf16[2,96,768]{2,1,0:T(8,128)(2,1)S(1)} %get-tuple-element.317), channel_id=1, source_target_pairs={{0,1},{1,2},{2,3},{3,0},{4,5},{5,6},{6,7},{7,4},{8,9},{9,10},{10,1... | collective-permute-start | bytes 884744 | tf_op jit(solution)/shard_map/ppermute | solution.py:955
  147.0 22.2 %collective-permute-start.31 = (bf16[2,96,768]{2,1,0:T(8,128)(2,1)S(1)}, bf16[2,96,768]{2,1,0:T(8,128)(2,1)S(1)}, u32[]{:S(2)}, u32[]{:S(2)}) collective-permute-start(bf16[2,96,768]{2,1,0:T(8,128)(2,1)S(1)} %get-tuple-element.309), channel_id=1, source_target_pairs={{0,16},{4,20},{8,24},{12,28},{16,0},{20,4},{24,8},{28,12},{1,17},{... | collective-permute-start | bytes 884744 | tf_op jit(solution)/shard_map/ppermute | solution.py:949
  148.1 21.2 %collective-permute-start.32 = (bf16[2,96,768]{2,1,0:T(8,128)(2,1)S(1)}, bf16[2,96,768]{2,1,0:T(8,128)(2,1)S(1)}, u32[]{:S(2)}, u32[]{:S(2)}) collective-permute-start(bf16[2,96,768]{2,1,0:T(8,128)(2,1)S(1)} %get-tuple-element.310), channel_id=1, source_target_pairs={{0,8},{4,12},{8,0},{12,4},{16,24},{20,28},{24,16},{28,20},{1,9},{5... | collective-permute-start | bytes 884744 | tf_op jit(solution)/shard_map/ppermute | solution.py:949
  150.2 19.1 %collective-permute-start.34 = (bf16[1,192,768]{2,1,0:T(8,128)(2,1)S(1)}, bf16[1,192,768]{2,1,0:T(8,128)(2,1)S(1)}, u32[]{:S(2)}, u32[]{:S(2)}) collective-permute-start(bf16[1,192,768]{2,1,0:T(8,128)(2,1)S(1)} %get-tuple-element.321), channel_id=1, source_target_pairs={{0,8},{4,12},{8,0},{12,4},{16,24},{20,28},{24,16},{28,20},{1,9},{5... | collective-permute-start | bytes 884744 | tf_op jit(solution)/shard_map/ppermute | solution.py:949
  151.0 18.3 %collective-permute-start.35 = (bf16[1,192,768]{2,1,0:T(8,128)(2,1)S(1)}, bf16[1,192,768]{2,1,0:T(8,128)(2,1)S(1)}, u32[]{:S(2)}, u32[]{:S(2)}) collective-permute-start(bf16[1,192,768]{2,1,0:T(8,128)(2,1)S(1)} %get-tuple-element.322), channel_id=1, source_target_pairs={{0,16},{4,20},{8,24},{12,28},{16,0},{20,4},{24,8},{28,12},{1,17},{... | collective-permute-start | bytes 884744 | tf_op jit(solution)/shard_map/ppermute | solution.py:949
  169.3 10.8 %collective-permute-start.37 = (bf16[2,400,768]{2,1,0:T(8,128)(2,1)}, bf16[2,400,768]{2,1,0:T(8,128)(2,1)S(1)}, u32[]{:S(2)}, u32[]{:S(2)}) collective-permute-start(bf16[2,400,768]{2,1,0:T(8,128)(2,1)} %get-tuple-element.343), channel_id=1, source_target_pairs={{0,4},{4,0},{8,12},{12,8},{16,20},{20,16},{24,28},{28,24},{1,5},{5... | collective-permute-start | bytes 3686408 | tf_op jit(solution)/shard_map/ppermute | solution.py:949
  170.1 10.0 %collective-permute-start.40 = (bf16[2,96,768]{2,1,0:T(8,128)(2,1)S(1)}, bf16[2,96,768]{2,1,0:T(8,128)(2,1)S(1)}, u32[]{:S(2)}, u32[]{:S(2)}) collective-permute-start(bf16[2,96,768]{2,1,0:T(8,128)(2,1)S(1)} %get-tuple-element.351), channel_id=1, source_target_pairs={{0,3},{1,0},{2,1},{3,2},{4,7},{5,4},{6,5},{7,6},{8,11},{9,8},{10,9... | collective-permute-start | bytes 884744 | tf_op jit(solution)/shard_map/ppermute | solution.py:955
  180.9 8.9 %collective-permute-start.42 = (bf16[1,208,768]{2,1,0:T(8,128)(2,1)S(1)}, bf16[1,208,768]{2,1,0:T(8,128)(2,1)S(1)}, u32[]{:S(2)}, u32[]{:S(2)}) collective-permute-start(bf16[1,208,768]{2,1,0:T(8,128)(2,1)S(1)} %get-tuple-element.361), channel_id=1, source_target_pairs={{0,16},{4,20},{8,24},{12,28},{16,0},{20,4},{24,8},{28,12},{1,17},{... | collective-permute-start | bytes 958472 | tf_op jit(solution)/shard_map/ppermute | solution.py:949
  182.0 7.8 %collective-permute-start.41 = (bf16[1,192,768]{2,1,0:T(8,128)(2,1)S(1)}, bf16[1,192,768]{2,1,0:T(8,128)(2,1)S(1)}, u32[]{:S(2)}, u32[]{:S(2)}) collective-permute-start(bf16[1,192,768]{2,1,0:T(8,128)(2,1)S(1)} %get-tuple-element.360), channel_id=1, source_target_pairs={{0,8},{4,12},{8,0},{12,4},{16,24},{20,28},{24,16},{28,20},{1,9},{5... | collective-permute-start | bytes 884744 | tf_op jit(solution)/shard_map/ppermute | solution.py:949
  182.8 15.2 %collective-permute-start.45 = (bf16[2,96,768]{2,1,0:T(8,128)(2,1)S(1)}, bf16[2,96,768]{2,1,0:T(8,128)(2,1)S(1)}, u32[]{:S(2)}, u32[]{:S(2)}) collective-permute-start(bf16[2,96,768]{2,1,0:T(8,128)(2,1)S(1)} %get-tuple-element.352), channel_id=1, source_target_pairs={{0,2},{1,3},{2,0},{3,1},{4,6},{5,7},{6,4},{7,5},{8,10},{9,11},{10,... | collective-permute-start | bytes 884744 | tf_op jit(solution)/shard_map/ppermute | solution.py:955
  190.5 7.5 %collective-permute-start.44 = (bf16[1,112,768]{2,1,0:T(8,128)(2,1)S(1)}, bf16[1,112,768]{2,1,0:T(8,128)(2,1)S(1)}, u32[]{:S(2)}, u32[]{:S(2)}) collective-permute-start(bf16[1,112,768]{2,1,0:T(8,128)(2,1)S(1)} %get-tuple-element.372), channel_id=1, source_target_pairs={{0,8},{4,12},{8,0},{12,4},{16,24},{20,28},{24,16},{28,20},{1,9},{5... | collective-permute-start | bytes 516104 | tf_op jit(solution)/shard_map/ppermute | solution.py:949
  191.8 6.2 %collective-permute-start.43 = (bf16[1,96,768]{2,1,0:T(8,128)(2,1)S(1)}, bf16[1,96,768]{2,1,0:T(8,128)(2,1)S(1)}, u32[]{:S(2)}, u32[]{:S(2)}) collective-permute-start(bf16[1,96,768]{2,1,0:T(8,128)(2,1)S(1)} %get-tuple-element.371), channel_id=1, source_target_pairs={{0,16},{4,20},{8,24},{12,28},{16,0},{20,4},{24,8},{28,12},{1,17},{... | collective-permute-start | bytes 442376 | tf_op jit(solution)/shard_map/ppermute | solution.py:949
  198.7 8.5 %collective-permute-start.49 = (bf16[112,768]{1,0:T(8,128)(2,1)S(1)}, bf16[112,768]{1,0:T(8,128)(2,1)S(1)}, u32[]{:S(2)}, u32[]{:S(2)}) collective-permute-start(bf16[112,768]{1,0:T(8,128)(2,1)S(1)} %get-tuple-element.383), channel_id=1, source_target_pairs={{0,1},{1,2},{2,3},{3,0},{4,5},{5,6},{6,7},{7,4},{8,9},{9,10},{10,1... | collective-permute-start | bytes 516104 | tf_op jit(solution)/shard_map/ppermute | solution.py:955
  199.2 15.9 %collective-permute-start.48 = (bf16[2,96,768]{2,1,0:T(8,128)(2,1)S(1)}, bf16[2,96,768]{2,1,0:T(8,128)(2,1)S(1)}, u32[]{:S(2)}, u32[]{:S(2)}) collective-permute-start(bf16[2,96,768]{2,1,0:T(8,128)(2,1)S(1)} %total.1.refs_0_), channel_id=1, source_target_pairs={{0,24},{4,28},{8,16},{12,20},{16,8},{20,12},{24,0},{28,4},{1,25},{... | collective-permute-start | bytes 884744 | tf_op jit(solution)/shard_map/ppermute | solution.py:949
  200.4 14.7 %collective-permute-start.47 = (bf16[2,96,768]{2,1,0:T(8,128)(2,1)S(1)}, bf16[2,96,768]{2,1,0:T(8,128)(2,1)S(1)}, u32[]{:S(2)}, u32[]{:S(2)}) collective-permute-start(bf16[2,96,768]{2,1,0:T(8,128)(2,1)S(1)} %total.1.refs_0_), channel_id=1, source_target_pairs={{0,16},{4,20},{8,24},{12,28},{16,0},{20,4},{24,8},{28,12},{1,17},{... | collective-permute-start | bytes 884744 | tf_op jit(solution)/shard_map/ppermute | solution.py:949
  201.4 13.6 %collective-permute-start.46 = (bf16[2,96,768]{2,1,0:T(8,128)(2,1)S(1)}, bf16[2,96,768]{2,1,0:T(8,128)(2,1)S(1)}, u32[]{:S(2)}, u32[]{:S(2)}) collective-permute-start(bf16[2,96,768]{2,1,0:T(8,128)(2,1)S(1)} %total.1.refs_0_), channel_id=1, source_target_pairs={{0,8},{4,12},{8,0},{12,4},{16,24},{20,28},{24,16},{28,20},{1,9},{5... | collective-permute-start | bytes 884744 | tf_op jit(solution)/shard_map/ppermute | solution.py:949
  202.7 11.2 %collective-permute-start.50 = (bf16[112,768]{1,0:T(8,128)(2,1)S(1)}, bf16[112,768]{1,0:T(8,128)(2,1)S(1)}, u32[]{:S(2)}, u32[]{:S(2)}) collective-permute-start(bf16[112,768]{1,0:T(8,128)(2,1)S(1)} %get-tuple-element.384), channel_id=1, source_target_pairs={{0,2},{1,3},{2,0},{3,1},{4,6},{5,7},{6,4},{7,5},{8,10},{9,11},{10,... | collective-permute-start | bytes 516104 | tf_op jit(solution)/shard_map/ppermute | solution.py:955
  207.2 7.9 %collective-permute-start.51 = (bf16[112,768]{1,0:T(8,128)(2,1)S(1)}, bf16[112,768]{1,0:T(8,128)(2,1)S(1)}, u32[]{:S(2)}, u32[]{:S(2)}) collective-permute-start(bf16[112,768]{1,0:T(8,128)(2,1)S(1)} %get-tuple-element.385), channel_id=1, source_target_pairs={{0,3},{1,0},{2,1},{3,2},{4,7},{5,4},{6,5},{7,6},{8,11},{9,8},{10,9... | collective-permute-start | bytes 516104 | tf_op jit(solution)/shard_map/ppermute | solution.py:955
  215.4 7.8 %collective-permute-start.55 = (bf16[1,96,768]{2,1,0:T(8,128)(2,1)S(1)}, bf16[1,96,768]{2,1,0:T(8,128)(2,1)S(1)}, u32[]{:S(2)}, u32[]{:S(2)}) collective-permute-start(bf16[1,96,768]{2,1,0:T(8,128)(2,1)S(1)} %get-tuple-element.402.refs_0_), channel_id=1, source_target_pairs={{0,24},{4,28},{8,16},{12,20},{16,8},{20,12},{24,0},{28,4},{1,25},{... | collective-permute-start | bytes 442376 | tf_op jit(solution)/shard_map/ppermute | solution.py:949
  216.6 9.1 %collective-permute-start.54 = (bf16[1,96,768]{2,1,0:T(8,128)(2,1)S(1)}, bf16[1,96,768]{2,1,0:T(8,128)(2,1)S(1)}, u32[]{:S(2)}, u32[]{:S(2)}) collective-permute-start(bf16[1,96,768]{2,1,0:T(8,128)(2,1)S(1)} %get-tuple-element.402.refs_0_), channel_id=1, source_target_pairs={{0,16},{4,20},{8,24},{12,28},{16,0},{20,4},{24,8},{28,12},{1,17},{... | collective-permute-start | bytes 442376 | tf_op jit(solution)/shard_map/ppermute | solution.py:949
  217.7 8.1 %collective-permute-start.53 = (bf16[1,96,768]{2,1,0:T(8,128)(2,1)S(1)}, bf16[1,96,768]{2,1,0:T(8,128)(2,1)S(1)}, u32[]{:S(2)}, u32[]{:S(2)}) collective-permute-start(bf16[1,96,768]{2,1,0:T(8,128)(2,1)S(1)} %get-tuple-element.402.refs_0_), channel_id=1, source_target_pairs={{0,8},{4,12},{8,0},{12,4},{16,24},{20,28},{24,16},{28,20},{1,9},{5... | collective-permute-start | bytes 442376 | tf_op jit(solution)/shard_map/ppermute | solution.py:949
  (39 other events, 327.8 us)

commit v6 on v5

--- a/solution.py
+++ b/solution.py
@@ -230,8 +230,10 @@
         move.store(lse_ref.at[s], lse_out.at[s])
         if s == 0:
             wait(got_prior)
-        for part in range(2):
-            rows = pl.ds(part * half, half)
+        pieces = 2 if s == shards - 1 else 1
+        size = BIG // pieces
+        for part in range(pieces):
+            rows = pl.ds(part * size, size)
             before = prior_ref[rows, :].astype(F32) if s == 0 else hid_ref[rows, :]
             hidden = before + dot_nn(o_ref[s, rows, :], mat[s, :width, :])
             hid_ref[rows, :] = hidden
@@ -410,8 +412,10 @@
         )
         if c == 0:
             wait(got_prior)
-        for part in range(2):
-            rows = pl.ds(part * half, half)
+        pieces = 2 if c == count - 1 and not last else 1
+        size = BIG // pieces
+        for part in range(pieces):
+            rows = pl.ds(part * size, size)
             gn = dot_nn(gq_all[c, rows, :], mat[c])
             if not (first and c == 0):
                 gn = gn + gn_ref[rows, :]
@@ -569,7 +573,9 @@
         if c == 0:
             wait(got_sums)
         ending = c == count - 1
-        for part in range(2):
+        pieces = 2 if ending else 1
+        size = n2_ref.shape[0] // pieces
+        for part in range(pieces):
             rows = pl.ds(part * size, size)
             gn = dot_nt(gp_ref[c, rows, :], i_mat[c])
             out = dot_nn(act_ref[c, rows, :], w_mat[c])
@@ -648,26 +654,19 @@
 
 
 def prep_kernel(rows, bits, count, *refs):
-    mats, (tab_ref, in_ref, down_ref, a_ref, f_ref, wide_ref, sems) = refs[:count], refs[count:]
+    mats, (tab_ref, a_ref, wide_ref, sem) = refs[:count], refs[count:]
     block = row_block(lax.axis_index("dp") & ((1 << bits) - 1), bits)
-    first = pl.ds(pl.multiple_of(block * rows, rows), rows)
-    copies = [
-        pltpu.make_async_copy(in_ref.at[first], f_ref.at[0], sems.at[0]),
-        pltpu.make_async_copy(down_ref.at[first], f_ref.at[1], sems.at[1]),
-    ]
     per = mats[0].shape[0] // rows
 
     def piece(j, mat):
         at = pl.ds(pl.multiple_of((block - j * per) * rows, rows), rows)
-        return pltpu.make_async_copy(mat.at[at], a_ref.at[pl.ds(0, rows)], sems.at[2])
+        return pltpu.make_async_copy(mat.at[at], a_ref.at[pl.ds(0, rows)], sem)
 
     for j, mat in enumerate(mats):
         @pl.when(block // per == j)
         def _():
             piece(j, mat).start()
 
-    for copy in copies:
-        copy.start()
     tab = tab_ref[...].astype(F32)
     heads, buckets = tab.shape
     tab = jnp.concatenate([tab, jnp.zeros((heads, TILE - buckets), F32)], axis=1)
@@ -680,22 +679,44 @@
         def _():
             piece(j, mat).wait()
 
-    for copy in copies:
-        copy.wait()
-
-
-def prep(mats, tab, w_in, w_down, rows, bits):
-    depth = w_in.shape[0]
+
+def prep(mats, tab, depth, rows, bits):
     return pl.pallas_call(
         functools.partial(prep_kernel, rows, bits, len(mats)),
-        in_specs=[ANY] * len(mats) + [VMEM, ANY, ANY],
-        out_specs=[VMEM, VMEM, VMEM],
-        out_shape=[like((rows + EXTRA, depth), BF), like((2, rows, depth), BF), like((1, EXTRA, TILE), BF)],
-        scratch_shapes=[pltpu.SemaphoreType.DMA((3,))],
+        in_specs=[ANY] * len(mats) + [VMEM],
+        out_specs=[VMEM, VMEM],
+        out_shape=[like((rows + EXTRA, depth), BF), like((1, EXTRA, TILE), BF)],
+        scratch_shapes=[pltpu.SemaphoreType.DMA],
         compiler_params=params(60),
         cost_estimate=cost(0),
         name="prep",
-    )(*mats, tab, w_in, w_down)
+    )(*mats, tab)
+
+
+def prep_ffn_kernel(rows, bits, in_ref, down_ref, f_ref, sems):
+    block = row_block(lax.axis_index("dp") & ((1 << bits) - 1), bits)
+    first = pl.ds(pl.multiple_of(block * rows, rows), rows)
+    copies = [
+        pltpu.make_async_copy(in_ref.at[first], f_ref.at[0], sems.at[0]),
+        pltpu.make_async_copy(down_ref.at[first], f_ref.at[1], sems.at[1]),
+    ]
+    for copy in copies:
+        copy.start()
+    for copy in copies:
+        copy.wait()
+
+
+def prep_ffn(w_in, w_down, rows, bits):
+    return pl.pallas_call(
+        functools.partial(prep_ffn_kernel, rows, bits),
+        in_specs=[ANY, ANY],
+        out_specs=VMEM,
+        out_shape=like((2, rows, w_in.shape[1]), BF),
+        scratch_shapes=[pltpu.SemaphoreType.DMA((2,))],
+        compiler_params=params(60),
+        cost_estimate=cost(0),
+        name="prep_ffn",
+    )(w_in, w_down)
 
 
 def join_kernel(count, *refs):
@@ -1007,10 +1028,10 @@
     ring = Ring(n_dp, n_mp, depth, ids)
     shifts = list(range(1, n_mp))
     hot = jnp.asarray(offset_one_hot(buckets), BF)
-    gain_one, gain_two = gain_attn[None], gain_ffn[None]
 
     a_own = [w_out, w_query.T, w_key.T, w_value.T]
-    a_piece, f_piece, tab_own = prep(a_own, rel_table.T, w_in, w_down, ring.rows, ring.bits)
+    a_piece, tab_own = prep(a_own, rel_table.T, depth, ring.rows, ring.bits)
+    f_piece = prep_ffn(w_in, w_down, ring.rows, ring.bits)
     v = {}
 
     def close(*keys):
@@ -1028,15 +1049,16 @@
     x_value = inputs.astype(F32)
     n1 = (rms(x_value)[0] * gain_attn.astype(F32)).astype(BF)
     *kept_own, v["hidden"] = attn_fwd(ids, None, n1, a_own, 0, 1, tab_own, hot, inputs, None, slots, heads)
-    v["gain1"], v["gain2"] = gain_one, gain_two
+    v["gain1"], v["gain2"] = gain_attn, gain_ffn
     close(*[("z", s) for s in shifts], "hidden", "gain1", "gain2")
-    gain_one, gain_two = v["gain1"], v["gain2"]
     v["a"], tab_rest = join([v["z", s] for s in shifts])
     close("a", "piece")
     swap("ax", "a", 2)
     swap("ay", "a", 4)
     v["f", f1] = ring.pull(v["piece"], f1)
-    close("ax", "ay", "a", ("f", f1), "piece")
+    v["gain1"], v["gain2"] = v["gain1"][None], v["gain2"][None]
+    close("ax", "ay", "a", ("f", f1), "piece", "gain1", "gain2")
+    gain_one, gain_two = v["gain1"], v["gain2"]
     swap("ayx", "ax", 4)
     v["a3"] = cat([v["a"], v["ax"], v["ay"]])
     swap("a3c", "a3", 1)

time: 235 us -> 235 us (level)
  transfers between devices with their start and end apart: 57 -> 57, of which waited for: 19 -> 19; matrix products, arithmetic and copies ran while one was open for 2% -> 2% of each run, Pallas kernels for 42% -> 43%
where the time goes in v6:
time: 235 us; the launch traced here: 230 us
  Pallas kernels  105 us (45%)
  starting transfers between devices  63.6 us (27%)
  waiting for transfers between devices  51.4 us (22%)
  local copies, waits for them, and re-layouts  5.52 us (2%)
  between operations  2.5 us (1%)
    ppermute x45, starting transfers between devices, swap(): return lax.ppermute(x, 'dp', [(i, i ^ mask) for i in range(self.n_dp)])  36.6 us
    pallas_call x2, Pallas kernels, attn_bwd(): pl.pallas_call(functools.partial(attn_bwd_kernel, slots, heads, masks, tu...  33 us
    ppermute x45, waiting for transfers between devices, swap(): return lax.ppermute(x, 'dp', [(i, i ^ mask) for i in range(self.n_dp)])  28.6 us
    pallas_call x2, Pallas kernels, ffn(): pl.pallas_call(functools.partial(ffn_kernel, tuple((0 if m is None else l...  27.9 us
    pallas_call x3, Pallas kernels, attn_fwd(): pl.pallas_call(functools.partial(attn_fwd_kernel, slots, heads, len(a_par...  24.9 us
    ppermute x6, starting transfers between devices, pull(): lax.ppermute(x, 'mp', [(i, (i - shift) % self.n_mp) for i in range(self.n...  16.3 us
    ppermute x6, waiting for transfers between devices, push(): lax.ppermute(x, 'mp', [(i, (i + shift) % self.n_mp) for i in range(self.n...  13.2 us
    ppermute x6, starting transfers between devices, push(): lax.ppermute(x, 'mp', [(i, (i + shift) % self.n_mp) for i in range(self.n...  10.7 us
  transfers between devices with their start and end apart: 57, of which 19 were waited for; matrix products, arithmetic and copies ran while one was open for 2% of the time, Pallas kernels for 43%

profile of v6, /device:TPU:0, one launch (start us, length us, event | category | flops | bytes accessed | tf_op | source)
XLA Modules:
  0.0 230.1 jit_solution(6473105383131533877)
XLA Ops:
  0.7 2.3 %prep.1 = (bf16[112,768]{1,0:T(8,128)(2,1)}, bf16[1,16,128]{2,1,0:T(8,128)(2,1)}) custom-call(bf16[192,768]{1,0:T(8,128)(2,1)} %refs_11_.1, bf16[192,768]{1,0:T(8,128)(2,1)} %bitcast.14, bf16[192,768]{1,0:T(8,128)(2,1)} %bitcast.17, bf16[192,768]{1,0:T(8,128)(2,1)} %bitcast.20, bf16[3,32]{1,0:T(4,128)(2,1)} %bitcast.24), custom_call_target="tpu_custom_call" | custom-call | tf_op jit(solution)/shard_map/prep/pallas_call | solution.py:684
  3.0 3.1 %collective-permute-start.2 = (bf16[112,768]{1,0:T(8,128)(2,1)}, bf16[112,768]{1,0:T(8,128)(2,1)S(1)}, u32[]{:S(2)}, u32[]{:S(2)}) collective-permute-start(bf16[112,768]{1,0:T(8,128)(2,1)} %get-tuple-element.215), channel_id=1, source_target_pairs={{0,1},{1,2},{2,3},{3,0},{4,5},{5,6},{6,7},{7,4},{8,9},{9,10},{10,1... | collective-permute-start | bytes 516104 | tf_op jit(solution)/shard_map/ppermute | solution.py:973
  6.1 2.6 %collective-permute-start.1 = (bf16[112,768]{1,0:T(8,128)(2,1)}, bf16[112,768]{1,0:T(8,128)(2,1)S(1)}, u32[]{:S(2)}, u32[]{:S(2)}) collective-permute-start(bf16[112,768]{1,0:T(8,128)(2,1)} %get-tuple-element.215), channel_id=1, source_target_pairs={{0,2},{1,3},{2,0},{3,1},{4,6},{5,7},{6,4},{7,5},{8,10},{9,11},{10,... | collective-permute-start | bytes 516104 | tf_op jit(solution)/shard_map/ppermute | solution.py:973
  8.7 1.3 collective-permute-start
  12.7 7.0 %attn_fwd.3 = (bf16[1,512,768]{2,1,0:T(8,128)(2,1)}, bf16[1,512,192]{2,1,0:T(8,128)(2,1)}, f32[1,512,128]{2,1,0:T(8,128)}, f32[512,768]{1,0:T(8,128)}) custom-call(s32[11]{0:T(128)} %pad_add_fusion.ids_ref, bf16[512,768]{1,0:T(8,128)(2,1)} %fusion.2.refs_0_, bf16[192,768]{1,0:T(8,128)(2,1)} %refs_11_.1, bf16[192,768]{1,0:T(8,128)(2,1)} %bitcast.15, ...), custom_call_target="tpu_custom_call" | custom-call | flops 16000000000 | bytes 16000000 | tf_op jit(solution)/shard_map/attn_fwd/pallas_call | solution.py:265
  19.8 1.7 prep_ffn.1
  22.2 1.5 collective-permute-start.4
  23.7 1.5 collective-permute-start.3
  25.2 3.9 %collective-permute-start.5 = (bf16[2,96,768]{2,1,0:T(8,128)(2,1)}, bf16[2,96,768]{2,1,0:T(8,128)(2,1)S(1)}, u32[]{:S(2)}, u32[]{:S(2)}) collective-permute-start(bf16[2,96,768]{2,1,0:T(8,128)(2,1)} %prep_ffn.1), channel_id=1, source_target_pairs={{0,3},{1,0},{2,1},{3,2},{4,7},{5,4},{6,5},{7,6},{8,11},{9,8},{10,9... | collective-permute-start | bytes 884744 | tf_op jit(solution)/shard_map/ppermute | solution.py:973
  30.2 4.6 %collective-permute-done.5.refs_0_ = bf16[2,96,768]{2,1,0:T(8,128)(2,1)S(1)} collective-permute-done((bf16[2,96,768]{2,1,0:T(8,128)(2,1)}, bf16[2,96,768]{2,1,0:T(8,128)(2,1)S(1)}, u32[]{:S(2)}, u32[]{:S(2)}) %collective-permute-start.5) | collective-permute-done | bytes 294944 | tf_op jit(solution)/shard_map/ppermute | solution.py:973
  36.7 4.0 %collective-permute-start.9 = (bf16[2,96,768]{2,1,0:T(8,128)(2,1)S(1)}, bf16[2,96,768]{2,1,0:T(8,128)(2,1)S(1)}, u32[]{:S(2)}, u32[]{:S(2)}) collective-permute-start(bf16[2,96,768]{2,1,0:T(8,128)(2,1)S(1)} %copy-done.14), channel_id=1, source_target_pairs={{0,1},{1,2},{2,3},{3,0},{4,5},{5,6},{6,7},{7,4},{8,9},{9,10},{10,1... | collective-permute-start | bytes 884744 | tf_op jit(solution)/shard_map/ppermute | solution.py:973
  40.7 3.9 %collective-permute-done.8.refs_1_ = bf16[2,96,768]{2,1,0:T(8,128)(2,1)S(1)} collective-permute-done((bf16[2,96,768]{2,1,0:T(8,128)(2,1)S(1)}, bf16[2,96,768]{2,1,0:T(8,128)(2,1)S(1)}, u32[]{:S(2)}, u32[]{:S(2)}) %collective-permute-start.8) | collective-permute-done | bytes 294944 | tf_op jit(solution)/shard_map/ppermute | solution.py:970
  44.7 3.2 %collective-permute-done.9.refs_0_ = bf16[2,96,768]{2,1,0:T(8,128)(2,1)S(1)} collective-permute-done((bf16[2,96,768]{2,1,0:T(8,128)(2,1)S(1)}, bf16[2,96,768]{2,1,0:T(8,128)(2,1)S(1)}, u32[]{:S(2)}, u32[]{:S(2)}) %collective-permute-start.9) | collective-permute-done | bytes 294944 | tf_op jit(solution)/shard_map/ppermute | solution.py:973
  48.5 1.5 collective-permute-start.13
  50.0 1.4 collective-permute-start.12
  51.5 1.4 collective-permute-start.11
  53.6 10.5 %attn_fwd.4 = (bf16[2,512,768]{2,1,0:T(8,128)(2,1)}, bf16[2,512,192]{2,1,0:T(8,128)(2,1)}, f32[2,512,128]{2,1,0:T(8,128)}, f32[512,768]{1,0:T(8,128)}) custom-call(s32[11]{0:T(128)} %pad_add_fusion.ids_ref, bf16[512,768]{1,0:T(8,128)(2,1)} %fusion.2.refs_0_, bf16[3,3,96,768]{3,2,1,0:T(8,128)(2,1)} %copy-done.2, bf16[1,3,96,768]{3,2,1,0:T(8,128)(2,1)} %bitcast.30, ...), custom_call_target="tpu_custom_call" | custom-call | flops 32000000000 | bytes 32000000 | tf_op jit(solution)/shard_map/attn_fwd/pallas_call | solution.py:265
  64.1 1.8 collective-permute-done.12.refs_0_
  67.9 7.4 %attn_fwd.5 = (bf16[1,512,768]{2,1,0:T(8,128)(2,1)}, bf16[1,512,192]{2,1,0:T(8,128)(2,1)}, f32[1,512,128]{2,1,0:T(8,128)}, f32[512,768]{1,0:T(8,128)}, bf16[512,768]{1,0:T(8,128)(2,1)}) custom-call(s32[11]{0:T(128)} %pad_add_fusion.ids_ref, bf16[512,768]{1,0:T(8,128)(2,1)} %fusion.2.refs_0_, bf16[3,3,96,768]{3,2,1,0:T(8,128)(2,1)} %copy-done.2, ...), custom_call_target="tpu_custom_call" | custom-call | flops 16000000000 | bytes 16000000 | tf_op jit(solution)/shard_map/attn_fwd/pallas_call | solution.py:265
  76.0 1.5 collective-permute-start.17
  77.5 13.9 %ffn.2 = (f32[512,768]{1,0:T(8,128)}, f32[512,768]{1,0:T(8,128)}, bf16[4,384,768]{2,1,0:T(8,128)(2,1)}, bf16[4,384,768]{2,1,0:T(8,128)(2,1)}) custom-call(s32[11]{0:T(128)} %pad_add_fusion.ids_ref, bf16[512,768]{1,0:T(8,128)(2,1)} %get-tuple-element.269.refs_0_, bf16[512,768]{1,0:T(8,128)(2,1)} %refs_1_.5, bf16[768,768]{1,0:T(8,128)(2,1)} %refs_2_.3, ...), custom_call_target="tpu_custom_call" | custom-call | flops 64000000000 | bytes 64000000 | tf_op jit(solution)/shard_map/ffn/pallas_call | solution.py:642
  91.5 3.0 %collective-permute-done.17.refs_7_ = bf16[2,2,96,768]{3,2,1,0:T(8,128)(2,1)S(1)} collective-permute-done((bf16[2,2,96,768]{3,2,1,0:T(8,128)(2,1)S(1)}, bf16[2,2,96,768]{3,2,1,0:T(8,128)(2,1)S(1)}, u32[]{:S(2)}, u32[]{:S(2)}) %collective-permute-start.17) | collective-permute-done | bytes 589856 | tf_op jit(solution)/shard_map/ppermute | solution.py:970
  95.0 4.5 %collective-permute-done.22.refs_9_ = bf16[2,2,96,768]{3,2,1,0:T(8,128)(2,1)S(1)} collective-permute-done((bf16[2,2,96,768]{3,2,1,0:T(8,128)(2,1)S(1)}, bf16[2,2,96,768]{3,2,1,0:T(8,128)(2,1)S(1)}, u32[]{:S(2)}, u32[]{:S(2)}) %collective-permute-start.22) | collective-permute-done | bytes 589856 | tf_op jit(solution)/shard_map/ppermute | solution.py:970
  101.0 1.7 copy-done.1
  105.5 14.0 %ffn.3 = (bf16[512,768]{1,0:T(8,128)(2,1)}, bf16[4,384,768]{2,1,0:T(8,128)(2,1)}, bf16[4,384,768]{2,1,0:T(8,128)(2,1)}, f32[512,768]{1,0:T(8,128)}, bf16[512,768]{1,0:T(8,128)(2,1)}, /*index=5*/f32[8,768]{1,0:T(8,128)}) custom-call(s32[11]{0:T(128)} %pad_add_fusion.ids_ref, bf16[512,768]{1,0:T(8,128)(2,1)} %get-tuple-element.269.refs_0_, ...), custom_call_target="tpu_custom_call" | custom-call | flops 64000000000 | bytes 64000000 | tf_op jit(solution)/shard_map/ffn/pallas_call | solution.py:642
  121.5 1.4 collective-permute-start.27
  122.9 1.5 collective-permute-done.28.refs_1_
  125.4 1.4 collective-permute-start.29
  127.9 15.9 %attn_bwd.2 = (bf16[2,384,768]{2,1,0:T(8,128)(2,1)}, bf16[2,384,768]{2,1,0:T(8,128)(2,1)}, f32[512,768]{1,0:T(8,128)}, f32[2,8,128]{2,1,0:T(8,128)}) custom-call(s32[11]{0:T(128)} %pad_add_fusion.ids_ref, bf16[512,768]{1,0:T(8,128)(2,1)} %fusion.2.refs_0_, bf16[512,768]{1,0:T(8,128)(2,1)} %get-tuple-element.329.refs_1_, ...), custom_call_target="tpu_custom_call" | custom-call | flops 64000000000 | bytes 64000000 | tf_op jit(solution)/shard_map/attn_bwd/pallas_call | solution.py:507
  144.6 1.4 collective-permute-start.36
  147.8 1.3 collective-permute-start.32
  151.8 17.1 %attn_bwd.3 = (bf16[2,400,768]{2,1,0:T(8,128)(2,1)}, bf16[2,400,768]{2,1,0:T(8,128)(2,1)}, bf16[512,768]{1,0:T(8,128)(2,1)}) custom-call(s32[11]{0:T(128)} %pad_add_fusion.ids_ref, bf16[512,768]{1,0:T(8,128)(2,1)} %fusion.2.refs_0_, bf16[512,768]{1,0:T(8,128)(2,1)} %get-tuple-element.329.refs_1_, bf16[128,512]{1,0:T(8,128)(2,1)} %constant.22.clone.refs_6_.refs_2_, ...), custom_call_target="tpu_custom_call" | custom-call | flops 64000000000 | bytes 64000000 | tf_op jit(solution)/shard_map/attn_bwd/pallas_call | solution.py:507
  169.8 2.6 %collective-permute-start.40 = (bf16[2,96,768]{2,1,0:T(8,128)(2,1)S(1)}, bf16[2,96,768]{2,1,0:T(8,128)(2,1)S(1)}, u32[]{:S(2)}, u32[]{:S(2)}) collective-permute-start(bf16[2,96,768]{2,1,0:T(8,128)(2,1)S(1)} %get-tuple-element.353), channel_id=1, source_target_pairs={{0,3},{1,0},{2,1},{3,2},{4,7},{5,4},{6,5},{7,6},{8,11},{9,8},{10,9... | collective-permute-start | bytes 884744 | tf_op jit(solution)/shard_map/ppermute | solution.py:976
  174.9 4.2 %collective-permute-done.38.refs_1_ = bf16[1,96,768]{2,1,0:T(8,128)(2,1)S(1)} collective-permute-done((bf16[1,96,768]{2,1,0:T(8,128)(2,1)S(1)}, bf16[1,96,768]{2,1,0:T(8,128)(2,1)S(1)}, u32[]{:S(2)}, u32[]{:S(2)}) %collective-permute-start.38) | collective-permute-done | bytes 147488 | tf_op jit(solution)/shard_map/ppermute | solution.py:970
  182.5 2.1 collective-permute-start.45
  185.2 4.3 %collective-permute-done.41.refs_1_ = bf16[1,192,768]{2,1,0:T(8,128)(2,1)S(1)} collective-permute-done((bf16[1,192,768]{2,1,0:T(8,128)(2,1)S(1)}, bf16[1,192,768]{2,1,0:T(8,128)(2,1)S(1)}, u32[]{:S(2)}, u32[]{:S(2)}) %collective-permute-start.41) | collective-permute-done | bytes 294944 | tf_op jit(solution)/shard_map/ppermute | solution.py:970
  190.2 1.3 collective-permute-start.44
  192.5 5.1 %collective-permute-done.45.refs_3_ = bf16[2,96,768]{2,1,0:T(8,128)(2,1)S(1)} collective-permute-done((bf16[2,96,768]{2,1,0:T(8,128)(2,1)S(1)}, bf16[2,96,768]{2,1,0:T(8,128)(2,1)S(1)}, u32[]{:S(2)}, u32[]{:S(2)}) %collective-permute-start.45) | collective-permute-done | bytes 294944 | tf_op jit(solution)/shard_map/ppermute | solution.py:976
  198.9 1.3 collective-permute-start.48
  201.2 1.3 collective-permute-start.46
  202.4 3.4 %collective-permute-start.50 = (bf16[112,768]{1,0:T(8,128)(2,1)S(1)}, bf16[112,768]{1,0:T(8,128)(2,1)S(1)}, u32[]{:S(2)}, u32[]{:S(2)}) collective-permute-start(bf16[112,768]{1,0:T(8,128)(2,1)S(1)} %get-tuple-element.386), channel_id=1, source_target_pairs={{0,2},{1,3},{2,0},{3,1},{4,6},{5,7},{6,4},{7,5},{8,10},{9,11},{10,... | collective-permute-start | bytes 516104 | tf_op jit(solution)/shard_map/ppermute | solution.py:976
  207.8 5.8 %collective-permute-done.50.refs_2_ = bf16[112,768]{1,0:T(8,128)(2,1)S(1)} collective-permute-done((bf16[112,768]{1,0:T(8,128)(2,1)S(1)}, bf16[112,768]{1,0:T(8,128)(2,1)S(1)}, u32[]{:S(2)}, u32[]{:S(2)}) %collective-permute-start.50) | collective-permute-done | bytes 172064 | tf_op jit(solution)/shard_map/ppermute | solution.py:976
  215.1 1.3 collective-permute-start.55
  217.4 1.3 collective-permute-start.53
  219.8 3.0 %finish.2 = (f32[768,768]{1,0:T(8,128)}, f32[768,768]{1,0:T(8,128)}) custom-call(s32[11]{0:T(128)S(1)} %copy-done.11, bf16[4,2,96,768]{3,2,1,0:T(8,128)(2,1)S(1)} %cat.10.refs_0_, bf16[4,2,96,768]{3,2,1,0:T(8,128)(2,1)S(1)} %collective-permute-done.52.refs_1_), custom_call_target="tpu_custom_call" | custom-call | tf_op jit(solution)/shard_map/finish/pallas_call | solution.py:934
  222.9 2.6 %collective-permute-done.54.refs_2_ = bf16[1,96,768]{2,1,0:T(8,128)(2,1)S(1)} collective-permute-done((bf16[1,96,768]{2,1,0:T(8,128)(2,1)S(1)}, bf16[1,96,768]{2,1,0:T(8,128)(2,1)S(1)}, u32[]{:S(2)}, u32[]{:S(2)}) %collective-permute-start.54) | collective-permute-done | bytes 147488 | tf_op jit(solution)/shard_map/ppermute | solution.py:970
  225.6 2.0 collective-permute-done.56.refs_1_
  227.6 2.1 finish.3
  (169 shorter events, 40.9 us)
Async XLA Ops:
  3.0 18.5 %collective-permute-start.2 = (bf16[112,768]{1,0:T(8,128)(2,1)}, bf16[112,768]{1,0:T(8,128)(2,1)S(1)}, u32[]{:S(2)}, u32[]{:S(2)}) collective-permute-start(bf16[112,768]{1,0:T(8,128)(2,1)} %get-tuple-element.215), channel_id=1, source_target_pairs={{0,1},{1,2},{2,3},{3,0},{4,5},{5,6},{6,7},{7,4},{8,9},{9,10},{10,1... | collective-permute-start | bytes 516104 | tf_op jit(solution)/shard_map/ppermute | solution.py:973
  6.1 15.4 %collective-permute-start.1 = (bf16[112,768]{1,0:T(8,128)(2,1)}, bf16[112,768]{1,0:T(8,128)(2,1)S(1)}, u32[]{:S(2)}, u32[]{:S(2)}) collective-permute-start(bf16[112,768]{1,0:T(8,128)(2,1)} %get-tuple-element.215), channel_id=1, source_target_pairs={{0,2},{1,3},{2,0},{3,1},{4,6},{5,7},{6,4},{7,5},{8,10},{9,11},{10,... | collective-permute-start | bytes 516104 | tf_op jit(solution)/shard_map/ppermute | solution.py:973
  8.7 12.8 %collective-permute-start = (bf16[112,768]{1,0:T(8,128)(2,1)}, bf16[112,768]{1,0:T(8,128)(2,1)S(1)}, u32[]{:S(2)}, u32[]{:S(2)}) collective-permute-start(bf16[112,768]{1,0:T(8,128)(2,1)} %get-tuple-element.215), channel_id=1, source_target_pairs={{0,3},{1,0},{2,1},{3,2},{4,7},{5,4},{6,5},{7,6},{8,11},{9,8},{10,9... | collective-permute-start | bytes 516104 | tf_op jit(solution)/shard_map/ppermute | solution.py:973
  22.2 12.7 %collective-permute-start.4 = (bf16[3,96,768]{2,1,0:T(8,128)(2,1)S(1)}, bf16[3,96,768]{2,1,0:T(8,128)(2,1)S(1)}, u32[]{:S(2)}, u32[]{:S(2)}) collective-permute-start(bf16[3,96,768]{2,1,0:T(8,128)(2,1)S(1)} %get-tuple-element.226.refs_0_), channel_id=1, source_target_pairs={{0,16},{4,20},{8,24},{12,28},{16,0},{20,4},{24,8},{28,12},{1,17},{... | collective-permute-start | bytes 1327112 | tf_op jit(solution)/shard_map/ppermute | solution.py:970
  23.7 11.1 %collective-permute-start.3 = (bf16[3,96,768]{2,1,0:T(8,128)(2,1)S(1)}, bf16[3,96,768]{2,1,0:T(8,128)(2,1)S(1)}, u32[]{:S(2)}, u32[]{:S(2)}) collective-permute-start(bf16[3,96,768]{2,1,0:T(8,128)(2,1)S(1)} %get-tuple-element.226.refs_0_), channel_id=1, source_target_pairs={{0,8},{4,12},{8,0},{12,4},{16,24},{20,28},{24,16},{28,20},{1,9},{5... | collective-permute-start | bytes 1327112 | tf_op jit(solution)/shard_map/ppermute | solution.py:970
  25.2 9.6 %collective-permute-start.5 = (bf16[2,96,768]{2,1,0:T(8,128)(2,1)}, bf16[2,96,768]{2,1,0:T(8,128)(2,1)S(1)}, u32[]{:S(2)}, u32[]{:S(2)}) collective-permute-start(bf16[2,96,768]{2,1,0:T(8,128)(2,1)} %prep_ffn.1), channel_id=1, source_target_pairs={{0,3},{1,0},{2,1},{3,2},{4,7},{5,4},{6,5},{7,6},{8,11},{9,8},{10,9... | collective-permute-start | bytes 884744 | tf_op jit(solution)/shard_map/ppermute | solution.py:973
  34.9 12.9 %collective-permute-start.7 = (bf16[3,3,96,768]{3,2,1,0:T(8,128)(2,1)S(1)}, bf16[3,3,96,768]{3,2,1,0:T(8,128)(2,1)S(1)}, u32[]{:S(2)}, u32[]{:S(2)}) collective-permute-start(bf16[3,3,96,768]{3,2,1,0:T(8,128)(2,1)S(1)} %cat.6.refs_1_.refs_3_), channel_id=1, source_target_pairs={{0,4},{4,0},{8,12},{12,8},{16,20},{20,16},{24,28},{28,24},{1,5},{5... | collective-permute-start | bytes 3981320 | tf_op jit(solution)/shard_map/ppermute | solution.py:970
  35.0 12.8 %collective-permute-start.6 = (bf16[3,96,768]{2,1,0:T(8,128)(2,1)S(1)}, bf16[3,96,768]{2,1,0:T(8,128)(2,1)S(1)}, u32[]{:S(2)}, u32[]{:S(2)}) collective-permute-start(bf16[3,96,768]{2,1,0:T(8,128)(2,1)S(1)} %collective-permute-done.3.refs_1_), channel_id=1, source_target_pairs={{0,16},{4,20},{8,24},{12,28},{16,0},{20,4},{24,8},{28,12},{1,17},{... | collective-permute-start | bytes 1327112 | tf_op jit(solution)/shard_map/ppermute | solution.py:970
  35.6 9.1 %collective-permute-start.8 = (bf16[2,96,768]{2,1,0:T(8,128)(2,1)S(1)}, bf16[2,96,768]{2,1,0:T(8,128)(2,1)S(1)}, u32[]{:S(2)}, u32[]{:S(2)}) collective-permute-start(bf16[2,96,768]{2,1,0:T(8,128)(2,1)S(1)} %collective-permute-done.5.refs_0_), channel_id=1, source_target_pairs={{0,8},{4,12},{8,0},{12,4},{16,24},{20,28},{24,16},{28,20},{1,9},{5... | collective-permute-start | bytes 884744 | tf_op jit(solution)/shard_map/ppermute | solution.py:970
  36.7 11.1 %collective-permute-start.9 = (bf16[2,96,768]{2,1,0:T(8,128)(2,1)S(1)}, bf16[2,96,768]{2,1,0:T(8,128)(2,1)S(1)}, u32[]{:S(2)}, u32[]{:S(2)}) collective-permute-start(bf16[2,96,768]{2,1,0:T(8,128)(2,1)S(1)} %copy-done.14), channel_id=1, source_target_pairs={{0,1},{1,2},{2,3},{3,0},{4,5},{5,6},{6,7},{7,4},{8,9},{9,10},{10,1... | collective-permute-start | bytes 884744 | tf_op jit(solution)/shard_map/ppermute | solution.py:973
  48.0 27.3 %collective-permute-start.15 = (bf16[2,2,96,768]{3,2,1,0:T(8,128)(2,1)S(1)}, bf16[2,2,96,768]{3,2,1,0:T(8,128)(2,1)S(1)}, u32[]{:S(2)}, u32[]{:S(2)}) collective-permute-start(bf16[2,2,96,768]{3,2,1,0:T(8,128)(2,1)S(1)} %cat.7.refs_4_), channel_id=1, source_target_pairs={{0,4},{4,0},{8,12},{12,8},{16,20},{20,16},{24,28},{28,24},{1,5},{5... | collective-permute-start | bytes 1769480 | tf_op jit(solution)/shard_map/ppermute | solution.py:970
  48.5 17.5 %collective-permute-start.13 = (bf16[2,2,96,768]{3,2,1,0:T(8,128)(2,1)S(1)}, bf16[2,2,96,768]{3,2,1,0:T(8,128)(2,1)S(1)}, u32[]{:S(2)}, u32[]{:S(2)}) collective-permute-start(bf16[2,2,96,768]{3,2,1,0:T(8,128)(2,1)S(1)} %cat.7.refs_4_), channel_id=1, source_target_pairs={{0,16},{4,20},{8,24},{12,28},{16,0},{20,4},{24,8},{28,12},{1,17},{... | collective-permute-start | bytes 1769480 | tf_op jit(solution)/shard_map/ppermute | solution.py:970
  50.0 15.9 %collective-permute-start.12 = (bf16[2,96,768]{2,1,0:T(8,128)(2,1)S(1)}, bf16[2,96,768]{2,1,0:T(8,128)(2,1)S(1)}, u32[]{:S(2)}, u32[]{:S(2)}) collective-permute-start(bf16[2,96,768]{2,1,0:T(8,128)(2,1)S(1)} %copy-done.14), channel_id=1, source_target_pairs={{0,2},{1,3},{2,0},{3,1},{4,6},{5,7},{6,4},{7,5},{8,10},{9,11},{10,... | collective-permute-start | bytes 884744 | tf_op jit(solution)/shard_map/ppermute | solution.py:973
  51.5 14.5 %collective-permute-start.11 = (bf16[2,96,768]{2,1,0:T(8,128)(2,1)S(1)}, bf16[2,96,768]{2,1,0:T(8,128)(2,1)S(1)}, u32[]{:S(2)}, u32[]{:S(2)}) collective-permute-start(bf16[2,96,768]{2,1,0:T(8,128)(2,1)S(1)} %collective-permute-done.9.refs_0_), channel_id=1, source_target_pairs={{0,8},{4,12},{8,0},{12,4},{16,24},{20,28},{24,16},{28,20},{1,9},{5... | collective-permute-start | bytes 884744 | tf_op jit(solution)/shard_map/ppermute | solution.py:970
  66.0 25.4 %collective-permute-start.20 = (bf16[2,2,96,768]{3,2,1,0:T(8,128)(2,1)S(1)}, bf16[2,2,96,768]{3,2,1,0:T(8,128)(2,1)S(1)}, u32[]{:S(2)}, u32[]{:S(2)}) collective-permute-start(bf16[2,2,96,768]{3,2,1,0:T(8,128)(2,1)S(1)} %cat.9.refs_2_), channel_id=1, source_target_pairs={{0,4},{4,0},{8,12},{12,8},{16,20},{20,16},{24,28},{28,24},{1,5},{5... | collective-permute-start | bytes 1769480 | tf_op jit(solution)/shard_map/ppermute | solution.py:970
  66.1 25.3 %collective-permute-start.18 = (bf16[2,2,96,768]{3,2,1,0:T(8,128)(2,1)S(1)}, bf16[2,2,96,768]{3,2,1,0:T(8,128)(2,1)S(1)}, u32[]{:S(2)}, u32[]{:S(2)}) collective-permute-start(bf16[2,2,96,768]{3,2,1,0:T(8,128)(2,1)S(1)} %cat.9.refs_2_), channel_id=1, source_target_pairs={{0,16},{4,20},{8,24},{12,28},{16,0},{20,4},{24,8},{28,12},{1,17},{... | collective-permute-start | bytes 1769480 | tf_op jit(solution)/shard_map/ppermute | solution.py:970
  66.7 9.1 %collective-permute-start.14 = (bf16[2,96,768]{2,1,0:T(8,128)(2,1)S(1)}, bf16[2,96,768]{2,1,0:T(8,128)(2,1)S(1)}, u32[]{:S(2)}, u32[]{:S(2)}) collective-permute-start(bf16[2,96,768]{2,1,0:T(8,128)(2,1)S(1)} %collective-permute-done.12.refs_0_), channel_id=1, source_target_pairs={{0,8},{4,12},{8,0},{12,4},{16,24},{20,28},{24,16},{28,20},{1,9},{5... | collective-permute-start | bytes 884744 | tf_op jit(solution)/shard_map/ppermute | solution.py:970
  67.9 7.9 %collective-permute-start.16 = (bf16[2,2,96,768]{3,2,1,0:T(8,128)(2,1)S(1)}, bf16[2,2,96,768]{3,2,1,0:T(8,128)(2,1)S(1)}, u32[]{:S(2)}, u32[]{:S(2)}) collective-permute-start(bf16[2,2,96,768]{3,2,1,0:T(8,128)(2,1)S(1)} %collective-permute-done.13.refs_5_), channel_id=1, source_target_pairs={{0,4},{4,0},{8,12},{12,8},{16,20},{20,16},{24,28},{28,24},{1,5},{5... | collective-permute-start | bytes 1769480 | tf_op jit(solution)/shard_map/ppermute | solution.py:970
  75.8 15.6 %collective-permute-start.19 = (bf16[2,2,96,768]{3,2,1,0:T(8,128)(2,1)S(1)}, bf16[2,2,96,768]{3,2,1,0:T(8,128)(2,1)S(1)}, u32[]{:S(2)}, u32[]{:S(2)}) collective-permute-start(bf16[2,2,96,768]{3,2,1,0:T(8,128)(2,1)S(1)} %cat.8.refs_6_), channel_id=1, source_target_pairs={{0,4},{4,0},{8,12},{12,8},{16,20},{20,16},{24,28},{28,24},{1,5},{5... | collective-permute-start | bytes 1769480 | tf_op jit(solution)/shard_map/ppermute | solution.py:970
  76.0 18.5 %collective-permute-start.17 = (bf16[2,2,96,768]{3,2,1,0:T(8,128)(2,1)S(1)}, bf16[2,2,96,768]{3,2,1,0:T(8,128)(2,1)S(1)}, u32[]{:S(2)}, u32[]{:S(2)}) collective-permute-start(bf16[2,2,96,768]{3,2,1,0:T(8,128)(2,1)S(1)} %cat.8.refs_6_), channel_id=1, source_target_pairs={{0,16},{4,20},{8,24},{12,28},{16,0},{20,4},{24,8},{28,12},{1,17},{... | collective-permute-start | bytes 1769480 | tf_op jit(solution)/shard_map/ppermute | solution.py:970
  94.5 6.4 %collective-permute-start.21 = (bf16[4,384,768]{2,1,0:T(8,128)(2,1)}, bf16[4,384,768]{2,1,0:T(8,128)(2,1)S(1)}, u32[]{:S(2)}, u32[]{:S(2)}) collective-permute-start(bf16[4,384,768]{2,1,0:T(8,128)(2,1)} %get-tuple-element.256), channel_id=1, source_target_pairs={{0,4},{4,0},{8,12},{12,8},{16,20},{20,16},{24,28},{28,24},{1,5},{5... | collective-permute-start | bytes 7077896 | tf_op jit(solution)/shard_map/ppermute | solution.py:970
  103.8 15.7 %collective-permute-start.24 = (bf16[2,192,768]{2,1,0:T(8,128)(2,1)S(1)}, bf16[2,192,768]{2,1,0:T(8,128)(2,1)S(1)}, u32[]{:S(2)}, u32[]{:S(2)}) collective-permute-start(bf16[2,192,768]{2,1,0:T(8,128)(2,1)S(1)} %get-tuple-element.278), channel_id=1, source_target_pairs={{0,8},{4,12},{8,0},{12,4},{16,24},{20,28},{24,16},{28,20},{1,9},{5... | collective-permute-start | bytes 1769480 | tf_op jit(solution)/shard_map/ppermute | solution.py:970
  104.4 15.1 %collective-permute-start.25 = (bf16[2,192,768]{2,1,0:T(8,128)(2,1)S(1)}, bf16[2,192,768]{2,1,0:T(8,128)(2,1)S(1)}, u32[]{:S(2)}, u32[]{:S(2)}) collective-permute-start(bf16[2,192,768]{2,1,0:T(8,128)(2,1)S(1)} %get-tuple-element.279), channel_id=1, source_target_pairs={{0,16},{4,20},{8,24},{12,28},{16,0},{20,4},{24,8},{28,12},{1,17},{... | collective-permute-start | bytes 1769480 | tf_op jit(solution)/shard_map/ppermute | solution.py:970
  120.4 23.3 %collective-permute-start.26 = (bf16[2,96,768]{2,1,0:T(8,128)(2,1)S(1)}, bf16[2,96,768]{2,1,0:T(8,128)(2,1)S(1)}, u32[]{:S(2)}, u32[]{:S(2)}) collective-permute-start(bf16[2,96,768]{2,1,0:T(8,128)(2,1)S(1)} %get-tuple-element.286), channel_id=1, source_target_pairs={{0,16},{4,20},{8,24},{12,28},{16,0},{20,4},{24,8},{28,12},{1,17},{... | collective-permute-start | bytes 884744 | tf_op jit(solution)/shard_map/ppermute | solution.py:970
  121.5 22.3 %collective-permute-start.27 = (bf16[2,96,768]{2,1,0:T(8,128)(2,1)S(1)}, bf16[2,96,768]{2,1,0:T(8,128)(2,1)S(1)}, u32[]{:S(2)}, u32[]{:S(2)}) collective-permute-start(bf16[2,96,768]{2,1,0:T(8,128)(2,1)S(1)} %get-tuple-element.287), channel_id=1, source_target_pairs={{0,8},{4,12},{8,0},{12,4},{16,24},{20,28},{24,16},{28,20},{1,9},{5... | collective-permute-start | bytes 884744 | tf_op jit(solution)/shard_map/ppermute | solution.py:970
  125.4 18.4 %collective-permute-start.29 = (bf16[2,192,768]{2,1,0:T(8,128)(2,1)S(1)}, bf16[2,192,768]{2,1,0:T(8,128)(2,1)S(1)}, u32[]{:S(2)}, u32[]{:S(2)}) collective-permute-start(bf16[2,192,768]{2,1,0:T(8,128)(2,1)S(1)} %get-tuple-element.294), channel_id=1, source_target_pairs={{0,8},{4,12},{8,0},{12,4},{16,24},{20,28},{24,16},{28,20},{1,9},{5... | collective-permute-start | bytes 1769480 | tf_op jit(solution)/shard_map/ppermute | solution.py:970
  126.9 17.0 %collective-permute-start.30 = (bf16[2,192,768]{2,1,0:T(8,128)(2,1)S(1)}, bf16[2,192,768]{2,1,0:T(8,128)(2,1)S(1)}, u32[]{:S(2)}, u32[]{:S(2)}) collective-permute-start(bf16[2,192,768]{2,1,0:T(8,128)(2,1)S(1)} %get-tuple-element.295), channel_id=1, source_target_pairs={{0,16},{4,20},{8,24},{12,28},{16,0},{20,4},{24,8},{28,12},{1,17},{... | collective-permute-start | bytes 1769480 | tf_op jit(solution)/shard_map/ppermute | solution.py:970
  144.6 24.4 %collective-permute-start.36 = (bf16[2,96,768]{2,1,0:T(8,128)(2,1)S(1)}, bf16[2,96,768]{2,1,0:T(8,128)(2,1)S(1)}, u32[]{:S(2)}, u32[]{:S(2)}) collective-permute-start(bf16[2,96,768]{2,1,0:T(8,128)(2,1)S(1)} %get-tuple-element.319), channel_id=1, source_target_pairs={{0,1},{1,2},{2,3},{3,0},{4,5},{5,6},{6,7},{7,4},{8,9},{9,10},{10,1... | collective-permute-start | bytes 884744 | tf_op jit(solution)/shard_map/ppermute | solution.py:976
  146.8 22.2 %collective-permute-start.31 = (bf16[2,96,768]{2,1,0:T(8,128)(2,1)S(1)}, bf16[2,96,768]{2,1,0:T(8,128)(2,1)S(1)}, u32[]{:S(2)}, u32[]{:S(2)}) collective-permute-start(bf16[2,96,768]{2,1,0:T(8,128)(2,1)S(1)} %get-tuple-element.311), channel_id=1, source_target_pairs={{0,16},{4,20},{8,24},{12,28},{16,0},{20,4},{24,8},{28,12},{1,17},{... | collective-permute-start | bytes 884744 | tf_op jit(solution)/shard_map/ppermute | solution.py:970
  147.8 21.1 %collective-permute-start.32 = (bf16[2,96,768]{2,1,0:T(8,128)(2,1)S(1)}, bf16[2,96,768]{2,1,0:T(8,128)(2,1)S(1)}, u32[]{:S(2)}, u32[]{:S(2)}) collective-permute-start(bf16[2,96,768]{2,1,0:T(8,128)(2,1)S(1)} %get-tuple-element.312), channel_id=1, source_target_pairs={{0,8},{4,12},{8,0},{12,4},{16,24},{20,28},{24,16},{28,20},{1,9},{5... | collective-permute-start | bytes 884744 | tf_op jit(solution)/shard_map/ppermute | solution.py:970
  150.0 19.0 %collective-permute-start.34 = (bf16[1,192,768]{2,1,0:T(8,128)(2,1)S(1)}, bf16[1,192,768]{2,1,0:T(8,128)(2,1)S(1)}, u32[]{:S(2)}, u32[]{:S(2)}) collective-permute-start(bf16[1,192,768]{2,1,0:T(8,128)(2,1)S(1)} %get-tuple-element.323), channel_id=1, source_target_pairs={{0,8},{4,12},{8,0},{12,4},{16,24},{20,28},{24,16},{28,20},{1,9},{5... | collective-permute-start | bytes 884744 | tf_op jit(solution)/shard_map/ppermute | solution.py:970
  150.8 18.2 %collective-permute-start.35 = (bf16[1,192,768]{2,1,0:T(8,128)(2,1)S(1)}, bf16[1,192,768]{2,1,0:T(8,128)(2,1)S(1)}, u32[]{:S(2)}, u32[]{:S(2)}) collective-permute-start(bf16[1,192,768]{2,1,0:T(8,128)(2,1)S(1)} %get-tuple-element.324), channel_id=1, source_target_pairs={{0,16},{4,20},{8,24},{12,28},{16,0},{20,4},{24,8},{28,12},{1,17},{... | collective-permute-start | bytes 884744 | tf_op jit(solution)/shard_map/ppermute | solution.py:970
  169.0 10.8 %collective-permute-start.37 = (bf16[2,400,768]{2,1,0:T(8,128)(2,1)}, bf16[2,400,768]{2,1,0:T(8,128)(2,1)S(1)}, u32[]{:S(2)}, u32[]{:S(2)}) collective-permute-start(bf16[2,400,768]{2,1,0:T(8,128)(2,1)} %get-tuple-element.345), channel_id=1, source_target_pairs={{0,4},{4,0},{8,12},{12,8},{16,20},{20,16},{24,28},{28,24},{1,5},{5... | collective-permute-start | bytes 3686408 | tf_op jit(solution)/shard_map/ppermute | solution.py:970
  169.8 10.0 %collective-permute-start.40 = (bf16[2,96,768]{2,1,0:T(8,128)(2,1)S(1)}, bf16[2,96,768]{2,1,0:T(8,128)(2,1)S(1)}, u32[]{:S(2)}, u32[]{:S(2)}) collective-permute-start(bf16[2,96,768]{2,1,0:T(8,128)(2,1)S(1)} %get-tuple-element.353), channel_id=1, source_target_pairs={{0,3},{1,0},{2,1},{3,2},{4,7},{5,4},{6,5},{7,6},{8,11},{9,8},{10,9... | collective-permute-start | bytes 884744 | tf_op jit(solution)/shard_map/ppermute | solution.py:976
  180.6 8.9 %collective-permute-start.42 = (bf16[1,208,768]{2,1,0:T(8,128)(2,1)S(1)}, bf16[1,208,768]{2,1,0:T(8,128)(2,1)S(1)}, u32[]{:S(2)}, u32[]{:S(2)}) collective-permute-start(bf16[1,208,768]{2,1,0:T(8,128)(2,1)S(1)} %get-tuple-element.363), channel_id=1, source_target_pairs={{0,16},{4,20},{8,24},{12,28},{16,0},{20,4},{24,8},{28,12},{1,17},{... | collective-permute-start | bytes 958472 | tf_op jit(solution)/shard_map/ppermute | solution.py:970
  181.7 7.8 %collective-permute-start.41 = (bf16[1,192,768]{2,1,0:T(8,128)(2,1)S(1)}, bf16[1,192,768]{2,1,0:T(8,128)(2,1)S(1)}, u32[]{:S(2)}, u32[]{:S(2)}) collective-permute-start(bf16[1,192,768]{2,1,0:T(8,128)(2,1)S(1)} %get-tuple-element.362), channel_id=1, source_target_pairs={{0,8},{4,12},{8,0},{12,4},{16,24},{20,28},{24,16},{28,20},{1,9},{5... | collective-permute-start | bytes 884744 | tf_op jit(solution)/shard_map/ppermute | solution.py:970
  182.5 15.2 %collective-permute-start.45 = (bf16[2,96,768]{2,1,0:T(8,128)(2,1)S(1)}, bf16[2,96,768]{2,1,0:T(8,128)(2,1)S(1)}, u32[]{:S(2)}, u32[]{:S(2)}) collective-permute-start(bf16[2,96,768]{2,1,0:T(8,128)(2,1)S(1)} %get-tuple-element.354), channel_id=1, source_target_pairs={{0,2},{1,3},{2,0},{3,1},{4,6},{5,7},{6,4},{7,5},{8,10},{9,11},{10,... | collective-permute-start | bytes 884744 | tf_op jit(solution)/shard_map/ppermute | solution.py:976
  190.2 7.5 %collective-permute-start.44 = (bf16[1,112,768]{2,1,0:T(8,128)(2,1)S(1)}, bf16[1,112,768]{2,1,0:T(8,128)(2,1)S(1)}, u32[]{:S(2)}, u32[]{:S(2)}) collective-permute-start(bf16[1,112,768]{2,1,0:T(8,128)(2,1)S(1)} %get-tuple-element.374), channel_id=1, source_target_pairs={{0,8},{4,12},{8,0},{12,4},{16,24},{20,28},{24,16},{28,20},{1,9},{5... | collective-permute-start | bytes 516104 | tf_op jit(solution)/shard_map/ppermute | solution.py:970
  191.5 6.2 %collective-permute-start.43 = (bf16[1,96,768]{2,1,0:T(8,128)(2,1)S(1)}, bf16[1,96,768]{2,1,0:T(8,128)(2,1)S(1)}, u32[]{:S(2)}, u32[]{:S(2)}) collective-permute-start(bf16[1,96,768]{2,1,0:T(8,128)(2,1)S(1)} %get-tuple-element.373), channel_id=1, source_target_pairs={{0,16},{4,20},{8,24},{12,28},{16,0},{20,4},{24,8},{28,12},{1,17},{... | collective-permute-start | bytes 442376 | tf_op jit(solution)/shard_map/ppermute | solution.py:970
  198.4 8.5 %collective-permute-start.49 = (bf16[112,768]{1,0:T(8,128)(2,1)S(1)}, bf16[112,768]{1,0:T(8,128)(2,1)S(1)}, u32[]{:S(2)}, u32[]{:S(2)}) collective-permute-start(bf16[112,768]{1,0:T(8,128)(2,1)S(1)} %get-tuple-element.385), channel_id=1, source_target_pairs={{0,1},{1,2},{2,3},{3,0},{4,5},{5,6},{6,7},{7,4},{8,9},{9,10},{10,1... | collective-permute-start | bytes 516104 | tf_op jit(solution)/shard_map/ppermute | solution.py:976
  198.9 15.9 %collective-permute-start.48 = (bf16[2,96,768]{2,1,0:T(8,128)(2,1)S(1)}, bf16[2,96,768]{2,1,0:T(8,128)(2,1)S(1)}, u32[]{:S(2)}, u32[]{:S(2)}) collective-permute-start(bf16[2,96,768]{2,1,0:T(8,128)(2,1)S(1)} %total.1.refs_0_), channel_id=1, source_target_pairs={{0,24},{4,28},{8,16},{12,20},{16,8},{20,12},{24,0},{28,4},{1,25},{... | collective-permute-start | bytes 884744 | tf_op jit(solution)/shard_map/ppermute | solution.py:970
  200.1 14.7 %collective-permute-start.47 = (bf16[2,96,768]{2,1,0:T(8,128)(2,1)S(1)}, bf16[2,96,768]{2,1,0:T(8,128)(2,1)S(1)}, u32[]{:S(2)}, u32[]{:S(2)}) collective-permute-start(bf16[2,96,768]{2,1,0:T(8,128)(2,1)S(1)} %total.1.refs_0_), channel_id=1, source_target_pairs={{0,16},{4,20},{8,24},{12,28},{16,0},{20,4},{24,8},{28,12},{1,17},{... | collective-permute-start | bytes 884744 | tf_op jit(solution)/shard_map/ppermute | solution.py:970
  201.2 13.7 %collective-permute-start.46 = (bf16[2,96,768]{2,1,0:T(8,128)(2,1)S(1)}, bf16[2,96,768]{2,1,0:T(8,128)(2,1)S(1)}, u32[]{:S(2)}, u32[]{:S(2)}) collective-permute-start(bf16[2,96,768]{2,1,0:T(8,128)(2,1)S(1)} %total.1.refs_0_), channel_id=1, source_target_pairs={{0,8},{4,12},{8,0},{12,4},{16,24},{20,28},{24,16},{28,20},{1,9},{5... | collective-permute-start | bytes 884744 | tf_op jit(solution)/shard_map/ppermute | solution.py:970
  202.4 11.2 %collective-permute-start.50 = (bf16[112,768]{1,0:T(8,128)(2,1)S(1)}, bf16[112,768]{1,0:T(8,128)(2,1)S(1)}, u32[]{:S(2)}, u32[]{:S(2)}) collective-permute-start(bf16[112,768]{1,0:T(8,128)(2,1)S(1)} %get-tuple-element.386), channel_id=1, source_target_pairs={{0,2},{1,3},{2,0},{3,1},{4,6},{5,7},{6,4},{7,5},{8,10},{9,11},{10,... | collective-permute-start | bytes 516104 | tf_op jit(solution)/shard_map/ppermute | solution.py:976
  206.9 7.9 %collective-permute-start.51 = (bf16[112,768]{1,0:T(8,128)(2,1)S(1)}, bf16[112,768]{1,0:T(8,128)(2,1)S(1)}, u32[]{:S(2)}, u32[]{:S(2)}) collective-permute-start(bf16[112,768]{1,0:T(8,128)(2,1)S(1)} %get-tuple-element.387), channel_id=1, source_target_pairs={{0,3},{1,0},{2,1},{3,2},{4,7},{5,4},{6,5},{7,6},{8,11},{9,8},{10,9... | collective-permute-start | bytes 516104 | tf_op jit(solution)/shard_map/ppermute | solution.py:976
  215.1 7.8 %collective-permute-start.55 = (bf16[1,96,768]{2,1,0:T(8,128)(2,1)S(1)}, bf16[1,96,768]{2,1,0:T(8,128)(2,1)S(1)}, u32[]{:S(2)}, u32[]{:S(2)}) collective-permute-start(bf16[1,96,768]{2,1,0:T(8,128)(2,1)S(1)} %get-tuple-element.404.refs_0_), channel_id=1, source_target_pairs={{0,24},{4,28},{8,16},{12,20},{16,8},{20,12},{24,0},{28,4},{1,25},{... | collective-permute-start | bytes 442376 | tf_op jit(solution)/shard_map/ppermute | solution.py:970
  216.3 9.1 %collective-permute-start.54 = (bf16[1,96,768]{2,1,0:T(8,128)(2,1)S(1)}, bf16[1,96,768]{2,1,0:T(8,128)(2,1)S(1)}, u32[]{:S(2)}, u32[]{:S(2)}) collective-permute-start(bf16[1,96,768]{2,1,0:T(8,128)(2,1)S(1)} %get-tuple-element.404.refs_0_), channel_id=1, source_target_pairs={{0,16},{4,20},{8,24},{12,28},{16,0},{20,4},{24,8},{28,12},{1,17},{... | collective-permute-start | bytes 442376 | tf_op jit(solution)/shard_map/ppermute | solution.py:970
  217.4 8.1 %collective-permute-start.53 = (bf16[1,96,768]{2,1,0:T(8,128)(2,1)S(1)}, bf16[1,96,768]{2,1,0:T(8,128)(2,1)S(1)}, u32[]{:S(2)}, u32[]{:S(2)}) collective-permute-start(bf16[1,96,768]{2,1,0:T(8,128)(2,1)S(1)} %get-tuple-element.404.refs_0_), channel_id=1, source_target_pairs={{0,8},{4,12},{8,0},{12,4},{16,24},{20,28},{24,16},{28,20},{1,9},{5... | collective-permute-start | bytes 442376 | tf_op jit(solution)/shard_map/ppermute | solution.py:970
  (39 other events, 334.7 us)
